TPU v7x, 32 devices: a whole 2x2x4 slice. The times are simulated.
32 devices in a mesh: group: 4 (over y, x), dev: 8 (over z, core).
Axes of the slice: x: 2, y: 2, z: 4, core: 2. Of those that a mesh axis runs over, the one named last changes fastest.
Arguments:
- level_set: float32 [512, 8192], P(None, ('group', 'dev')), may hold values from -8 to 8
- speed: float32 [512, 8192], P(None, ('group', 'dev')), may hold values from 0.25 to 1
- peer_slabs: int32 [256, 40], P(('group', 'dev')), may hold values from -1 to 1535, as said below
- region_slabs: int32 [64, 16], P(('group', 'dev')), may hold values from 0 to 511, as said below
- halo_source: int32 [6, 8192], P(None, ('group', 'dev')), may hold values from 0 to 1887, as said below
Outputs:
- offset: float32 [512, 8192], P(None, ('group', 'dev'))
Inputs may be any that keep to these rules, and one draw needn't show every extreme that they name: `peer_slabs`: row (device, e) lists the local slab ids that the device sends to device e of its region, -1 in empty slots. Every device fills all 40 slots of at least one row, and receives 40 slabs from at least one device. `region_slabs`: local slab ids of the leaf faces that border the previous region (row 0) and the next region (row 1). `halo_source`: an entry of the halo table of the column's device; only slots that the sender fills are named.
All inputs are finite; a program needn't handle non-finite values.
Results may differ from a plain program's by a relative error of at most 0.0003.
Values sent between devices are 32-bit elements; how exact they have to be, the bound alone decides.
No kernel may reach another device: no remote copies, remote signals or barrier semaphores. Data moves between devices by JAX's collectives and lax.ppermute only.
A program may use at most 64 MiB of HBM per device.

v0:
```python
import functools

import jax
import jax.numpy as jnp
from jax import lax
from jax.experimental import pallas as pl
from jax.experimental.pallas import tpu as pltpu
from jax.sharding import PartitionSpec as P

OFFSET_STEPS = 2
REDIST_PASSES = 2

advect_scale = 0.3
relax_scale = 0.3
weno_floor = 1e-06

LANES = 128


class Plan:
    def __init__(self, count, peers, slots, border, layers):
        self.count = count
        self.peers = peers
        self.slots = slots
        self.border = border
        self.layers = layers
        self.halves = count // LANES
        self.local_tiles = 6 * self.halves
        self.groups = 8 * layers
        self.per_tile = LANES // slots
        self.peer_tiles = -(-peers // self.per_tile)
        used = (peers - (self.peer_tiles - 1) * self.per_tile) * slots
        if used + 2 * border <= LANES:
            self.border_tile = self.peer_tiles - 1
            self.border_lane = used
        else:
            self.border_tile = self.peer_tiles
            self.border_lane = 0
        self.far_tiles = self.border_tile + 1
        self.pieces = min(LANES // slots, self.groups)
        self.piece_groups = -(-self.groups // self.pieces)
        self.border_pieces = min(LANES // border, self.groups)
        self.border_groups = -(-self.groups // self.border_pieces)

    def message(self):
        return (self.peers, 8 * self.piece_groups, LANES)

    def border_message(self):
        return (8 * self.border_groups, LANES)


def lane_ids():
    return lax.broadcasted_iota(jnp.int32, (8, LANES), 1)


def turn(block, shift):
    shift = shift % LANES
    return block if shift == 0 else pltpu.roll(block, shift, 1)


def in_block(lanes, start, size):
    return jnp.logical_and(lanes >= start, lanes < start + size)


def half(h):
    return pl.ds(h * LANES, LANES)


def rows8(start):
    return pl.ds(pl.multiple_of(start, 8), 8)


def bits_of(tile, tiles):
    return [(tile & (1 << b)) != 0 for b in range(max(tiles - 1, 1).bit_length())]


def pick_tile(values, masks):
    def pick(lowest, bit):
        if bit < 0:
            return values(lowest)
        first = pick(lowest, bit - 1)
        if lowest + (1 << bit) >= values.count:
            return first
        return jnp.where(masks[bit], pick(lowest + (1 << bit), bit - 1), first)

    return pick(0, len(masks) - 1)


class Taken:
    def __init__(self, sources, lane):
        self.sources = sources
        self.lane = lane
        self.count = len(sources)

    def __call__(self, tile):
        return jnp.take_along_axis(
            self.sources[tile], self.lane, axis=1, mode="promise_in_bounds"
        )


def gather(sources, code):
    return pick_tile(Taken(sources, code & (LANES - 1)), bits_of(code >> 7, len(sources)))


def local_sources(plan, phi, ends, g):
    w = plan.layers
    if w == 1:
        along_y = g * 64
    else:
        along_y = (g // w) * 64 + lax.rem(g, w) * 8
    starts = [g * 8, (8 - w) * 64 + g * 8, along_y, along_y + (8 - w) * 8]
    found = []
    for start in starts:
        for h in range(plan.halves):
            found.append(phi[h, rows8(start), :])
    for end in range(2):
        for h in range(plan.halves):
            if w == 1:
                found.append(phi[h, pl.ds(g * 64 + 7 * end, 8, stride=8), :])
            else:
                found.append(ends[end, h, rows8(g * 8), :])
    return found


def fill_ends(plan, phi, ends):
    w = plan.layers
    if w == 1:
        return

    @pl.loop(0, 8)
    def _(i):
        for end in range(2):
            for l in range(w):
                k = l + end * (8 - w)
                for h in range(plan.halves):
                    ends[end, h, pl.ds(i * 8 * w + l, 8, stride=w), :] = phi[
                        h, pl.ds(i * 64 + k, 8, stride=8), :
                    ]


def pack_sends(plan, phi, ends, send_code, table, outgoing, low, high):
    lanes = lane_ids()
    w = plan.layers

    @pl.loop(0, plan.groups)
    def _(g):
        sources = local_sources(plan, phi, ends, g)
        for t in range(plan.far_tiles):
            code = jnp.broadcast_to(send_code[pl.ds(t, 1), :], (8, LANES))
            table[t, rows8(g * 8), :] = gather(sources, code)

    for e in range(plan.peers):
        t, eq = divmod(e, plan.per_tile)
        for gi in range(plan.piece_groups):
            block = None
            for p in range(plan.pieces):
                g = p * plan.piece_groups + gi
                if g >= plan.groups:
                    continue
                part = turn(table[t, pl.ds(g * 8, 8), :], (p - eq) * plan.slots)
                if block is None:
                    block = part
                else:
                    block = jnp.where(lanes >= p * plan.slots, part, block)
            outgoing[e, pl.ds(gi * 8, 8), :] = block
    for side, target in enumerate((low, high)):
        for gi in range(plan.border_groups):
            block = None
            for p in range(plan.border_pieces):
                g = p * plan.border_groups + gi
                if g >= plan.groups:
                    continue
                part = turn(
                    table[plan.border_tile, pl.ds(g * 8, 8), :],
                    (p - side) * plan.border - plan.border_lane,
                )
                if block is None:
                    block = part
                else:
                    block = jnp.where(lanes >= p * plan.border, part, block)
            target[pl.ds(gi * 8, 8), :] = block


def unpack_far(plan, arrived, before, after, table):
    lanes = lane_ids()
    for g in range(plan.groups):
        p, gi = divmod(g, plan.piece_groups)
        bp, bgi = divmod(g, plan.border_groups)
        for t in range(plan.far_tiles):
            block = None
            if t < plan.peer_tiles:
                for eq in range(min(plan.per_tile, plan.peers - t * plan.per_tile)):
                    e = t * plan.per_tile + eq
                    part = turn(arrived[e, pl.ds(gi * 8, 8), :], (eq - p) * plan.slots)
                    if block is None:
                        block = part
                    else:
                        block = jnp.where(lanes >= eq * plan.slots, part, block)
            if t == plan.border_tile:
                for q, source in enumerate((before, after)):
                    start = plan.border_lane + q * plan.border
                    part = turn(source[pl.ds(bgi * 8, 8), :], start - bp * plan.border)
                    if block is None:
                        block = part
                    else:
                        block = jnp.where(lanes >= start, part, block)
            table[t, pl.ds(g * 8, 8), :] = block


def pull_local(plan, phi, ends, halo_code, halos):
    @pl.loop(0, plan.groups)
    def _(g):
        sources = local_sources(plan, phi, ends, g)
        for s in range(6):
            for h in range(plan.halves):
                code = jnp.broadcast_to(halo_code[pl.ds(s, 1), half(h)], (8, LANES))
                halos[s, h, rows8(g * 8), :] = gather(sources, code)


def pull_far(plan, table, halo_code, near, halos):
    start = plan.local_tiles * LANES

    @pl.loop(0, plan.groups)
    def _(g):
        sources = [table[t, rows8(g * 8), :] for t in range(plan.far_tiles)]
        for s in range(6):
            for h in range(plan.halves):
                code = jnp.broadcast_to(halo_code[pl.ds(s, 1), half(h)], (8, LANES))
                far = gather(sources, code - start)
                here = near[s, h, rows8(g * 8), :]
                halos[s, h, rows8(g * 8), :] = jnp.where(code >= start, far, here)


def weno_line(q):
    first = [q[m + 1] - q[m] for m in range(13)]
    second = [first[m + 1] - first[m] for m in range(12)]
    third = [second[m + 1] - second[m] for m in range(11)]
    fourth = [(third[m] - third[m + 1]) * (1.0 / 3.0) for m in range(10)]
    bend = [t * t * (4.0 / 3.0) + weno_floor for t in third]
    backward, negated = [], []
    for m in range(9):
        s1, s2 = second[m + 1], second[m + 2]
        a = bend[m] + s1 * (s1 + third[m])
        b = bend[m + 1] + s1 * s2
        c = bend[m + 2] + s2 * (s2 - third[m + 2])
        a, b, c = a * a, b * b, c * c
        x = b * c
        z = a * b
        total = x + z + 6.0 * (a * c)
        xu = x * fourth[m]
        zu = z * fourth[m + 1]
        slope = s1 + s2
        middle = first[m + 2] + third[m + 1] * (1.0 / 12.0)
        if m < 8:
            fix = (xu + 1.5 * zu) * pl.reciprocal(total + 2.0 * z, approx=True)
            backward.append(middle + 0.25 * slope + fix)
        if m > 0:
            fix = (zu + 1.5 * xu) * pl.reciprocal(total + 2.0 * x, approx=True)
            negated.append(fix + 0.25 * slope - middle)
    found = []
    for n in range(8):
        steep = jnp.maximum(jnp.maximum(backward[n], negated[n]), 0.0)
        found.append(steep * steep)
    return found


def advect(plan, phi, speed, halos, squares, moved, sign):
    w = plan.layers
    for h in range(plan.halves):
        at = half(h)

        @pl.loop(0, 8)
        def _(i):
            line = [halos[4, h, pl.ds(i * 8 * w + l, 8, stride=w), :] for l in range(w)]
            line += [phi[h, pl.ds(i * 64 + k, 8, stride=8), :] for k in range(8)]
            line += [halos[5, h, pl.ds(i * 8 * w + l, 8, stride=w), :] for l in range(w)]
            for k, value in enumerate(weno_line(line)):
                squares[pl.ds(i * 64 + k, 8, stride=8), :] = value
            line = [halos[2, h, rows8((i * w + l) * 8), :] for l in range(w)]
            line += [phi[h, rows8(i * 64 + j * 8), :] for j in range(8)]
            line += [halos[3, h, rows8((i * w + l) * 8), :] for l in range(w)]
            for j, value in enumerate(weno_line(line)):
                squares[rows8(i * 64 + j * 8), :] += value

        @pl.loop(0, 8)
        def _(j):
            line = [halos[0, h, rows8((l * 8 + j) * 8), :] for l in range(w)]
            line += [phi[h, rows8(i * 64 + j * 8), :] for i in range(8)]
            line += [halos[1, h, rows8((l * 8 + j) * 8), :] for l in range(w)]
            for i, value in enumerate(weno_line(line)):
                here = rows8(i * 64 + j * 8)
                total = squares[here, :] + value
                value = line[w + i] - advect_scale * speed[here, at] * jnp.sqrt(total)
                moved[h, here, :] = value
                sign[h, here, :] = value * lax.rsqrt(value * value + 1.0)


def relax(plan, phi, sign, halos, moved, joined):
    row = lax.broadcasted_iota(jnp.int32, (8, LANES), 0)
    for h in range(plan.halves):
        at = half(h)

        def plane(i, previous, following):
            centre = [phi[h, rows8(i * 64 + j * 8), :] for j in range(8)]
            along_y = [halos[2, h, rows8(i * 8), :]] + centre + [halos[3, h, rows8(i * 8), :]]
            for j in range(8):
                here = rows8(i * 64 + j * 8)
                value = centre[j]
                sense = sign[h, here, :]
                facing = jnp.where(sense > 0.0, 1.0, -1.0)
                first = jnp.broadcast_to(halos[4, h, pl.ds(i * 8 + j, 1), :], (8, LANES))
                last = jnp.broadcast_to(halos[5, h, pl.ds(i * 8 + j, 1), :], (8, LANES))
                low_z = jnp.where(row == 0, first, pltpu.roll(value, 1, 0))
                high_z = jnp.where(row == 7, last, pltpu.roll(value, 7, 0))
                pairs = (
                    (previous(j), following(j)),
                    (along_y[j], along_y[j + 2]),
                    (low_z, high_z),
                )
                total = None
                for low, high in pairs:
                    steep = jnp.maximum((value - low) * facing, (value - high) * facing)
                    steep = jnp.maximum(steep, 0.0)
                    steep = steep * steep
                    total = steep if total is None else total + steep
                value = value - relax_scale * sense * (jnp.sqrt(total) - 1.0)
                if joined:
                    moved[here, at] = value
                else:
                    moved[h, here, :] = value

        def inner(i, j):
            return phi[h, rows8(i * 64 + j * 8), :]

        plane(0, lambda j: halos[0, h, pl.ds(j * 8, 8), :], lambda j: inner(1, j))

        @pl.loop(1, 7)
        def _(i):
            plane(i, lambda j: inner(i - 1, j), lambda j: inner(i + 1, j))

        plane(7, lambda j: inner(6, j), lambda j: halos[1, h, pl.ds(j * 8, 8), :])


def first_kernel(
    plan, level_set, peer_slabs, region_slabs, halo_source,
    phi, outgoing, low, high, send_code, halo_code, ends, table, padded, peer, region, entries, ready,
):
    copies = [
        pltpu.make_async_copy(source, target, ready.at[n])
        for n, (source, target) in enumerate(
            ((peer_slabs, peer), (region_slabs, region), (halo_source, entries))
        )
    ]
    for h in range(plan.halves):
        copies.append(
            pltpu.make_async_copy(level_set.at[:, half(h)], phi.at[h], ready.at[3 + h])
        )
    for copy in copies:
        copy.start()
    for copy in copies:
        copy.wait()
    lanes = lane_ids()
    padded[...] = jnp.zeros_like(padded)
    padded[pl.ds(0, plan.peers), pl.ds(0, plan.slots)] = jnp.maximum(peer[...], 0)
    padded[pl.ds(plan.peers, 2), pl.ds(0, plan.border)] = region[...]

    def wide(row):
        return jnp.broadcast_to(padded[pl.ds(row, 1), :], (8, LANES))

    send_code[...] = jnp.zeros_like(send_code)
    for t in range(plan.far_tiles):
        block = jnp.zeros((8, LANES), jnp.int32)
        if t < plan.peer_tiles:
            for eq in range(min(plan.per_tile, plan.peers - t * plan.per_tile)):
                part = turn(wide(t * plan.per_tile + eq), eq * plan.slots)
                block = jnp.where(in_block(lanes, eq * plan.slots, plan.slots), part, block)
        if t == plan.border_tile:
            for side in range(2):
                start = plan.border_lane + side * plan.border
                part = turn(wide(plan.peers + side), start)
                block = jnp.where(in_block(lanes, start, plan.border), part, block)
        send_code[pl.ds(t, 1), :] = block[0:1]

    entry = entries[...]
    far = entry - plan.local_tiles * LANES
    tile_span = plan.per_tile * plan.slots
    tile = jnp.zeros_like(entry)
    for k in range(1, plan.peer_tiles):
        tile += (far >= k * tile_span).astype(jnp.int32)
    code = (plan.local_tiles + tile) * LANES + far - tile * tile_span
    edge = far - plan.peers * plan.slots
    edge_code = (plan.local_tiles + plan.border_tile) * LANES + plan.border_lane + edge
    code = jnp.where(edge >= 0, edge_code, code)
    halo_code[...] = jnp.where(far >= 0, code, entry)

    fill_ends(plan, phi, ends)
    pack_sends(plan, phi, ends, send_code, table, outgoing, low, high)


def near_kernel(plan, phi, halo_code, near, ends):
    fill_ends(plan, phi, ends)
    pull_local(plan, phi, ends, halo_code, near)


def advect_kernel(
    plan, sends, phi, near, speed, arrived, before, after, send_code, halo_code,
    moved, sign, outgoing, low, high, ends, table, halos, squares,
):
    unpack_far(plan, arrived, before, after, table)
    pull_far(plan, table, halo_code, near, halos)
    advect(plan, phi, speed, halos, squares, moved, sign)
    pack_sends(sends, moved, ends, send_code, table, outgoing, low, high)


def relax_kernel(plan, sends, phi, near, sign, arrived, before, after, send_code, halo_code, *rest):
    if sends is None:
        (moved, ends, table, halos) = rest
    else:
        (moved, outgoing, low, high, ends, table, halos) = rest
    unpack_far(plan, arrived, before, after, table)
    pull_far(plan, table, halo_code, near, halos)
    relax(plan, phi, sign, halos, moved, sends is None)
    if sends is not None:
        fill_ends(sends, moved, ends)
        pack_sends(sends, moved, ends, send_code, table, outgoing, low, high)


def f32(shape):
    return jax.ShapeDtypeStruct(shape, jnp.float32)


def call(kernel, out_shape, scratch, flops, *operands, space=pltpu.VMEM):
    whole = pl.BlockSpec(memory_space=pltpu.VMEM)
    size = sum(x.size * 4 for x in operands) + sum(x.size * 4 for x in out_shape)
    return pl.pallas_call(
        kernel,
        out_shape=out_shape,
        in_specs=[pl.BlockSpec(memory_space=space)] * len(operands),
        out_specs=[whole] * len(out_shape),
        scratch_shapes=scratch,
        cost_estimate=pl.CostEstimate(flops=flops, bytes_accessed=size, transcendentals=0),
        compiler_params=pltpu.CompilerParams(vmem_limit_bytes=8 * 1024 * 1024),
    )(*operands)


def exchange(outgoing, low, high):
    count = lax.axis_size("group")
    up = [(i, (i + 1) % count) for i in range(count)]
    down = [(target, source) for source, target in up]
    arrived = lax.all_to_all(outgoing, "dev", split_axis=0, concat_axis=0, tiled=True)
    before = lax.ppermute(high, "group", up)
    after = lax.ppermute(low, "group", down)
    return arrived, before, after


def per_device(level_set, speed, peer_slabs, region_slabs, halo_source):
    rows, count = level_set.shape
    peers, slots = peer_slabs.shape
    border = region_slabs.shape[1]
    wide = Plan(count, peers, slots, border, 3)
    thin = Plan(count, peers, slots, border, 1)
    code_rows = -(-wide.far_tiles // 8) * 8

    def ends(plan):
        return pltpu.VMEM((2, wide.halves, 64 * plan.layers, LANES), jnp.float32)

    def table(plan):
        return pltpu.VMEM((plan.far_tiles, 64 * plan.layers, LANES), jnp.float32)

    def halos(plan):
        return pltpu.VMEM((6, wide.halves, 64 * plan.layers, LANES), jnp.float32)

    def sent(plan):
        return [f32(plan.message()), f32(plan.border_message()), f32(plan.border_message())]

    field = f32((wide.halves, rows, LANES))
    pad_rows = -(-(peers + 2) // 8) * 8
    phi, *message, send_code, halo_code = call(
        functools.partial(first_kernel, wide),
        [field]
        + sent(wide)
        + [
            jax.ShapeDtypeStruct((code_rows, LANES), jnp.int32),
            jax.ShapeDtypeStruct(halo_source.shape, jnp.int32),
        ],
        [
            ends(wide),
            table(wide),
            pltpu.VMEM((pad_rows, LANES), jnp.int32),
            pltpu.VMEM(peer_slabs.shape, jnp.int32),
            pltpu.VMEM(region_slabs.shape, jnp.int32),
            pltpu.VMEM(halo_source.shape, jnp.int32),
            pltpu.SemaphoreType.DMA((3 + wide.halves,)),
        ],
        1000000,
        *(
            pltpu.with_memory_space_constraint(x, pltpu.HBM)
            for x in (level_set, peer_slabs, region_slabs, halo_source)
        ),
        space=pltpu.HBM,
    )

    def near_halos(plan, phi):
        return call(
            functools.partial(near_kernel, plan),
            [f32((6, plan.halves, 64 * plan.layers, LANES))],
            [ends(plan)],
            rows * count * 100 * plan.layers,
            phi, halo_code,
        )[0]

    for offset_step in range(OFFSET_STEPS):
        phi, sign, *message = call(
            functools.partial(advect_kernel, wide, thin),
            [field, field] + sent(thin),
            [ends(wide), table(wide), halos(wide), pltpu.VMEM((rows, LANES), jnp.float32)],
            rows * count * 300,
            phi, near_halos(wide, phi), speed, *exchange(*message), send_code, halo_code,
        )
        for redist_pass in range(REDIST_PASSES):
            if redist_pass < REDIST_PASSES - 1:
                sends = thin
            elif offset_step < OFFSET_STEPS - 1:
                sends = wide
            else:
                sends = None
            largest = thin if sends is None else sends
            phi, *message = call(
                functools.partial(relax_kernel, thin, sends),
                [f32((rows, count))] if sends is None else [field] + sent(sends),
                [ends(largest), table(largest), halos(thin)],
                rows * count * 60,
                phi, near_halos(thin, phi), sign, *exchange(*message), send_code, halo_code,
            )
    return phi


def solution(mesh):
    return jax.shard_map(
        per_device,
        mesh=mesh,
        in_specs=(
            P(None, ("group", "dev")),
            P(None, ("group", "dev")),
            P(("group", "dev"), None),
            P(("group", "dev"), None),
            P(None, ("group", "dev")),
        ),
        out_specs=P(None, ("group", "dev")),
        check_vma=False,
    )
```

profile of v0, /device:TPU:0, one launch (start us, length us, event | category | flops | bytes accessed | tf_op | source)
XLA Modules:
  0.0 121.3 jit_solution(1457159513091445130)
XLA Ops:
  0.0 5.3 %shard_map.55 = (f32[2,512,128]{2,1,0:T(8,128)S(1)}, f32[8,64,128]{2,1,0:T(8,128)}, f32[24,128]{1,0:T(8,128)S(1)}, f32[24,128]{1,0:T(8,128)S(1)}, s32[8,128]{1,0:T(8,128)S(1)}, /*index=5*/s32[6,256]{1,0:T(8,128)S(1)}) custom-call(f32[512,256]{1,0:T(8,128)} %level_set.1, s32[8,40]{1,0:T(8,128)} %peer_slabs.1, s32[2,16]{1,0:T(2,128)} %region_slabs.1, ...), custom_call_target="tpu_custom_call" | custom-call | flops 1000000 | bytes 1353088 | tf_op jit(solution)/shard_map/pallas_call | solution.py:435
  5.3 6.5 %all-to-all-start = ((f32[8,64,128]{2,1,0:T(8,128)}), f32[8,64,128]{2,1,0:T(8,128)S(1)}, u32[]{:S(2)}, u32[]{:S(2)}) async-start(f32[8,64,128]{2,1,0:T(8,128)} %get-tuple-element.35), calls=%async_computation | async-start | bytes 524288 | tf_op jit(solution)/shard_map/all_to_all | solution.py:450
  11.7 1.5 %collective-permute-start = (f32[24,128]{1,0:T(8,128)S(1)}, f32[24,128]{1,0:T(8,128)S(1)}, u32[]{:S(2)}, u32[]{:S(2)}) collective-permute-start(f32[24,128]{1,0:T(8,128)S(1)} %get-tuple-element.36), channel_id=1, source_target_pairs={{0,8},{8,16},{16,24},{24,0},{1,9},{9,17},{17,25},{25,1},{2,10},{10... | collective-permute-start | bytes 36872 | tf_op jit(solution)/shard_map/ppermute | solution.py:451
  13.2 1.4 %collective-permute-start.1 = (f32[24,128]{1,0:T(8,128)S(1)}, f32[24,128]{1,0:T(8,128)S(1)}, u32[]{:S(2)}, u32[]{:S(2)}) collective-permute-start(f32[24,128]{1,0:T(8,128)S(1)} %get-tuple-element.37), channel_id=1, source_target_pairs={{8,0},{16,8},{24,16},{0,24},{9,1},{17,9},{25,17},{1,25},{10,2},{18... | collective-permute-start | bytes 36872 | tf_op jit(solution)/shard_map/ppermute | solution.py:452
  14.7 6.5 %shard_map.56.near = f32[6,2,192,128]{3,2,1,0:T(8,128)S(1)} custom-call(f32[2,512,128]{2,1,0:T(8,128)S(1)} %get-tuple-element.33.phi, s32[6,256]{1,0:T(8,128)S(1)} %get-tuple-element.34.halo_code), custom_call_target="tpu_custom_call" | custom-call | flops 39321600 | bytes 1710080 | tf_op jit(solution)/shard_map/pallas_call | solution.py:435
  23.8 8.8 %shard_map.57 = (f32[2,512,128]{2,1,0:T(8,128)S(1)}, f32[2,512,128]{2,1,0:T(8,128)S(1)}, f32[8,24,128]{2,1,0:T(8,128)S(1)}, f32[8,128]{1,0:T(8,128)S(1)}, f32[8,128]{1,0:T(8,128)S(1)}) custom-call(f32[2,512,128]{2,1,0:T(8,128)S(1)} %get-tuple-element.33.phi, f32[6,2,192,128]{3,2,1,0:T(8,128)S(1)} %shard_map.56.near, f32[512,256]{1,0:T(8,128)S(1)} %copy-done, ...), custom_call_target="tpu_custom_call" | custom-call | flops 39321600 | bytes 3680256 | tf_op jit(solution)/shard_map/pallas_call | solution.py:435
  33.9 5.1 %all-to-all-start.1 = ((f32[8,24,128]{2,1,0:T(8,128)}), f32[8,24,128]{2,1,0:T(8,128)S(1)}, u32[]{:S(2)}, u32[]{:S(2)}) async-start(f32[8,24,128]{2,1,0:T(8,128)} %copy-done.1), calls=%async_computation.1 | async-start | bytes 196608 | tf_op jit(solution)/shard_map/all_to_all | solution.py:450
  39.6 2.3 %collective-permute-start.3 = (f32[8,128]{1,0:T(8,128)S(1)}, f32[8,128]{1,0:T(8,128)S(1)}, u32[]{:S(2)}, u32[]{:S(2)}) collective-permute-start(f32[8,128]{1,0:T(8,128)S(1)} %get-tuple-element.43), channel_id=1, source_target_pairs={{8,0},{16,8},{24,16},{0,24},{9,1},{17,9},{25,17},{1,25},{10,2},{18... | collective-permute-start | bytes 12296 | tf_op jit(solution)/shard_map/ppermute | solution.py:452
  41.9 2.1 %shard_map.58.near = f32[6,2,64,128]{3,2,1,0:T(8,128)S(1)} custom-call(f32[2,512,128]{2,1,0:T(8,128)S(1)} %get-tuple-element.39.phi, s32[6,256]{1,0:T(8,128)S(1)} %get-tuple-element.34.halo_code), custom_call_target="tpu_custom_call" | custom-call | flops 13107200 | bytes 923648 | tf_op jit(solution)/shard_map/pallas_call | solution.py:435
  44.1 1.3 %all-to-all-done.1.arrived = f32[8,24,128]{2,1,0:T(8,128)S(1)} async-done(((f32[8,24,128]{2,1,0:T(8,128)}), f32[8,24,128]{2,1,0:T(8,128)S(1)}, u32[]{:S(2)}, u32[]{:S(2)}) %all-to-all-start.1) | async-done | bytes 98336 | tf_op jit(solution)/shard_map/all_to_all | solution.py:450
  45.3 4.0 %shard_map.59 = (f32[2,512,128]{2,1,0:T(8,128)S(1)}, f32[8,24,128]{2,1,0:T(8,128)}, f32[8,128]{1,0:T(8,128)S(1)}, f32[8,128]{1,0:T(8,128)S(1)}) custom-call(f32[2,512,128]{2,1,0:T(8,128)S(1)} %get-tuple-element.39.phi, f32[6,2,64,128]{3,2,1,0:T(8,128)S(1)} %shard_map.58.near, f32[2,512,128]{2,1,0:T(8,128)S(1)} %get-tuple-element.40.sign, ...), custom_call_target="tpu_custom_call" | custom-call | flops 7864320 | bytes 2189312 | tf_op jit(solution)/shard_map/pallas_call | solution.py:435
  49.3 3.8 %all-to-all-start.2 = ((f32[8,24,128]{2,1,0:T(8,128)}), f32[8,24,128]{2,1,0:T(8,128)S(1)}, u32[]{:S(2)}, u32[]{:S(2)}) async-start(f32[8,24,128]{2,1,0:T(8,128)} %get-tuple-element.45), calls=%async_computation.2 | async-start | bytes 196608 | tf_op jit(solution)/shard_map/all_to_all | solution.py:450
  53.1 2.4 %collective-permute-start.4 = (f32[8,128]{1,0:T(8,128)S(1)}, f32[8,128]{1,0:T(8,128)S(1)}, u32[]{:S(2)}, u32[]{:S(2)}) collective-permute-start(f32[8,128]{1,0:T(8,128)S(1)} %get-tuple-element.46), channel_id=1, source_target_pairs={{0,8},{8,16},{16,24},{24,0},{1,9},{9,17},{17,25},{25,1},{2,10},{10... | collective-permute-start | bytes 12296 | tf_op jit(solution)/shard_map/ppermute | solution.py:451
  56.1 2.1 %shard_map.60.near = f32[6,2,64,128]{3,2,1,0:T(8,128)S(1)} custom-call(f32[2,512,128]{2,1,0:T(8,128)S(1)} %get-tuple-element.44.phi, s32[6,256]{1,0:T(8,128)S(1)} %get-tuple-element.34.halo_code), custom_call_target="tpu_custom_call" | custom-call | flops 13107200 | bytes 923648 | tf_op jit(solution)/shard_map/pallas_call | solution.py:435
  58.2 1.0 collective-permute-done.5.after
  59.5 6.3 %shard_map.61 = (f32[2,512,128]{2,1,0:T(8,128)S(1)}, f32[8,64,128]{2,1,0:T(8,128)}, f32[24,128]{1,0:T(8,128)}, f32[24,128]{1,0:T(8,128)}) custom-call(f32[2,512,128]{2,1,0:T(8,128)S(1)} %get-tuple-element.44.phi, f32[6,2,64,128]{3,2,1,0:T(8,128)S(1)} %shard_map.60.near, f32[2,512,128]{2,1,0:T(8,128)S(1)} %get-tuple-element.40.sign, ...), custom_call_target="tpu_custom_call" | custom-call | flops 7864320 | bytes 2369536 | tf_op jit(solution)/shard_map/pallas_call | solution.py:435
  65.8 4.8 %all-to-all-start.3 = ((f32[8,64,128]{2,1,0:T(8,128)}), f32[8,64,128]{2,1,0:T(8,128)S(1)}, u32[]{:S(2)}, u32[]{:S(2)}) async-start(f32[8,64,128]{2,1,0:T(8,128)} %get-tuple-element.49), calls=%async_computation.3 | async-start | bytes 524288 | tf_op jit(solution)/shard_map/all_to_all | solution.py:450
  70.5 1.5 %collective-permute-start.6 = (f32[24,128]{1,0:T(8,128)}, f32[24,128]{1,0:T(8,128)S(1)}, u32[]{:S(2)}, u32[]{:S(2)}) collective-permute-start(f32[24,128]{1,0:T(8,128)} %get-tuple-element.50), channel_id=1, source_target_pairs={{0,8},{8,16},{16,24},{24,0},{1,9},{9,17},{17,25},{25,1},{2,10},{10... | collective-permute-start | bytes 36872 | tf_op jit(solution)/shard_map/ppermute | solution.py:451
  72.0 1.5 %collective-permute-start.7 = (f32[24,128]{1,0:T(8,128)}, f32[24,128]{1,0:T(8,128)S(1)}, u32[]{:S(2)}, u32[]{:S(2)}) collective-permute-start(f32[24,128]{1,0:T(8,128)} %get-tuple-element.51), channel_id=1, source_target_pairs={{8,0},{16,8},{24,16},{0,24},{9,1},{17,9},{25,17},{1,25},{10,2},{18... | collective-permute-start | bytes 36872 | tf_op jit(solution)/shard_map/ppermute | solution.py:452
  73.5 6.5 %shard_map.62.near = f32[6,2,192,128]{3,2,1,0:T(8,128)S(1)} custom-call(f32[2,512,128]{2,1,0:T(8,128)S(1)} %get-tuple-element.48.phi, s32[6,256]{1,0:T(8,128)S(1)} %get-tuple-element.34.halo_code), custom_call_target="tpu_custom_call" | custom-call | flops 39321600 | bytes 1710080 | tf_op jit(solution)/shard_map/pallas_call | solution.py:435
  82.6 8.8 %shard_map.63 = (f32[2,512,128]{2,1,0:T(8,128)S(1)}, f32[2,512,128]{2,1,0:T(8,128)S(1)}, f32[8,24,128]{2,1,0:T(8,128)S(1)}, f32[8,128]{1,0:T(8,128)S(1)}, f32[8,128]{1,0:T(8,128)S(1)}) custom-call(f32[2,512,128]{2,1,0:T(8,128)S(1)} %get-tuple-element.48.phi, f32[6,2,192,128]{3,2,1,0:T(8,128)S(1)} %shard_map.62.near, f32[512,256]{1,0:T(8,128)S(1)} %copy-done, ...), custom_call_target="tpu_custom_call" | custom-call | flops 39321600 | bytes 3680256 | tf_op jit(solution)/shard_map/pallas_call | solution.py:435
  92.7 5.1 %all-to-all-start.4 = ((f32[8,24,128]{2,1,0:T(8,128)}), f32[8,24,128]{2,1,0:T(8,128)S(1)}, u32[]{:S(2)}, u32[]{:S(2)}) async-start(f32[8,24,128]{2,1,0:T(8,128)} %copy-done.2), calls=%async_computation.4 | async-start | bytes 196608 | tf_op jit(solution)/shard_map/all_to_all | solution.py:450
  98.4 2.4 %collective-permute-start.9 = (f32[8,128]{1,0:T(8,128)S(1)}, f32[8,128]{1,0:T(8,128)S(1)}, u32[]{:S(2)}, u32[]{:S(2)}) collective-permute-start(f32[8,128]{1,0:T(8,128)S(1)} %get-tuple-element.56), channel_id=1, source_target_pairs={{8,0},{16,8},{24,16},{0,24},{9,1},{17,9},{25,17},{1,25},{10,2},{18... | collective-permute-start | bytes 12296 | tf_op jit(solution)/shard_map/ppermute | solution.py:452
  100.7 2.1 %shard_map.64.near = f32[6,2,64,128]{3,2,1,0:T(8,128)S(1)} custom-call(f32[2,512,128]{2,1,0:T(8,128)S(1)} %get-tuple-element.52.phi, s32[6,256]{1,0:T(8,128)S(1)} %get-tuple-element.34.halo_code), custom_call_target="tpu_custom_call" | custom-call | flops 13107200 | bytes 923648 | tf_op jit(solution)/shard_map/pallas_call | solution.py:435
  102.8 1.3 %all-to-all-done.4.arrived = f32[8,24,128]{2,1,0:T(8,128)S(1)} async-done(((f32[8,24,128]{2,1,0:T(8,128)}), f32[8,24,128]{2,1,0:T(8,128)S(1)}, u32[]{:S(2)}, u32[]{:S(2)}) %all-to-all-start.4) | async-done | bytes 98336 | tf_op jit(solution)/shard_map/all_to_all | solution.py:450
  104.1 4.0 %shard_map.65 = (f32[2,512,128]{2,1,0:T(8,128)S(1)}, f32[8,24,128]{2,1,0:T(8,128)}, f32[8,128]{1,0:T(8,128)S(1)}, f32[8,128]{1,0:T(8,128)S(1)}) custom-call(f32[2,512,128]{2,1,0:T(8,128)S(1)} %get-tuple-element.52.phi, f32[6,2,64,128]{3,2,1,0:T(8,128)S(1)} %shard_map.64.near, f32[2,512,128]{2,1,0:T(8,128)S(1)} %get-tuple-element.53.sign, ...), custom_call_target="tpu_custom_call" | custom-call | flops 7864320 | bytes 2189312 | tf_op jit(solution)/shard_map/pallas_call | solution.py:435
  108.1 3.8 %all-to-all-start.5 = ((f32[8,24,128]{2,1,0:T(8,128)}), f32[8,24,128]{2,1,0:T(8,128)S(1)}, u32[]{:S(2)}, u32[]{:S(2)}) async-start(f32[8,24,128]{2,1,0:T(8,128)} %get-tuple-element.58), calls=%async_computation.5 | async-start | bytes 196608 | tf_op jit(solution)/shard_map/all_to_all | solution.py:450
  111.9 1.5 %collective-permute-start.10 = (f32[8,128]{1,0:T(8,128)S(1)}, f32[8,128]{1,0:T(8,128)S(1)}, u32[]{:S(2)}, u32[]{:S(2)}) collective-permute-start(f32[8,128]{1,0:T(8,128)S(1)} %get-tuple-element.59), channel_id=1, source_target_pairs={{0,8},{8,16},{16,24},{24,0},{1,9},{9,17},{17,25},{25,1},{2,10},{10... | collective-permute-start | bytes 12296 | tf_op jit(solution)/shard_map/ppermute | solution.py:451
  113.4 1.5 %collective-permute-start.11 = (f32[8,128]{1,0:T(8,128)S(1)}, f32[8,128]{1,0:T(8,128)S(1)}, u32[]{:S(2)}, u32[]{:S(2)}) collective-permute-start(f32[8,128]{1,0:T(8,128)S(1)} %get-tuple-element.60), channel_id=1, source_target_pairs={{8,0},{16,8},{24,16},{0,24},{9,1},{17,9},{25,17},{1,25},{10,2},{18... | collective-permute-start | bytes 12296 | tf_op jit(solution)/shard_map/ppermute | solution.py:452
  114.9 2.1 %shard_map.66.near = f32[6,2,64,128]{3,2,1,0:T(8,128)S(1)} custom-call(f32[2,512,128]{2,1,0:T(8,128)S(1)} %get-tuple-element.57.phi, s32[6,256]{1,0:T(8,128)S(1)} %get-tuple-element.34.halo_code), custom_call_target="tpu_custom_call" | custom-call | flops 13107200 | bytes 923648 | tf_op jit(solution)/shard_map/pallas_call | solution.py:435
  117.0 1.3 %all-to-all-done.5.arrived = f32[8,24,128]{2,1,0:T(8,128)S(1)} async-done(((f32[8,24,128]{2,1,0:T(8,128)}), f32[8,24,128]{2,1,0:T(8,128)S(1)}, u32[]{:S(2)}, u32[]{:S(2)}) %all-to-all-start.5) | async-done | bytes 98336 | tf_op jit(solution)/shard_map/all_to_all | solution.py:450
  118.3 3.0 %shard_map.67 = f32[512,256]{1,0:T(8,128)} custom-call(f32[2,512,128]{2,1,0:T(8,128)S(1)} %get-tuple-element.57.phi, f32[6,2,64,128]{3,2,1,0:T(8,128)S(1)} %shard_map.66.near, f32[2,512,128]{2,1,0:T(8,128)S(1)} %get-tuple-element.53.sign, f32[8,24,128]{2,1,0:T(8,128)S(1)} %all-to-all-done.5.arrived, f32[8,128]{1,0:T(8,128)S(1)} %collective-permute-done.10.before, ...), custom_call_target="tpu_custom_call" | custom-call | flops 7864320 | bytes 2082816 | tf_op jit(solution)/shard_map/pallas_call | solution.py:435
  (43 shorter events, 9.7 us)
Async XLA Ops:
  5.3 17.2 %copy-start = (f32[512,256]{1,0:T(8,128)S(1)}, f32[512,256]{1,0:T(8,128)}, u32[]{:S(2)}) copy-start(f32[512,256]{1,0:T(8,128)} %speed.3) | copy-start | bytes 1572868
  5.3 17.1 %all-to-all-start = ((f32[8,64,128]{2,1,0:T(8,128)}), f32[8,64,128]{2,1,0:T(8,128)S(1)}, u32[]{:S(2)}, u32[]{:S(2)}) async-start(f32[8,64,128]{2,1,0:T(8,128)} %get-tuple-element.35), calls=%async_computation | async-start | bytes 524288 | tf_op jit(solution)/shard_map/all_to_all | solution.py:450
  11.7 9.5 %collective-permute-start = (f32[24,128]{1,0:T(8,128)S(1)}, f32[24,128]{1,0:T(8,128)S(1)}, u32[]{:S(2)}, u32[]{:S(2)}) collective-permute-start(f32[24,128]{1,0:T(8,128)S(1)} %get-tuple-element.36), channel_id=1, source_target_pairs={{0,8},{8,16},{16,24},{24,0},{1,9},{9,17},{17,25},{25,1},{2,10},{10... | collective-permute-start | bytes 36872 | tf_op jit(solution)/shard_map/ppermute | solution.py:451
  13.2 8.6 %collective-permute-start.1 = (f32[24,128]{1,0:T(8,128)S(1)}, f32[24,128]{1,0:T(8,128)S(1)}, u32[]{:S(2)}, u32[]{:S(2)}) collective-permute-start(f32[24,128]{1,0:T(8,128)S(1)} %get-tuple-element.37), channel_id=1, source_target_pairs={{8,0},{16,8},{24,16},{0,24},{9,1},{17,9},{25,17},{1,25},{10,2},{18... | collective-permute-start | bytes 36872 | tf_op jit(solution)/shard_map/ppermute | solution.py:452
  21.2 0.6 copy-start.3
  21.8 0.6 copy-start.7
  22.4 0.7 copy-start.4
  23.1 0.7 copy-start.8
  32.7 0.6 copy-start.1
  33.3 0.6 copy-start.11
  33.9 11.4 %all-to-all-start.1 = ((f32[8,24,128]{2,1,0:T(8,128)}), f32[8,24,128]{2,1,0:T(8,128)S(1)}, u32[]{:S(2)}, u32[]{:S(2)}) async-start(f32[8,24,128]{2,1,0:T(8,128)} %copy-done.1), calls=%async_computation.1 | async-start | bytes 196608 | tf_op jit(solution)/shard_map/all_to_all | solution.py:450
  39.0 5.0 %collective-permute-start.2 = (f32[8,128]{1,0:T(8,128)}, f32[8,128]{1,0:T(8,128)S(1)}, u32[]{:S(2)}, u32[]{:S(2)}) collective-permute-start(f32[8,128]{1,0:T(8,128)} %copy-done.11), channel_id=1, source_target_pairs={{0,8},{8,16},{16,24},{24,0},{1,9},{9,17},{17,25},{25,1},{2,10},{10... | collective-permute-start | bytes 12296 | tf_op jit(solution)/shard_map/ppermute | solution.py:451
  39.6 4.5 %collective-permute-start.3 = (f32[8,128]{1,0:T(8,128)S(1)}, f32[8,128]{1,0:T(8,128)S(1)}, u32[]{:S(2)}, u32[]{:S(2)}) collective-permute-start(f32[8,128]{1,0:T(8,128)S(1)} %get-tuple-element.43), channel_id=1, source_target_pairs={{8,0},{16,8},{24,16},{0,24},{9,1},{17,9},{25,17},{1,25},{10,2},{18... | collective-permute-start | bytes 12296 | tf_op jit(solution)/shard_map/ppermute | solution.py:452
  49.3 10.2 %all-to-all-start.2 = ((f32[8,24,128]{2,1,0:T(8,128)}), f32[8,24,128]{2,1,0:T(8,128)S(1)}, u32[]{:S(2)}, u32[]{:S(2)}) async-start(f32[8,24,128]{2,1,0:T(8,128)} %get-tuple-element.45), calls=%async_computation.2 | async-start | bytes 196608 | tf_op jit(solution)/shard_map/all_to_all | solution.py:450
  53.1 5.0 %collective-permute-start.4 = (f32[8,128]{1,0:T(8,128)S(1)}, f32[8,128]{1,0:T(8,128)S(1)}, u32[]{:S(2)}, u32[]{:S(2)}) collective-permute-start(f32[8,128]{1,0:T(8,128)S(1)} %get-tuple-element.46), channel_id=1, source_target_pairs={{0,8},{8,16},{16,24},{24,0},{1,9},{9,17},{17,25},{25,1},{2,10},{10... | collective-permute-start | bytes 12296 | tf_op jit(solution)/shard_map/ppermute | solution.py:451
  55.6 3.6 %collective-permute-start.5 = (f32[8,128]{1,0:T(8,128)S(1)}, f32[8,128]{1,0:T(8,128)S(1)}, u32[]{:S(2)}, u32[]{:S(2)}) collective-permute-start(f32[8,128]{1,0:T(8,128)S(1)} %get-tuple-element.47), channel_id=1, source_target_pairs={{8,0},{16,8},{24,16},{0,24},{9,1},{17,9},{25,17},{1,25},{10,2},{18... | collective-permute-start | bytes 12296 | tf_op jit(solution)/shard_map/ppermute | solution.py:452
  65.8 15.5 %all-to-all-start.3 = ((f32[8,64,128]{2,1,0:T(8,128)}), f32[8,64,128]{2,1,0:T(8,128)S(1)}, u32[]{:S(2)}, u32[]{:S(2)}) async-start(f32[8,64,128]{2,1,0:T(8,128)} %get-tuple-element.49), calls=%async_computation.3 | async-start | bytes 524288 | tf_op jit(solution)/shard_map/all_to_all | solution.py:450
  70.5 9.5 %collective-permute-start.6 = (f32[24,128]{1,0:T(8,128)}, f32[24,128]{1,0:T(8,128)S(1)}, u32[]{:S(2)}, u32[]{:S(2)}) collective-permute-start(f32[24,128]{1,0:T(8,128)} %get-tuple-element.50), channel_id=1, source_target_pairs={{0,8},{8,16},{16,24},{24,0},{1,9},{9,17},{17,25},{25,1},{2,10},{10... | collective-permute-start | bytes 36872 | tf_op jit(solution)/shard_map/ppermute | solution.py:451
  72.0 8.6 %collective-permute-start.7 = (f32[24,128]{1,0:T(8,128)}, f32[24,128]{1,0:T(8,128)S(1)}, u32[]{:S(2)}, u32[]{:S(2)}) collective-permute-start(f32[24,128]{1,0:T(8,128)} %get-tuple-element.51), channel_id=1, source_target_pairs={{8,0},{16,8},{24,16},{0,24},{9,1},{17,9},{25,17},{1,25},{10,2},{18... | collective-permute-start | bytes 36872 | tf_op jit(solution)/shard_map/ppermute | solution.py:452
  80.0 0.6 copy-start.5
  80.6 0.6 copy-start.9
  81.2 0.7 copy-start.6
  81.9 0.7 copy-start.10
  91.5 0.6 copy-start.2
  92.1 0.6 copy-start.12
  92.7 11.4 %all-to-all-start.4 = ((f32[8,24,128]{2,1,0:T(8,128)}), f32[8,24,128]{2,1,0:T(8,128)S(1)}, u32[]{:S(2)}, u32[]{:S(2)}) async-start(f32[8,24,128]{2,1,0:T(8,128)} %copy-done.2), calls=%async_computation.4 | async-start | bytes 196608 | tf_op jit(solution)/shard_map/all_to_all | solution.py:450
  97.8 5.0 %collective-permute-start.8 = (f32[8,128]{1,0:T(8,128)}, f32[8,128]{1,0:T(8,128)S(1)}, u32[]{:S(2)}, u32[]{:S(2)}) collective-permute-start(f32[8,128]{1,0:T(8,128)} %copy-done.12), channel_id=1, source_target_pairs={{0,8},{8,16},{16,24},{24,0},{1,9},{9,17},{17,25},{25,1},{2,10},{10... | collective-permute-start | bytes 12296 | tf_op jit(solution)/shard_map/ppermute | solution.py:451
  98.4 4.5 %collective-permute-start.9 = (f32[8,128]{1,0:T(8,128)S(1)}, f32[8,128]{1,0:T(8,128)S(1)}, u32[]{:S(2)}, u32[]{:S(2)}) collective-permute-start(f32[8,128]{1,0:T(8,128)S(1)} %get-tuple-element.56), channel_id=1, source_target_pairs={{8,0},{16,8},{24,16},{0,24},{9,1},{17,9},{25,17},{1,25},{10,2},{18... | collective-permute-start | bytes 12296 | tf_op jit(solution)/shard_map/ppermute | solution.py:452
  108.1 10.2 %all-to-all-start.5 = ((f32[8,24,128]{2,1,0:T(8,128)}), f32[8,24,128]{2,1,0:T(8,128)S(1)}, u32[]{:S(2)}, u32[]{:S(2)}) async-start(f32[8,24,128]{2,1,0:T(8,128)} %get-tuple-element.58), calls=%async_computation.5 | async-start | bytes 196608 | tf_op jit(solution)/shard_map/all_to_all | solution.py:450
  111.9 5.0 %collective-permute-start.10 = (f32[8,128]{1,0:T(8,128)S(1)}, f32[8,128]{1,0:T(8,128)S(1)}, u32[]{:S(2)}, u32[]{:S(2)}) collective-permute-start(f32[8,128]{1,0:T(8,128)S(1)} %get-tuple-element.59), channel_id=1, source_target_pairs={{0,8},{8,16},{16,24},{24,0},{1,9},{9,17},{17,25},{25,1},{2,10},{10... | collective-permute-start | bytes 12296 | tf_op jit(solution)/shard_map/ppermute | solution.py:451
  113.4 3.6 %collective-permute-start.11 = (f32[8,128]{1,0:T(8,128)S(1)}, f32[8,128]{1,0:T(8,128)S(1)}, u32[]{:S(2)}, u32[]{:S(2)}) collective-permute-start(f32[8,128]{1,0:T(8,128)S(1)} %get-tuple-element.60), channel_id=1, source_target_pairs={{8,0},{16,8},{24,16},{0,24},{9,1},{17,9},{25,17},{1,25},{10,2},{18... | collective-permute-start | bytes 12296 | tf_op jit(solution)/shard_map/ppermute | solution.py:452
where the time goes:
time: 122 us; the launch traced here: 121 us
  Pallas kernels  61.6 us (50%)
  starting transfers between devices  46.7 us (38%)
  local copies, waits for them, and re-layouts  7.68 us (6%)
  waiting for transfers between devices  5.18 us (4%)
    pallas_call x13, Pallas kernels, call(): pl.pallas_call(kernel, out_shape=out_shape, in_specs=[pl.BlockSpec(memory...  61.6 us
    all_to_all x6, starting transfers between devices, exchange(): lax.all_to_all(outgoing, 'dev', split_axis=0, concat_axis=0, tiled=True)  29.1 us
    ppermute x6, starting transfers between devices, exchange(): after = lax.ppermute(low, 'group', down)  9.56 us
    ppermute x6, starting transfers between devices, exchange(): before = lax.ppermute(high, 'group', up)  7.99 us
    unnamed x26, local copies, waits for them, and re-layouts  7.68 us
    all_to_all x6, waiting for transfers between devices, exchange(): lax.all_to_all(outgoing, 'dev', split_axis=0, concat_axis=0, tiled=True)  4.16 us
  transfers between devices with their start and end apart: 18, of which 5 were waited for; matrix products, arithmetic and copies ran while one was open for 0% of the time, Pallas kernels for 18%

commit v1 on v0

--- a/solution.py
+++ b/solution.py
@@ -149,62 +149,72 @@
             code = jnp.broadcast_to(send_code[pl.ds(t, 1), :], (8, LANES))
             table[t, rows8(g * 8), :] = gather(sources, code)
 
-    for e in range(plan.peers):
-        t, eq = divmod(e, plan.per_tile)
-        for gi in range(plan.piece_groups):
+    last = plan.groups - 1
+
+    @pl.loop(0, plan.piece_groups)
+    def _(gi):
+        for e in range(plan.peers):
+            t, eq = divmod(e, plan.per_tile)
             block = None
             for p in range(plan.pieces):
-                g = p * plan.piece_groups + gi
-                if g >= plan.groups:
-                    continue
-                part = turn(table[t, pl.ds(g * 8, 8), :], (p - eq) * plan.slots)
+                g = jnp.minimum(p * plan.piece_groups + gi, last)
+                part = turn(table[t, rows8(g * 8), :], (p - eq) * plan.slots)
                 if block is None:
                     block = part
                 else:
                     block = jnp.where(lanes >= p * plan.slots, part, block)
-            outgoing[e, pl.ds(gi * 8, 8), :] = block
-    for side, target in enumerate((low, high)):
-        for gi in range(plan.border_groups):
+            outgoing[e, rows8(gi * 8), :] = block
+
+    @pl.loop(0, plan.border_groups)
+    def _(gi):
+        for side, target in enumerate((low, high)):
             block = None
             for p in range(plan.border_pieces):
-                g = p * plan.border_groups + gi
-                if g >= plan.groups:
-                    continue
+                g = jnp.minimum(p * plan.border_groups + gi, last)
                 part = turn(
-                    table[plan.border_tile, pl.ds(g * 8, 8), :],
+                    table[plan.border_tile, rows8(g * 8), :],
                     (p - side) * plan.border - plan.border_lane,
                 )
                 if block is None:
                     block = part
                 else:
                     block = jnp.where(lanes >= p * plan.border, part, block)
-            target[pl.ds(gi * 8, 8), :] = block
+            target[rows8(gi * 8), :] = block
 
 
 def unpack_far(plan, arrived, before, after, table):
     lanes = lane_ids()
-    for g in range(plan.groups):
-        p, gi = divmod(g, plan.piece_groups)
-        bp, bgi = divmod(g, plan.border_groups)
-        for t in range(plan.far_tiles):
-            block = None
-            if t < plan.peer_tiles:
+    for p in range(plan.pieces):
+        first = p * plan.piece_groups
+
+        @pl.loop(0, max(min(plan.piece_groups, plan.groups - first), 0))
+        def _(gi):
+            for t in range(plan.peer_tiles):
+                block = None
                 for eq in range(min(plan.per_tile, plan.peers - t * plan.per_tile)):
-                    e = t * plan.per_tile + eq
-                    part = turn(arrived[e, pl.ds(gi * 8, 8), :], (eq - p) * plan.slots)
+                    source = arrived[t * plan.per_tile + eq, rows8(gi * 8), :]
+                    part = turn(source, (eq - p) * plan.slots)
                     if block is None:
                         block = part
                     else:
                         block = jnp.where(lanes >= eq * plan.slots, part, block)
-            if t == plan.border_tile:
-                for q, source in enumerate((before, after)):
-                    start = plan.border_lane + q * plan.border
-                    part = turn(source[pl.ds(bgi * 8, 8), :], start - bp * plan.border)
-                    if block is None:
-                        block = part
-                    else:
-                        block = jnp.where(lanes >= start, part, block)
-            table[t, pl.ds(g * 8, 8), :] = block
+                table[t, rows8((first + gi) * 8), :] = block
+
+    for p in range(plan.border_pieces):
+        first = p * plan.border_groups
+
+        @pl.loop(0, max(min(plan.border_groups, plan.groups - first), 0))
+        def _(gi):
+            here = rows8((first + gi) * 8)
+            if plan.border_tile < plan.peer_tiles:
+                block = table[plan.border_tile, here, :]
+            else:
+                block = jnp.zeros((8, LANES), jnp.float32)
+            for q, source in enumerate((before, after)):
+                start = plan.border_lane + q * plan.border
+                part = turn(source[rows8(gi * 8), :], start - p * plan.border)
+                block = jnp.where(lanes >= start, part, block)
+            table[plan.border_tile, here, :] = block
 
 
 def pull_local(plan, phi, ends, halo_code, halos):
@@ -264,81 +274,84 @@
     return found
 
 
-def advect(plan, phi, speed, halos, squares, moved, sign):
+def advect(plan, phi, speed, ready, halos, squares, moved):
     w = plan.layers
-    for h in range(plan.halves):
-        at = half(h)
-
-        @pl.loop(0, 8)
-        def _(i):
-            line = [halos[4, h, pl.ds(i * 8 * w + l, 8, stride=w), :] for l in range(w)]
-            line += [phi[h, pl.ds(i * 64 + k, 8, stride=8), :] for k in range(8)]
-            line += [halos[5, h, pl.ds(i * 8 * w + l, 8, stride=w), :] for l in range(w)]
-            for k, value in enumerate(weno_line(line)):
-                squares[pl.ds(i * 64 + k, 8, stride=8), :] = value
-            line = [halos[2, h, rows8((i * w + l) * 8), :] for l in range(w)]
-            line += [phi[h, rows8(i * 64 + j * 8), :] for j in range(8)]
-            line += [halos[3, h, rows8((i * w + l) * 8), :] for l in range(w)]
-            for j, value in enumerate(weno_line(line)):
-                squares[rows8(i * 64 + j * 8), :] += value
-
-        @pl.loop(0, 8)
-        def _(j):
-            line = [halos[0, h, rows8((l * 8 + j) * 8), :] for l in range(w)]
-            line += [phi[h, rows8(i * 64 + j * 8), :] for i in range(8)]
-            line += [halos[1, h, rows8((l * 8 + j) * 8), :] for l in range(w)]
-            for i, value in enumerate(weno_line(line)):
-                here = rows8(i * 64 + j * 8)
-                total = squares[here, :] + value
-                value = line[w + i] - advect_scale * speed[here, at] * jnp.sqrt(total)
+
+    @pl.loop(0, 8 * plan.halves)
+    def _(q):
+        h, i = q >> 3, q & 7
+        line = [halos[4, h, pl.ds(i * 8 * w + l, 8, stride=w), :] for l in range(w)]
+        line += [phi[h, pl.ds(i * 64 + k, 8, stride=8), :] for k in range(8)]
+        line += [halos[5, h, pl.ds(i * 8 * w + l, 8, stride=w), :] for l in range(w)]
+        for k, value in enumerate(weno_line(line)):
+            squares[h, pl.ds(i * 64 + k, 8, stride=8), :] = value
+        line = [halos[2, h, rows8((i * w + l) * 8), :] for l in range(w)]
+        line += [phi[h, rows8(i * 64 + j * 8), :] for j in range(8)]
+        line += [halos[3, h, rows8((i * w + l) * 8), :] for l in range(w)]
+        for j, value in enumerate(weno_line(line)):
+            squares[h, rows8(i * 64 + j * 8), :] += value
+
+    ready()
+
+    @pl.loop(0, 8 * plan.halves)
+    def _(q):
+        h, j = q >> 3, q & 7
+        line = [halos[0, h, rows8((l * 8 + j) * 8), :] for l in range(w)]
+        line += [phi[h, rows8(i * 64 + j * 8), :] for i in range(8)]
+        line += [halos[1, h, rows8((l * 8 + j) * 8), :] for l in range(w)]
+        for i, value in enumerate(weno_line(line)):
+            here = rows8(i * 64 + j * 8)
+            total = squares[h, here, :] + value
+            change = advect_scale * speed[h, here, :] * jnp.sqrt(total)
+            moved[h, here, :] = line[w + i] - change
+
+
+def steepness(value, low, high, facing):
+    steep = jnp.maximum((value - low) * facing, (value - high) * facing)
+    steep = jnp.maximum(steep, 0.0)
+    return steep * steep
+
+
+def relax(plan, phi, origin, halos, squares, moved, joined):
+    @pl.loop(0, 8 * plan.halves)
+    def _(q):
+        h, i = q >> 3, q & 7
+        line = [halos[4, h, rows8(i * 8), :]]
+        line += [phi[h, pl.ds(i * 64 + k, 8, stride=8), :] for k in range(8)]
+        line += [halos[5, h, rows8(i * 8), :]]
+        for k in range(8):
+            here = pl.ds(i * 64 + k, 8, stride=8)
+            facing = jnp.where(origin[h, here, :] > 0.0, 1.0, -1.0)
+            squares[h, here, :] = steepness(line[k + 1], line[k], line[k + 2], facing)
+
+    @pl.loop(0, 8 * plan.halves)
+    def _(q):
+        h, j = q >> 3, q & 7
+        line = [halos[0, h, rows8(j * 8), :]]
+        line += [phi[h, rows8(i * 64 + j * 8), :] for i in range(8)]
+        line += [halos[1, h, rows8(j * 8), :]]
+        for i in range(8):
+            here = rows8(i * 64 + j * 8)
+            facing = jnp.where(origin[h, here, :] > 0.0, 1.0, -1.0)
+            squares[h, here, :] += steepness(line[i + 1], line[i], line[i + 2], facing)
+
+    @pl.loop(0, 8 * plan.halves)
+    def _(q):
+        h, i = q >> 3, q & 7
+        line = [halos[2, h, rows8(i * 8), :]]
+        line += [phi[h, rows8(i * 64 + j * 8), :] for j in range(8)]
+        line += [halos[3, h, rows8(i * 8), :]]
+        for j in range(8):
+            here = rows8(i * 64 + j * 8)
+            start = origin[h, here, :]
+            facing = jnp.where(start > 0.0, 1.0, -1.0)
+            total = squares[h, here, :] + steepness(line[j + 1], line[j], line[j + 2], facing)
+            sign = start * lax.rsqrt(start * start + 1.0)
+            value = line[j + 1] - relax_scale * sign * (jnp.sqrt(total) - 1.0)
+            if joined:
+                moved[here, pl.ds(pl.multiple_of(h * LANES, LANES), LANES)] = value
+            else:
                 moved[h, here, :] = value
-                sign[h, here, :] = value * lax.rsqrt(value * value + 1.0)
-
-
-def relax(plan, phi, sign, halos, moved, joined):
-    row = lax.broadcasted_iota(jnp.int32, (8, LANES), 0)
-    for h in range(plan.halves):
-        at = half(h)
-
-        def plane(i, previous, following):
-            centre = [phi[h, rows8(i * 64 + j * 8), :] for j in range(8)]
-            along_y = [halos[2, h, rows8(i * 8), :]] + centre + [halos[3, h, rows8(i * 8), :]]
-            for j in range(8):
-                here = rows8(i * 64 + j * 8)
-                value = centre[j]
-                sense = sign[h, here, :]
-                facing = jnp.where(sense > 0.0, 1.0, -1.0)
-                first = jnp.broadcast_to(halos[4, h, pl.ds(i * 8 + j, 1), :], (8, LANES))
-                last = jnp.broadcast_to(halos[5, h, pl.ds(i * 8 + j, 1), :], (8, LANES))
-                low_z = jnp.where(row == 0, first, pltpu.roll(value, 1, 0))
-                high_z = jnp.where(row == 7, last, pltpu.roll(value, 7, 0))
-                pairs = (
-                    (previous(j), following(j)),
-                    (along_y[j], along_y[j + 2]),
-                    (low_z, high_z),
-                )
-                total = None
-                for low, high in pairs:
-                    steep = jnp.maximum((value - low) * facing, (value - high) * facing)
-                    steep = jnp.maximum(steep, 0.0)
-                    steep = steep * steep
-                    total = steep if total is None else total + steep
-                value = value - relax_scale * sense * (jnp.sqrt(total) - 1.0)
-                if joined:
-                    moved[here, at] = value
-                else:
-                    moved[h, here, :] = value
-
-        def inner(i, j):
-            return phi[h, rows8(i * 64 + j * 8), :]
-
-        plane(0, lambda j: halos[0, h, pl.ds(j * 8, 8), :], lambda j: inner(1, j))
-
-        @pl.loop(1, 7)
-        def _(i):
-            plane(i, lambda j: inner(i - 1, j), lambda j: inner(i + 1, j))
-
-        plane(7, lambda j: inner(6, j), lambda j: halos[1, h, pl.ds(j * 8, 8), :])
 
 
 def first_kernel(
@@ -404,22 +417,35 @@
 
 def advect_kernel(
     plan, sends, phi, near, speed, arrived, before, after, send_code, halo_code,
-    moved, sign, outgoing, low, high, ends, table, halos, squares,
+    moved, outgoing, low, high, ends, table, halos, squares, fast, loaded,
 ):
+    copies = [
+        pltpu.make_async_copy(speed.at[:, half(h)], fast.at[h], loaded.at[h])
+        for h in range(plan.halves)
+    ]
+    for copy in copies:
+        copy.start()
+
+    def ready():
+        for copy in copies:
+            copy.wait()
+
     unpack_far(plan, arrived, before, after, table)
     pull_far(plan, table, halo_code, near, halos)
-    advect(plan, phi, speed, halos, squares, moved, sign)
+    advect(plan, phi, fast, ready, halos, squares, moved)
     pack_sends(sends, moved, ends, send_code, table, outgoing, low, high)
 
 
-def relax_kernel(plan, sends, phi, near, sign, arrived, before, after, send_code, halo_code, *rest):
+def relax_kernel(
+    plan, sends, phi, origin, near, arrived, before, after, send_code, halo_code, *rest
+):
     if sends is None:
-        (moved, ends, table, halos) = rest
+        (moved, table, halos, squares) = rest
     else:
-        (moved, outgoing, low, high, ends, table, halos) = rest
+        (moved, outgoing, low, high, ends, table, halos, squares) = rest
     unpack_far(plan, arrived, before, after, table)
     pull_far(plan, table, halo_code, near, halos)
-    relax(plan, phi, sign, halos, moved, sends is None)
+    relax(plan, phi, origin, halos, squares, moved, sends is None)
     if sends is not None:
         fill_ends(sends, moved, ends)
         pack_sends(sends, moved, ends, send_code, table, outgoing, low, high)
@@ -429,17 +455,22 @@
     return jax.ShapeDtypeStruct(shape, jnp.float32)
 
 
-def call(kernel, out_shape, scratch, flops, *operands, space=pltpu.VMEM):
+def call(kernel, out_shape, scratch, flops, *operands, far=()):
     whole = pl.BlockSpec(memory_space=pltpu.VMEM)
+    apart = pl.BlockSpec(memory_space=pltpu.HBM)
     size = sum(x.size * 4 for x in operands) + sum(x.size * 4 for x in out_shape)
+    operands = [
+        pltpu.with_memory_space_constraint(x, pltpu.HBM) if n in far else x
+        for n, x in enumerate(operands)
+    ]
     return pl.pallas_call(
         kernel,
         out_shape=out_shape,
-        in_specs=[pl.BlockSpec(memory_space=space)] * len(operands),
+        in_specs=[apart if n in far else whole for n in range(len(operands))],
         out_specs=[whole] * len(out_shape),
         scratch_shapes=scratch,
         cost_estimate=pl.CostEstimate(flops=flops, bytes_accessed=size, transcendentals=0),
-        compiler_params=pltpu.CompilerParams(vmem_limit_bytes=8 * 1024 * 1024),
+        compiler_params=pltpu.CompilerParams(vmem_limit_bytes=12 * 1024 * 1024),
     )(*operands)
 
 
@@ -493,11 +524,8 @@
             pltpu.SemaphoreType.DMA((3 + wide.halves,)),
         ],
         1000000,
-        *(
-            pltpu.with_memory_space_constraint(x, pltpu.HBM)
-            for x in (level_set, peer_slabs, region_slabs, halo_source)
-        ),
-        space=pltpu.HBM,
+        level_set, peer_slabs, region_slabs, halo_source,
+        far=(0, 1, 2, 3),
     )
 
     def near_halos(plan, phi):
@@ -509,14 +537,18 @@
             phi, halo_code,
         )[0]
 
+    block = pltpu.VMEM((wide.halves, rows, LANES), jnp.float32)
     for offset_step in range(OFFSET_STEPS):
-        phi, sign, *message = call(
+        phi, *message = call(
             functools.partial(advect_kernel, wide, thin),
-            [field, field] + sent(thin),
-            [ends(wide), table(wide), halos(wide), pltpu.VMEM((rows, LANES), jnp.float32)],
+            [field] + sent(thin),
+            [ends(wide), table(wide), halos(wide), block, block]
+            + [pltpu.SemaphoreType.DMA((wide.halves,))],
             rows * count * 300,
             phi, near_halos(wide, phi), speed, *exchange(*message), send_code, halo_code,
+            far=(2,),
         )
+        origin = phi
         for redist_pass in range(REDIST_PASSES):
             if redist_pass < REDIST_PASSES - 1:
                 sends = thin
@@ -524,13 +556,16 @@
                 sends = wide
             else:
                 sends = None
-            largest = thin if sends is None else sends
+            if sends is None:
+                out, scratch = [f32((rows, count))], [table(thin)]
+            else:
+                out, scratch = [field] + sent(sends), [ends(sends), table(sends)]
             phi, *message = call(
                 functools.partial(relax_kernel, thin, sends),
-                [f32((rows, count))] if sends is None else [field] + sent(sends),
-                [ends(largest), table(largest), halos(thin)],
+                out,
+                scratch + [halos(thin), block],
                 rows * count * 60,
-                phi, near_halos(thin, phi), sign, *exchange(*message), send_code, halo_code,
+                phi, origin, near_halos(thin, phi), *exchange(*message), send_code, halo_code,
             )
     return phi
 

time: 122 us -> 127 us (1.041)
  Pallas kernels: 61.6 us -> 74.6 us
  local copies, waits for them, and re-layouts: 7.68 us -> 0 us
    pallas_call x13, Pallas kernels: 61.6 us -> 74.6 us  [call(): pl.pallas_call(kernel, out_shape=out_shape, in_specs=[apart if n in far e...]
    unnamed x26 -> x0, local copies, waits for them, and re-layouts: 7.68 us -> none
  transfers between devices with their start and end apart: 18 -> 18, of which waited for: 5 -> 7; matrix products, arithmetic and copies ran while one was open for 0% -> 0% of each run, Pallas kernels for 18% -> 17%
where the time goes in v1:
time: 127 us; the launch traced here: 126 us
  Pallas kernels  74.6 us (59%)
  starting transfers between devices  46.1 us (36%)
  waiting for transfers between devices  5.7 us (4%)
    pallas_call x13, Pallas kernels, call(): pl.pallas_call(kernel, out_shape=out_shape, in_specs=[apart if n in far e...  74.6 us
    all_to_all x6, starting transfers between devices, exchange(): lax.all_to_all(outgoing, 'dev', split_axis=0, concat_axis=0, tiled=True)  28.5 us
    ppermute x6, starting transfers between devices, exchange(): after = lax.ppermute(low, 'group', down)  9.56 us
    ppermute x6, starting transfers between devices, exchange(): before = lax.ppermute(high, 'group', up)  7.99 us
    all_to_all x6, waiting for transfers between devices, exchange(): lax.all_to_all(outgoing, 'dev', split_axis=0, concat_axis=0, tiled=True)  4.67 us
  transfers between devices with their start and end apart: 18, of which 7 were waited for; matrix products, arithmetic and copies ran while one was open for 0% of the time, Pallas kernels for 17%

profile of v1, /device:TPU:0, one launch (start us, length us, event | category | flops | bytes accessed | tf_op | source)
XLA Modules:
  0.0 126.5 jit_solution(2909406436945588006)
XLA Ops:
  0.0 5.9 %shard_map.55 = (f32[2,512,128]{2,1,0:T(8,128)S(1)}, f32[8,64,128]{2,1,0:T(8,128)}, f32[24,128]{1,0:T(8,128)S(1)}, f32[24,128]{1,0:T(8,128)S(1)}, s32[8,128]{1,0:T(8,128)S(1)}, /*index=5*/s32[6,256]{1,0:T(8,128)S(1)}) custom-call(f32[512,256]{1,0:T(8,128)} %level_set.1, s32[8,40]{1,0:T(8,128)} %peer_slabs.1, s32[2,16]{1,0:T(2,128)} %region_slabs.1, ...), custom_call_target="tpu_custom_call" | custom-call | flops 1000000 | bytes 1353088 | tf_op jit(solution)/shard_map/pallas_call | solution.py:466
  5.9 6.3 %all-to-all-start = ((f32[8,64,128]{2,1,0:T(8,128)}), f32[8,64,128]{2,1,0:T(8,128)S(1)}, u32[]{:S(2)}, u32[]{:S(2)}) async-start(f32[8,64,128]{2,1,0:T(8,128)} %get-tuple-element.33), calls=%async_computation | async-start | bytes 524288 | tf_op jit(solution)/shard_map/all_to_all | solution.py:481
  12.2 1.5 %collective-permute-start = (f32[24,128]{1,0:T(8,128)S(1)}, f32[24,128]{1,0:T(8,128)S(1)}, u32[]{:S(2)}, u32[]{:S(2)}) collective-permute-start(f32[24,128]{1,0:T(8,128)S(1)} %get-tuple-element.34), channel_id=1, source_target_pairs={{0,8},{8,16},{16,24},{24,0},{1,9},{9,17},{17,25},{25,1},{2,10},{10... | collective-permute-start | bytes 36872 | tf_op jit(solution)/shard_map/ppermute | solution.py:482
  13.7 1.4 %collective-permute-start.1 = (f32[24,128]{1,0:T(8,128)S(1)}, f32[24,128]{1,0:T(8,128)S(1)}, u32[]{:S(2)}, u32[]{:S(2)}) collective-permute-start(f32[24,128]{1,0:T(8,128)S(1)} %get-tuple-element.35), channel_id=1, source_target_pairs={{8,0},{16,8},{24,16},{0,24},{9,1},{17,9},{25,17},{1,25},{10,2},{18... | collective-permute-start | bytes 36872 | tf_op jit(solution)/shard_map/ppermute | solution.py:483
  15.2 6.5 %shard_map.56.near = f32[6,2,192,128]{3,2,1,0:T(8,128)S(1)} custom-call(f32[2,512,128]{2,1,0:T(8,128)S(1)} %get-tuple-element.31.phi, s32[6,256]{1,0:T(8,128)S(1)} %get-tuple-element.32.halo_code), custom_call_target="tpu_custom_call" | custom-call | flops 39321600 | bytes 1710080 | tf_op jit(solution)/shard_map/pallas_call | solution.py:466
  22.0 12.6 %shard_map.57 = (f32[2,512,128]{2,1,0:T(8,128)S(1)}, f32[8,24,128]{2,1,0:T(8,128)}, f32[8,128]{1,0:T(8,128)S(1)}, f32[8,128]{1,0:T(8,128)S(1)}) custom-call(f32[2,512,128]{2,1,0:T(8,128)S(1)} %get-tuple-element.31.phi, f32[6,2,192,128]{3,2,1,0:T(8,128)S(1)} %shard_map.56.near, f32[512,256]{1,0:T(8,128)} %speed.3, f32[8,64,128]{2,1,0:T(8,128)S(1)} %all-to-all-done.arrived, ...), custom_call_target="tpu_custom_call" | custom-call | flops 39321600 | bytes 3155968 | tf_op jit(solution)/shard_map/pallas_call | solution.py:466
  34.6 4.9 %all-to-all-start.1 = ((f32[8,24,128]{2,1,0:T(8,128)}), f32[8,24,128]{2,1,0:T(8,128)S(1)}, u32[]{:S(2)}, u32[]{:S(2)}) async-start(f32[8,24,128]{2,1,0:T(8,128)} %get-tuple-element.38), calls=%async_computation.1 | async-start | bytes 196608 | tf_op jit(solution)/shard_map/all_to_all | solution.py:481
  40.1 2.3 %collective-permute-start.3 = (f32[8,128]{1,0:T(8,128)S(1)}, f32[8,128]{1,0:T(8,128)S(1)}, u32[]{:S(2)}, u32[]{:S(2)}) collective-permute-start(f32[8,128]{1,0:T(8,128)S(1)} %get-tuple-element.40), channel_id=1, source_target_pairs={{8,0},{16,8},{24,16},{0,24},{9,1},{17,9},{25,17},{1,25},{10,2},{18... | collective-permute-start | bytes 12296 | tf_op jit(solution)/shard_map/ppermute | solution.py:483
  42.4 2.1 %shard_map.58.near = f32[6,2,64,128]{3,2,1,0:T(8,128)S(1)} custom-call(f32[2,512,128]{2,1,0:T(8,128)S(1)} %get-tuple-element.37.phi.origin, s32[6,256]{1,0:T(8,128)S(1)} %get-tuple-element.32.halo_code), custom_call_target="tpu_custom_call" | custom-call | flops 13107200 | bytes 923648 | tf_op jit(solution)/shard_map/pallas_call | solution.py:466
  44.5 1.3 %all-to-all-done.1.arrived = f32[8,24,128]{2,1,0:T(8,128)S(1)} async-done(((f32[8,24,128]{2,1,0:T(8,128)}), f32[8,24,128]{2,1,0:T(8,128)S(1)}, u32[]{:S(2)}, u32[]{:S(2)}) %all-to-all-start.1) | async-done | bytes 98336 | tf_op jit(solution)/shard_map/all_to_all | solution.py:481
  45.8 5.1 %shard_map.59 = (f32[2,512,128]{2,1,0:T(8,128)S(1)}, f32[8,24,128]{2,1,0:T(8,128)}, f32[8,128]{1,0:T(8,128)S(1)}, f32[8,128]{1,0:T(8,128)S(1)}) custom-call(f32[2,512,128]{2,1,0:T(8,128)S(1)} %get-tuple-element.37.phi.origin, f32[2,512,128]{2,1,0:T(8,128)S(1)} %get-tuple-element.37.phi.origin, f32[6,2,64,128]{3,2,1,0:T(8,128)S(1)} %shard_map.58.near, ...), custom_call_target="tpu_custom_call" | custom-call | flops 7864320 | bytes 2189312 | tf_op jit(solution)/shard_map/pallas_call | solution.py:466
  50.9 3.8 %all-to-all-start.2 = ((f32[8,24,128]{2,1,0:T(8,128)}), f32[8,24,128]{2,1,0:T(8,128)S(1)}, u32[]{:S(2)}, u32[]{:S(2)}) async-start(f32[8,24,128]{2,1,0:T(8,128)} %get-tuple-element.42), calls=%async_computation.2 | async-start | bytes 196608 | tf_op jit(solution)/shard_map/all_to_all | solution.py:481
  54.7 2.4 %collective-permute-start.4 = (f32[8,128]{1,0:T(8,128)S(1)}, f32[8,128]{1,0:T(8,128)S(1)}, u32[]{:S(2)}, u32[]{:S(2)}) collective-permute-start(f32[8,128]{1,0:T(8,128)S(1)} %get-tuple-element.43), channel_id=1, source_target_pairs={{0,8},{8,16},{16,24},{24,0},{1,9},{9,17},{17,25},{25,1},{2,10},{10... | collective-permute-start | bytes 12296 | tf_op jit(solution)/shard_map/ppermute | solution.py:482
  57.6 2.1 %shard_map.60.near = f32[6,2,64,128]{3,2,1,0:T(8,128)S(1)} custom-call(f32[2,512,128]{2,1,0:T(8,128)S(1)} %get-tuple-element.41.phi, s32[6,256]{1,0:T(8,128)S(1)} %get-tuple-element.32.halo_code), custom_call_target="tpu_custom_call" | custom-call | flops 13107200 | bytes 923648 | tf_op jit(solution)/shard_map/pallas_call | solution.py:466
  59.8 1.0 collective-permute-done.5.after
  61.1 7.9 %shard_map.61 = (f32[2,512,128]{2,1,0:T(8,128)S(1)}, f32[8,64,128]{2,1,0:T(8,128)}, f32[24,128]{1,0:T(8,128)S(1)}, f32[24,128]{1,0:T(8,128)S(1)}) custom-call(f32[2,512,128]{2,1,0:T(8,128)S(1)} %get-tuple-element.41.phi, f32[2,512,128]{2,1,0:T(8,128)S(1)} %get-tuple-element.37.phi.origin, f32[6,2,64,128]{3,2,1,0:T(8,128)S(1)} %shard_map.60.near, ...), custom_call_target="tpu_custom_call" | custom-call | flops 7864320 | bytes 2369536 | tf_op jit(solution)/shard_map/pallas_call | solution.py:466
  68.9 4.8 %all-to-all-start.3 = ((f32[8,64,128]{2,1,0:T(8,128)}), f32[8,64,128]{2,1,0:T(8,128)S(1)}, u32[]{:S(2)}, u32[]{:S(2)}) async-start(f32[8,64,128]{2,1,0:T(8,128)} %get-tuple-element.46), calls=%async_computation.3 | async-start | bytes 524288 | tf_op jit(solution)/shard_map/all_to_all | solution.py:481
  73.7 1.5 %collective-permute-start.6 = (f32[24,128]{1,0:T(8,128)S(1)}, f32[24,128]{1,0:T(8,128)S(1)}, u32[]{:S(2)}, u32[]{:S(2)}) collective-permute-start(f32[24,128]{1,0:T(8,128)S(1)} %get-tuple-element.47), channel_id=1, source_target_pairs={{0,8},{8,16},{16,24},{24,0},{1,9},{9,17},{17,25},{25,1},{2,10},{10... | collective-permute-start | bytes 36872 | tf_op jit(solution)/shard_map/ppermute | solution.py:482
  75.2 1.5 %collective-permute-start.7 = (f32[24,128]{1,0:T(8,128)S(1)}, f32[24,128]{1,0:T(8,128)S(1)}, u32[]{:S(2)}, u32[]{:S(2)}) collective-permute-start(f32[24,128]{1,0:T(8,128)S(1)} %get-tuple-element.48), channel_id=1, source_target_pairs={{8,0},{16,8},{24,16},{0,24},{9,1},{17,9},{25,17},{1,25},{10,2},{18... | collective-permute-start | bytes 36872 | tf_op jit(solution)/shard_map/ppermute | solution.py:483
  76.7 6.5 %shard_map.62.near = f32[6,2,192,128]{3,2,1,0:T(8,128)S(1)} custom-call(f32[2,512,128]{2,1,0:T(8,128)S(1)} %get-tuple-element.45.phi, s32[6,256]{1,0:T(8,128)S(1)} %get-tuple-element.32.halo_code), custom_call_target="tpu_custom_call" | custom-call | flops 39321600 | bytes 1710080 | tf_op jit(solution)/shard_map/pallas_call | solution.py:466
  83.5 12.6 %shard_map.63 = (f32[2,512,128]{2,1,0:T(8,128)S(1)}, f32[8,24,128]{2,1,0:T(8,128)}, f32[8,128]{1,0:T(8,128)S(1)}, f32[8,128]{1,0:T(8,128)S(1)}) custom-call(f32[2,512,128]{2,1,0:T(8,128)S(1)} %get-tuple-element.45.phi, f32[6,2,192,128]{3,2,1,0:T(8,128)S(1)} %shard_map.62.near, f32[512,256]{1,0:T(8,128)} %speed.3, f32[8,64,128]{2,1,0:T(8,128)S(1)} %all-to-all-done.3.arrived, ...), custom_call_target="tpu_custom_call" | custom-call | flops 39321600 | bytes 3155968 | tf_op jit(solution)/shard_map/pallas_call | solution.py:466
  96.1 4.9 %all-to-all-start.4 = ((f32[8,24,128]{2,1,0:T(8,128)}), f32[8,24,128]{2,1,0:T(8,128)S(1)}, u32[]{:S(2)}, u32[]{:S(2)}) async-start(f32[8,24,128]{2,1,0:T(8,128)} %get-tuple-element.50), calls=%async_computation.4 | async-start | bytes 196608 | tf_op jit(solution)/shard_map/all_to_all | solution.py:481
  101.5 2.4 %collective-permute-start.9 = (f32[8,128]{1,0:T(8,128)S(1)}, f32[8,128]{1,0:T(8,128)S(1)}, u32[]{:S(2)}, u32[]{:S(2)}) collective-permute-start(f32[8,128]{1,0:T(8,128)S(1)} %get-tuple-element.52), channel_id=1, source_target_pairs={{8,0},{16,8},{24,16},{0,24},{9,1},{17,9},{25,17},{1,25},{10,2},{18... | collective-permute-start | bytes 12296 | tf_op jit(solution)/shard_map/ppermute | solution.py:483
  103.9 2.1 %shard_map.64.near = f32[6,2,64,128]{3,2,1,0:T(8,128)S(1)} custom-call(f32[2,512,128]{2,1,0:T(8,128)S(1)} %get-tuple-element.49.phi.origin, s32[6,256]{1,0:T(8,128)S(1)} %get-tuple-element.32.halo_code), custom_call_target="tpu_custom_call" | custom-call | flops 13107200 | bytes 923648 | tf_op jit(solution)/shard_map/pallas_call | solution.py:466
  106.0 1.3 %all-to-all-done.4.arrived = f32[8,24,128]{2,1,0:T(8,128)S(1)} async-done(((f32[8,24,128]{2,1,0:T(8,128)}), f32[8,24,128]{2,1,0:T(8,128)S(1)}, u32[]{:S(2)}, u32[]{:S(2)}) %all-to-all-start.4) | async-done | bytes 98336 | tf_op jit(solution)/shard_map/all_to_all | solution.py:481
  107.3 5.1 %shard_map.65 = (f32[2,512,128]{2,1,0:T(8,128)S(1)}, f32[8,24,128]{2,1,0:T(8,128)}, f32[8,128]{1,0:T(8,128)S(1)}, f32[8,128]{1,0:T(8,128)S(1)}) custom-call(f32[2,512,128]{2,1,0:T(8,128)S(1)} %get-tuple-element.49.phi.origin, f32[2,512,128]{2,1,0:T(8,128)S(1)} %get-tuple-element.49.phi.origin, f32[6,2,64,128]{3,2,1,0:T(8,128)S(1)} %shard_map.64.near, ...), custom_call_target="tpu_custom_call" | custom-call | flops 7864320 | bytes 2189312 | tf_op jit(solution)/shard_map/pallas_call | solution.py:466
  112.4 3.8 %all-to-all-start.5 = ((f32[8,24,128]{2,1,0:T(8,128)}), f32[8,24,128]{2,1,0:T(8,128)S(1)}, u32[]{:S(2)}, u32[]{:S(2)}) async-start(f32[8,24,128]{2,1,0:T(8,128)} %get-tuple-element.54), calls=%async_computation.5 | async-start | bytes 196608 | tf_op jit(solution)/shard_map/all_to_all | solution.py:481
  116.2 1.5 %collective-permute-start.10 = (f32[8,128]{1,0:T(8,128)S(1)}, f32[8,128]{1,0:T(8,128)S(1)}, u32[]{:S(2)}, u32[]{:S(2)}) collective-permute-start(f32[8,128]{1,0:T(8,128)S(1)} %get-tuple-element.55), channel_id=1, source_target_pairs={{0,8},{8,16},{16,24},{24,0},{1,9},{9,17},{17,25},{25,1},{2,10},{10... | collective-permute-start | bytes 12296 | tf_op jit(solution)/shard_map/ppermute | solution.py:482
  117.7 1.5 %collective-permute-start.11 = (f32[8,128]{1,0:T(8,128)S(1)}, f32[8,128]{1,0:T(8,128)S(1)}, u32[]{:S(2)}, u32[]{:S(2)}) collective-permute-start(f32[8,128]{1,0:T(8,128)S(1)} %get-tuple-element.56), channel_id=1, source_target_pairs={{8,0},{16,8},{24,16},{0,24},{9,1},{17,9},{25,17},{1,25},{10,2},{18... | collective-permute-start | bytes 12296 | tf_op jit(solution)/shard_map/ppermute | solution.py:483
  119.1 2.1 %shard_map.66.near = f32[6,2,64,128]{3,2,1,0:T(8,128)S(1)} custom-call(f32[2,512,128]{2,1,0:T(8,128)S(1)} %get-tuple-element.53.phi, s32[6,256]{1,0:T(8,128)S(1)} %get-tuple-element.32.halo_code), custom_call_target="tpu_custom_call" | custom-call | flops 13107200 | bytes 923648 | tf_op jit(solution)/shard_map/pallas_call | solution.py:466
  121.3 1.3 %all-to-all-done.5.arrived = f32[8,24,128]{2,1,0:T(8,128)S(1)} async-done(((f32[8,24,128]{2,1,0:T(8,128)}), f32[8,24,128]{2,1,0:T(8,128)S(1)}, u32[]{:S(2)}, u32[]{:S(2)}) %all-to-all-start.5) | async-done | bytes 98336 | tf_op jit(solution)/shard_map/all_to_all | solution.py:481
  122.5 3.9 %shard_map.67 = f32[512,256]{1,0:T(8,128)} custom-call(f32[2,512,128]{2,1,0:T(8,128)S(1)} %get-tuple-element.53.phi, f32[2,512,128]{2,1,0:T(8,128)S(1)} %get-tuple-element.49.phi.origin, f32[6,2,64,128]{3,2,1,0:T(8,128)S(1)} %shard_map.66.near, f32[8,24,128]{2,1,0:T(8,128)S(1)} %all-to-all-done.5.arrived, f32[8,128]{1,0:T(8,128)S(1)} %collective-permute-done.10.before, ...), custom_call_target="tpu_custom_call" | custom-call | flops 7864320 | bytes 2082816 | tf_op jit(solution)/shard_map/pallas_call | solution.py:466
  (17 shorter events, 2.5 us)
Async XLA Ops:
  5.9 16.1 %all-to-all-start = ((f32[8,64,128]{2,1,0:T(8,128)}), f32[8,64,128]{2,1,0:T(8,128)S(1)}, u32[]{:S(2)}, u32[]{:S(2)}) async-start(f32[8,64,128]{2,1,0:T(8,128)} %get-tuple-element.33), calls=%async_computation | async-start | bytes 524288 | tf_op jit(solution)/shard_map/all_to_all | solution.py:481
  12.2 9.5 %collective-permute-start = (f32[24,128]{1,0:T(8,128)S(1)}, f32[24,128]{1,0:T(8,128)S(1)}, u32[]{:S(2)}, u32[]{:S(2)}) collective-permute-start(f32[24,128]{1,0:T(8,128)S(1)} %get-tuple-element.34), channel_id=1, source_target_pairs={{0,8},{8,16},{16,24},{24,0},{1,9},{9,17},{17,25},{25,1},{2,10},{10... | collective-permute-start | bytes 36872 | tf_op jit(solution)/shard_map/ppermute | solution.py:482
  13.7 8.0 %collective-permute-start.1 = (f32[24,128]{1,0:T(8,128)S(1)}, f32[24,128]{1,0:T(8,128)S(1)}, u32[]{:S(2)}, u32[]{:S(2)}) collective-permute-start(f32[24,128]{1,0:T(8,128)S(1)} %get-tuple-element.35), channel_id=1, source_target_pairs={{8,0},{16,8},{24,16},{0,24},{9,1},{17,9},{25,17},{1,25},{10,2},{18... | collective-permute-start | bytes 36872 | tf_op jit(solution)/shard_map/ppermute | solution.py:483
  34.6 11.2 %all-to-all-start.1 = ((f32[8,24,128]{2,1,0:T(8,128)}), f32[8,24,128]{2,1,0:T(8,128)S(1)}, u32[]{:S(2)}, u32[]{:S(2)}) async-start(f32[8,24,128]{2,1,0:T(8,128)} %get-tuple-element.38), calls=%async_computation.1 | async-start | bytes 196608 | tf_op jit(solution)/shard_map/all_to_all | solution.py:481
  39.5 5.0 %collective-permute-start.2 = (f32[8,128]{1,0:T(8,128)S(1)}, f32[8,128]{1,0:T(8,128)S(1)}, u32[]{:S(2)}, u32[]{:S(2)}) collective-permute-start(f32[8,128]{1,0:T(8,128)S(1)} %get-tuple-element.39), channel_id=1, source_target_pairs={{0,8},{8,16},{16,24},{24,0},{1,9},{9,17},{17,25},{25,1},{2,10},{10... | collective-permute-start | bytes 12296 | tf_op jit(solution)/shard_map/ppermute | solution.py:482
  40.1 4.5 %collective-permute-start.3 = (f32[8,128]{1,0:T(8,128)S(1)}, f32[8,128]{1,0:T(8,128)S(1)}, u32[]{:S(2)}, u32[]{:S(2)}) collective-permute-start(f32[8,128]{1,0:T(8,128)S(1)} %get-tuple-element.40), channel_id=1, source_target_pairs={{8,0},{16,8},{24,16},{0,24},{9,1},{17,9},{25,17},{1,25},{10,2},{18... | collective-permute-start | bytes 12296 | tf_op jit(solution)/shard_map/ppermute | solution.py:483
  50.9 10.2 %all-to-all-start.2 = ((f32[8,24,128]{2,1,0:T(8,128)}), f32[8,24,128]{2,1,0:T(8,128)S(1)}, u32[]{:S(2)}, u32[]{:S(2)}) async-start(f32[8,24,128]{2,1,0:T(8,128)} %get-tuple-element.42), calls=%async_computation.2 | async-start | bytes 196608 | tf_op jit(solution)/shard_map/all_to_all | solution.py:481
  54.7 5.0 %collective-permute-start.4 = (f32[8,128]{1,0:T(8,128)S(1)}, f32[8,128]{1,0:T(8,128)S(1)}, u32[]{:S(2)}, u32[]{:S(2)}) collective-permute-start(f32[8,128]{1,0:T(8,128)S(1)} %get-tuple-element.43), channel_id=1, source_target_pairs={{0,8},{8,16},{16,24},{24,0},{1,9},{9,17},{17,25},{25,1},{2,10},{10... | collective-permute-start | bytes 12296 | tf_op jit(solution)/shard_map/ppermute | solution.py:482
  57.1 3.6 %collective-permute-start.5 = (f32[8,128]{1,0:T(8,128)S(1)}, f32[8,128]{1,0:T(8,128)S(1)}, u32[]{:S(2)}, u32[]{:S(2)}) collective-permute-start(f32[8,128]{1,0:T(8,128)S(1)} %get-tuple-element.44), channel_id=1, source_target_pairs={{8,0},{16,8},{24,16},{0,24},{9,1},{17,9},{25,17},{1,25},{10,2},{18... | collective-permute-start | bytes 12296 | tf_op jit(solution)/shard_map/ppermute | solution.py:483
  68.9 14.5 %all-to-all-start.3 = ((f32[8,64,128]{2,1,0:T(8,128)}), f32[8,64,128]{2,1,0:T(8,128)S(1)}, u32[]{:S(2)}, u32[]{:S(2)}) async-start(f32[8,64,128]{2,1,0:T(8,128)} %get-tuple-element.46), calls=%async_computation.3 | async-start | bytes 524288 | tf_op jit(solution)/shard_map/all_to_all | solution.py:481
  73.7 9.5 %collective-permute-start.6 = (f32[24,128]{1,0:T(8,128)S(1)}, f32[24,128]{1,0:T(8,128)S(1)}, u32[]{:S(2)}, u32[]{:S(2)}) collective-permute-start(f32[24,128]{1,0:T(8,128)S(1)} %get-tuple-element.47), channel_id=1, source_target_pairs={{0,8},{8,16},{16,24},{24,0},{1,9},{9,17},{17,25},{25,1},{2,10},{10... | collective-permute-start | bytes 36872 | tf_op jit(solution)/shard_map/ppermute | solution.py:482
  75.2 8.0 %collective-permute-start.7 = (f32[24,128]{1,0:T(8,128)S(1)}, f32[24,128]{1,0:T(8,128)S(1)}, u32[]{:S(2)}, u32[]{:S(2)}) collective-permute-start(f32[24,128]{1,0:T(8,128)S(1)} %get-tuple-element.48), channel_id=1, source_target_pairs={{8,0},{16,8},{24,16},{0,24},{9,1},{17,9},{25,17},{1,25},{10,2},{18... | collective-permute-start | bytes 36872 | tf_op jit(solution)/shard_map/ppermute | solution.py:483
  96.1 11.2 %all-to-all-start.4 = ((f32[8,24,128]{2,1,0:T(8,128)}), f32[8,24,128]{2,1,0:T(8,128)S(1)}, u32[]{:S(2)}, u32[]{:S(2)}) async-start(f32[8,24,128]{2,1,0:T(8,128)} %get-tuple-element.50), calls=%async_computation.4 | async-start | bytes 196608 | tf_op jit(solution)/shard_map/all_to_all | solution.py:481
  101.0 5.0 %collective-permute-start.8 = (f32[8,128]{1,0:T(8,128)S(1)}, f32[8,128]{1,0:T(8,128)S(1)}, u32[]{:S(2)}, u32[]{:S(2)}) collective-permute-start(f32[8,128]{1,0:T(8,128)S(1)} %get-tuple-element.51), channel_id=1, source_target_pairs={{0,8},{8,16},{16,24},{24,0},{1,9},{9,17},{17,25},{25,1},{2,10},{10... | collective-permute-start | bytes 12296 | tf_op jit(solution)/shard_map/ppermute | solution.py:482
  101.5 4.5 %collective-permute-start.9 = (f32[8,128]{1,0:T(8,128)S(1)}, f32[8,128]{1,0:T(8,128)S(1)}, u32[]{:S(2)}, u32[]{:S(2)}) collective-permute-start(f32[8,128]{1,0:T(8,128)S(1)} %get-tuple-element.52), channel_id=1, source_target_pairs={{8,0},{16,8},{24,16},{0,24},{9,1},{17,9},{25,17},{1,25},{10,2},{18... | collective-permute-start | bytes 12296 | tf_op jit(solution)/shard_map/ppermute | solution.py:483
  112.4 10.2 %all-to-all-start.5 = ((f32[8,24,128]{2,1,0:T(8,128)}), f32[8,24,128]{2,1,0:T(8,128)S(1)}, u32[]{:S(2)}, u32[]{:S(2)}) async-start(f32[8,24,128]{2,1,0:T(8,128)} %get-tuple-element.54), calls=%async_computation.5 | async-start | bytes 196608 | tf_op jit(solution)/shard_map/all_to_all | solution.py:481
  116.2 5.0 %collective-permute-start.10 = (f32[8,128]{1,0:T(8,128)S(1)}, f32[8,128]{1,0:T(8,128)S(1)}, u32[]{:S(2)}, u32[]{:S(2)}) collective-permute-start(f32[8,128]{1,0:T(8,128)S(1)} %get-tuple-element.55), channel_id=1, source_target_pairs={{0,8},{8,16},{16,24},{24,0},{1,9},{9,17},{17,25},{25,1},{2,10},{10... | collective-permute-start | bytes 12296 | tf_op jit(solution)/shard_map/ppermute | solution.py:482
  117.7 3.6 %collective-permute-start.11 = (f32[8,128]{1,0:T(8,128)S(1)}, f32[8,128]{1,0:T(8,128)S(1)}, u32[]{:S(2)}, u32[]{:S(2)}) collective-permute-start(f32[8,128]{1,0:T(8,128)S(1)} %get-tuple-element.56), channel_id=1, source_target_pairs={{8,0},{16,8},{24,16},{0,24},{9,1},{17,9},{25,17},{1,25},{10,2},{18... | collective-permute-start | bytes 12296 | tf_op jit(solution)/shard_map/ppermute | solution.py:483

commit v2 on v0

--- a/solution.py
+++ b/solution.py
@@ -264,7 +264,7 @@
     return found
 
 
-def advect(plan, phi, speed, halos, squares, moved, sign):
+def advect(plan, phi, speed, ready, halos, squares, moved):
     w = plan.layers
     for h in range(plan.halves):
         at = half(h)
@@ -282,6 +282,9 @@
             for j, value in enumerate(weno_line(line)):
                 squares[rows8(i * 64 + j * 8), :] += value
 
+        if h == 0:
+            ready()
+
         @pl.loop(0, 8)
         def _(j):
             line = [halos[0, h, rows8((l * 8 + j) * 8), :] for l in range(w)]
@@ -290,12 +293,11 @@
             for i, value in enumerate(weno_line(line)):
                 here = rows8(i * 64 + j * 8)
                 total = squares[here, :] + value
-                value = line[w + i] - advect_scale * speed[here, at] * jnp.sqrt(total)
+                value = line[w + i] - advect_scale * speed[h, here, :] * jnp.sqrt(total)
                 moved[h, here, :] = value
-                sign[h, here, :] = value * lax.rsqrt(value * value + 1.0)
-
-
-def relax(plan, phi, sign, halos, moved, joined):
+
+
+def relax(plan, phi, origin, halos, moved, joined):
     row = lax.broadcasted_iota(jnp.int32, (8, LANES), 0)
     for h in range(plan.halves):
         at = half(h)
@@ -306,8 +308,9 @@
             for j in range(8):
                 here = rows8(i * 64 + j * 8)
                 value = centre[j]
-                sense = sign[h, here, :]
-                facing = jnp.where(sense > 0.0, 1.0, -1.0)
+                start = origin[h, here, :]
+                sense = start * lax.rsqrt(start * start + 1.0)
+                facing = jnp.where(start > 0.0, 1.0, -1.0)
                 first = jnp.broadcast_to(halos[4, h, pl.ds(i * 8 + j, 1), :], (8, LANES))
                 last = jnp.broadcast_to(halos[5, h, pl.ds(i * 8 + j, 1), :], (8, LANES))
                 low_z = jnp.where(row == 0, first, pltpu.roll(value, 1, 0))
@@ -404,22 +407,35 @@
 
 def advect_kernel(
     plan, sends, phi, near, speed, arrived, before, after, send_code, halo_code,
-    moved, sign, outgoing, low, high, ends, table, halos, squares,
+    moved, outgoing, low, high, ends, table, halos, squares, fast, loaded,
 ):
+    copies = [
+        pltpu.make_async_copy(speed.at[:, half(h)], fast.at[h], loaded.at[h])
+        for h in range(plan.halves)
+    ]
+    for copy in copies:
+        copy.start()
+
+    def ready():
+        for copy in copies:
+            copy.wait()
+
     unpack_far(plan, arrived, before, after, table)
     pull_far(plan, table, halo_code, near, halos)
-    advect(plan, phi, speed, halos, squares, moved, sign)
+    advect(plan, phi, fast, ready, halos, squares, moved)
     pack_sends(sends, moved, ends, send_code, table, outgoing, low, high)
 
 
-def relax_kernel(plan, sends, phi, near, sign, arrived, before, after, send_code, halo_code, *rest):
+def relax_kernel(
+    plan, sends, phi, origin, near, arrived, before, after, send_code, halo_code, *rest
+):
     if sends is None:
-        (moved, ends, table, halos) = rest
+        (moved, table, halos) = rest
     else:
         (moved, outgoing, low, high, ends, table, halos) = rest
     unpack_far(plan, arrived, before, after, table)
     pull_far(plan, table, halo_code, near, halos)
-    relax(plan, phi, sign, halos, moved, sends is None)
+    relax(plan, phi, origin, halos, moved, sends is None)
     if sends is not None:
         fill_ends(sends, moved, ends)
         pack_sends(sends, moved, ends, send_code, table, outgoing, low, high)
@@ -429,17 +445,22 @@
     return jax.ShapeDtypeStruct(shape, jnp.float32)
 
 
-def call(kernel, out_shape, scratch, flops, *operands, space=pltpu.VMEM):
+def call(kernel, out_shape, scratch, flops, *operands, far=()):
     whole = pl.BlockSpec(memory_space=pltpu.VMEM)
+    apart = pl.BlockSpec(memory_space=pltpu.HBM)
     size = sum(x.size * 4 for x in operands) + sum(x.size * 4 for x in out_shape)
+    operands = [
+        pltpu.with_memory_space_constraint(x, pltpu.HBM) if n in far else x
+        for n, x in enumerate(operands)
+    ]
     return pl.pallas_call(
         kernel,
         out_shape=out_shape,
-        in_specs=[pl.BlockSpec(memory_space=space)] * len(operands),
+        in_specs=[apart if n in far else whole for n in range(len(operands))],
         out_specs=[whole] * len(out_shape),
         scratch_shapes=scratch,
         cost_estimate=pl.CostEstimate(flops=flops, bytes_accessed=size, transcendentals=0),
-        compiler_params=pltpu.CompilerParams(vmem_limit_bytes=8 * 1024 * 1024),
+        compiler_params=pltpu.CompilerParams(vmem_limit_bytes=12 * 1024 * 1024),
     )(*operands)
 
 
@@ -493,11 +514,8 @@
             pltpu.SemaphoreType.DMA((3 + wide.halves,)),
         ],
         1000000,
-        *(
-            pltpu.with_memory_space_constraint(x, pltpu.HBM)
-            for x in (level_set, peer_slabs, region_slabs, halo_source)
-        ),
-        space=pltpu.HBM,
+        level_set, peer_slabs, region_slabs, halo_source,
+        far=(0, 1, 2, 3),
     )
 
     def near_halos(plan, phi):
@@ -509,14 +527,19 @@
             phi, halo_code,
         )[0]
 
+    block = pltpu.VMEM((wide.halves, rows, LANES), jnp.float32)
     for offset_step in range(OFFSET_STEPS):
-        phi, sign, *message = call(
+        phi, *message = call(
             functools.partial(advect_kernel, wide, thin),
-            [field, field] + sent(thin),
-            [ends(wide), table(wide), halos(wide), pltpu.VMEM((rows, LANES), jnp.float32)],
+            [field] + sent(thin),
+            [ends(wide), table(wide), halos(wide)]
+            + [pltpu.VMEM((rows, LANES), jnp.float32), block]
+            + [pltpu.SemaphoreType.DMA((wide.halves,))],
             rows * count * 300,
             phi, near_halos(wide, phi), speed, *exchange(*message), send_code, halo_code,
+            far=(2,),
         )
+        origin = phi
         for redist_pass in range(REDIST_PASSES):
             if redist_pass < REDIST_PASSES - 1:
                 sends = thin
@@ -524,13 +547,16 @@
                 sends = wide
             else:
                 sends = None
-            largest = thin if sends is None else sends
+            if sends is None:
+                out, scratch = [f32((rows, count))], [table(thin)]
+            else:
+                out, scratch = [field] + sent(sends), [ends(sends), table(sends)]
             phi, *message = call(
                 functools.partial(relax_kernel, thin, sends),
-                [f32((rows, count))] if sends is None else [field] + sent(sends),
-                [ends(largest), table(largest), halos(thin)],
+                out,
+                scratch + [halos(thin)],
                 rows * count * 60,
-                phi, near_halos(thin, phi), sign, *exchange(*message), send_code, halo_code,
+                phi, origin, near_halos(thin, phi), *exchange(*message), send_code, halo_code,
             )
     return phi
 

time: 122 us -> 115 us (0.943)
  local copies, waits for them, and re-layouts: 7.68 us -> 0 us
    unnamed x26 -> x0, local copies, waits for them, and re-layouts: 7.68 us -> none
  transfers between devices with their start and end apart: 18 -> 18, of which waited for: 5 -> 7; matrix products, arithmetic and copies ran while one was open for 0% -> 0% of each run, Pallas kernels for 18% -> 19%
where the time goes in v2:
time: 115 us
  Pallas kernels  62.7 us (55%)
  starting transfers between devices  46.1 us (40%)
  waiting for transfers between devices  5.7 us (5%)
    pallas_call x13, Pallas kernels, call(): pl.pallas_call(kernel, out_shape=out_shape, in_specs=[apart if n in far e...  62.7 us
    all_to_all x6, starting transfers between devices, exchange(): lax.all_to_all(outgoing, 'dev', split_axis=0, concat_axis=0, tiled=True)  28.5 us
    ppermute x6, starting transfers between devices, exchange(): after = lax.ppermute(low, 'group', down)  9.56 us
    ppermute x6, starting transfers between devices, exchange(): before = lax.ppermute(high, 'group', up)  7.99 us
    all_to_all x6, waiting for transfers between devices, exchange(): lax.all_to_all(outgoing, 'dev', split_axis=0, concat_axis=0, tiled=True)  4.67 us
  transfers between devices with their start and end apart: 18, of which 7 were waited for; matrix products, arithmetic and copies ran while one was open for 0% of the time, Pallas kernels for 19%

profile of v2, /device:TPU:0, one launch (start us, length us, event | category | flops | bytes accessed | tf_op | source)
XLA Modules:
  0.0 114.6 jit_solution(8463224059587465955)
XLA Ops:
  0.0 5.3 %shard_map.55 = (f32[2,512,128]{2,1,0:T(8,128)S(1)}, f32[8,64,128]{2,1,0:T(8,128)}, f32[24,128]{1,0:T(8,128)S(1)}, f32[24,128]{1,0:T(8,128)S(1)}, s32[8,128]{1,0:T(8,128)S(1)}, /*index=5*/s32[6,256]{1,0:T(8,128)S(1)}) custom-call(f32[512,256]{1,0:T(8,128)} %level_set.1, s32[8,40]{1,0:T(8,128)} %peer_slabs.1, s32[2,16]{1,0:T(2,128)} %region_slabs.1, ...), custom_call_target="tpu_custom_call" | custom-call | flops 1000000 | bytes 1353088 | tf_op jit(solution)/shard_map/pallas_call | solution.py:456
  5.3 6.3 %all-to-all-start = ((f32[8,64,128]{2,1,0:T(8,128)}), f32[8,64,128]{2,1,0:T(8,128)S(1)}, u32[]{:S(2)}, u32[]{:S(2)}) async-start(f32[8,64,128]{2,1,0:T(8,128)} %get-tuple-element.33), calls=%async_computation | async-start | bytes 524288 | tf_op jit(solution)/shard_map/all_to_all | solution.py:471
  11.6 1.5 %collective-permute-start = (f32[24,128]{1,0:T(8,128)S(1)}, f32[24,128]{1,0:T(8,128)S(1)}, u32[]{:S(2)}, u32[]{:S(2)}) collective-permute-start(f32[24,128]{1,0:T(8,128)S(1)} %get-tuple-element.34), channel_id=1, source_target_pairs={{0,8},{8,16},{16,24},{24,0},{1,9},{9,17},{17,25},{25,1},{2,10},{10... | collective-permute-start | bytes 36872 | tf_op jit(solution)/shard_map/ppermute | solution.py:472
  13.1 1.4 %collective-permute-start.1 = (f32[24,128]{1,0:T(8,128)S(1)}, f32[24,128]{1,0:T(8,128)S(1)}, u32[]{:S(2)}, u32[]{:S(2)}) collective-permute-start(f32[24,128]{1,0:T(8,128)S(1)} %get-tuple-element.35), channel_id=1, source_target_pairs={{8,0},{16,8},{24,16},{0,24},{9,1},{17,9},{25,17},{1,25},{10,2},{18... | collective-permute-start | bytes 36872 | tf_op jit(solution)/shard_map/ppermute | solution.py:473
  14.5 6.5 %shard_map.56.near = f32[6,2,192,128]{3,2,1,0:T(8,128)S(1)} custom-call(f32[2,512,128]{2,1,0:T(8,128)S(1)} %get-tuple-element.31.phi, s32[6,256]{1,0:T(8,128)S(1)} %get-tuple-element.32.halo_code), custom_call_target="tpu_custom_call" | custom-call | flops 39321600 | bytes 1710080 | tf_op jit(solution)/shard_map/pallas_call | solution.py:456
  21.3 9.3 %shard_map.57 = (f32[2,512,128]{2,1,0:T(8,128)S(1)}, f32[8,24,128]{2,1,0:T(8,128)}, f32[8,128]{1,0:T(8,128)S(1)}, f32[8,128]{1,0:T(8,128)S(1)}) custom-call(f32[2,512,128]{2,1,0:T(8,128)S(1)} %get-tuple-element.31.phi, f32[6,2,192,128]{3,2,1,0:T(8,128)S(1)} %shard_map.56.near, f32[512,256]{1,0:T(8,128)} %speed.3, f32[8,64,128]{2,1,0:T(8,128)S(1)} %all-to-all-done.arrived, ...), custom_call_target="tpu_custom_call" | custom-call | flops 39321600 | bytes 3155968 | tf_op jit(solution)/shard_map/pallas_call | solution.py:456
  30.6 4.9 %all-to-all-start.1 = ((f32[8,24,128]{2,1,0:T(8,128)}), f32[8,24,128]{2,1,0:T(8,128)S(1)}, u32[]{:S(2)}, u32[]{:S(2)}) async-start(f32[8,24,128]{2,1,0:T(8,128)} %get-tuple-element.38), calls=%async_computation.1 | async-start | bytes 196608 | tf_op jit(solution)/shard_map/all_to_all | solution.py:471
  36.1 2.3 %collective-permute-start.3 = (f32[8,128]{1,0:T(8,128)S(1)}, f32[8,128]{1,0:T(8,128)S(1)}, u32[]{:S(2)}, u32[]{:S(2)}) collective-permute-start(f32[8,128]{1,0:T(8,128)S(1)} %get-tuple-element.40), channel_id=1, source_target_pairs={{8,0},{16,8},{24,16},{0,24},{9,1},{17,9},{25,17},{1,25},{10,2},{18... | collective-permute-start | bytes 12296 | tf_op jit(solution)/shard_map/ppermute | solution.py:473
  38.4 2.1 %shard_map.58.near = f32[6,2,64,128]{3,2,1,0:T(8,128)S(1)} custom-call(f32[2,512,128]{2,1,0:T(8,128)S(1)} %get-tuple-element.37.phi.origin, s32[6,256]{1,0:T(8,128)S(1)} %get-tuple-element.32.halo_code), custom_call_target="tpu_custom_call" | custom-call | flops 13107200 | bytes 923648 | tf_op jit(solution)/shard_map/pallas_call | solution.py:456
  40.6 1.3 %all-to-all-done.1.arrived = f32[8,24,128]{2,1,0:T(8,128)S(1)} async-done(((f32[8,24,128]{2,1,0:T(8,128)}), f32[8,24,128]{2,1,0:T(8,128)S(1)}, u32[]{:S(2)}, u32[]{:S(2)}) %all-to-all-start.1) | async-done | bytes 98336 | tf_op jit(solution)/shard_map/all_to_all | solution.py:471
  41.8 4.0 %shard_map.59 = (f32[2,512,128]{2,1,0:T(8,128)S(1)}, f32[8,24,128]{2,1,0:T(8,128)}, f32[8,128]{1,0:T(8,128)S(1)}, f32[8,128]{1,0:T(8,128)S(1)}) custom-call(f32[2,512,128]{2,1,0:T(8,128)S(1)} %get-tuple-element.37.phi.origin, f32[2,512,128]{2,1,0:T(8,128)S(1)} %get-tuple-element.37.phi.origin, f32[6,2,64,128]{3,2,1,0:T(8,128)S(1)} %shard_map.58.near, ...), custom_call_target="tpu_custom_call" | custom-call | flops 7864320 | bytes 2189312 | tf_op jit(solution)/shard_map/pallas_call | solution.py:456
  45.9 3.8 %all-to-all-start.2 = ((f32[8,24,128]{2,1,0:T(8,128)}), f32[8,24,128]{2,1,0:T(8,128)S(1)}, u32[]{:S(2)}, u32[]{:S(2)}) async-start(f32[8,24,128]{2,1,0:T(8,128)} %get-tuple-element.42), calls=%async_computation.2 | async-start | bytes 196608 | tf_op jit(solution)/shard_map/all_to_all | solution.py:471
  49.7 2.4 %collective-permute-start.4 = (f32[8,128]{1,0:T(8,128)S(1)}, f32[8,128]{1,0:T(8,128)S(1)}, u32[]{:S(2)}, u32[]{:S(2)}) collective-permute-start(f32[8,128]{1,0:T(8,128)S(1)} %get-tuple-element.43), channel_id=1, source_target_pairs={{0,8},{8,16},{16,24},{24,0},{1,9},{9,17},{17,25},{25,1},{2,10},{10... | collective-permute-start | bytes 12296 | tf_op jit(solution)/shard_map/ppermute | solution.py:472
  52.6 2.1 %shard_map.60.near = f32[6,2,64,128]{3,2,1,0:T(8,128)S(1)} custom-call(f32[2,512,128]{2,1,0:T(8,128)S(1)} %get-tuple-element.41.phi, s32[6,256]{1,0:T(8,128)S(1)} %get-tuple-element.32.halo_code), custom_call_target="tpu_custom_call" | custom-call | flops 13107200 | bytes 923648 | tf_op jit(solution)/shard_map/pallas_call | solution.py:456
  54.7 1.0 collective-permute-done.5.after
  56.0 6.3 %shard_map.61 = (f32[2,512,128]{2,1,0:T(8,128)S(1)}, f32[8,64,128]{2,1,0:T(8,128)}, f32[24,128]{1,0:T(8,128)S(1)}, f32[24,128]{1,0:T(8,128)S(1)}) custom-call(f32[2,512,128]{2,1,0:T(8,128)S(1)} %get-tuple-element.41.phi, f32[2,512,128]{2,1,0:T(8,128)S(1)} %get-tuple-element.37.phi.origin, f32[6,2,64,128]{3,2,1,0:T(8,128)S(1)} %shard_map.60.near, ...), custom_call_target="tpu_custom_call" | custom-call | flops 7864320 | bytes 2369536 | tf_op jit(solution)/shard_map/pallas_call | solution.py:456
  62.4 4.8 %all-to-all-start.3 = ((f32[8,64,128]{2,1,0:T(8,128)}), f32[8,64,128]{2,1,0:T(8,128)S(1)}, u32[]{:S(2)}, u32[]{:S(2)}) async-start(f32[8,64,128]{2,1,0:T(8,128)} %get-tuple-element.46), calls=%async_computation.3 | async-start | bytes 524288 | tf_op jit(solution)/shard_map/all_to_all | solution.py:471
  67.2 1.5 %collective-permute-start.6 = (f32[24,128]{1,0:T(8,128)S(1)}, f32[24,128]{1,0:T(8,128)S(1)}, u32[]{:S(2)}, u32[]{:S(2)}) collective-permute-start(f32[24,128]{1,0:T(8,128)S(1)} %get-tuple-element.47), channel_id=1, source_target_pairs={{0,8},{8,16},{16,24},{24,0},{1,9},{9,17},{17,25},{25,1},{2,10},{10... | collective-permute-start | bytes 36872 | tf_op jit(solution)/shard_map/ppermute | solution.py:472
  68.6 1.5 %collective-permute-start.7 = (f32[24,128]{1,0:T(8,128)S(1)}, f32[24,128]{1,0:T(8,128)S(1)}, u32[]{:S(2)}, u32[]{:S(2)}) collective-permute-start(f32[24,128]{1,0:T(8,128)S(1)} %get-tuple-element.48), channel_id=1, source_target_pairs={{8,0},{16,8},{24,16},{0,24},{9,1},{17,9},{25,17},{1,25},{10,2},{18... | collective-permute-start | bytes 36872 | tf_op jit(solution)/shard_map/ppermute | solution.py:473
  70.1 6.5 %shard_map.62.near = f32[6,2,192,128]{3,2,1,0:T(8,128)S(1)} custom-call(f32[2,512,128]{2,1,0:T(8,128)S(1)} %get-tuple-element.45.phi, s32[6,256]{1,0:T(8,128)S(1)} %get-tuple-element.32.halo_code), custom_call_target="tpu_custom_call" | custom-call | flops 39321600 | bytes 1710080 | tf_op jit(solution)/shard_map/pallas_call | solution.py:456
  76.9 9.3 %shard_map.63 = (f32[2,512,128]{2,1,0:T(8,128)S(1)}, f32[8,24,128]{2,1,0:T(8,128)}, f32[8,128]{1,0:T(8,128)S(1)}, f32[8,128]{1,0:T(8,128)S(1)}) custom-call(f32[2,512,128]{2,1,0:T(8,128)S(1)} %get-tuple-element.45.phi, f32[6,2,192,128]{3,2,1,0:T(8,128)S(1)} %shard_map.62.near, f32[512,256]{1,0:T(8,128)} %speed.3, f32[8,64,128]{2,1,0:T(8,128)S(1)} %all-to-all-done.3.arrived, ...), custom_call_target="tpu_custom_call" | custom-call | flops 39321600 | bytes 3155968 | tf_op jit(solution)/shard_map/pallas_call | solution.py:456
  86.2 4.9 %all-to-all-start.4 = ((f32[8,24,128]{2,1,0:T(8,128)}), f32[8,24,128]{2,1,0:T(8,128)S(1)}, u32[]{:S(2)}, u32[]{:S(2)}) async-start(f32[8,24,128]{2,1,0:T(8,128)} %get-tuple-element.50), calls=%async_computation.4 | async-start | bytes 196608 | tf_op jit(solution)/shard_map/all_to_all | solution.py:471
  91.6 2.4 %collective-permute-start.9 = (f32[8,128]{1,0:T(8,128)S(1)}, f32[8,128]{1,0:T(8,128)S(1)}, u32[]{:S(2)}, u32[]{:S(2)}) collective-permute-start(f32[8,128]{1,0:T(8,128)S(1)} %get-tuple-element.52), channel_id=1, source_target_pairs={{8,0},{16,8},{24,16},{0,24},{9,1},{17,9},{25,17},{1,25},{10,2},{18... | collective-permute-start | bytes 12296 | tf_op jit(solution)/shard_map/ppermute | solution.py:473
  94.0 2.1 %shard_map.64.near = f32[6,2,64,128]{3,2,1,0:T(8,128)S(1)} custom-call(f32[2,512,128]{2,1,0:T(8,128)S(1)} %get-tuple-element.49.phi.origin, s32[6,256]{1,0:T(8,128)S(1)} %get-tuple-element.32.halo_code), custom_call_target="tpu_custom_call" | custom-call | flops 13107200 | bytes 923648 | tf_op jit(solution)/shard_map/pallas_call | solution.py:456
  96.1 1.3 %all-to-all-done.4.arrived = f32[8,24,128]{2,1,0:T(8,128)S(1)} async-done(((f32[8,24,128]{2,1,0:T(8,128)}), f32[8,24,128]{2,1,0:T(8,128)S(1)}, u32[]{:S(2)}, u32[]{:S(2)}) %all-to-all-start.4) | async-done | bytes 98336 | tf_op jit(solution)/shard_map/all_to_all | solution.py:471
  97.4 4.0 %shard_map.65 = (f32[2,512,128]{2,1,0:T(8,128)S(1)}, f32[8,24,128]{2,1,0:T(8,128)}, f32[8,128]{1,0:T(8,128)S(1)}, f32[8,128]{1,0:T(8,128)S(1)}) custom-call(f32[2,512,128]{2,1,0:T(8,128)S(1)} %get-tuple-element.49.phi.origin, f32[2,512,128]{2,1,0:T(8,128)S(1)} %get-tuple-element.49.phi.origin, f32[6,2,64,128]{3,2,1,0:T(8,128)S(1)} %shard_map.64.near, ...), custom_call_target="tpu_custom_call" | custom-call | flops 7864320 | bytes 2189312 | tf_op jit(solution)/shard_map/pallas_call | solution.py:456
  101.4 3.8 %all-to-all-start.5 = ((f32[8,24,128]{2,1,0:T(8,128)}), f32[8,24,128]{2,1,0:T(8,128)S(1)}, u32[]{:S(2)}, u32[]{:S(2)}) async-start(f32[8,24,128]{2,1,0:T(8,128)} %get-tuple-element.54), calls=%async_computation.5 | async-start | bytes 196608 | tf_op jit(solution)/shard_map/all_to_all | solution.py:471
  105.2 1.5 %collective-permute-start.10 = (f32[8,128]{1,0:T(8,128)S(1)}, f32[8,128]{1,0:T(8,128)S(1)}, u32[]{:S(2)}, u32[]{:S(2)}) collective-permute-start(f32[8,128]{1,0:T(8,128)S(1)} %get-tuple-element.55), channel_id=1, source_target_pairs={{0,8},{8,16},{16,24},{24,0},{1,9},{9,17},{17,25},{25,1},{2,10},{10... | collective-permute-start | bytes 12296 | tf_op jit(solution)/shard_map/ppermute | solution.py:472
  106.7 1.5 %collective-permute-start.11 = (f32[8,128]{1,0:T(8,128)S(1)}, f32[8,128]{1,0:T(8,128)S(1)}, u32[]{:S(2)}, u32[]{:S(2)}) collective-permute-start(f32[8,128]{1,0:T(8,128)S(1)} %get-tuple-element.56), channel_id=1, source_target_pairs={{8,0},{16,8},{24,16},{0,24},{9,1},{17,9},{25,17},{1,25},{10,2},{18... | collective-permute-start | bytes 12296 | tf_op jit(solution)/shard_map/ppermute | solution.py:473
  108.2 2.1 %shard_map.66.near = f32[6,2,64,128]{3,2,1,0:T(8,128)S(1)} custom-call(f32[2,512,128]{2,1,0:T(8,128)S(1)} %get-tuple-element.53.phi, s32[6,256]{1,0:T(8,128)S(1)} %get-tuple-element.32.halo_code), custom_call_target="tpu_custom_call" | custom-call | flops 13107200 | bytes 923648 | tf_op jit(solution)/shard_map/pallas_call | solution.py:456
  110.3 1.3 %all-to-all-done.5.arrived = f32[8,24,128]{2,1,0:T(8,128)S(1)} async-done(((f32[8,24,128]{2,1,0:T(8,128)}), f32[8,24,128]{2,1,0:T(8,128)S(1)}, u32[]{:S(2)}, u32[]{:S(2)}) %all-to-all-start.5) | async-done | bytes 98336 | tf_op jit(solution)/shard_map/all_to_all | solution.py:471
  111.6 3.0 %shard_map.67 = f32[512,256]{1,0:T(8,128)} custom-call(f32[2,512,128]{2,1,0:T(8,128)S(1)} %get-tuple-element.53.phi, f32[2,512,128]{2,1,0:T(8,128)S(1)} %get-tuple-element.49.phi.origin, f32[6,2,64,128]{3,2,1,0:T(8,128)S(1)} %shard_map.66.near, f32[8,24,128]{2,1,0:T(8,128)S(1)} %all-to-all-done.5.arrived, f32[8,128]{1,0:T(8,128)S(1)} %collective-permute-done.10.before, ...), custom_call_target="tpu_custom_call" | custom-call | flops 7864320 | bytes 2082816 | tf_op jit(solution)/shard_map/pallas_call | solution.py:456
  (17 shorter events, 2.5 us)
Async XLA Ops:
  5.3 16.1 %all-to-all-start = ((f32[8,64,128]{2,1,0:T(8,128)}), f32[8,64,128]{2,1,0:T(8,128)S(1)}, u32[]{:S(2)}, u32[]{:S(2)}) async-start(f32[8,64,128]{2,1,0:T(8,128)} %get-tuple-element.33), calls=%async_computation | async-start | bytes 524288 | tf_op jit(solution)/shard_map/all_to_all | solution.py:471
  11.6 9.5 %collective-permute-start = (f32[24,128]{1,0:T(8,128)S(1)}, f32[24,128]{1,0:T(8,128)S(1)}, u32[]{:S(2)}, u32[]{:S(2)}) collective-permute-start(f32[24,128]{1,0:T(8,128)S(1)} %get-tuple-element.34), channel_id=1, source_target_pairs={{0,8},{8,16},{16,24},{24,0},{1,9},{9,17},{17,25},{25,1},{2,10},{10... | collective-permute-start | bytes 36872 | tf_op jit(solution)/shard_map/ppermute | solution.py:472
  13.1 8.0 %collective-permute-start.1 = (f32[24,128]{1,0:T(8,128)S(1)}, f32[24,128]{1,0:T(8,128)S(1)}, u32[]{:S(2)}, u32[]{:S(2)}) collective-permute-start(f32[24,128]{1,0:T(8,128)S(1)} %get-tuple-element.35), channel_id=1, source_target_pairs={{8,0},{16,8},{24,16},{0,24},{9,1},{17,9},{25,17},{1,25},{10,2},{18... | collective-permute-start | bytes 36872 | tf_op jit(solution)/shard_map/ppermute | solution.py:473
  30.6 11.2 %all-to-all-start.1 = ((f32[8,24,128]{2,1,0:T(8,128)}), f32[8,24,128]{2,1,0:T(8,128)S(1)}, u32[]{:S(2)}, u32[]{:S(2)}) async-start(f32[8,24,128]{2,1,0:T(8,128)} %get-tuple-element.38), calls=%async_computation.1 | async-start | bytes 196608 | tf_op jit(solution)/shard_map/all_to_all | solution.py:471
  35.5 5.0 %collective-permute-start.2 = (f32[8,128]{1,0:T(8,128)S(1)}, f32[8,128]{1,0:T(8,128)S(1)}, u32[]{:S(2)}, u32[]{:S(2)}) collective-permute-start(f32[8,128]{1,0:T(8,128)S(1)} %get-tuple-element.39), channel_id=1, source_target_pairs={{0,8},{8,16},{16,24},{24,0},{1,9},{9,17},{17,25},{25,1},{2,10},{10... | collective-permute-start | bytes 12296 | tf_op jit(solution)/shard_map/ppermute | solution.py:472
  36.1 4.5 %collective-permute-start.3 = (f32[8,128]{1,0:T(8,128)S(1)}, f32[8,128]{1,0:T(8,128)S(1)}, u32[]{:S(2)}, u32[]{:S(2)}) collective-permute-start(f32[8,128]{1,0:T(8,128)S(1)} %get-tuple-element.40), channel_id=1, source_target_pairs={{8,0},{16,8},{24,16},{0,24},{9,1},{17,9},{25,17},{1,25},{10,2},{18... | collective-permute-start | bytes 12296 | tf_op jit(solution)/shard_map/ppermute | solution.py:473
  45.9 10.2 %all-to-all-start.2 = ((f32[8,24,128]{2,1,0:T(8,128)}), f32[8,24,128]{2,1,0:T(8,128)S(1)}, u32[]{:S(2)}, u32[]{:S(2)}) async-start(f32[8,24,128]{2,1,0:T(8,128)} %get-tuple-element.42), calls=%async_computation.2 | async-start | bytes 196608 | tf_op jit(solution)/shard_map/all_to_all | solution.py:471
  49.7 5.0 %collective-permute-start.4 = (f32[8,128]{1,0:T(8,128)S(1)}, f32[8,128]{1,0:T(8,128)S(1)}, u32[]{:S(2)}, u32[]{:S(2)}) collective-permute-start(f32[8,128]{1,0:T(8,128)S(1)} %get-tuple-element.43), channel_id=1, source_target_pairs={{0,8},{8,16},{16,24},{24,0},{1,9},{9,17},{17,25},{25,1},{2,10},{10... | collective-permute-start | bytes 12296 | tf_op jit(solution)/shard_map/ppermute | solution.py:472
  52.1 3.6 %collective-permute-start.5 = (f32[8,128]{1,0:T(8,128)S(1)}, f32[8,128]{1,0:T(8,128)S(1)}, u32[]{:S(2)}, u32[]{:S(2)}) collective-permute-start(f32[8,128]{1,0:T(8,128)S(1)} %get-tuple-element.44), channel_id=1, source_target_pairs={{8,0},{16,8},{24,16},{0,24},{9,1},{17,9},{25,17},{1,25},{10,2},{18... | collective-permute-start | bytes 12296 | tf_op jit(solution)/shard_map/ppermute | solution.py:473
  62.4 14.5 %all-to-all-start.3 = ((f32[8,64,128]{2,1,0:T(8,128)}), f32[8,64,128]{2,1,0:T(8,128)S(1)}, u32[]{:S(2)}, u32[]{:S(2)}) async-start(f32[8,64,128]{2,1,0:T(8,128)} %get-tuple-element.46), calls=%async_computation.3 | async-start | bytes 524288 | tf_op jit(solution)/shard_map/all_to_all | solution.py:471
  67.2 9.5 %collective-permute-start.6 = (f32[24,128]{1,0:T(8,128)S(1)}, f32[24,128]{1,0:T(8,128)S(1)}, u32[]{:S(2)}, u32[]{:S(2)}) collective-permute-start(f32[24,128]{1,0:T(8,128)S(1)} %get-tuple-element.47), channel_id=1, source_target_pairs={{0,8},{8,16},{16,24},{24,0},{1,9},{9,17},{17,25},{25,1},{2,10},{10... | collective-permute-start | bytes 36872 | tf_op jit(solution)/shard_map/ppermute | solution.py:472
  68.6 8.0 %collective-permute-start.7 = (f32[24,128]{1,0:T(8,128)S(1)}, f32[24,128]{1,0:T(8,128)S(1)}, u32[]{:S(2)}, u32[]{:S(2)}) collective-permute-start(f32[24,128]{1,0:T(8,128)S(1)} %get-tuple-element.48), channel_id=1, source_target_pairs={{8,0},{16,8},{24,16},{0,24},{9,1},{17,9},{25,17},{1,25},{10,2},{18... | collective-permute-start | bytes 36872 | tf_op jit(solution)/shard_map/ppermute | solution.py:473
  86.2 11.2 %all-to-all-start.4 = ((f32[8,24,128]{2,1,0:T(8,128)}), f32[8,24,128]{2,1,0:T(8,128)S(1)}, u32[]{:S(2)}, u32[]{:S(2)}) async-start(f32[8,24,128]{2,1,0:T(8,128)} %get-tuple-element.50), calls=%async_computation.4 | async-start | bytes 196608 | tf_op jit(solution)/shard_map/all_to_all | solution.py:471
  91.0 5.0 %collective-permute-start.8 = (f32[8,128]{1,0:T(8,128)S(1)}, f32[8,128]{1,0:T(8,128)S(1)}, u32[]{:S(2)}, u32[]{:S(2)}) collective-permute-start(f32[8,128]{1,0:T(8,128)S(1)} %get-tuple-element.51), channel_id=1, source_target_pairs={{0,8},{8,16},{16,24},{24,0},{1,9},{9,17},{17,25},{25,1},{2,10},{10... | collective-permute-start | bytes 12296 | tf_op jit(solution)/shard_map/ppermute | solution.py:472
  91.6 4.5 %collective-permute-start.9 = (f32[8,128]{1,0:T(8,128)S(1)}, f32[8,128]{1,0:T(8,128)S(1)}, u32[]{:S(2)}, u32[]{:S(2)}) collective-permute-start(f32[8,128]{1,0:T(8,128)S(1)} %get-tuple-element.52), channel_id=1, source_target_pairs={{8,0},{16,8},{24,16},{0,24},{9,1},{17,9},{25,17},{1,25},{10,2},{18... | collective-permute-start | bytes 12296 | tf_op jit(solution)/shard_map/ppermute | solution.py:473
  101.4 10.2 %all-to-all-start.5 = ((f32[8,24,128]{2,1,0:T(8,128)}), f32[8,24,128]{2,1,0:T(8,128)S(1)}, u32[]{:S(2)}, u32[]{:S(2)}) async-start(f32[8,24,128]{2,1,0:T(8,128)} %get-tuple-element.54), calls=%async_computation.5 | async-start | bytes 196608 | tf_op jit(solution)/shard_map/all_to_all | solution.py:471
  105.2 5.0 %collective-permute-start.10 = (f32[8,128]{1,0:T(8,128)S(1)}, f32[8,128]{1,0:T(8,128)S(1)}, u32[]{:S(2)}, u32[]{:S(2)}) collective-permute-start(f32[8,128]{1,0:T(8,128)S(1)} %get-tuple-element.55), channel_id=1, source_target_pairs={{0,8},{8,16},{16,24},{24,0},{1,9},{9,17},{17,25},{25,1},{2,10},{10... | collective-permute-start | bytes 12296 | tf_op jit(solution)/shard_map/ppermute | solution.py:472
  106.7 3.6 %collective-permute-start.11 = (f32[8,128]{1,0:T(8,128)S(1)}, f32[8,128]{1,0:T(8,128)S(1)}, u32[]{:S(2)}, u32[]{:S(2)}) collective-permute-start(f32[8,128]{1,0:T(8,128)S(1)} %get-tuple-element.56), channel_id=1, source_target_pairs={{8,0},{16,8},{24,16},{0,24},{9,1},{17,9},{25,17},{1,25},{10,2},{18... | collective-permute-start | bytes 12296 | tf_op jit(solution)/shard_map/ppermute | solution.py:473

commit v3 on v2

--- a/solution.py
+++ b/solution.py
@@ -142,12 +142,14 @@
     lanes = lane_ids()
     w = plan.layers
 
-    @pl.loop(0, plan.groups)
-    def _(g):
-        sources = local_sources(plan, phi, ends, g)
-        for t in range(plan.far_tiles):
-            code = jnp.broadcast_to(send_code[pl.ds(t, 1), :], (8, LANES))
-            table[t, rows8(g * 8), :] = gather(sources, code)
+    @pl.loop(0, plan.groups // 4)
+    def _(q):
+        for v in range(4):
+            g = q * 4 + v
+            sources = local_sources(plan, phi, ends, g)
+            for t in range(plan.far_tiles):
+                code = jnp.broadcast_to(send_code[pl.ds(t, 1), :], (8, LANES))
+                table[t, rows8(g * 8), :] = gather(sources, code)
 
     for e in range(plan.peers):
         t, eq = divmod(e, plan.per_tile)
@@ -207,38 +209,33 @@
             table[t, pl.ds(g * 8, 8), :] = block
 
 
-def pull_local(plan, phi, ends, halo_code, halos):
-    @pl.loop(0, plan.groups)
-    def _(g):
-        sources = local_sources(plan, phi, ends, g)
-        for s in range(6):
-            for h in range(plan.halves):
-                code = jnp.broadcast_to(halo_code[pl.ds(s, 1), half(h)], (8, LANES))
-                halos[s, h, rows8(g * 8), :] = gather(sources, code)
-
-
-def pull_far(plan, table, halo_code, near, halos):
+def pull_local(plan, phi, ends, halo_code, halos, g):
+    sources = local_sources(plan, phi, ends, g)
+    for s in range(6):
+        for h in range(plan.halves):
+            code = jnp.broadcast_to(halo_code[pl.ds(s, 1), half(h)], (8, LANES))
+            halos[s, h, rows8(g * 8), :] = gather(sources, code)
+
+
+def pull_far(plan, table, halo_code, near, halos, sides, g):
     start = plan.local_tiles * LANES
-
-    @pl.loop(0, plan.groups)
-    def _(g):
-        sources = [table[t, rows8(g * 8), :] for t in range(plan.far_tiles)]
-        for s in range(6):
-            for h in range(plan.halves):
-                code = jnp.broadcast_to(halo_code[pl.ds(s, 1), half(h)], (8, LANES))
-                far = gather(sources, code - start)
-                here = near[s, h, rows8(g * 8), :]
-                halos[s, h, rows8(g * 8), :] = jnp.where(code >= start, far, here)
-
-
-def weno_line(q):
-    first = [q[m + 1] - q[m] for m in range(13)]
-    second = [first[m + 1] - first[m] for m in range(12)]
-    third = [second[m + 1] - second[m] for m in range(11)]
-    fourth = [(third[m] - third[m + 1]) * (1.0 / 3.0) for m in range(10)]
+    sources = [table[t, rows8(g * 8), :] for t in range(plan.far_tiles)]
+    for s in sides:
+        for h in range(plan.halves):
+            code = jnp.broadcast_to(halo_code[pl.ds(s, 1), half(h)], (8, LANES))
+            far = gather(sources, code - start)
+            here = near[s, h, rows8(g * 8), :]
+            halos[s, h, rows8(g * 8), :] = jnp.where(code >= start, far, here)
+
+
+def weno_windows(q):
+    first = [q[m + 1] - q[m] for m in range(7)]
+    second = [first[m + 1] - first[m] for m in range(6)]
+    third = [second[m + 1] - second[m] for m in range(5)]
+    fourth = [(third[m] - third[m + 1]) * (1.0 / 3.0) for m in range(4)]
     bend = [t * t * (4.0 / 3.0) + weno_floor for t in third]
-    backward, negated = [], []
-    for m in range(9):
+    found = []
+    for m in range(3):
         s1, s2 = second[m + 1], second[m + 2]
         a = bend[m] + s1 * (s1 + third[m])
         b = bend[m + 1] + s1 * s2
@@ -249,99 +246,172 @@
         total = x + z + 6.0 * (a * c)
         xu = x * fourth[m]
         zu = z * fourth[m + 1]
-        slope = s1 + s2
+        slope = 0.25 * (s1 + s2)
         middle = first[m + 2] + third[m + 1] * (1.0 / 12.0)
-        if m < 8:
-            fix = (xu + 1.5 * zu) * pl.reciprocal(total + 2.0 * z, approx=True)
-            backward.append(middle + 0.25 * slope + fix)
-        if m > 0:
-            fix = (zu + 1.5 * xu) * pl.reciprocal(total + 2.0 * x, approx=True)
-            negated.append(fix + 0.25 * slope - middle)
-    found = []
-    for n in range(8):
-        steep = jnp.maximum(jnp.maximum(backward[n], negated[n]), 0.0)
-        found.append(steep * steep)
+        fix = (xu + 1.5 * zu) * pl.reciprocal(total + 2.0 * z, approx=True)
+        backward = middle + slope + fix
+        fix = (zu + 1.5 * xu) * pl.reciprocal(total + 2.0 * x, approx=True)
+        found.append((backward, fix + slope - middle))
     return found
 
 
-def advect(plan, phi, speed, ready, halos, squares, moved):
+def inner_values(values):
+    three, four, five = weno_windows(values)
+    return [three[1], jnp.maximum(three[0], four[1]), jnp.maximum(four[0], five[1]), five[0]]
+
+
+def line_values(low, values, high, inner):
+    zero, one, two = weno_windows(low + values[:5])
+    six, seven, last = weno_windows(values[3:] + high)
+    steep = [
+        jnp.maximum(zero[0], one[1]),
+        jnp.maximum(one[0], two[1]),
+        jnp.maximum(two[0], inner[0]),
+        inner[1],
+        inner[2],
+        jnp.maximum(inner[3], six[1]),
+        jnp.maximum(six[0], seven[1]),
+        jnp.maximum(seven[0], last[1]),
+    ]
+    steep = [jnp.maximum(value, 0.0) for value in steep]
+    return [value * value for value in steep]
+
+
+def line_at(phi, h, axis, q):
+    if axis == 0:
+        return [phi[h, rows8(m * 64 + q * 8), :] for m in range(8)]
+    if axis == 1:
+        return [phi[h, rows8(q * 64 + m * 8), :] for m in range(8)]
+    return [phi[h, pl.ds(q * 64 + m, 8, stride=8), :] for m in range(8)]
+
+
+def inner_at(inner, h, axis, q):
+    return [inner[axis, h, rows8(q * 32 + m * 8), :] for m in range(4)]
+
+
+def advect(plan, phi, speed, ready, near, inner, table, halo_code, halos, squares, moved):
     w = plan.layers
-    for h in range(plan.halves):
+
+    def stage_planes(i):
+        for l in range(w):
+            pull_far(plan, table, halo_code, near, halos, (2, 3, 4, 5), i * w + l)
+
+    def stage_columns(j):
+        for l in range(w):
+            pull_far(plan, table, halo_code, near, halos, (0, 1), l * 8 + j)
+
+    stage_planes(0)
+
+    @pl.loop(0, 8)
+    def _(i):
+        lines = []
+        for h in range(plan.halves):
+            ends = [
+                [halos[s, h, pl.ds(i * 8 * w + l, 8, stride=w), :] for l in range(w)]
+                for s in (4, 5)
+            ]
+            lines.append((ends[0], line_at(phi, h, 2, i), ends[1], inner_at(inner, h, 2, i)))
+            ends = [
+                [halos[s, h, rows8((i * w + l) * 8), :] for l in range(w)] for s in (2, 3)
+            ]
+            lines.append((ends[0], line_at(phi, h, 1, i), ends[1], inner_at(inner, h, 1, i)))
+        stage_planes(jnp.minimum(i + 1, 7))
+        for h in range(plan.halves):
+            for k, value in enumerate(line_values(*lines[2 * h])):
+                squares[h, pl.ds(i * 64 + k, 8, stride=8), :] = value
+            for j, value in enumerate(line_values(*lines[2 * h + 1])):
+                squares[h, rows8(i * 64 + j * 8), :] += value
+
+    ready()
+    stage_columns(0)
+
+    @pl.loop(0, 8)
+    def _(j):
+        lines = []
+        for h in range(plan.halves):
+            ends = [
+                [halos[s, h, rows8((l * 8 + j) * 8), :] for l in range(w)] for s in (0, 1)
+            ]
+            lines.append((ends[0], line_at(phi, h, 0, j), ends[1], inner_at(inner, h, 0, j)))
+        stage_columns(jnp.minimum(j + 1, 7))
+        for h in range(plan.halves):
+            for i, value in enumerate(line_values(*lines[h])):
+                here = rows8(i * 64 + j * 8)
+                total = squares[h, here, :] + value
+                change = advect_scale * speed[h, here, :] * jnp.sqrt(total)
+                moved[h, here, :] = lines[h][1][i] - change
+
+
+def relax(plan, phi, origin, near, table, halo_code, halos, moved, joined):
+    row = lax.broadcasted_iota(jnp.int32, (8, LANES), 0)
+
+    @pl.loop(0, 2)
+    def _(q):
+        for v in range(4):
+            pull_far(plan, table, halo_code, near, halos, (0, 1), q * 4 + v)
+
+    def stage(i):
+        pull_far(plan, table, halo_code, near, halos, (2, 3, 4, 5), i)
+
+    def plane(i, h, previous, following, sides):
         at = half(h)
-
-        @pl.loop(0, 8)
-        def _(i):
-            line = [halos[4, h, pl.ds(i * 8 * w + l, 8, stride=w), :] for l in range(w)]
-            line += [phi[h, pl.ds(i * 64 + k, 8, stride=8), :] for k in range(8)]
-            line += [halos[5, h, pl.ds(i * 8 * w + l, 8, stride=w), :] for l in range(w)]
-            for k, value in enumerate(weno_line(line)):
-                squares[pl.ds(i * 64 + k, 8, stride=8), :] = value
-            line = [halos[2, h, rows8((i * w + l) * 8), :] for l in range(w)]
-            line += [phi[h, rows8(i * 64 + j * 8), :] for j in range(8)]
-            line += [halos[3, h, rows8((i * w + l) * 8), :] for l in range(w)]
-            for j, value in enumerate(weno_line(line)):
-                squares[rows8(i * 64 + j * 8), :] += value
-
-        if h == 0:
-            ready()
-
-        @pl.loop(0, 8)
-        def _(j):
-            line = [halos[0, h, rows8((l * 8 + j) * 8), :] for l in range(w)]
-            line += [phi[h, rows8(i * 64 + j * 8), :] for i in range(8)]
-            line += [halos[1, h, rows8((l * 8 + j) * 8), :] for l in range(w)]
-            for i, value in enumerate(weno_line(line)):
-                here = rows8(i * 64 + j * 8)
-                total = squares[here, :] + value
-                value = line[w + i] - advect_scale * speed[h, here, :] * jnp.sqrt(total)
+        centre = [phi[h, rows8(i * 64 + j * 8), :] for j in range(8)]
+        along_y = [sides[0]] + centre + [sides[1]]
+        for j in range(8):
+            here = rows8(i * 64 + j * 8)
+            value = centre[j]
+            start = origin[h, here, :]
+            sense = start * lax.rsqrt(start * start + 1.0)
+            facing = jnp.where(start > 0.0, 1.0, -1.0)
+            first = jnp.broadcast_to(sides[2][j : j + 1], (8, LANES))
+            last = jnp.broadcast_to(sides[3][j : j + 1], (8, LANES))
+            low_z = jnp.where(row == 0, first, pltpu.roll(value, 1, 0))
+            high_z = jnp.where(row == 7, last, pltpu.roll(value, 7, 0))
+            pairs = (
+                (previous(j), following(j)),
+                (along_y[j], along_y[j + 2]),
+                (low_z, high_z),
+            )
+            total = None
+            for low, high in pairs:
+                steep = jnp.maximum((value - low) * facing, (value - high) * facing)
+                steep = jnp.maximum(steep, 0.0)
+                steep = steep * steep
+                total = steep if total is None else total + steep
+            value = value - relax_scale * sense * (jnp.sqrt(total) - 1.0)
+            if joined:
+                moved[here, at] = value
+            else:
                 moved[h, here, :] = value
 
-
-def relax(plan, phi, origin, halos, moved, joined):
-    row = lax.broadcasted_iota(jnp.int32, (8, LANES), 0)
-    for h in range(plan.halves):
-        at = half(h)
-
-        def plane(i, previous, following):
-            centre = [phi[h, rows8(i * 64 + j * 8), :] for j in range(8)]
-            along_y = [halos[2, h, rows8(i * 8), :]] + centre + [halos[3, h, rows8(i * 8), :]]
-            for j in range(8):
-                here = rows8(i * 64 + j * 8)
-                value = centre[j]
-                start = origin[h, here, :]
-                sense = start * lax.rsqrt(start * start + 1.0)
-                facing = jnp.where(start > 0.0, 1.0, -1.0)
-                first = jnp.broadcast_to(halos[4, h, pl.ds(i * 8 + j, 1), :], (8, LANES))
-                last = jnp.broadcast_to(halos[5, h, pl.ds(i * 8 + j, 1), :], (8, LANES))
-                low_z = jnp.where(row == 0, first, pltpu.roll(value, 1, 0))
-                high_z = jnp.where(row == 7, last, pltpu.roll(value, 7, 0))
-                pairs = (
-                    (previous(j), following(j)),
-                    (along_y[j], along_y[j + 2]),
-                    (low_z, high_z),
-                )
-                total = None
-                for low, high in pairs:
-                    steep = jnp.maximum((value - low) * facing, (value - high) * facing)
-                    steep = jnp.maximum(steep, 0.0)
-                    steep = steep * steep
-                    total = steep if total is None else total + steep
-                value = value - relax_scale * sense * (jnp.sqrt(total) - 1.0)
-                if joined:
-                    moved[here, at] = value
-                else:
-                    moved[h, here, :] = value
-
-        def inner(i, j):
-            return phi[h, rows8(i * 64 + j * 8), :]
-
-        plane(0, lambda j: halos[0, h, pl.ds(j * 8, 8), :], lambda j: inner(1, j))
-
-        @pl.loop(1, 7)
-        def _(i):
-            plane(i, lambda j: inner(i - 1, j), lambda j: inner(i + 1, j))
-
-        plane(7, lambda j: inner(6, j), lambda j: halos[1, h, pl.ds(j * 8, 8), :])
+    def planes(i, low, high):
+        sides = [
+            [halos[s, h, rows8(i * 8), :] for s in (2, 3, 4, 5)] for h in range(plan.halves)
+        ]
+        if not isinstance(i, int) or i < 7:
+            stage(i + 1)
+        for h in range(plan.halves):
+
+            def previous(j):
+                if low is None:
+                    return phi[h, rows8((i - 1) * 64 + j * 8), :]
+                return halos[low, h, pl.ds(j * 8, 8), :]
+
+            def following(j):
+                if high is None:
+                    return phi[h, rows8((i + 1) * 64 + j * 8), :]
+                return halos[high, h, pl.ds(j * 8, 8), :]
+
+            plane(i, h, previous, following, sides[h])
+
+    stage(0)
+    planes(0, 0, None)
+
+    @pl.loop(1, 7)
+    def _(i):
+        planes(i, None, None)
+
+    planes(7, None, 1)
 
 
 def first_kernel(
@@ -400,13 +470,30 @@
     pack_sends(plan, phi, ends, send_code, table, outgoing, low, high)
 
 
-def near_kernel(plan, phi, halo_code, near, ends):
+def near_kernel(plan, phi, halo_code, near, *rest):
+    if plan.layers == 1:
+
+        @pl.loop(0, plan.groups // 2)
+        def _(q):
+            for v in range(2):
+                pull_local(plan, phi, None, halo_code, near, q * 2 + v)
+
+        return
+    inner, ends = rest
     fill_ends(plan, phi, ends)
-    pull_local(plan, phi, ends, halo_code, near)
+    for axis in range(3):
+
+        @pl.loop(0, 8)
+        def _(q):
+            lines = [line_at(phi, h, axis, q) for h in range(plan.halves)]
+            pull_local(plan, phi, ends, halo_code, near, axis * 8 + q)
+            for h in range(plan.halves):
+                for m, value in enumerate(inner_values(lines[h])):
+                    inner[axis, h, rows8(q * 32 + m * 8), :] = value
 
 
 def advect_kernel(
-    plan, sends, phi, near, speed, arrived, before, after, send_code, halo_code,
+    plan, sends, phi, near, inner, speed, arrived, before, after, send_code, halo_code,
     moved, outgoing, low, high, ends, table, halos, squares, fast, loaded,
 ):
     copies = [
@@ -421,8 +508,7 @@
             copy.wait()
 
     unpack_far(plan, arrived, before, after, table)
-    pull_far(plan, table, halo_code, near, halos)
-    advect(plan, phi, fast, ready, halos, squares, moved)
+    advect(plan, phi, fast, ready, near, inner, table, halo_code, halos, squares, moved)
     pack_sends(sends, moved, ends, send_code, table, outgoing, low, high)
 
 
@@ -434,8 +520,7 @@
     else:
         (moved, outgoing, low, high, ends, table, halos) = rest
     unpack_far(plan, arrived, before, after, table)
-    pull_far(plan, table, halo_code, near, halos)
-    relax(plan, phi, origin, halos, moved, sends is None)
+    relax(plan, phi, origin, near, table, halo_code, halos, moved, sends is None)
     if sends is not None:
         fill_ends(sends, moved, ends)
         pack_sends(sends, moved, ends, send_code, table, outgoing, low, high)
@@ -519,25 +604,24 @@
     )
 
     def near_halos(plan, phi):
-        return call(
-            functools.partial(near_kernel, plan),
-            [f32((6, plan.halves, 64 * plan.layers, LANES))],
-            [ends(plan)],
-            rows * count * 100 * plan.layers,
-            phi, halo_code,
-        )[0]
+        out = [f32((6, plan.halves, 64 * plan.layers, LANES))]
+        scratch = []
+        if plan.layers > 1:
+            out.append(f32((3, plan.halves, rows // 2, LANES)))
+            scratch.append(ends(plan))
+        flops = rows * count * 100 * plan.layers
+        return call(functools.partial(near_kernel, plan), out, scratch, flops, phi, halo_code)
 
     block = pltpu.VMEM((wide.halves, rows, LANES), jnp.float32)
     for offset_step in range(OFFSET_STEPS):
         phi, *message = call(
             functools.partial(advect_kernel, wide, thin),
             [field] + sent(thin),
-            [ends(wide), table(wide), halos(wide)]
-            + [pltpu.VMEM((rows, LANES), jnp.float32), block]
+            [ends(wide), table(wide), halos(wide), block, block]
             + [pltpu.SemaphoreType.DMA((wide.halves,))],
             rows * count * 300,
-            phi, near_halos(wide, phi), speed, *exchange(*message), send_code, halo_code,
-            far=(2,),
+            phi, *near_halos(wide, phi), speed, *exchange(*message), send_code, halo_code,
+            far=(3,),
         )
         origin = phi
         for redist_pass in range(REDIST_PASSES):
@@ -556,7 +640,7 @@
                 out,
                 scratch + [halos(thin)],
                 rows * count * 60,
-                phi, origin, near_halos(thin, phi), *exchange(*message), send_code, halo_code,
+                phi, origin, *near_halos(thin, phi), *exchange(*message), send_code, halo_code,
             )
     return phi
 

time: 115 us -> 110 us (0.957)
  Pallas kernels: 62.7 us -> 52.4 us
  local copies, waits for them, and re-layouts: 0 us -> 4.03 us
    pallas_call x13, Pallas kernels: 62.7 us -> 52.4 us  [call(): pl.pallas_call(kernel, out_shape=out_shape, in_specs=[apart if n in far e...]
    unnamed x0 -> x8, local copies, waits for them, and re-layouts: none -> 4.03 us
    ppermute x6, waiting for transfers between devices: 1.01 us -> 2.16 us  [exchange(): after = lax.ppermute(low, 'group', down)]
  transfers between devices with their start and end apart: 18 -> 18, of which waited for: 7 -> 5; matrix products, arithmetic and copies ran while one was open for 0% -> 0% of each run, Pallas kernels for 19% -> 19%
where the time goes in v3:
time: 110 us; the launch traced here: 109 us
  Pallas kernels  52.4 us (48%)
  starting transfers between devices  46.2 us (42%)
  waiting for transfers between devices  6.39 us (6%)
  local copies, waits for them, and re-layouts  4.03 us (4%)
    pallas_call x13, Pallas kernels, call(): pl.pallas_call(kernel, out_shape=out_shape, in_specs=[apart if n in far e...  52.4 us
    all_to_all x6, starting transfers between devices, exchange(): lax.all_to_all(outgoing, 'dev', split_axis=0, concat_axis=0, tiled=True)  28.7 us
    ppermute x6, starting transfers between devices, exchange(): after = lax.ppermute(low, 'group', down)  9.62 us
    ppermute x6, starting transfers between devices, exchange(): before = lax.ppermute(high, 'group', up)  7.93 us
    all_to_all x6, waiting for transfers between devices, exchange(): lax.all_to_all(outgoing, 'dev', split_axis=0, concat_axis=0, tiled=True)  4.21 us
    unnamed x8, local copies, waits for them, and re-layouts  4.03 us
  transfers between devices with their start and end apart: 18, of which 5 were waited for; matrix products, arithmetic and copies ran while one was open for 0% of the time, Pallas kernels for 19%

profile of v3, /device:TPU:0, one launch (start us, length us, event | category | flops | bytes accessed | tf_op | source)
XLA Modules:
  0.0 109.2 jit_solution(2936599580845267408)
XLA Ops:
  0.0 3.8 %shard_map.55 = (f32[2,512,128]{2,1,0:T(8,128)S(1)}, f32[8,64,128]{2,1,0:T(8,128)}, f32[24,128]{1,0:T(8,128)S(1)}, f32[24,128]{1,0:T(8,128)S(1)}, s32[8,128]{1,0:T(8,128)S(1)}, /*index=5*/s32[6,256]{1,0:T(8,128)S(1)}) custom-call(f32[512,256]{1,0:T(8,128)} %level_set.1, s32[8,40]{1,0:T(8,128)} %peer_slabs.1, s32[2,16]{1,0:T(2,128)} %region_slabs.1, ...), custom_call_target="tpu_custom_call" | custom-call | flops 1000000 | bytes 1353088 | tf_op jit(solution)/shard_map/pallas_call | solution.py:541
  3.8 6.3 %all-to-all-start = ((f32[8,64,128]{2,1,0:T(8,128)}), f32[8,64,128]{2,1,0:T(8,128)S(1)}, u32[]{:S(2)}, u32[]{:S(2)}) async-start(f32[8,64,128]{2,1,0:T(8,128)} %get-tuple-element.39), calls=%async_computation | async-start | bytes 524288 | tf_op jit(solution)/shard_map/all_to_all | solution.py:556
  10.2 1.5 %collective-permute-start = (f32[24,128]{1,0:T(8,128)S(1)}, f32[24,128]{1,0:T(8,128)S(1)}, u32[]{:S(2)}, u32[]{:S(2)}) collective-permute-start(f32[24,128]{1,0:T(8,128)S(1)} %get-tuple-element.40), channel_id=1, source_target_pairs={{0,8},{8,16},{16,24},{24,0},{1,9},{9,17},{17,25},{25,1},{2,10},{10... | collective-permute-start | bytes 36872 | tf_op jit(solution)/shard_map/ppermute | solution.py:557
  11.6 1.4 %collective-permute-start.1 = (f32[24,128]{1,0:T(8,128)S(1)}, f32[24,128]{1,0:T(8,128)S(1)}, u32[]{:S(2)}, u32[]{:S(2)}) collective-permute-start(f32[24,128]{1,0:T(8,128)S(1)} %get-tuple-element.41), channel_id=1, source_target_pairs={{8,0},{16,8},{24,16},{0,24},{9,1},{17,9},{25,17},{1,25},{10,2},{18... | collective-permute-start | bytes 36872 | tf_op jit(solution)/shard_map/ppermute | solution.py:558
  13.1 6.6 %shard_map.56 = (f32[6,2,192,128]{3,2,1,0:T(8,128)S(1)}, f32[3,2,256,128]{3,2,1,0:T(8,128)S(1)}) custom-call(f32[2,512,128]{2,1,0:T(8,128)S(1)} %get-tuple-element.35.phi, s32[6,256]{1,0:T(8,128)S(1)} %get-tuple-element.36.halo_code), custom_call_target="tpu_custom_call" | custom-call | flops 39321600 | bytes 2496512 | tf_op jit(solution)/shard_map/pallas_call | solution.py:541
  21.8 7.1 %shard_map.57 = (f32[2,512,128]{2,1,0:T(8,128)S(1)}, f32[8,24,128]{2,1,0:T(8,128)}, f32[8,128]{1,0:T(8,128)S(1)}, f32[8,128]{1,0:T(8,128)S(1)}) custom-call(f32[2,512,128]{2,1,0:T(8,128)S(1)} %get-tuple-element.35.phi, f32[6,2,192,128]{3,2,1,0:T(8,128)S(1)} %get-tuple-element.37.near, f32[3,2,256,128]{3,2,1,0:T(8,128)S(1)} %copy-done.1, f32[512,256]{1,0:T(8,128)} %speed.3, ...), custom_call_target="tpu_custom_call" | custom-call | flops 39321600 | bytes 3942400 | tf_op jit(solution)/shard_map/pallas_call | solution.py:541
  28.8 5.1 %all-to-all-start.1 = ((f32[8,24,128]{2,1,0:T(8,128)}), f32[8,24,128]{2,1,0:T(8,128)S(1)}, u32[]{:S(2)}, u32[]{:S(2)}) async-start(f32[8,24,128]{2,1,0:T(8,128)} %get-tuple-element.44), calls=%async_computation.1 | async-start | bytes 196608 | tf_op jit(solution)/shard_map/all_to_all | solution.py:556
  34.5 2.3 %collective-permute-start.3 = (f32[8,128]{1,0:T(8,128)S(1)}, f32[8,128]{1,0:T(8,128)S(1)}, u32[]{:S(2)}, u32[]{:S(2)}) collective-permute-start(f32[8,128]{1,0:T(8,128)S(1)} %get-tuple-element.46), channel_id=1, source_target_pairs={{8,0},{16,8},{24,16},{0,24},{9,1},{17,9},{25,17},{1,25},{10,2},{18... | collective-permute-start | bytes 12296 | tf_op jit(solution)/shard_map/ppermute | solution.py:558
  36.9 1.8 %shard_map.58.near = f32[6,2,64,128]{3,2,1,0:T(8,128)S(1)} custom-call(f32[2,512,128]{2,1,0:T(8,128)S(1)} %get-tuple-element.43.phi.origin, s32[6,256]{1,0:T(8,128)S(1)} %get-tuple-element.36.halo_code), custom_call_target="tpu_custom_call" | custom-call | flops 13107200 | bytes 923648 | tf_op jit(solution)/shard_map/pallas_call | solution.py:541
  38.7 1.6 %all-to-all-done.1.arrived = f32[8,24,128]{2,1,0:T(8,128)S(1)} async-done(((f32[8,24,128]{2,1,0:T(8,128)}), f32[8,24,128]{2,1,0:T(8,128)S(1)}, u32[]{:S(2)}, u32[]{:S(2)}) %all-to-all-start.1) | async-done | bytes 98336 | tf_op jit(solution)/shard_map/all_to_all | solution.py:556
  40.3 3.3 %shard_map.59 = (f32[2,512,128]{2,1,0:T(8,128)S(1)}, f32[8,24,128]{2,1,0:T(8,128)}, f32[8,128]{1,0:T(8,128)S(1)}, f32[8,128]{1,0:T(8,128)S(1)}) custom-call(f32[2,512,128]{2,1,0:T(8,128)S(1)} %get-tuple-element.43.phi.origin, f32[2,512,128]{2,1,0:T(8,128)S(1)} %get-tuple-element.43.phi.origin, f32[6,2,64,128]{3,2,1,0:T(8,128)S(1)} %shard_map.58.near, ...), custom_call_target="tpu_custom_call" | custom-call | flops 7864320 | bytes 2189312 | tf_op jit(solution)/shard_map/pallas_call | solution.py:541
  43.6 3.5 %all-to-all-start.2 = ((f32[8,24,128]{2,1,0:T(8,128)}), f32[8,24,128]{2,1,0:T(8,128)S(1)}, u32[]{:S(2)}, u32[]{:S(2)}) async-start(f32[8,24,128]{2,1,0:T(8,128)} %get-tuple-element.48), calls=%async_computation.2 | async-start | bytes 196608 | tf_op jit(solution)/shard_map/all_to_all | solution.py:556
  47.1 2.7 %collective-permute-start.4 = (f32[8,128]{1,0:T(8,128)S(1)}, f32[8,128]{1,0:T(8,128)S(1)}, u32[]{:S(2)}, u32[]{:S(2)}) collective-permute-start(f32[8,128]{1,0:T(8,128)S(1)} %get-tuple-element.49), channel_id=1, source_target_pairs={{0,8},{8,16},{16,24},{24,0},{1,9},{9,17},{17,25},{25,1},{2,10},{10... | collective-permute-start | bytes 12296 | tf_op jit(solution)/shard_map/ppermute | solution.py:557
  50.0 1.8 %shard_map.60.near = f32[6,2,64,128]{3,2,1,0:T(8,128)S(1)} custom-call(f32[2,512,128]{2,1,0:T(8,128)S(1)} %get-tuple-element.47.phi, s32[6,256]{1,0:T(8,128)S(1)} %get-tuple-element.36.halo_code), custom_call_target="tpu_custom_call" | custom-call | flops 13107200 | bytes 923648 | tf_op jit(solution)/shard_map/pallas_call | solution.py:541
  51.9 1.6 %collective-permute-done.5.after = f32[8,128]{1,0:T(8,128)S(1)} collective-permute-done((f32[8,128]{1,0:T(8,128)S(1)}, f32[8,128]{1,0:T(8,128)S(1)}, u32[]{:S(2)}, u32[]{:S(2)}) %collective-permute-start.5) | collective-permute-done | bytes 4128 | tf_op jit(solution)/shard_map/ppermute | solution.py:558
  53.5 4.6 %shard_map.61 = (f32[2,512,128]{2,1,0:T(8,128)S(1)}, f32[8,64,128]{2,1,0:T(8,128)}, f32[24,128]{1,0:T(8,128)S(1)}, f32[24,128]{1,0:T(8,128)S(1)}) custom-call(f32[2,512,128]{2,1,0:T(8,128)S(1)} %get-tuple-element.47.phi, f32[2,512,128]{2,1,0:T(8,128)S(1)} %get-tuple-element.43.phi.origin, f32[6,2,64,128]{3,2,1,0:T(8,128)S(1)} %shard_map.60.near, ...), custom_call_target="tpu_custom_call" | custom-call | flops 7864320 | bytes 2369536 | tf_op jit(solution)/shard_map/pallas_call | solution.py:541
  58.1 5.1 %all-to-all-start.3 = ((f32[8,64,128]{2,1,0:T(8,128)}), f32[8,64,128]{2,1,0:T(8,128)S(1)}, u32[]{:S(2)}, u32[]{:S(2)}) async-start(f32[8,64,128]{2,1,0:T(8,128)} %get-tuple-element.54), calls=%async_computation.3 | async-start | bytes 524288 | tf_op jit(solution)/shard_map/all_to_all | solution.py:556
  63.2 1.2 %collective-permute-start.6 = (f32[24,128]{1,0:T(8,128)S(1)}, f32[24,128]{1,0:T(8,128)S(1)}, u32[]{:S(2)}, u32[]{:S(2)}) collective-permute-start(f32[24,128]{1,0:T(8,128)S(1)} %get-tuple-element.55), channel_id=1, source_target_pairs={{0,8},{8,16},{16,24},{24,0},{1,9},{9,17},{17,25},{25,1},{2,10},{10... | collective-permute-start | bytes 36872 | tf_op jit(solution)/shard_map/ppermute | solution.py:557
  64.3 1.8 %collective-permute-start.7 = (f32[24,128]{1,0:T(8,128)S(1)}, f32[24,128]{1,0:T(8,128)S(1)}, u32[]{:S(2)}, u32[]{:S(2)}) collective-permute-start(f32[24,128]{1,0:T(8,128)S(1)} %get-tuple-element.56), channel_id=1, source_target_pairs={{8,0},{16,8},{24,16},{0,24},{9,1},{17,9},{25,17},{1,25},{10,2},{18... | collective-permute-start | bytes 36872 | tf_op jit(solution)/shard_map/ppermute | solution.py:558
  66.1 6.6 %shard_map.62 = (f32[6,2,192,128]{3,2,1,0:T(8,128)S(1)}, f32[3,2,256,128]{3,2,1,0:T(8,128)S(1)}) custom-call(f32[2,512,128]{2,1,0:T(8,128)S(1)} %get-tuple-element.51.phi, s32[6,256]{1,0:T(8,128)S(1)} %get-tuple-element.36.halo_code), custom_call_target="tpu_custom_call" | custom-call | flops 39321600 | bytes 2496512 | tf_op jit(solution)/shard_map/pallas_call | solution.py:541
  73.6 1.1 %copy-done.3 = f32[3,2,256,128]{3,2,1,0:T(8,128)S(1)} copy-done((f32[3,2,256,128]{3,2,1,0:T(8,128)S(1)}, f32[3,2,256,128]{3,2,1,0:T(8,128)}, u32[]{:S(2)}) %copy-start.3) | copy-done | bytes 786456
  74.8 7.1 %shard_map.63 = (f32[2,512,128]{2,1,0:T(8,128)S(1)}, f32[8,24,128]{2,1,0:T(8,128)}, f32[8,128]{1,0:T(8,128)S(1)}, f32[8,128]{1,0:T(8,128)S(1)}) custom-call(f32[2,512,128]{2,1,0:T(8,128)S(1)} %get-tuple-element.51.phi, f32[6,2,192,128]{3,2,1,0:T(8,128)S(1)} %get-tuple-element.52.near, f32[3,2,256,128]{3,2,1,0:T(8,128)S(1)} %copy-done.3, f32[512,256]{1,0:T(8,128)} %speed.3, ...), custom_call_target="tpu_custom_call" | custom-call | flops 39321600 | bytes 3942400 | tf_op jit(solution)/shard_map/pallas_call | solution.py:541
  81.8 5.1 %all-to-all-start.4 = ((f32[8,24,128]{2,1,0:T(8,128)}), f32[8,24,128]{2,1,0:T(8,128)S(1)}, u32[]{:S(2)}, u32[]{:S(2)}) async-start(f32[8,24,128]{2,1,0:T(8,128)} %get-tuple-element.58), calls=%async_computation.4 | async-start | bytes 196608 | tf_op jit(solution)/shard_map/all_to_all | solution.py:556
  87.2 2.7 %collective-permute-start.9 = (f32[8,128]{1,0:T(8,128)S(1)}, f32[8,128]{1,0:T(8,128)S(1)}, u32[]{:S(2)}, u32[]{:S(2)}) collective-permute-start(f32[8,128]{1,0:T(8,128)S(1)} %get-tuple-element.60), channel_id=1, source_target_pairs={{8,0},{16,8},{24,16},{0,24},{9,1},{17,9},{25,17},{1,25},{10,2},{18... | collective-permute-start | bytes 12296 | tf_op jit(solution)/shard_map/ppermute | solution.py:558
  89.9 1.8 %shard_map.64.near = f32[6,2,64,128]{3,2,1,0:T(8,128)S(1)} custom-call(f32[2,512,128]{2,1,0:T(8,128)S(1)} %get-tuple-element.57.phi.origin, s32[6,256]{1,0:T(8,128)S(1)} %get-tuple-element.36.halo_code), custom_call_target="tpu_custom_call" | custom-call | flops 13107200 | bytes 923648 | tf_op jit(solution)/shard_map/pallas_call | solution.py:541
  91.7 1.6 %all-to-all-done.4.arrived = f32[8,24,128]{2,1,0:T(8,128)S(1)} async-done(((f32[8,24,128]{2,1,0:T(8,128)}), f32[8,24,128]{2,1,0:T(8,128)S(1)}, u32[]{:S(2)}, u32[]{:S(2)}) %all-to-all-start.4) | async-done | bytes 98336 | tf_op jit(solution)/shard_map/all_to_all | solution.py:556
  93.3 3.3 %shard_map.65 = (f32[2,512,128]{2,1,0:T(8,128)S(1)}, f32[8,24,128]{2,1,0:T(8,128)}, f32[8,128]{1,0:T(8,128)S(1)}, f32[8,128]{1,0:T(8,128)S(1)}) custom-call(f32[2,512,128]{2,1,0:T(8,128)S(1)} %get-tuple-element.57.phi.origin, f32[2,512,128]{2,1,0:T(8,128)S(1)} %get-tuple-element.57.phi.origin, f32[6,2,64,128]{3,2,1,0:T(8,128)S(1)} %shard_map.64.near, ...), custom_call_target="tpu_custom_call" | custom-call | flops 7864320 | bytes 2189312 | tf_op jit(solution)/shard_map/pallas_call | solution.py:541
  96.6 3.5 %all-to-all-start.5 = ((f32[8,24,128]{2,1,0:T(8,128)}), f32[8,24,128]{2,1,0:T(8,128)S(1)}, u32[]{:S(2)}, u32[]{:S(2)}) async-start(f32[8,24,128]{2,1,0:T(8,128)} %get-tuple-element.62), calls=%async_computation.5 | async-start | bytes 196608 | tf_op jit(solution)/shard_map/all_to_all | solution.py:556
  100.1 1.7 %collective-permute-start.10 = (f32[8,128]{1,0:T(8,128)S(1)}, f32[8,128]{1,0:T(8,128)S(1)}, u32[]{:S(2)}, u32[]{:S(2)}) collective-permute-start(f32[8,128]{1,0:T(8,128)S(1)} %get-tuple-element.63), channel_id=1, source_target_pairs={{0,8},{8,16},{16,24},{24,0},{1,9},{9,17},{17,25},{25,1},{2,10},{10... | collective-permute-start | bytes 12296 | tf_op jit(solution)/shard_map/ppermute | solution.py:557
  101.8 1.2 %collective-permute-start.11 = (f32[8,128]{1,0:T(8,128)S(1)}, f32[8,128]{1,0:T(8,128)S(1)}, u32[]{:S(2)}, u32[]{:S(2)}) collective-permute-start(f32[8,128]{1,0:T(8,128)S(1)} %get-tuple-element.64), channel_id=1, source_target_pairs={{8,0},{16,8},{24,16},{0,24},{9,1},{17,9},{25,17},{1,25},{10,2},{18... | collective-permute-start | bytes 12296 | tf_op jit(solution)/shard_map/ppermute | solution.py:558
  103.0 1.8 %shard_map.66.near = f32[6,2,64,128]{3,2,1,0:T(8,128)S(1)} custom-call(f32[2,512,128]{2,1,0:T(8,128)S(1)} %get-tuple-element.61.phi, s32[6,256]{1,0:T(8,128)S(1)} %get-tuple-element.36.halo_code), custom_call_target="tpu_custom_call" | custom-call | flops 13107200 | bytes 923648 | tf_op jit(solution)/shard_map/pallas_call | solution.py:541
  106.5 2.8 %shard_map.67 = f32[512,256]{1,0:T(8,128)} custom-call(f32[2,512,128]{2,1,0:T(8,128)S(1)} %get-tuple-element.61.phi, f32[2,512,128]{2,1,0:T(8,128)S(1)} %get-tuple-element.57.phi.origin, f32[6,2,64,128]{3,2,1,0:T(8,128)S(1)} %shard_map.66.near, f32[8,24,128]{2,1,0:T(8,128)S(1)} %all-to-all-done.5.arrived, f32[8,128]{1,0:T(8,128)S(1)} %collective-permute-done.10.before, ...), custom_call_target="tpu_custom_call" | custom-call | flops 7864320 | bytes 2082816 | tf_op jit(solution)/shard_map/pallas_call | solution.py:541
  (25 shorter events, 5.6 us)
Async XLA Ops:
  3.8 16.8 %all-to-all-start = ((f32[8,64,128]{2,1,0:T(8,128)}), f32[8,64,128]{2,1,0:T(8,128)S(1)}, u32[]{:S(2)}, u32[]{:S(2)}) async-start(f32[8,64,128]{2,1,0:T(8,128)} %get-tuple-element.39), calls=%async_computation | async-start | bytes 524288 | tf_op jit(solution)/shard_map/all_to_all | solution.py:556
  10.2 10.5 %collective-permute-start = (f32[24,128]{1,0:T(8,128)S(1)}, f32[24,128]{1,0:T(8,128)S(1)}, u32[]{:S(2)}, u32[]{:S(2)}) collective-permute-start(f32[24,128]{1,0:T(8,128)S(1)} %get-tuple-element.40), channel_id=1, source_target_pairs={{0,8},{8,16},{16,24},{24,0},{1,9},{9,17},{17,25},{25,1},{2,10},{10... | collective-permute-start | bytes 36872 | tf_op jit(solution)/shard_map/ppermute | solution.py:557
  11.6 9.0 %collective-permute-start.1 = (f32[24,128]{1,0:T(8,128)S(1)}, f32[24,128]{1,0:T(8,128)S(1)}, u32[]{:S(2)}, u32[]{:S(2)}) collective-permute-start(f32[24,128]{1,0:T(8,128)S(1)} %get-tuple-element.41), channel_id=1, source_target_pairs={{8,0},{16,8},{24,16},{0,24},{9,1},{17,9},{25,17},{1,25},{10,2},{18... | collective-permute-start | bytes 36872 | tf_op jit(solution)/shard_map/ppermute | solution.py:558
  19.7 0.9 copy-start
  20.6 1.1 %copy-start.1 = (f32[3,2,256,128]{3,2,1,0:T(8,128)S(1)}, f32[3,2,256,128]{3,2,1,0:T(8,128)}, u32[]{:S(2)}) copy-start(f32[3,2,256,128]{3,2,1,0:T(8,128)} %copy-done) | copy-start | bytes 2359300
  28.8 11.5 %all-to-all-start.1 = ((f32[8,24,128]{2,1,0:T(8,128)}), f32[8,24,128]{2,1,0:T(8,128)S(1)}, u32[]{:S(2)}, u32[]{:S(2)}) async-start(f32[8,24,128]{2,1,0:T(8,128)} %get-tuple-element.44), calls=%async_computation.1 | async-start | bytes 196608 | tf_op jit(solution)/shard_map/all_to_all | solution.py:556
  33.9 4.7 %collective-permute-start.2 = (f32[8,128]{1,0:T(8,128)S(1)}, f32[8,128]{1,0:T(8,128)S(1)}, u32[]{:S(2)}, u32[]{:S(2)}) collective-permute-start(f32[8,128]{1,0:T(8,128)S(1)} %get-tuple-element.45), channel_id=1, source_target_pairs={{0,8},{8,16},{16,24},{24,0},{1,9},{9,17},{17,25},{25,1},{2,10},{10... | collective-permute-start | bytes 12296 | tf_op jit(solution)/shard_map/ppermute | solution.py:557
  34.5 4.2 %collective-permute-start.3 = (f32[8,128]{1,0:T(8,128)S(1)}, f32[8,128]{1,0:T(8,128)S(1)}, u32[]{:S(2)}, u32[]{:S(2)}) collective-permute-start(f32[8,128]{1,0:T(8,128)S(1)} %get-tuple-element.46), channel_id=1, source_target_pairs={{8,0},{16,8},{24,16},{0,24},{9,1},{17,9},{25,17},{1,25},{10,2},{18... | collective-permute-start | bytes 12296 | tf_op jit(solution)/shard_map/ppermute | solution.py:558
  43.6 9.9 %all-to-all-start.2 = ((f32[8,24,128]{2,1,0:T(8,128)}), f32[8,24,128]{2,1,0:T(8,128)S(1)}, u32[]{:S(2)}, u32[]{:S(2)}) async-start(f32[8,24,128]{2,1,0:T(8,128)} %get-tuple-element.48), calls=%async_computation.2 | async-start | bytes 196608 | tf_op jit(solution)/shard_map/all_to_all | solution.py:556
  47.1 4.7 %collective-permute-start.4 = (f32[8,128]{1,0:T(8,128)S(1)}, f32[8,128]{1,0:T(8,128)S(1)}, u32[]{:S(2)}, u32[]{:S(2)}) collective-permute-start(f32[8,128]{1,0:T(8,128)S(1)} %get-tuple-element.49), channel_id=1, source_target_pairs={{0,8},{8,16},{16,24},{24,0},{1,9},{9,17},{17,25},{25,1},{2,10},{10... | collective-permute-start | bytes 12296 | tf_op jit(solution)/shard_map/ppermute | solution.py:557
  49.8 3.6 %collective-permute-start.5 = (f32[8,128]{1,0:T(8,128)S(1)}, f32[8,128]{1,0:T(8,128)S(1)}, u32[]{:S(2)}, u32[]{:S(2)}) collective-permute-start(f32[8,128]{1,0:T(8,128)S(1)} %get-tuple-element.50), channel_id=1, source_target_pairs={{8,0},{16,8},{24,16},{0,24},{9,1},{17,9},{25,17},{1,25},{10,2},{18... | collective-permute-start | bytes 12296 | tf_op jit(solution)/shard_map/ppermute | solution.py:558
  58.1 15.6 %all-to-all-start.3 = ((f32[8,64,128]{2,1,0:T(8,128)}), f32[8,64,128]{2,1,0:T(8,128)S(1)}, u32[]{:S(2)}, u32[]{:S(2)}) async-start(f32[8,64,128]{2,1,0:T(8,128)} %get-tuple-element.54), calls=%async_computation.3 | async-start | bytes 524288 | tf_op jit(solution)/shard_map/all_to_all | solution.py:556
  63.2 10.5 %collective-permute-start.6 = (f32[24,128]{1,0:T(8,128)S(1)}, f32[24,128]{1,0:T(8,128)S(1)}, u32[]{:S(2)}, u32[]{:S(2)}) collective-permute-start(f32[24,128]{1,0:T(8,128)S(1)} %get-tuple-element.55), channel_id=1, source_target_pairs={{0,8},{8,16},{16,24},{24,0},{1,9},{9,17},{17,25},{25,1},{2,10},{10... | collective-permute-start | bytes 36872 | tf_op jit(solution)/shard_map/ppermute | solution.py:557
  64.3 9.3 %collective-permute-start.7 = (f32[24,128]{1,0:T(8,128)S(1)}, f32[24,128]{1,0:T(8,128)S(1)}, u32[]{:S(2)}, u32[]{:S(2)}) collective-permute-start(f32[24,128]{1,0:T(8,128)S(1)} %get-tuple-element.56), channel_id=1, source_target_pairs={{8,0},{16,8},{24,16},{0,24},{9,1},{17,9},{25,17},{1,25},{10,2},{18... | collective-permute-start | bytes 36872 | tf_op jit(solution)/shard_map/ppermute | solution.py:558
  72.7 0.9 copy-start.2
  73.6 1.1 %copy-start.3 = (f32[3,2,256,128]{3,2,1,0:T(8,128)S(1)}, f32[3,2,256,128]{3,2,1,0:T(8,128)}, u32[]{:S(2)}) copy-start(f32[3,2,256,128]{3,2,1,0:T(8,128)} %copy-done.2) | copy-start | bytes 2359300
  81.8 11.5 %all-to-all-start.4 = ((f32[8,24,128]{2,1,0:T(8,128)}), f32[8,24,128]{2,1,0:T(8,128)S(1)}, u32[]{:S(2)}, u32[]{:S(2)}) async-start(f32[8,24,128]{2,1,0:T(8,128)} %get-tuple-element.58), calls=%async_computation.4 | async-start | bytes 196608 | tf_op jit(solution)/shard_map/all_to_all | solution.py:556
  87.0 4.7 %collective-permute-start.8 = (f32[8,128]{1,0:T(8,128)S(1)}, f32[8,128]{1,0:T(8,128)S(1)}, u32[]{:S(2)}, u32[]{:S(2)}) collective-permute-start(f32[8,128]{1,0:T(8,128)S(1)} %get-tuple-element.59), channel_id=1, source_target_pairs={{0,8},{8,16},{16,24},{24,0},{1,9},{9,17},{17,25},{25,1},{2,10},{10... | collective-permute-start | bytes 12296 | tf_op jit(solution)/shard_map/ppermute | solution.py:557
  87.2 4.5 %collective-permute-start.9 = (f32[8,128]{1,0:T(8,128)S(1)}, f32[8,128]{1,0:T(8,128)S(1)}, u32[]{:S(2)}, u32[]{:S(2)}) collective-permute-start(f32[8,128]{1,0:T(8,128)S(1)} %get-tuple-element.60), channel_id=1, source_target_pairs={{8,0},{16,8},{24,16},{0,24},{9,1},{17,9},{25,17},{1,25},{10,2},{18... | collective-permute-start | bytes 12296 | tf_op jit(solution)/shard_map/ppermute | solution.py:558
  96.6 9.9 %all-to-all-start.5 = ((f32[8,24,128]{2,1,0:T(8,128)}), f32[8,24,128]{2,1,0:T(8,128)S(1)}, u32[]{:S(2)}, u32[]{:S(2)}) async-start(f32[8,24,128]{2,1,0:T(8,128)} %get-tuple-element.62), calls=%async_computation.5 | async-start | bytes 196608 | tf_op jit(solution)/shard_map/all_to_all | solution.py:556
  100.1 4.7 %collective-permute-start.10 = (f32[8,128]{1,0:T(8,128)S(1)}, f32[8,128]{1,0:T(8,128)S(1)}, u32[]{:S(2)}, u32[]{:S(2)}) collective-permute-start(f32[8,128]{1,0:T(8,128)S(1)} %get-tuple-element.63), channel_id=1, source_target_pairs={{0,8},{8,16},{16,24},{24,0},{1,9},{9,17},{17,25},{25,1},{2,10},{10... | collective-permute-start | bytes 12296 | tf_op jit(solution)/shard_map/ppermute | solution.py:557
  101.8 3.6 %collective-permute-start.11 = (f32[8,128]{1,0:T(8,128)S(1)}, f32[8,128]{1,0:T(8,128)S(1)}, u32[]{:S(2)}, u32[]{:S(2)}) collective-permute-start(f32[8,128]{1,0:T(8,128)S(1)} %get-tuple-element.64), channel_id=1, source_target_pairs={{8,0},{16,8},{24,16},{0,24},{9,1},{17,9},{25,17},{1,25},{10,2},{18... | collective-permute-start | bytes 12296 | tf_op jit(solution)/shard_map/ppermute | solution.py:558

commit v4 on v3

--- a/solution.py
+++ b/solution.py
@@ -301,6 +301,7 @@
             pull_far(plan, table, halo_code, near, halos, (0, 1), l * 8 + j)
 
     stage_planes(0)
+    ready()
 
     @pl.loop(0, 8)
     def _(i):
@@ -322,7 +323,6 @@
             for j, value in enumerate(line_values(*lines[2 * h + 1])):
                 squares[h, rows8(i * 64 + j * 8), :] += value
 
-    ready()
     stage_columns(0)
 
     @pl.loop(0, 8)
@@ -479,7 +479,8 @@
                 pull_local(plan, phi, None, halo_code, near, q * 2 + v)
 
         return
-    inner, ends = rest
+    inner, ends, kept, done = rest
+    copies = [pltpu.make_async_copy(kept.at[a], inner.at[a], done.at[a]) for a in range(3)]
     fill_ends(plan, phi, ends)
     for axis in range(3):
 
@@ -489,14 +490,19 @@
             pull_local(plan, phi, ends, halo_code, near, axis * 8 + q)
             for h in range(plan.halves):
                 for m, value in enumerate(inner_values(lines[h])):
-                    inner[axis, h, rows8(q * 32 + m * 8), :] = value
+                    kept[axis, h, rows8(q * 32 + m * 8), :] = value
+
+        copies[axis].start()
+    for copy in copies:
+        copy.wait()
 
 
 def advect_kernel(
     plan, sends, phi, near, inner, speed, arrived, before, after, send_code, halo_code,
-    moved, outgoing, low, high, ends, table, halos, squares, fast, loaded,
+    moved, outgoing, low, high, ends, table, halos, squares, fast, kept, loaded, found,
 ):
-    copies = [
+    copies = [pltpu.make_async_copy(inner.at[a], kept.at[a], found.at[a]) for a in range(3)]
+    copies += [
         pltpu.make_async_copy(speed.at[:, half(h)], fast.at[h], loaded.at[h])
         for h in range(plan.halves)
     ]
@@ -508,7 +514,7 @@
             copy.wait()
 
     unpack_far(plan, arrived, before, after, table)
-    advect(plan, phi, fast, ready, near, inner, table, halo_code, halos, squares, moved)
+    advect(plan, phi, fast, ready, near, kept, table, halo_code, halos, squares, moved)
     pack_sends(sends, moved, ends, send_code, table, outgoing, low, high)
 
 
@@ -530,7 +536,7 @@
     return jax.ShapeDtypeStruct(shape, jnp.float32)
 
 
-def call(kernel, out_shape, scratch, flops, *operands, far=()):
+def call(kernel, out_shape, scratch, flops, *operands, far=(), far_out=()):
     whole = pl.BlockSpec(memory_space=pltpu.VMEM)
     apart = pl.BlockSpec(memory_space=pltpu.HBM)
     size = sum(x.size * 4 for x in operands) + sum(x.size * 4 for x in out_shape)
@@ -540,9 +546,11 @@
     ]
     return pl.pallas_call(
         kernel,
-        out_shape=out_shape,
+        out_shape=[
+            pltpu.HBM(x.shape, x.dtype) if n in far_out else x for n, x in enumerate(out_shape)
+        ],
         in_specs=[apart if n in far else whole for n in range(len(operands))],
-        out_specs=[whole] * len(out_shape),
+        out_specs=[apart if n in far_out else whole for n in range(len(out_shape))],
         scratch_shapes=scratch,
         cost_estimate=pl.CostEstimate(flops=flops, bytes_accessed=size, transcendentals=0),
         compiler_params=pltpu.CompilerParams(vmem_limit_bytes=12 * 1024 * 1024),
@@ -607,21 +615,25 @@
         out = [f32((6, plan.halves, 64 * plan.layers, LANES))]
         scratch = []
         if plan.layers > 1:
-            out.append(f32((3, plan.halves, rows // 2, LANES)))
-            scratch.append(ends(plan))
+            out.append(f32(inner_shape))
+            scratch = [ends(plan), pltpu.VMEM(inner_shape, jnp.float32)]
+            scratch.append(pltpu.SemaphoreType.DMA((3,)))
         flops = rows * count * 100 * plan.layers
-        return call(functools.partial(near_kernel, plan), out, scratch, flops, phi, halo_code)
-
+        kernel = functools.partial(near_kernel, plan)
+        return call(kernel, out, scratch, flops, phi, halo_code, far_out=(1,))
+
+    inner_shape = (3, wide.halves, rows // 2, LANES)
     block = pltpu.VMEM((wide.halves, rows, LANES), jnp.float32)
     for offset_step in range(OFFSET_STEPS):
         phi, *message = call(
             functools.partial(advect_kernel, wide, thin),
             [field] + sent(thin),
             [ends(wide), table(wide), halos(wide), block, block]
-            + [pltpu.SemaphoreType.DMA((wide.halves,))],
+            + [pltpu.VMEM(inner_shape, jnp.float32)]
+            + [pltpu.SemaphoreType.DMA((wide.halves,)), pltpu.SemaphoreType.DMA((3,))],
             rows * count * 300,
             phi, *near_halos(wide, phi), speed, *exchange(*message), send_code, halo_code,
-            far=(3,),
+            far=(2, 3),
         )
         origin = phi
         for redist_pass in range(REDIST_PASSES):

time: 110 us -> 109 us (level)
  local copies, waits for them, and re-layouts: 4.03 us -> 0 us
  Pallas kernels: 52.4 us -> 55.3 us
    unnamed x8 -> x0, local copies, waits for them, and re-layouts: 4.03 us -> none
    pallas_call x13, Pallas kernels: 52.4 us -> 55.3 us  [call(): pl.pallas_call(kernel, out_shape=[pltpu.HBM(x.shape, x.dtype) if n in far...]
  transfers between devices with their start and end apart: 18 -> 18, of which waited for: 5 -> 5; matrix products, arithmetic and copies ran while one was open for 0% -> 0% of each run, Pallas kernels for 19% -> 20%
where the time goes in v4:
time: 109 us; the launch traced here: 108 us
  Pallas kernels  55.3 us (51%)
  starting transfers between devices  46.3 us (42%)
  waiting for transfers between devices  6.39 us (6%)
    pallas_call x13, Pallas kernels, call(): pl.pallas_call(kernel, out_shape=[pltpu.HBM(x.shape, x.dtype) if n in far...  55.3 us
    all_to_all x6, starting transfers between devices, exchange(): lax.all_to_all(outgoing, 'dev', split_axis=0, concat_axis=0, tiled=True)  28.7 us
    ppermute x6, starting transfers between devices, exchange(): after = lax.ppermute(low, 'group', down)  9.62 us
    ppermute x6, starting transfers between devices, exchange(): before = lax.ppermute(high, 'group', up)  7.93 us
    all_to_all x6, waiting for transfers between devices, exchange(): lax.all_to_all(outgoing, 'dev', split_axis=0, concat_axis=0, tiled=True)  4.21 us
  transfers between devices with their start and end apart: 18, of which 5 were waited for; matrix products, arithmetic and copies ran while one was open for 0% of the time, Pallas kernels for 20%

profile of v4, /device:TPU:0, one launch (start us, length us, event | category | flops | bytes accessed | tf_op | source)
XLA Modules:
  0.0 108.1 jit_solution(14603222237719620373)
XLA Ops:
  0.0 3.8 %shard_map.55 = (f32[2,512,128]{2,1,0:T(8,128)S(1)}, f32[8,64,128]{2,1,0:T(8,128)}, f32[24,128]{1,0:T(8,128)S(1)}, f32[24,128]{1,0:T(8,128)S(1)}, s32[8,128]{1,0:T(8,128)S(1)}, /*index=5*/s32[6,256]{1,0:T(8,128)S(1)}) custom-call(f32[512,256]{1,0:T(8,128)} %level_set.1, s32[8,40]{1,0:T(8,128)} %peer_slabs.1, s32[2,16]{1,0:T(2,128)} %region_slabs.1, ...), custom_call_target="tpu_custom_call" | custom-call | flops 1000000 | bytes 1353088 | tf_op jit(solution)/shard_map/pallas_call | solution.py:547
  3.8 6.3 %all-to-all-start = ((f32[8,64,128]{2,1,0:T(8,128)}), f32[8,64,128]{2,1,0:T(8,128)S(1)}, u32[]{:S(2)}, u32[]{:S(2)}) async-start(f32[8,64,128]{2,1,0:T(8,128)} %get-tuple-element.39), calls=%async_computation | async-start | bytes 524288 | tf_op jit(solution)/shard_map/all_to_all | solution.py:564
  10.2 1.5 %collective-permute-start = (f32[24,128]{1,0:T(8,128)S(1)}, f32[24,128]{1,0:T(8,128)S(1)}, u32[]{:S(2)}, u32[]{:S(2)}) collective-permute-start(f32[24,128]{1,0:T(8,128)S(1)} %get-tuple-element.40), channel_id=1, source_target_pairs={{0,8},{8,16},{16,24},{24,0},{1,9},{9,17},{17,25},{25,1},{2,10},{10... | collective-permute-start | bytes 36872 | tf_op jit(solution)/shard_map/ppermute | solution.py:565
  11.6 1.4 %collective-permute-start.1 = (f32[24,128]{1,0:T(8,128)S(1)}, f32[24,128]{1,0:T(8,128)S(1)}, u32[]{:S(2)}, u32[]{:S(2)}) collective-permute-start(f32[24,128]{1,0:T(8,128)S(1)} %get-tuple-element.41), channel_id=1, source_target_pairs={{8,0},{16,8},{24,16},{0,24},{9,1},{17,9},{25,17},{1,25},{10,2},{18... | collective-permute-start | bytes 36872 | tf_op jit(solution)/shard_map/ppermute | solution.py:566
  13.1 7.2 %shard_map.56 = (f32[6,2,192,128]{3,2,1,0:T(8,128)S(1)}, f32[3,2,256,128]{3,2,1,0:T(8,128)}) custom-call(f32[2,512,128]{2,1,0:T(8,128)S(1)} %get-tuple-element.35.phi, s32[6,256]{1,0:T(8,128)S(1)} %get-tuple-element.36.halo_code), custom_call_target="tpu_custom_call" | custom-call | flops 39321600 | bytes 2496512 | tf_op jit(solution)/shard_map/pallas_call | solution.py:547
  20.3 8.0 %shard_map.57 = (f32[2,512,128]{2,1,0:T(8,128)S(1)}, f32[8,24,128]{2,1,0:T(8,128)}, f32[8,128]{1,0:T(8,128)S(1)}, f32[8,128]{1,0:T(8,128)S(1)}) custom-call(f32[2,512,128]{2,1,0:T(8,128)S(1)} %get-tuple-element.35.phi, f32[6,2,192,128]{3,2,1,0:T(8,128)S(1)} %get-tuple-element.37.near, f32[3,2,256,128]{3,2,1,0:T(8,128)} %get-tuple-element.38.inner, ...), custom_call_target="tpu_custom_call" | custom-call | flops 39321600 | bytes 3942400 | tf_op jit(solution)/shard_map/pallas_call | solution.py:547
  28.3 5.1 %all-to-all-start.1 = ((f32[8,24,128]{2,1,0:T(8,128)}), f32[8,24,128]{2,1,0:T(8,128)S(1)}, u32[]{:S(2)}, u32[]{:S(2)}) async-start(f32[8,24,128]{2,1,0:T(8,128)} %get-tuple-element.44), calls=%async_computation.1 | async-start | bytes 196608 | tf_op jit(solution)/shard_map/all_to_all | solution.py:564
  34.0 2.3 %collective-permute-start.3 = (f32[8,128]{1,0:T(8,128)S(1)}, f32[8,128]{1,0:T(8,128)S(1)}, u32[]{:S(2)}, u32[]{:S(2)}) collective-permute-start(f32[8,128]{1,0:T(8,128)S(1)} %get-tuple-element.46), channel_id=1, source_target_pairs={{8,0},{16,8},{24,16},{0,24},{9,1},{17,9},{25,17},{1,25},{10,2},{18... | collective-permute-start | bytes 12296 | tf_op jit(solution)/shard_map/ppermute | solution.py:566
  36.3 1.8 %shard_map.58.near = f32[6,2,64,128]{3,2,1,0:T(8,128)S(1)} custom-call(f32[2,512,128]{2,1,0:T(8,128)S(1)} %get-tuple-element.43.phi.origin, s32[6,256]{1,0:T(8,128)S(1)} %get-tuple-element.36.halo_code), custom_call_target="tpu_custom_call" | custom-call | flops 13107200 | bytes 923648 | tf_op jit(solution)/shard_map/pallas_call | solution.py:547
  38.2 1.6 %all-to-all-done.1.arrived = f32[8,24,128]{2,1,0:T(8,128)S(1)} async-done(((f32[8,24,128]{2,1,0:T(8,128)}), f32[8,24,128]{2,1,0:T(8,128)S(1)}, u32[]{:S(2)}, u32[]{:S(2)}) %all-to-all-start.1) | async-done | bytes 98336 | tf_op jit(solution)/shard_map/all_to_all | solution.py:564
  39.7 3.3 %shard_map.59 = (f32[2,512,128]{2,1,0:T(8,128)S(1)}, f32[8,24,128]{2,1,0:T(8,128)}, f32[8,128]{1,0:T(8,128)S(1)}, f32[8,128]{1,0:T(8,128)S(1)}) custom-call(f32[2,512,128]{2,1,0:T(8,128)S(1)} %get-tuple-element.43.phi.origin, f32[2,512,128]{2,1,0:T(8,128)S(1)} %get-tuple-element.43.phi.origin, f32[6,2,64,128]{3,2,1,0:T(8,128)S(1)} %shard_map.58.near, ...), custom_call_target="tpu_custom_call" | custom-call | flops 7864320 | bytes 2189312 | tf_op jit(solution)/shard_map/pallas_call | solution.py:547
  43.0 3.5 %all-to-all-start.2 = ((f32[8,24,128]{2,1,0:T(8,128)}), f32[8,24,128]{2,1,0:T(8,128)S(1)}, u32[]{:S(2)}, u32[]{:S(2)}) async-start(f32[8,24,128]{2,1,0:T(8,128)} %get-tuple-element.48), calls=%async_computation.2 | async-start | bytes 196608 | tf_op jit(solution)/shard_map/all_to_all | solution.py:564
  46.6 2.7 %collective-permute-start.4 = (f32[8,128]{1,0:T(8,128)S(1)}, f32[8,128]{1,0:T(8,128)S(1)}, u32[]{:S(2)}, u32[]{:S(2)}) collective-permute-start(f32[8,128]{1,0:T(8,128)S(1)} %get-tuple-element.49), channel_id=1, source_target_pairs={{0,8},{8,16},{16,24},{24,0},{1,9},{9,17},{17,25},{25,1},{2,10},{10... | collective-permute-start | bytes 12296 | tf_op jit(solution)/shard_map/ppermute | solution.py:565
  49.5 1.8 %shard_map.60.near = f32[6,2,64,128]{3,2,1,0:T(8,128)S(1)} custom-call(f32[2,512,128]{2,1,0:T(8,128)S(1)} %get-tuple-element.47.phi, s32[6,256]{1,0:T(8,128)S(1)} %get-tuple-element.36.halo_code), custom_call_target="tpu_custom_call" | custom-call | flops 13107200 | bytes 923648 | tf_op jit(solution)/shard_map/pallas_call | solution.py:547
  51.3 1.6 %collective-permute-done.5.after = f32[8,128]{1,0:T(8,128)S(1)} collective-permute-done((f32[8,128]{1,0:T(8,128)S(1)}, f32[8,128]{1,0:T(8,128)S(1)}, u32[]{:S(2)}, u32[]{:S(2)}) %collective-permute-start.5) | collective-permute-done | bytes 4128 | tf_op jit(solution)/shard_map/ppermute | solution.py:566
  52.9 4.6 %shard_map.61 = (f32[2,512,128]{2,1,0:T(8,128)S(1)}, f32[8,64,128]{2,1,0:T(8,128)}, f32[24,128]{1,0:T(8,128)S(1)}, f32[24,128]{1,0:T(8,128)S(1)}) custom-call(f32[2,512,128]{2,1,0:T(8,128)S(1)} %get-tuple-element.47.phi, f32[2,512,128]{2,1,0:T(8,128)S(1)} %get-tuple-element.43.phi.origin, f32[6,2,64,128]{3,2,1,0:T(8,128)S(1)} %shard_map.60.near, ...), custom_call_target="tpu_custom_call" | custom-call | flops 7864320 | bytes 2369536 | tf_op jit(solution)/shard_map/pallas_call | solution.py:547
  57.5 5.1 %all-to-all-start.3 = ((f32[8,64,128]{2,1,0:T(8,128)}), f32[8,64,128]{2,1,0:T(8,128)S(1)}, u32[]{:S(2)}, u32[]{:S(2)}) async-start(f32[8,64,128]{2,1,0:T(8,128)} %get-tuple-element.54), calls=%async_computation.3 | async-start | bytes 524288 | tf_op jit(solution)/shard_map/all_to_all | solution.py:564
  62.6 1.2 %collective-permute-start.6 = (f32[24,128]{1,0:T(8,128)S(1)}, f32[24,128]{1,0:T(8,128)S(1)}, u32[]{:S(2)}, u32[]{:S(2)}) collective-permute-start(f32[24,128]{1,0:T(8,128)S(1)} %get-tuple-element.55), channel_id=1, source_target_pairs={{0,8},{8,16},{16,24},{24,0},{1,9},{9,17},{17,25},{25,1},{2,10},{10... | collective-permute-start | bytes 36872 | tf_op jit(solution)/shard_map/ppermute | solution.py:565
  63.8 1.8 %collective-permute-start.7 = (f32[24,128]{1,0:T(8,128)S(1)}, f32[24,128]{1,0:T(8,128)S(1)}, u32[]{:S(2)}, u32[]{:S(2)}) collective-permute-start(f32[24,128]{1,0:T(8,128)S(1)} %get-tuple-element.56), channel_id=1, source_target_pairs={{8,0},{16,8},{24,16},{0,24},{9,1},{17,9},{25,17},{1,25},{10,2},{18... | collective-permute-start | bytes 36872 | tf_op jit(solution)/shard_map/ppermute | solution.py:566
  65.5 7.2 %shard_map.62 = (f32[6,2,192,128]{3,2,1,0:T(8,128)S(1)}, f32[3,2,256,128]{3,2,1,0:T(8,128)}) custom-call(f32[2,512,128]{2,1,0:T(8,128)S(1)} %get-tuple-element.51.phi, s32[6,256]{1,0:T(8,128)S(1)} %get-tuple-element.36.halo_code), custom_call_target="tpu_custom_call" | custom-call | flops 39321600 | bytes 2496512 | tf_op jit(solution)/shard_map/pallas_call | solution.py:547
  72.7 8.0 %shard_map.63 = (f32[2,512,128]{2,1,0:T(8,128)S(1)}, f32[8,24,128]{2,1,0:T(8,128)}, f32[8,128]{1,0:T(8,128)S(1)}, f32[8,128]{1,0:T(8,128)S(1)}) custom-call(f32[2,512,128]{2,1,0:T(8,128)S(1)} %get-tuple-element.51.phi, f32[6,2,192,128]{3,2,1,0:T(8,128)S(1)} %get-tuple-element.52.near, f32[3,2,256,128]{3,2,1,0:T(8,128)} %get-tuple-element.53.inner, ...), custom_call_target="tpu_custom_call" | custom-call | flops 39321600 | bytes 3942400 | tf_op jit(solution)/shard_map/pallas_call | solution.py:547
  80.7 5.1 %all-to-all-start.4 = ((f32[8,24,128]{2,1,0:T(8,128)}), f32[8,24,128]{2,1,0:T(8,128)S(1)}, u32[]{:S(2)}, u32[]{:S(2)}) async-start(f32[8,24,128]{2,1,0:T(8,128)} %get-tuple-element.58), calls=%async_computation.4 | async-start | bytes 196608 | tf_op jit(solution)/shard_map/all_to_all | solution.py:564
  86.1 2.7 %collective-permute-start.9 = (f32[8,128]{1,0:T(8,128)S(1)}, f32[8,128]{1,0:T(8,128)S(1)}, u32[]{:S(2)}, u32[]{:S(2)}) collective-permute-start(f32[8,128]{1,0:T(8,128)S(1)} %get-tuple-element.60), channel_id=1, source_target_pairs={{8,0},{16,8},{24,16},{0,24},{9,1},{17,9},{25,17},{1,25},{10,2},{18... | collective-permute-start | bytes 12296 | tf_op jit(solution)/shard_map/ppermute | solution.py:566
  88.8 1.8 %shard_map.64.near = f32[6,2,64,128]{3,2,1,0:T(8,128)S(1)} custom-call(f32[2,512,128]{2,1,0:T(8,128)S(1)} %get-tuple-element.57.phi.origin, s32[6,256]{1,0:T(8,128)S(1)} %get-tuple-element.36.halo_code), custom_call_target="tpu_custom_call" | custom-call | flops 13107200 | bytes 923648 | tf_op jit(solution)/shard_map/pallas_call | solution.py:547
  90.6 1.6 %all-to-all-done.4.arrived = f32[8,24,128]{2,1,0:T(8,128)S(1)} async-done(((f32[8,24,128]{2,1,0:T(8,128)}), f32[8,24,128]{2,1,0:T(8,128)S(1)}, u32[]{:S(2)}, u32[]{:S(2)}) %all-to-all-start.4) | async-done | bytes 98336 | tf_op jit(solution)/shard_map/all_to_all | solution.py:564
  92.2 3.3 %shard_map.65 = (f32[2,512,128]{2,1,0:T(8,128)S(1)}, f32[8,24,128]{2,1,0:T(8,128)}, f32[8,128]{1,0:T(8,128)S(1)}, f32[8,128]{1,0:T(8,128)S(1)}) custom-call(f32[2,512,128]{2,1,0:T(8,128)S(1)} %get-tuple-element.57.phi.origin, f32[2,512,128]{2,1,0:T(8,128)S(1)} %get-tuple-element.57.phi.origin, f32[6,2,64,128]{3,2,1,0:T(8,128)S(1)} %shard_map.64.near, ...), custom_call_target="tpu_custom_call" | custom-call | flops 7864320 | bytes 2189312 | tf_op jit(solution)/shard_map/pallas_call | solution.py:547
  95.5 3.5 %all-to-all-start.5 = ((f32[8,24,128]{2,1,0:T(8,128)}), f32[8,24,128]{2,1,0:T(8,128)S(1)}, u32[]{:S(2)}, u32[]{:S(2)}) async-start(f32[8,24,128]{2,1,0:T(8,128)} %get-tuple-element.62), calls=%async_computation.5 | async-start | bytes 196608 | tf_op jit(solution)/shard_map/all_to_all | solution.py:564
  99.0 1.7 %collective-permute-start.10 = (f32[8,128]{1,0:T(8,128)S(1)}, f32[8,128]{1,0:T(8,128)S(1)}, u32[]{:S(2)}, u32[]{:S(2)}) collective-permute-start(f32[8,128]{1,0:T(8,128)S(1)} %get-tuple-element.63), channel_id=1, source_target_pairs={{0,8},{8,16},{16,24},{24,0},{1,9},{9,17},{17,25},{25,1},{2,10},{10... | collective-permute-start | bytes 12296 | tf_op jit(solution)/shard_map/ppermute | solution.py:565
  100.7 1.2 %collective-permute-start.11 = (f32[8,128]{1,0:T(8,128)S(1)}, f32[8,128]{1,0:T(8,128)S(1)}, u32[]{:S(2)}, u32[]{:S(2)}) collective-permute-start(f32[8,128]{1,0:T(8,128)S(1)} %get-tuple-element.64), channel_id=1, source_target_pairs={{8,0},{16,8},{24,16},{0,24},{9,1},{17,9},{25,17},{1,25},{10,2},{18... | collective-permute-start | bytes 12296 | tf_op jit(solution)/shard_map/ppermute | solution.py:566
  101.9 1.8 %shard_map.66.near = f32[6,2,64,128]{3,2,1,0:T(8,128)S(1)} custom-call(f32[2,512,128]{2,1,0:T(8,128)S(1)} %get-tuple-element.61.phi, s32[6,256]{1,0:T(8,128)S(1)} %get-tuple-element.36.halo_code), custom_call_target="tpu_custom_call" | custom-call | flops 13107200 | bytes 923648 | tf_op jit(solution)/shard_map/pallas_call | solution.py:547
  104.3 1.0 all-to-all-done.5.arrived
  105.4 2.8 %shard_map.67 = f32[512,256]{1,0:T(8,128)} custom-call(f32[2,512,128]{2,1,0:T(8,128)S(1)} %get-tuple-element.61.phi, f32[2,512,128]{2,1,0:T(8,128)S(1)} %get-tuple-element.57.phi.origin, f32[6,2,64,128]{3,2,1,0:T(8,128)S(1)} %shard_map.66.near, f32[8,24,128]{2,1,0:T(8,128)S(1)} %all-to-all-done.5.arrived, f32[8,128]{1,0:T(8,128)S(1)} %collective-permute-done.10.before, ...), custom_call_target="tpu_custom_call" | custom-call | flops 7864320 | bytes 2082816 | tf_op jit(solution)/shard_map/pallas_call | solution.py:547
  (17 shorter events, 1.7 us)
Async XLA Ops:
  3.8 16.5 %all-to-all-start = ((f32[8,64,128]{2,1,0:T(8,128)}), f32[8,64,128]{2,1,0:T(8,128)S(1)}, u32[]{:S(2)}, u32[]{:S(2)}) async-start(f32[8,64,128]{2,1,0:T(8,128)} %get-tuple-element.39), calls=%async_computation | async-start | bytes 524288 | tf_op jit(solution)/shard_map/all_to_all | solution.py:564
  10.2 10.1 %collective-permute-start = (f32[24,128]{1,0:T(8,128)S(1)}, f32[24,128]{1,0:T(8,128)S(1)}, u32[]{:S(2)}, u32[]{:S(2)}) collective-permute-start(f32[24,128]{1,0:T(8,128)S(1)} %get-tuple-element.40), channel_id=1, source_target_pairs={{0,8},{8,16},{16,24},{24,0},{1,9},{9,17},{17,25},{25,1},{2,10},{10... | collective-permute-start | bytes 36872 | tf_op jit(solution)/shard_map/ppermute | solution.py:565
  11.6 8.6 %collective-permute-start.1 = (f32[24,128]{1,0:T(8,128)S(1)}, f32[24,128]{1,0:T(8,128)S(1)}, u32[]{:S(2)}, u32[]{:S(2)}) collective-permute-start(f32[24,128]{1,0:T(8,128)S(1)} %get-tuple-element.41), channel_id=1, source_target_pairs={{8,0},{16,8},{24,16},{0,24},{9,1},{17,9},{25,17},{1,25},{10,2},{18... | collective-permute-start | bytes 36872 | tf_op jit(solution)/shard_map/ppermute | solution.py:566
  28.3 11.5 %all-to-all-start.1 = ((f32[8,24,128]{2,1,0:T(8,128)}), f32[8,24,128]{2,1,0:T(8,128)S(1)}, u32[]{:S(2)}, u32[]{:S(2)}) async-start(f32[8,24,128]{2,1,0:T(8,128)} %get-tuple-element.44), calls=%async_computation.1 | async-start | bytes 196608 | tf_op jit(solution)/shard_map/all_to_all | solution.py:564
  33.4 4.7 %collective-permute-start.2 = (f32[8,128]{1,0:T(8,128)S(1)}, f32[8,128]{1,0:T(8,128)S(1)}, u32[]{:S(2)}, u32[]{:S(2)}) collective-permute-start(f32[8,128]{1,0:T(8,128)S(1)} %get-tuple-element.45), channel_id=1, source_target_pairs={{0,8},{8,16},{16,24},{24,0},{1,9},{9,17},{17,25},{25,1},{2,10},{10... | collective-permute-start | bytes 12296 | tf_op jit(solution)/shard_map/ppermute | solution.py:565
  34.0 4.2 %collective-permute-start.3 = (f32[8,128]{1,0:T(8,128)S(1)}, f32[8,128]{1,0:T(8,128)S(1)}, u32[]{:S(2)}, u32[]{:S(2)}) collective-permute-start(f32[8,128]{1,0:T(8,128)S(1)} %get-tuple-element.46), channel_id=1, source_target_pairs={{8,0},{16,8},{24,16},{0,24},{9,1},{17,9},{25,17},{1,25},{10,2},{18... | collective-permute-start | bytes 12296 | tf_op jit(solution)/shard_map/ppermute | solution.py:566
  43.0 9.9 %all-to-all-start.2 = ((f32[8,24,128]{2,1,0:T(8,128)}), f32[8,24,128]{2,1,0:T(8,128)S(1)}, u32[]{:S(2)}, u32[]{:S(2)}) async-start(f32[8,24,128]{2,1,0:T(8,128)} %get-tuple-element.48), calls=%async_computation.2 | async-start | bytes 196608 | tf_op jit(solution)/shard_map/all_to_all | solution.py:564
  46.6 4.7 %collective-permute-start.4 = (f32[8,128]{1,0:T(8,128)S(1)}, f32[8,128]{1,0:T(8,128)S(1)}, u32[]{:S(2)}, u32[]{:S(2)}) collective-permute-start(f32[8,128]{1,0:T(8,128)S(1)} %get-tuple-element.49), channel_id=1, source_target_pairs={{0,8},{8,16},{16,24},{24,0},{1,9},{9,17},{17,25},{25,1},{2,10},{10... | collective-permute-start | bytes 12296 | tf_op jit(solution)/shard_map/ppermute | solution.py:565
  49.3 3.6 %collective-permute-start.5 = (f32[8,128]{1,0:T(8,128)S(1)}, f32[8,128]{1,0:T(8,128)S(1)}, u32[]{:S(2)}, u32[]{:S(2)}) collective-permute-start(f32[8,128]{1,0:T(8,128)S(1)} %get-tuple-element.50), channel_id=1, source_target_pairs={{8,0},{16,8},{24,16},{0,24},{9,1},{17,9},{25,17},{1,25},{10,2},{18... | collective-permute-start | bytes 12296 | tf_op jit(solution)/shard_map/ppermute | solution.py:566
  57.5 15.2 %all-to-all-start.3 = ((f32[8,64,128]{2,1,0:T(8,128)}), f32[8,64,128]{2,1,0:T(8,128)S(1)}, u32[]{:S(2)}, u32[]{:S(2)}) async-start(f32[8,64,128]{2,1,0:T(8,128)} %get-tuple-element.54), calls=%async_computation.3 | async-start | bytes 524288 | tf_op jit(solution)/shard_map/all_to_all | solution.py:564
  62.6 10.1 %collective-permute-start.6 = (f32[24,128]{1,0:T(8,128)S(1)}, f32[24,128]{1,0:T(8,128)S(1)}, u32[]{:S(2)}, u32[]{:S(2)}) collective-permute-start(f32[24,128]{1,0:T(8,128)S(1)} %get-tuple-element.55), channel_id=1, source_target_pairs={{0,8},{8,16},{16,24},{24,0},{1,9},{9,17},{17,25},{25,1},{2,10},{10... | collective-permute-start | bytes 36872 | tf_op jit(solution)/shard_map/ppermute | solution.py:565
  63.8 8.9 %collective-permute-start.7 = (f32[24,128]{1,0:T(8,128)S(1)}, f32[24,128]{1,0:T(8,128)S(1)}, u32[]{:S(2)}, u32[]{:S(2)}) collective-permute-start(f32[24,128]{1,0:T(8,128)S(1)} %get-tuple-element.56), channel_id=1, source_target_pairs={{8,0},{16,8},{24,16},{0,24},{9,1},{17,9},{25,17},{1,25},{10,2},{18... | collective-permute-start | bytes 36872 | tf_op jit(solution)/shard_map/ppermute | solution.py:566
  80.7 11.5 %all-to-all-start.4 = ((f32[8,24,128]{2,1,0:T(8,128)}), f32[8,24,128]{2,1,0:T(8,128)S(1)}, u32[]{:S(2)}, u32[]{:S(2)}) async-start(f32[8,24,128]{2,1,0:T(8,128)} %get-tuple-element.58), calls=%async_computation.4 | async-start | bytes 196608 | tf_op jit(solution)/shard_map/all_to_all | solution.py:564
  85.9 4.7 %collective-permute-start.8 = (f32[8,128]{1,0:T(8,128)S(1)}, f32[8,128]{1,0:T(8,128)S(1)}, u32[]{:S(2)}, u32[]{:S(2)}) collective-permute-start(f32[8,128]{1,0:T(8,128)S(1)} %get-tuple-element.59), channel_id=1, source_target_pairs={{0,8},{8,16},{16,24},{24,0},{1,9},{9,17},{17,25},{25,1},{2,10},{10... | collective-permute-start | bytes 12296 | tf_op jit(solution)/shard_map/ppermute | solution.py:565
  86.1 4.5 %collective-permute-start.9 = (f32[8,128]{1,0:T(8,128)S(1)}, f32[8,128]{1,0:T(8,128)S(1)}, u32[]{:S(2)}, u32[]{:S(2)}) collective-permute-start(f32[8,128]{1,0:T(8,128)S(1)} %get-tuple-element.60), channel_id=1, source_target_pairs={{8,0},{16,8},{24,16},{0,24},{9,1},{17,9},{25,17},{1,25},{10,2},{18... | collective-permute-start | bytes 12296 | tf_op jit(solution)/shard_map/ppermute | solution.py:566
  95.5 9.9 %all-to-all-start.5 = ((f32[8,24,128]{2,1,0:T(8,128)}), f32[8,24,128]{2,1,0:T(8,128)S(1)}, u32[]{:S(2)}, u32[]{:S(2)}) async-start(f32[8,24,128]{2,1,0:T(8,128)} %get-tuple-element.62), calls=%async_computation.5 | async-start | bytes 196608 | tf_op jit(solution)/shard_map/all_to_all | solution.py:564
  99.0 4.7 %collective-permute-start.10 = (f32[8,128]{1,0:T(8,128)S(1)}, f32[8,128]{1,0:T(8,128)S(1)}, u32[]{:S(2)}, u32[]{:S(2)}) collective-permute-start(f32[8,128]{1,0:T(8,128)S(1)} %get-tuple-element.63), channel_id=1, source_target_pairs={{0,8},{8,16},{16,24},{24,0},{1,9},{9,17},{17,25},{25,1},{2,10},{10... | collective-permute-start | bytes 12296 | tf_op jit(solution)/shard_map/ppermute | solution.py:565
  100.7 3.6 %collective-permute-start.11 = (f32[8,128]{1,0:T(8,128)S(1)}, f32[8,128]{1,0:T(8,128)S(1)}, u32[]{:S(2)}, u32[]{:S(2)}) collective-permute-start(f32[8,128]{1,0:T(8,128)S(1)} %get-tuple-element.64), channel_id=1, source_target_pairs={{8,0},{16,8},{24,16},{0,24},{9,1},{17,9},{25,17},{1,25},{10,2},{18... | collective-permute-start | bytes 12296 | tf_op jit(solution)/shard_map/ppermute | solution.py:566

commit v5 on v4

--- a/solution.py
+++ b/solution.py
@@ -217,7 +217,8 @@
             halos[s, h, rows8(g * 8), :] = gather(sources, code)
 
 
-def pull_far(plan, table, halo_code, near, halos, sides, g):
+def pull_far(plan, table, halo_code, near, halos, sides, g, row=None):
+    row = g if row is None else row
     start = plan.local_tiles * LANES
     sources = [table[t, rows8(g * 8), :] for t in range(plan.far_tiles)]
     for s in sides:
@@ -225,7 +226,7 @@
             code = jnp.broadcast_to(halo_code[pl.ds(s, 1), half(h)], (8, LANES))
             far = gather(sources, code - start)
             here = near[s, h, rows8(g * 8), :]
-            halos[s, h, rows8(g * 8), :] = jnp.where(code >= start, far, here)
+            halos[s - sides[0], h, rows8(row * 8), :] = jnp.where(code >= start, far, here)
 
 
 def weno_windows(q):
@@ -240,10 +241,9 @@
         a = bend[m] + s1 * (s1 + third[m])
         b = bend[m + 1] + s1 * s2
         c = bend[m + 2] + s2 * (s2 - third[m + 2])
-        a, b, c = a * a, b * b, c * c
-        x = b * c
-        z = a * b
-        total = x + z + 6.0 * (a * c)
+        a, b, c = (pl.reciprocal(value, approx=True) for value in (a, b, c))
+        x, z = a * a, c * c
+        total = x + z + (6.0 * b) * b
         xu = x * fourth[m]
         zu = z * fourth[m + 1]
         slope = 0.25 * (s1 + s2)
@@ -292,66 +292,78 @@
 def advect(plan, phi, speed, ready, near, inner, table, halo_code, halos, squares, moved):
     w = plan.layers
 
-    def stage_planes(i):
+    def stage_planes(i, target):
         for l in range(w):
-            pull_far(plan, table, halo_code, near, halos, (2, 3, 4, 5), i * w + l)
-
-    def stage_columns(j):
+            pull_far(plan, table, halo_code, near, target, (2, 3, 4, 5), i * w + l, l)
+
+    def stage_columns(j, target):
         for l in range(w):
-            pull_far(plan, table, halo_code, near, halos, (0, 1), l * 8 + j)
-
-    stage_planes(0)
-    ready()
-
-    @pl.loop(0, 8)
-    def _(i):
-        lines = []
+            pull_far(plan, table, halo_code, near, target, (0, 1), l * 8 + j, l)
+
+    def stacked(source, side, h):
+        return [source[side, h, pl.ds(l * 8, 8), :] for l in range(w)]
+
+    def spread(source, side, h):
+        return [source[side, h, pl.ds(l, 8, stride=w), :] for l in range(w)]
+
+    def plane(i, source):
         for h in range(plan.halves):
-            ends = [
-                [halos[s, h, pl.ds(i * 8 * w + l, 8, stride=w), :] for l in range(w)]
-                for s in (4, 5)
-            ]
-            lines.append((ends[0], line_at(phi, h, 2, i), ends[1], inner_at(inner, h, 2, i)))
-            ends = [
-                [halos[s, h, rows8((i * w + l) * 8), :] for l in range(w)] for s in (2, 3)
-            ]
-            lines.append((ends[0], line_at(phi, h, 1, i), ends[1], inner_at(inner, h, 1, i)))
-        stage_planes(jnp.minimum(i + 1, 7))
+            low, high = spread(source, 2, h), spread(source, 3, h)
+            values = line_values(low, line_at(phi, h, 2, i), high, inner_at(inner, h, 2, i))
+            for k, value in enumerate(values):
+                squares[h, pl.ds(i * 64 + k, 8, stride=8), :] = value
         for h in range(plan.halves):
-            for k, value in enumerate(line_values(*lines[2 * h])):
-                squares[h, pl.ds(i * 64 + k, 8, stride=8), :] = value
-            for j, value in enumerate(line_values(*lines[2 * h + 1])):
+            low, high = stacked(source, 0, h), stacked(source, 1, h)
+            values = line_values(low, line_at(phi, h, 1, i), high, inner_at(inner, h, 1, i))
+            for j, value in enumerate(values):
                 squares[h, rows8(i * 64 + j * 8), :] += value
 
-    stage_columns(0)
-
-    @pl.loop(0, 8)
-    def _(j):
-        lines = []
+    def column(j, source):
         for h in range(plan.halves):
-            ends = [
-                [halos[s, h, rows8((l * 8 + j) * 8), :] for l in range(w)] for s in (0, 1)
-            ]
-            lines.append((ends[0], line_at(phi, h, 0, j), ends[1], inner_at(inner, h, 0, j)))
-        stage_columns(jnp.minimum(j + 1, 7))
-        for h in range(plan.halves):
-            for i, value in enumerate(line_values(*lines[h])):
+            low, high = stacked(source, 0, h), stacked(source, 1, h)
+            line = line_at(phi, h, 0, j)
+            values = line_values(low, line, high, inner_at(inner, h, 0, j))
+            for i, value in enumerate(values):
                 here = rows8(i * 64 + j * 8)
                 total = squares[h, here, :] + value
                 change = advect_scale * speed[h, here, :] * jnp.sqrt(total)
-                moved[h, here, :] = lines[h][1][i] - change
-
-
-def relax(plan, phi, origin, near, table, halo_code, halos, moved, joined):
+                moved[h, here, :] = line[i] - change
+
+    even, odd = halos
+    stage_planes(0, even)
+    ready(0)
+
+    @pl.loop(0, 4)
+    def _(q):
+        i = 2 * q
+        stage_planes(i + 1, odd)
+        plane(i, even)
+        stage_planes(jnp.minimum(i + 2, 7), even)
+        plane(i + 1, odd)
+
+    stage_columns(0, even)
+    ready(1)
+
+    @pl.loop(0, 4)
+    def _(q):
+        j = 2 * q
+        stage_columns(j + 1, odd)
+        column(j, even)
+        stage_columns(jnp.minimum(j + 2, 7), even)
+        column(j + 1, odd)
+
+
+def relax(plan, phi, origin, near, table, halo_code, halos, moved, finish):
     row = lax.broadcasted_iota(jnp.int32, (8, LANES), 0)
+    columns, faces = halos
 
     @pl.loop(0, 2)
     def _(q):
         for v in range(4):
-            pull_far(plan, table, halo_code, near, halos, (0, 1), q * 4 + v)
+            pull_far(plan, table, halo_code, near, columns, (0, 1), q * 4 + v)
 
     def stage(i):
-        pull_far(plan, table, halo_code, near, halos, (2, 3, 4, 5), i)
+        pull_far(plan, table, halo_code, near, faces, (2, 3, 4, 5), i)
 
     def plane(i, h, previous, following, sides):
         at = half(h)
@@ -379,14 +391,14 @@
                 steep = steep * steep
                 total = steep if total is None else total + steep
             value = value - relax_scale * sense * (jnp.sqrt(total) - 1.0)
-            if joined:
+            if finish is not None:
                 moved[here, at] = value
             else:
                 moved[h, here, :] = value
 
     def planes(i, low, high):
         sides = [
-            [halos[s, h, rows8(i * 8), :] for s in (2, 3, 4, 5)] for h in range(plan.halves)
+            [faces[s, h, rows8(i * 8), :] for s in range(4)] for h in range(plan.halves)
         ]
         if not isinstance(i, int) or i < 7:
             stage(i + 1)
@@ -395,14 +407,16 @@
             def previous(j):
                 if low is None:
                     return phi[h, rows8((i - 1) * 64 + j * 8), :]
-                return halos[low, h, pl.ds(j * 8, 8), :]
+                return columns[low, h, pl.ds(j * 8, 8), :]
 
             def following(j):
                 if high is None:
                     return phi[h, rows8((i + 1) * 64 + j * 8), :]
-                return halos[high, h, pl.ds(j * 8, 8), :]
+                return columns[high, h, pl.ds(j * 8, 8), :]
 
             plane(i, h, previous, following, sides[h])
+        if finish is not None:
+            finish(i)
 
     stage(0)
     planes(0, 0, None)
@@ -430,7 +444,7 @@
         )
     for copy in copies:
         copy.start()
-    for copy in copies:
+    for copy in copies[:3]:
         copy.wait()
     lanes = lane_ids()
     padded[...] = jnp.zeros_like(padded)
@@ -465,6 +479,8 @@
     edge_code = (plan.local_tiles + plan.border_tile) * LANES + plan.border_lane + edge
     code = jnp.where(edge >= 0, edge_code, code)
     halo_code[...] = jnp.where(far >= 0, code, entry)
+    for copy in copies[3:]:
+        copy.wait()
 
     fill_ends(plan, phi, ends)
     pack_sends(plan, phi, ends, send_code, table, outgoing, low, high)
@@ -499,22 +515,21 @@
 
 def advect_kernel(
     plan, sends, phi, near, inner, speed, arrived, before, after, send_code, halo_code,
-    moved, outgoing, low, high, ends, table, halos, squares, fast, kept, loaded, found,
+    moved, outgoing, low, high, ends, table, even, odd, squares, fast, kept, loaded, found,
 ):
-    copies = [pltpu.make_async_copy(inner.at[a], kept.at[a], found.at[a]) for a in range(3)]
-    copies += [
-        pltpu.make_async_copy(speed.at[:, half(h)], fast.at[h], loaded.at[h])
-        for h in range(plan.halves)
-    ]
-    for copy in copies:
+    first = [pltpu.make_async_copy(inner.at[a], kept.at[a], found.at[a]) for a in (2, 1)]
+    second = [pltpu.make_async_copy(inner.at[0], kept.at[0], found.at[0])]
+    for h in range(plan.halves):
+        second.append(pltpu.make_async_copy(speed.at[:, half(h)], fast.at[h], loaded.at[h]))
+    for copy in first + second:
         copy.start()
 
-    def ready():
-        for copy in copies:
+    def ready(stage):
+        for copy in (first, second)[stage]:
             copy.wait()
 
     unpack_far(plan, arrived, before, after, table)
-    advect(plan, phi, fast, ready, near, kept, table, halo_code, halos, squares, moved)
+    advect(plan, phi, fast, ready, near, kept, table, halo_code, (even, odd), squares, moved)
     pack_sends(sends, moved, ends, send_code, table, outgoing, low, high)
 
 
@@ -522,12 +537,26 @@
     plan, sends, phi, origin, near, arrived, before, after, send_code, halo_code, *rest
 ):
     if sends is None:
-        (moved, table, halos) = rest
+        (result, table, columns, faces, moved, written) = rest
+
+        def part(i):
+            rows = rows8(i * 64)
+            rows = pl.ds(rows.start, 64)
+            return pltpu.make_async_copy(moved.at[rows], result.at[rows], written.at[i])
+
+        def finish(i):
+            part(i).start()
+
     else:
-        (moved, outgoing, low, high, ends, table, halos) = rest
+        (moved, outgoing, low, high, ends, table, columns, faces) = rest
+        finish = None
     unpack_far(plan, arrived, before, after, table)
-    relax(plan, phi, origin, near, table, halo_code, halos, moved, sends is None)
-    if sends is not None:
+    halos = (columns, faces)
+    relax(plan, phi, origin, near, table, halo_code, halos, moved, finish)
+    if sends is None:
+        for i in range(8):
+            part(i).wait()
+    else:
         fill_ends(sends, moved, ends)
         pack_sends(sends, moved, ends, send_code, table, outgoing, low, high)
 
@@ -581,8 +610,8 @@
     def table(plan):
         return pltpu.VMEM((plan.far_tiles, 64 * plan.layers, LANES), jnp.float32)
 
-    def halos(plan):
-        return pltpu.VMEM((6, wide.halves, 64 * plan.layers, LANES), jnp.float32)
+    def halos(sides, groups):
+        return pltpu.VMEM((sides, wide.halves, 8 * groups, LANES), jnp.float32)
 
     def sent(plan):
         return [f32(plan.message()), f32(plan.border_message()), f32(plan.border_message())]
@@ -628,7 +657,7 @@
         phi, *message = call(
             functools.partial(advect_kernel, wide, thin),
             [field] + sent(thin),
-            [ends(wide), table(wide), halos(wide), block, block]
+            [ends(wide), table(wide), halos(4, 3), halos(4, 3), block, block]
             + [pltpu.VMEM(inner_shape, jnp.float32)]
             + [pltpu.SemaphoreType.DMA((wide.halves,)), pltpu.SemaphoreType.DMA((3,))],
             rows * count * 300,
@@ -645,14 +674,17 @@
                 sends = None
             if sends is None:
                 out, scratch = [f32((rows, count))], [table(thin)]
+                extra = [pltpu.VMEM((rows, count), jnp.float32), pltpu.SemaphoreType.DMA((8,))]
             else:
                 out, scratch = [field] + sent(sends), [ends(sends), table(sends)]
+                extra = []
             phi, *message = call(
                 functools.partial(relax_kernel, thin, sends),
                 out,
-                scratch + [halos(thin)],
+                scratch + [halos(2, 8), halos(4, 8)] + extra,
                 rows * count * 60,
                 phi, origin, *near_halos(thin, phi), *exchange(*message), send_code, halo_code,
+                far_out=(0,) if sends is None else (),
             )
     return phi
 

time: 109 us -> 105 us (0.963)
  Pallas kernels: 55.3 us -> 51.4 us
    pallas_call x13, Pallas kernels: 55.3 us -> 51.4 us  [call(): pl.pallas_call(kernel, out_shape=[pltpu.HBM(x.shape, x.dtype) if n in far...]
  transfers between devices with their start and end apart: 18 -> 18, of which waited for: 5 -> 5; matrix products, arithmetic and copies ran while one was open for 0% -> 0% of each run, Pallas kernels for 20% -> 21%
where the time goes in v5:
time: 105 us; the launch traced here: 104 us
  Pallas kernels  51.4 us (49%)
  starting transfers between devices  46.3 us (44%)
  waiting for transfers between devices  6.39 us (6%)
    pallas_call x13, Pallas kernels, call(): pl.pallas_call(kernel, out_shape=[pltpu.HBM(x.shape, x.dtype) if n in far...  51.4 us
    all_to_all x6, starting transfers between devices, exchange(): lax.all_to_all(outgoing, 'dev', split_axis=0, concat_axis=0, tiled=True)  28.7 us
    ppermute x6, starting transfers between devices, exchange(): after = lax.ppermute(low, 'group', down)  9.62 us
    ppermute x6, starting transfers between devices, exchange(): before = lax.ppermute(high, 'group', up)  7.93 us
    all_to_all x6, waiting for transfers between devices, exchange(): lax.all_to_all(outgoing, 'dev', split_axis=0, concat_axis=0, tiled=True)  4.21 us
    ppermute x6, waiting for transfers between devices, exchange(): after = lax.ppermute(low, 'group', down)  2.16 us
  transfers between devices with their start and end apart: 18, of which 5 were waited for; matrix products, arithmetic and copies ran while one was open for 0% of the time, Pallas kernels for 21%

profile of v5, /device:TPU:0, one launch (start us, length us, event | category | flops | bytes accessed | tf_op | source)
XLA Modules:
  0.0 104.2 jit_solution(8136104269865075514)
XLA Ops:
  0.0 3.7 %shard_map.55 = (f32[2,512,128]{2,1,0:T(8,128)S(1)}, f32[8,64,128]{2,1,0:T(8,128)}, f32[24,128]{1,0:T(8,128)S(1)}, f32[24,128]{1,0:T(8,128)S(1)}, s32[8,128]{1,0:T(8,128)S(1)}, /*index=5*/s32[6,256]{1,0:T(8,128)S(1)}) custom-call(f32[512,256]{1,0:T(8,128)} %level_set.1, s32[8,40]{1,0:T(8,128)} %peer_slabs.1, s32[2,16]{1,0:T(2,128)} %region_slabs.1, ...), custom_call_target="tpu_custom_call" | custom-call | flops 1000000 | bytes 1353088 | tf_op jit(solution)/shard_map/pallas_call | solution.py:576
  3.7 6.3 %all-to-all-start = ((f32[8,64,128]{2,1,0:T(8,128)}), f32[8,64,128]{2,1,0:T(8,128)S(1)}, u32[]{:S(2)}, u32[]{:S(2)}) async-start(f32[8,64,128]{2,1,0:T(8,128)} %get-tuple-element.39), calls=%async_computation | async-start | bytes 524288 | tf_op jit(solution)/shard_map/all_to_all | solution.py:593
  10.1 1.5 %collective-permute-start = (f32[24,128]{1,0:T(8,128)S(1)}, f32[24,128]{1,0:T(8,128)S(1)}, u32[]{:S(2)}, u32[]{:S(2)}) collective-permute-start(f32[24,128]{1,0:T(8,128)S(1)} %get-tuple-element.40), channel_id=1, source_target_pairs={{0,8},{8,16},{16,24},{24,0},{1,9},{9,17},{17,25},{25,1},{2,10},{10... | collective-permute-start | bytes 36872 | tf_op jit(solution)/shard_map/ppermute | solution.py:594
  11.6 1.4 %collective-permute-start.1 = (f32[24,128]{1,0:T(8,128)S(1)}, f32[24,128]{1,0:T(8,128)S(1)}, u32[]{:S(2)}, u32[]{:S(2)}) collective-permute-start(f32[24,128]{1,0:T(8,128)S(1)} %get-tuple-element.41), channel_id=1, source_target_pairs={{8,0},{16,8},{24,16},{0,24},{9,1},{17,9},{25,17},{1,25},{10,2},{18... | collective-permute-start | bytes 36872 | tf_op jit(solution)/shard_map/ppermute | solution.py:595
  13.0 7.2 %shard_map.56 = (f32[6,2,192,128]{3,2,1,0:T(8,128)S(1)}, f32[3,2,256,128]{3,2,1,0:T(8,128)}) custom-call(f32[2,512,128]{2,1,0:T(8,128)S(1)} %get-tuple-element.35.phi, s32[6,256]{1,0:T(8,128)S(1)} %get-tuple-element.36.halo_code), custom_call_target="tpu_custom_call" | custom-call | flops 39321600 | bytes 2496512 | tf_op jit(solution)/shard_map/pallas_call | solution.py:576
  20.2 6.1 %shard_map.57 = (f32[2,512,128]{2,1,0:T(8,128)S(1)}, f32[8,24,128]{2,1,0:T(8,128)}, f32[8,128]{1,0:T(8,128)S(1)}, f32[8,128]{1,0:T(8,128)S(1)}) custom-call(f32[2,512,128]{2,1,0:T(8,128)S(1)} %get-tuple-element.35.phi, f32[6,2,192,128]{3,2,1,0:T(8,128)S(1)} %get-tuple-element.37.near, f32[3,2,256,128]{3,2,1,0:T(8,128)} %get-tuple-element.38.inner, ...), custom_call_target="tpu_custom_call" | custom-call | flops 39321600 | bytes 3942400 | tf_op jit(solution)/shard_map/pallas_call | solution.py:576
  26.3 5.1 %all-to-all-start.1 = ((f32[8,24,128]{2,1,0:T(8,128)}), f32[8,24,128]{2,1,0:T(8,128)S(1)}, u32[]{:S(2)}, u32[]{:S(2)}) async-start(f32[8,24,128]{2,1,0:T(8,128)} %get-tuple-element.44), calls=%async_computation.1 | async-start | bytes 196608 | tf_op jit(solution)/shard_map/all_to_all | solution.py:593
  32.0 2.3 %collective-permute-start.3 = (f32[8,128]{1,0:T(8,128)S(1)}, f32[8,128]{1,0:T(8,128)S(1)}, u32[]{:S(2)}, u32[]{:S(2)}) collective-permute-start(f32[8,128]{1,0:T(8,128)S(1)} %get-tuple-element.46), channel_id=1, source_target_pairs={{8,0},{16,8},{24,16},{0,24},{9,1},{17,9},{25,17},{1,25},{10,2},{18... | collective-permute-start | bytes 12296 | tf_op jit(solution)/shard_map/ppermute | solution.py:595
  34.4 1.8 %shard_map.58.near = f32[6,2,64,128]{3,2,1,0:T(8,128)S(1)} custom-call(f32[2,512,128]{2,1,0:T(8,128)S(1)} %get-tuple-element.43.phi.origin, s32[6,256]{1,0:T(8,128)S(1)} %get-tuple-element.36.halo_code), custom_call_target="tpu_custom_call" | custom-call | flops 13107200 | bytes 923648 | tf_op jit(solution)/shard_map/pallas_call | solution.py:576
  36.2 1.6 %all-to-all-done.1.arrived = f32[8,24,128]{2,1,0:T(8,128)S(1)} async-done(((f32[8,24,128]{2,1,0:T(8,128)}), f32[8,24,128]{2,1,0:T(8,128)S(1)}, u32[]{:S(2)}, u32[]{:S(2)}) %all-to-all-start.1) | async-done | bytes 98336 | tf_op jit(solution)/shard_map/all_to_all | solution.py:593
  37.8 3.3 %shard_map.59 = (f32[2,512,128]{2,1,0:T(8,128)S(1)}, f32[8,24,128]{2,1,0:T(8,128)}, f32[8,128]{1,0:T(8,128)S(1)}, f32[8,128]{1,0:T(8,128)S(1)}) custom-call(f32[2,512,128]{2,1,0:T(8,128)S(1)} %get-tuple-element.43.phi.origin, f32[2,512,128]{2,1,0:T(8,128)S(1)} %get-tuple-element.43.phi.origin, f32[6,2,64,128]{3,2,1,0:T(8,128)S(1)} %shard_map.58.near, ...), custom_call_target="tpu_custom_call" | custom-call | flops 7864320 | bytes 2189312 | tf_op jit(solution)/shard_map/pallas_call | solution.py:576
  41.1 3.5 %all-to-all-start.2 = ((f32[8,24,128]{2,1,0:T(8,128)}), f32[8,24,128]{2,1,0:T(8,128)S(1)}, u32[]{:S(2)}, u32[]{:S(2)}) async-start(f32[8,24,128]{2,1,0:T(8,128)} %get-tuple-element.48), calls=%async_computation.2 | async-start | bytes 196608 | tf_op jit(solution)/shard_map/all_to_all | solution.py:593
  44.6 2.7 %collective-permute-start.4 = (f32[8,128]{1,0:T(8,128)S(1)}, f32[8,128]{1,0:T(8,128)S(1)}, u32[]{:S(2)}, u32[]{:S(2)}) collective-permute-start(f32[8,128]{1,0:T(8,128)S(1)} %get-tuple-element.49), channel_id=1, source_target_pairs={{0,8},{8,16},{16,24},{24,0},{1,9},{9,17},{17,25},{25,1},{2,10},{10... | collective-permute-start | bytes 12296 | tf_op jit(solution)/shard_map/ppermute | solution.py:594
  47.5 1.8 %shard_map.60.near = f32[6,2,64,128]{3,2,1,0:T(8,128)S(1)} custom-call(f32[2,512,128]{2,1,0:T(8,128)S(1)} %get-tuple-element.47.phi, s32[6,256]{1,0:T(8,128)S(1)} %get-tuple-element.36.halo_code), custom_call_target="tpu_custom_call" | custom-call | flops 13107200 | bytes 923648 | tf_op jit(solution)/shard_map/pallas_call | solution.py:576
  49.3 1.6 %collective-permute-done.5.after = f32[8,128]{1,0:T(8,128)S(1)} collective-permute-done((f32[8,128]{1,0:T(8,128)S(1)}, f32[8,128]{1,0:T(8,128)S(1)}, u32[]{:S(2)}, u32[]{:S(2)}) %collective-permute-start.5) | collective-permute-done | bytes 4128 | tf_op jit(solution)/shard_map/ppermute | solution.py:595
  50.9 4.6 %shard_map.61 = (f32[2,512,128]{2,1,0:T(8,128)S(1)}, f32[8,64,128]{2,1,0:T(8,128)}, f32[24,128]{1,0:T(8,128)S(1)}, f32[24,128]{1,0:T(8,128)S(1)}) custom-call(f32[2,512,128]{2,1,0:T(8,128)S(1)} %get-tuple-element.47.phi, f32[2,512,128]{2,1,0:T(8,128)S(1)} %get-tuple-element.43.phi.origin, f32[6,2,64,128]{3,2,1,0:T(8,128)S(1)} %shard_map.60.near, ...), custom_call_target="tpu_custom_call" | custom-call | flops 7864320 | bytes 2369536 | tf_op jit(solution)/shard_map/pallas_call | solution.py:576
  55.6 5.1 %all-to-all-start.3 = ((f32[8,64,128]{2,1,0:T(8,128)}), f32[8,64,128]{2,1,0:T(8,128)S(1)}, u32[]{:S(2)}, u32[]{:S(2)}) async-start(f32[8,64,128]{2,1,0:T(8,128)} %get-tuple-element.54), calls=%async_computation.3 | async-start | bytes 524288 | tf_op jit(solution)/shard_map/all_to_all | solution.py:593
  60.7 1.2 %collective-permute-start.6 = (f32[24,128]{1,0:T(8,128)S(1)}, f32[24,128]{1,0:T(8,128)S(1)}, u32[]{:S(2)}, u32[]{:S(2)}) collective-permute-start(f32[24,128]{1,0:T(8,128)S(1)} %get-tuple-element.55), channel_id=1, source_target_pairs={{0,8},{8,16},{16,24},{24,0},{1,9},{9,17},{17,25},{25,1},{2,10},{10... | collective-permute-start | bytes 36872 | tf_op jit(solution)/shard_map/ppermute | solution.py:594
  61.8 1.8 %collective-permute-start.7 = (f32[24,128]{1,0:T(8,128)S(1)}, f32[24,128]{1,0:T(8,128)S(1)}, u32[]{:S(2)}, u32[]{:S(2)}) collective-permute-start(f32[24,128]{1,0:T(8,128)S(1)} %get-tuple-element.56), channel_id=1, source_target_pairs={{8,0},{16,8},{24,16},{0,24},{9,1},{17,9},{25,17},{1,25},{10,2},{18... | collective-permute-start | bytes 36872 | tf_op jit(solution)/shard_map/ppermute | solution.py:595
  63.6 7.2 %shard_map.62 = (f32[6,2,192,128]{3,2,1,0:T(8,128)S(1)}, f32[3,2,256,128]{3,2,1,0:T(8,128)}) custom-call(f32[2,512,128]{2,1,0:T(8,128)S(1)} %get-tuple-element.51.phi, s32[6,256]{1,0:T(8,128)S(1)} %get-tuple-element.36.halo_code), custom_call_target="tpu_custom_call" | custom-call | flops 39321600 | bytes 2496512 | tf_op jit(solution)/shard_map/pallas_call | solution.py:576
  70.8 6.1 %shard_map.63 = (f32[2,512,128]{2,1,0:T(8,128)S(1)}, f32[8,24,128]{2,1,0:T(8,128)}, f32[8,128]{1,0:T(8,128)S(1)}, f32[8,128]{1,0:T(8,128)S(1)}) custom-call(f32[2,512,128]{2,1,0:T(8,128)S(1)} %get-tuple-element.51.phi, f32[6,2,192,128]{3,2,1,0:T(8,128)S(1)} %get-tuple-element.52.near, f32[3,2,256,128]{3,2,1,0:T(8,128)} %get-tuple-element.53.inner, ...), custom_call_target="tpu_custom_call" | custom-call | flops 39321600 | bytes 3942400 | tf_op jit(solution)/shard_map/pallas_call | solution.py:576
  76.9 5.1 %all-to-all-start.4 = ((f32[8,24,128]{2,1,0:T(8,128)}), f32[8,24,128]{2,1,0:T(8,128)S(1)}, u32[]{:S(2)}, u32[]{:S(2)}) async-start(f32[8,24,128]{2,1,0:T(8,128)} %get-tuple-element.58), calls=%async_computation.4 | async-start | bytes 196608 | tf_op jit(solution)/shard_map/all_to_all | solution.py:593
  82.3 2.7 %collective-permute-start.9 = (f32[8,128]{1,0:T(8,128)S(1)}, f32[8,128]{1,0:T(8,128)S(1)}, u32[]{:S(2)}, u32[]{:S(2)}) collective-permute-start(f32[8,128]{1,0:T(8,128)S(1)} %get-tuple-element.60), channel_id=1, source_target_pairs={{8,0},{16,8},{24,16},{0,24},{9,1},{17,9},{25,17},{1,25},{10,2},{18... | collective-permute-start | bytes 12296 | tf_op jit(solution)/shard_map/ppermute | solution.py:595
  84.9 1.8 %shard_map.64.near = f32[6,2,64,128]{3,2,1,0:T(8,128)S(1)} custom-call(f32[2,512,128]{2,1,0:T(8,128)S(1)} %get-tuple-element.57.phi.origin, s32[6,256]{1,0:T(8,128)S(1)} %get-tuple-element.36.halo_code), custom_call_target="tpu_custom_call" | custom-call | flops 13107200 | bytes 923648 | tf_op jit(solution)/shard_map/pallas_call | solution.py:576
  86.8 1.6 %all-to-all-done.4.arrived = f32[8,24,128]{2,1,0:T(8,128)S(1)} async-done(((f32[8,24,128]{2,1,0:T(8,128)}), f32[8,24,128]{2,1,0:T(8,128)S(1)}, u32[]{:S(2)}, u32[]{:S(2)}) %all-to-all-start.4) | async-done | bytes 98336 | tf_op jit(solution)/shard_map/all_to_all | solution.py:593
  88.4 3.3 %shard_map.65 = (f32[2,512,128]{2,1,0:T(8,128)S(1)}, f32[8,24,128]{2,1,0:T(8,128)}, f32[8,128]{1,0:T(8,128)S(1)}, f32[8,128]{1,0:T(8,128)S(1)}) custom-call(f32[2,512,128]{2,1,0:T(8,128)S(1)} %get-tuple-element.57.phi.origin, f32[2,512,128]{2,1,0:T(8,128)S(1)} %get-tuple-element.57.phi.origin, f32[6,2,64,128]{3,2,1,0:T(8,128)S(1)} %shard_map.64.near, ...), custom_call_target="tpu_custom_call" | custom-call | flops 7864320 | bytes 2189312 | tf_op jit(solution)/shard_map/pallas_call | solution.py:576
  91.7 3.5 %all-to-all-start.5 = ((f32[8,24,128]{2,1,0:T(8,128)}), f32[8,24,128]{2,1,0:T(8,128)S(1)}, u32[]{:S(2)}, u32[]{:S(2)}) async-start(f32[8,24,128]{2,1,0:T(8,128)} %get-tuple-element.62), calls=%async_computation.5 | async-start | bytes 196608 | tf_op jit(solution)/shard_map/all_to_all | solution.py:593
  95.2 1.7 %collective-permute-start.10 = (f32[8,128]{1,0:T(8,128)S(1)}, f32[8,128]{1,0:T(8,128)S(1)}, u32[]{:S(2)}, u32[]{:S(2)}) collective-permute-start(f32[8,128]{1,0:T(8,128)S(1)} %get-tuple-element.63), channel_id=1, source_target_pairs={{0,8},{8,16},{16,24},{24,0},{1,9},{9,17},{17,25},{25,1},{2,10},{10... | collective-permute-start | bytes 12296 | tf_op jit(solution)/shard_map/ppermute | solution.py:594
  96.9 1.2 %collective-permute-start.11 = (f32[8,128]{1,0:T(8,128)S(1)}, f32[8,128]{1,0:T(8,128)S(1)}, u32[]{:S(2)}, u32[]{:S(2)}) collective-permute-start(f32[8,128]{1,0:T(8,128)S(1)} %get-tuple-element.64), channel_id=1, source_target_pairs={{8,0},{16,8},{24,16},{0,24},{9,1},{17,9},{25,17},{1,25},{10,2},{18... | collective-permute-start | bytes 12296 | tf_op jit(solution)/shard_map/ppermute | solution.py:595
  98.1 1.8 %shard_map.66.near = f32[6,2,64,128]{3,2,1,0:T(8,128)S(1)} custom-call(f32[2,512,128]{2,1,0:T(8,128)S(1)} %get-tuple-element.61.phi, s32[6,256]{1,0:T(8,128)S(1)} %get-tuple-element.36.halo_code), custom_call_target="tpu_custom_call" | custom-call | flops 13107200 | bytes 923648 | tf_op jit(solution)/shard_map/pallas_call | solution.py:576
  100.5 1.0 all-to-all-done.5.arrived
  101.5 2.7 %shard_map.67 = f32[512,256]{1,0:T(8,128)} custom-call(f32[2,512,128]{2,1,0:T(8,128)S(1)} %get-tuple-element.61.phi, f32[2,512,128]{2,1,0:T(8,128)S(1)} %get-tuple-element.57.phi.origin, f32[6,2,64,128]{3,2,1,0:T(8,128)S(1)} %shard_map.66.near, f32[8,24,128]{2,1,0:T(8,128)S(1)} %all-to-all-done.5.arrived, f32[8,128]{1,0:T(8,128)S(1)} %collective-permute-done.10.before, ...), custom_call_target="tpu_custom_call" | custom-call | flops 7864320 | bytes 2082816 | tf_op jit(solution)/shard_map/pallas_call | solution.py:576
  (17 shorter events, 1.7 us)
Async XLA Ops:
  3.7 16.5 %all-to-all-start = ((f32[8,64,128]{2,1,0:T(8,128)}), f32[8,64,128]{2,1,0:T(8,128)S(1)}, u32[]{:S(2)}, u32[]{:S(2)}) async-start(f32[8,64,128]{2,1,0:T(8,128)} %get-tuple-element.39), calls=%async_computation | async-start | bytes 524288 | tf_op jit(solution)/shard_map/all_to_all | solution.py:593
  10.1 10.1 %collective-permute-start = (f32[24,128]{1,0:T(8,128)S(1)}, f32[24,128]{1,0:T(8,128)S(1)}, u32[]{:S(2)}, u32[]{:S(2)}) collective-permute-start(f32[24,128]{1,0:T(8,128)S(1)} %get-tuple-element.40), channel_id=1, source_target_pairs={{0,8},{8,16},{16,24},{24,0},{1,9},{9,17},{17,25},{25,1},{2,10},{10... | collective-permute-start | bytes 36872 | tf_op jit(solution)/shard_map/ppermute | solution.py:594
  11.6 8.6 %collective-permute-start.1 = (f32[24,128]{1,0:T(8,128)S(1)}, f32[24,128]{1,0:T(8,128)S(1)}, u32[]{:S(2)}, u32[]{:S(2)}) collective-permute-start(f32[24,128]{1,0:T(8,128)S(1)} %get-tuple-element.41), channel_id=1, source_target_pairs={{8,0},{16,8},{24,16},{0,24},{9,1},{17,9},{25,17},{1,25},{10,2},{18... | collective-permute-start | bytes 36872 | tf_op jit(solution)/shard_map/ppermute | solution.py:595
  26.3 11.5 %all-to-all-start.1 = ((f32[8,24,128]{2,1,0:T(8,128)}), f32[8,24,128]{2,1,0:T(8,128)S(1)}, u32[]{:S(2)}, u32[]{:S(2)}) async-start(f32[8,24,128]{2,1,0:T(8,128)} %get-tuple-element.44), calls=%async_computation.1 | async-start | bytes 196608 | tf_op jit(solution)/shard_map/all_to_all | solution.py:593
  31.4 4.7 %collective-permute-start.2 = (f32[8,128]{1,0:T(8,128)S(1)}, f32[8,128]{1,0:T(8,128)S(1)}, u32[]{:S(2)}, u32[]{:S(2)}) collective-permute-start(f32[8,128]{1,0:T(8,128)S(1)} %get-tuple-element.45), channel_id=1, source_target_pairs={{0,8},{8,16},{16,24},{24,0},{1,9},{9,17},{17,25},{25,1},{2,10},{10... | collective-permute-start | bytes 12296 | tf_op jit(solution)/shard_map/ppermute | solution.py:594
  32.0 4.2 %collective-permute-start.3 = (f32[8,128]{1,0:T(8,128)S(1)}, f32[8,128]{1,0:T(8,128)S(1)}, u32[]{:S(2)}, u32[]{:S(2)}) collective-permute-start(f32[8,128]{1,0:T(8,128)S(1)} %get-tuple-element.46), channel_id=1, source_target_pairs={{8,0},{16,8},{24,16},{0,24},{9,1},{17,9},{25,17},{1,25},{10,2},{18... | collective-permute-start | bytes 12296 | tf_op jit(solution)/shard_map/ppermute | solution.py:595
  41.1 9.9 %all-to-all-start.2 = ((f32[8,24,128]{2,1,0:T(8,128)}), f32[8,24,128]{2,1,0:T(8,128)S(1)}, u32[]{:S(2)}, u32[]{:S(2)}) async-start(f32[8,24,128]{2,1,0:T(8,128)} %get-tuple-element.48), calls=%async_computation.2 | async-start | bytes 196608 | tf_op jit(solution)/shard_map/all_to_all | solution.py:593
  44.6 4.7 %collective-permute-start.4 = (f32[8,128]{1,0:T(8,128)S(1)}, f32[8,128]{1,0:T(8,128)S(1)}, u32[]{:S(2)}, u32[]{:S(2)}) collective-permute-start(f32[8,128]{1,0:T(8,128)S(1)} %get-tuple-element.49), channel_id=1, source_target_pairs={{0,8},{8,16},{16,24},{24,0},{1,9},{9,17},{17,25},{25,1},{2,10},{10... | collective-permute-start | bytes 12296 | tf_op jit(solution)/shard_map/ppermute | solution.py:594
  47.3 3.6 %collective-permute-start.5 = (f32[8,128]{1,0:T(8,128)S(1)}, f32[8,128]{1,0:T(8,128)S(1)}, u32[]{:S(2)}, u32[]{:S(2)}) collective-permute-start(f32[8,128]{1,0:T(8,128)S(1)} %get-tuple-element.50), channel_id=1, source_target_pairs={{8,0},{16,8},{24,16},{0,24},{9,1},{17,9},{25,17},{1,25},{10,2},{18... | collective-permute-start | bytes 12296 | tf_op jit(solution)/shard_map/ppermute | solution.py:595
  55.6 15.2 %all-to-all-start.3 = ((f32[8,64,128]{2,1,0:T(8,128)}), f32[8,64,128]{2,1,0:T(8,128)S(1)}, u32[]{:S(2)}, u32[]{:S(2)}) async-start(f32[8,64,128]{2,1,0:T(8,128)} %get-tuple-element.54), calls=%async_computation.3 | async-start | bytes 524288 | tf_op jit(solution)/shard_map/all_to_all | solution.py:593
  60.7 10.1 %collective-permute-start.6 = (f32[24,128]{1,0:T(8,128)S(1)}, f32[24,128]{1,0:T(8,128)S(1)}, u32[]{:S(2)}, u32[]{:S(2)}) collective-permute-start(f32[24,128]{1,0:T(8,128)S(1)} %get-tuple-element.55), channel_id=1, source_target_pairs={{0,8},{8,16},{16,24},{24,0},{1,9},{9,17},{17,25},{25,1},{2,10},{10... | collective-permute-start | bytes 36872 | tf_op jit(solution)/shard_map/ppermute | solution.py:594
  61.8 8.9 %collective-permute-start.7 = (f32[24,128]{1,0:T(8,128)S(1)}, f32[24,128]{1,0:T(8,128)S(1)}, u32[]{:S(2)}, u32[]{:S(2)}) collective-permute-start(f32[24,128]{1,0:T(8,128)S(1)} %get-tuple-element.56), channel_id=1, source_target_pairs={{8,0},{16,8},{24,16},{0,24},{9,1},{17,9},{25,17},{1,25},{10,2},{18... | collective-permute-start | bytes 36872 | tf_op jit(solution)/shard_map/ppermute | solution.py:595
  76.9 11.5 %all-to-all-start.4 = ((f32[8,24,128]{2,1,0:T(8,128)}), f32[8,24,128]{2,1,0:T(8,128)S(1)}, u32[]{:S(2)}, u32[]{:S(2)}) async-start(f32[8,24,128]{2,1,0:T(8,128)} %get-tuple-element.58), calls=%async_computation.4 | async-start | bytes 196608 | tf_op jit(solution)/shard_map/all_to_all | solution.py:593
  82.0 4.7 %collective-permute-start.8 = (f32[8,128]{1,0:T(8,128)S(1)}, f32[8,128]{1,0:T(8,128)S(1)}, u32[]{:S(2)}, u32[]{:S(2)}) collective-permute-start(f32[8,128]{1,0:T(8,128)S(1)} %get-tuple-element.59), channel_id=1, source_target_pairs={{0,8},{8,16},{16,24},{24,0},{1,9},{9,17},{17,25},{25,1},{2,10},{10... | collective-permute-start | bytes 12296 | tf_op jit(solution)/shard_map/ppermute | solution.py:594
  82.3 4.5 %collective-permute-start.9 = (f32[8,128]{1,0:T(8,128)S(1)}, f32[8,128]{1,0:T(8,128)S(1)}, u32[]{:S(2)}, u32[]{:S(2)}) collective-permute-start(f32[8,128]{1,0:T(8,128)S(1)} %get-tuple-element.60), channel_id=1, source_target_pairs={{8,0},{16,8},{24,16},{0,24},{9,1},{17,9},{25,17},{1,25},{10,2},{18... | collective-permute-start | bytes 12296 | tf_op jit(solution)/shard_map/ppermute | solution.py:595
  91.7 9.9 %all-to-all-start.5 = ((f32[8,24,128]{2,1,0:T(8,128)}), f32[8,24,128]{2,1,0:T(8,128)S(1)}, u32[]{:S(2)}, u32[]{:S(2)}) async-start(f32[8,24,128]{2,1,0:T(8,128)} %get-tuple-element.62), calls=%async_computation.5 | async-start | bytes 196608 | tf_op jit(solution)/shard_map/all_to_all | solution.py:593
  95.2 4.7 %collective-permute-start.10 = (f32[8,128]{1,0:T(8,128)S(1)}, f32[8,128]{1,0:T(8,128)S(1)}, u32[]{:S(2)}, u32[]{:S(2)}) collective-permute-start(f32[8,128]{1,0:T(8,128)S(1)} %get-tuple-element.63), channel_id=1, source_target_pairs={{0,8},{8,16},{16,24},{24,0},{1,9},{9,17},{17,25},{25,1},{2,10},{10... | collective-permute-start | bytes 12296 | tf_op jit(solution)/shard_map/ppermute | solution.py:594
  96.9 3.6 %collective-permute-start.11 = (f32[8,128]{1,0:T(8,128)S(1)}, f32[8,128]{1,0:T(8,128)S(1)}, u32[]{:S(2)}, u32[]{:S(2)}) collective-permute-start(f32[8,128]{1,0:T(8,128)S(1)} %get-tuple-element.64), channel_id=1, source_target_pairs={{8,0},{16,8},{24,16},{0,24},{9,1},{17,9},{25,17},{1,25},{10,2},{18... | collective-permute-start | bytes 12296 | tf_op jit(solution)/shard_map/ppermute | solution.py:595

commit v6 on v5

--- a/solution.py
+++ b/solution.py
@@ -217,16 +217,21 @@
             halos[s, h, rows8(g * 8), :] = gather(sources, code)
 
 
-def pull_far(plan, table, halo_code, near, halos, sides, g, row=None):
-    row = g if row is None else row
+def far_values(plan, table, halo_code, near, sides, g):
     start = plan.local_tiles * LANES
     sources = [table[t, rows8(g * 8), :] for t in range(plan.far_tiles)]
+    found = {}
     for s in sides:
         for h in range(plan.halves):
             code = jnp.broadcast_to(halo_code[pl.ds(s, 1), half(h)], (8, LANES))
             far = gather(sources, code - start)
-            here = near[s, h, rows8(g * 8), :]
-            halos[s - sides[0], h, rows8(row * 8), :] = jnp.where(code >= start, far, here)
+            found[s, h] = jnp.where(code >= start, far, near[s, h, rows8(g * 8), :])
+    return found
+
+
+def pull_far(plan, table, halo_code, near, halos, sides, g, row):
+    for (s, h), value in far_values(plan, table, halo_code, near, sides, g).items():
+        halos[s - sides[0], h, rows8(row * 8), :] = value
 
 
 def weno_windows(q):
@@ -353,79 +358,90 @@
         column(j + 1, odd)
 
 
-def relax(plan, phi, origin, near, table, halo_code, halos, moved, finish):
+def steepness(value, low, high, facing):
+    steep = jnp.maximum((value - low) * facing, (value - high) * facing)
+    steep = jnp.maximum(steep, 0.0)
+    return steep * steep
+
+
+def facing_of(start):
+    return jnp.where(start > 0.0, 1.0, -1.0)
+
+
+def relax_inner(plan, phi, origin, inner, i):
     row = lax.broadcasted_iota(jnp.int32, (8, LANES), 0)
-    columns, faces = halos
+    middle = jnp.logical_and(row > 0, row < 7)
+    inside = jnp.where(jnp.logical_and(i > 0, i < 7), 1.0, 0.0)
+    below, above = jnp.maximum(i - 1, 0), jnp.minimum(i + 1, 7)
+    for h in range(plan.halves):
+        line = line_at(phi, h, 1, i)
+        for j, value in enumerate(line):
+            here = rows8(i * 64 + j * 8)
+            facing = facing_of(origin[h, here, :])
+            low = phi[h, rows8(below * 64 + j * 8), :]
+            high = phi[h, rows8(above * 64 + j * 8), :]
+            total = inside * steepness(value, low, high, facing)
+            if 0 < j < 7:
+                total += steepness(value, line[j - 1], line[j + 1], facing)
+            low, high = pltpu.roll(value, 1, 0), pltpu.roll(value, 7, 0)
+            total += jnp.where(middle, steepness(value, low, high, facing), 0.0)
+            inner[h, here, :] = total
+
+
+def relax(plan, phi, origin, near, inner, table, halo_code, part, moved, finish):
+    @pl.loop(0, 4)
+    def _(q):
+        for v in range(2):
+            i = q * 2 + v
+            halo = far_values(plan, table, halo_code, near, (2, 3, 4, 5), i)
+            for h in range(plan.halves):
+                for j in range(8):
+                    here = rows8(i * 64 + j * 8)
+                    if 0 < j < 7:
+                        part[h, here, :] = jnp.zeros((8, LANES), jnp.float32)
+                        continue
+                    side, other = (2, 1) if j == 0 else (3, 6)
+                    value = phi[h, here, :]
+                    beside = phi[h, rows8(i * 64 + other * 8), :]
+                    facing = facing_of(origin[h, here, :])
+                    part[h, here, :] = steepness(value, halo[side, h], beside, facing)
+                for side, k, other in ((4, 0, 1), (5, 7, 6)):
+                    here = pl.ds(i * 64 + k, 8, stride=8)
+                    value = phi[h, here, :]
+                    beside = phi[h, pl.ds(i * 64 + other, 8, stride=8), :]
+                    facing = facing_of(origin[h, here, :])
+                    part[h, here, :] += steepness(value, halo[side, h], beside, facing)
 
     @pl.loop(0, 2)
     def _(q):
         for v in range(4):
-            pull_far(plan, table, halo_code, near, columns, (0, 1), q * 4 + v)
-
-    def stage(i):
-        pull_far(plan, table, halo_code, near, faces, (2, 3, 4, 5), i)
-
-    def plane(i, h, previous, following, sides):
-        at = half(h)
-        centre = [phi[h, rows8(i * 64 + j * 8), :] for j in range(8)]
-        along_y = [sides[0]] + centre + [sides[1]]
-        for j in range(8):
-            here = rows8(i * 64 + j * 8)
-            value = centre[j]
-            start = origin[h, here, :]
-            sense = start * lax.rsqrt(start * start + 1.0)
-            facing = jnp.where(start > 0.0, 1.0, -1.0)
-            first = jnp.broadcast_to(sides[2][j : j + 1], (8, LANES))
-            last = jnp.broadcast_to(sides[3][j : j + 1], (8, LANES))
-            low_z = jnp.where(row == 0, first, pltpu.roll(value, 1, 0))
-            high_z = jnp.where(row == 7, last, pltpu.roll(value, 7, 0))
-            pairs = (
-                (previous(j), following(j)),
-                (along_y[j], along_y[j + 2]),
-                (low_z, high_z),
-            )
-            total = None
-            for low, high in pairs:
-                steep = jnp.maximum((value - low) * facing, (value - high) * facing)
-                steep = jnp.maximum(steep, 0.0)
-                steep = steep * steep
-                total = steep if total is None else total + steep
-            value = value - relax_scale * sense * (jnp.sqrt(total) - 1.0)
+            j = q * 4 + v
+            halo = far_values(plan, table, halo_code, near, (0, 1), j)
+            for h in range(plan.halves):
+                for side, i, other in ((0, 0, 1), (1, 7, 6)):
+                    here = rows8(i * 64 + j * 8)
+                    value = phi[h, here, :]
+                    beside = phi[h, rows8(other * 64 + j * 8), :]
+                    facing = facing_of(origin[h, here, :])
+                    part[h, here, :] += steepness(value, halo[side, h], beside, facing)
+
+    @pl.loop(0, 4)
+    def _(q):
+        for v in range(2):
+            i = q * 2 + v
+            for h in range(plan.halves):
+                for j in range(8):
+                    here = rows8(i * 64 + j * 8)
+                    start = origin[h, here, :]
+                    sense = start * lax.rsqrt(start * start + 1.0)
+                    slope = jnp.sqrt(inner[h, here, :] + part[h, here, :])
+                    value = phi[h, here, :] - relax_scale * sense * (slope - 1.0)
+                    if finish is not None:
+                        moved[here, half(h)] = value
+                    else:
+                        moved[h, here, :] = value
             if finish is not None:
-                moved[here, at] = value
-            else:
-                moved[h, here, :] = value
-
-    def planes(i, low, high):
-        sides = [
-            [faces[s, h, rows8(i * 8), :] for s in range(4)] for h in range(plan.halves)
-        ]
-        if not isinstance(i, int) or i < 7:
-            stage(i + 1)
-        for h in range(plan.halves):
-
-            def previous(j):
-                if low is None:
-                    return phi[h, rows8((i - 1) * 64 + j * 8), :]
-                return columns[low, h, pl.ds(j * 8, 8), :]
-
-            def following(j):
-                if high is None:
-                    return phi[h, rows8((i + 1) * 64 + j * 8), :]
-                return columns[high, h, pl.ds(j * 8, 8), :]
-
-            plane(i, h, previous, following, sides[h])
-        if finish is not None:
-            finish(i)
-
-    stage(0)
-    planes(0, 0, None)
-
-    @pl.loop(1, 7)
-    def _(i):
-        planes(i, None, None)
-
-    planes(7, None, 1)
+                finish(i)
 
 
 def first_kernel(
@@ -486,15 +502,15 @@
     pack_sends(plan, phi, ends, send_code, table, outgoing, low, high)
 
 
-def near_kernel(plan, phi, halo_code, near, *rest):
-    if plan.layers == 1:
-
-        @pl.loop(0, plan.groups // 2)
-        def _(q):
-            for v in range(2):
-                pull_local(plan, phi, None, halo_code, near, q * 2 + v)
-
-        return
+def near_thin_kernel(plan, phi, origin, halo_code, near, inner):
+    @pl.loop(0, plan.groups // 2)
+    def _(q):
+        for v in range(2):
+            pull_local(plan, phi, None, halo_code, near, q * 2 + v)
+            relax_inner(plan, phi, origin, inner, q * 2 + v)
+
+
+def near_wide_kernel(plan, phi, halo_code, near, *rest):
     inner, ends, kept, done = rest
     copies = [pltpu.make_async_copy(kept.at[a], inner.at[a], done.at[a]) for a in range(3)]
     fill_ends(plan, phi, ends)
@@ -534,28 +550,27 @@
 
 
 def relax_kernel(
-    plan, sends, phi, origin, near, arrived, before, after, send_code, halo_code, *rest
+    plan, sends, phi, origin, near, inner, arrived, before, after, send_code, halo_code, *rest
 ):
     if sends is None:
-        (result, table, columns, faces, moved, written) = rest
-
-        def part(i):
+        (result, table, part, moved, written) = rest
+
+        def plane_copy(i):
             rows = rows8(i * 64)
             rows = pl.ds(rows.start, 64)
             return pltpu.make_async_copy(moved.at[rows], result.at[rows], written.at[i])
 
         def finish(i):
-            part(i).start()
+            plane_copy(i).start()
 
     else:
-        (moved, outgoing, low, high, ends, table, columns, faces) = rest
+        (moved, outgoing, low, high, ends, table, part) = rest
         finish = None
     unpack_far(plan, arrived, before, after, table)
-    halos = (columns, faces)
-    relax(plan, phi, origin, near, table, halo_code, halos, moved, finish)
+    relax(plan, phi, origin, near, inner, table, halo_code, part, moved, finish)
     if sends is None:
         for i in range(8):
-            part(i).wait()
+            plane_copy(i).wait()
     else:
         fill_ends(sends, moved, ends)
         pack_sends(sends, moved, ends, send_code, table, outgoing, low, high)
@@ -640,16 +655,17 @@
         far=(0, 1, 2, 3),
     )
 
-    def near_halos(plan, phi):
+    def near_halos(plan, *fields):
         out = [f32((6, plan.halves, 64 * plan.layers, LANES))]
-        scratch = []
-        if plan.layers > 1:
-            out.append(f32(inner_shape))
-            scratch = [ends(plan), pltpu.VMEM(inner_shape, jnp.float32)]
-            scratch.append(pltpu.SemaphoreType.DMA((3,)))
         flops = rows * count * 100 * plan.layers
-        kernel = functools.partial(near_kernel, plan)
-        return call(kernel, out, scratch, flops, phi, halo_code, far_out=(1,))
+        if plan.layers == 1:
+            kernel = functools.partial(near_thin_kernel, plan)
+            return call(kernel, out + [field], [], flops, *fields, halo_code)
+        out.append(f32(inner_shape))
+        scratch = [ends(plan), pltpu.VMEM(inner_shape, jnp.float32)]
+        scratch.append(pltpu.SemaphoreType.DMA((3,)))
+        kernel = functools.partial(near_wide_kernel, plan)
+        return call(kernel, out, scratch, flops, *fields, halo_code, far_out=(1,))
 
     inner_shape = (3, wide.halves, rows // 2, LANES)
     block = pltpu.VMEM((wide.halves, rows, LANES), jnp.float32)
@@ -681,9 +697,9 @@
             phi, *message = call(
                 functools.partial(relax_kernel, thin, sends),
                 out,
-                scratch + [halos(2, 8), halos(4, 8)] + extra,
+                scratch + [block] + extra,
                 rows * count * 60,
-                phi, origin, *near_halos(thin, phi), *exchange(*message), send_code, halo_code,
+                phi, origin, *near_halos(thin, phi, origin), *exchange(*message), send_code, halo_code,
                 far_out=(0,) if sends is None else (),
             )
     return phi

time: 105 us -> 104 us (level)
  waiting for transfers between devices: 6.39 us -> 4.69 us
    ppermute x6, waiting for transfers between devices: 2.16 us -> 0.76 us  [exchange(): after = lax.ppermute(low, 'group', down)]
  transfers between devices with their start and end apart: 18 -> 18, of which waited for: 5 -> 5; matrix products, arithmetic and copies ran while one was open for 0% -> 0% of each run, Pallas kernels for 21% -> 23%
where the time goes in v6:
time: 104 us; the launch traced here: 103 us
  Pallas kernels  51.4 us (49%)
  starting transfers between devices  46.7 us (45%)
  waiting for transfers between devices  4.69 us (5%)
    pallas_call x13, Pallas kernels, call(): pl.pallas_call(kernel, out_shape=[pltpu.HBM(x.shape, x.dtype) if n in far...  51.4 us
    all_to_all x6, starting transfers between devices, exchange(): lax.all_to_all(outgoing, 'dev', split_axis=0, concat_axis=0, tiled=True)  29.1 us
    ppermute x6, starting transfers between devices, exchange(): after = lax.ppermute(low, 'group', down)  9.31 us
    ppermute x6, starting transfers between devices, exchange(): before = lax.ppermute(high, 'group', up)  8.24 us
    all_to_all x6, waiting for transfers between devices, exchange(): lax.all_to_all(outgoing, 'dev', split_axis=0, concat_axis=0, tiled=True)  3.91 us
  transfers between devices with their start and end apart: 18, of which 5 were waited for; matrix products, arithmetic and copies ran while one was open for 0% of the time, Pallas kernels for 23%

profile of v6, /device:TPU:0, one launch (start us, length us, event | category | flops | bytes accessed | tf_op | source)
XLA Modules:
  0.0 103.0 jit_solution(15954827260020239035)
XLA Ops:
  0.0 3.7 %shard_map.55 = (f32[2,512,128]{2,1,0:T(8,128)S(1)}, f32[8,64,128]{2,1,0:T(8,128)}, f32[24,128]{1,0:T(8,128)S(1)}, f32[24,128]{1,0:T(8,128)S(1)}, s32[8,128]{1,0:T(8,128)S(1)}, /*index=5*/s32[6,256]{1,0:T(8,128)S(1)}) custom-call(f32[512,256]{1,0:T(8,128)} %level_set.1, s32[8,40]{1,0:T(8,128)} %peer_slabs.1, s32[2,16]{1,0:T(2,128)} %region_slabs.1, ...), custom_call_target="tpu_custom_call" | custom-call | flops 1000000 | bytes 1353088 | tf_op jit(solution)/shard_map/pallas_call | solution.py:591
  3.7 6.3 %all-to-all-start = ((f32[8,64,128]{2,1,0:T(8,128)}), f32[8,64,128]{2,1,0:T(8,128)S(1)}, u32[]{:S(2)}, u32[]{:S(2)}) async-start(f32[8,64,128]{2,1,0:T(8,128)} %get-tuple-element.47), calls=%async_computation | async-start | bytes 524288 | tf_op jit(solution)/shard_map/all_to_all | solution.py:608
  10.1 1.5 %collective-permute-start = (f32[24,128]{1,0:T(8,128)S(1)}, f32[24,128]{1,0:T(8,128)S(1)}, u32[]{:S(2)}, u32[]{:S(2)}) collective-permute-start(f32[24,128]{1,0:T(8,128)S(1)} %get-tuple-element.48), channel_id=1, source_target_pairs={{0,8},{8,16},{16,24},{24,0},{1,9},{9,17},{17,25},{25,1},{2,10},{10... | collective-permute-start | bytes 36872 | tf_op jit(solution)/shard_map/ppermute | solution.py:609
  11.6 1.4 %collective-permute-start.1 = (f32[24,128]{1,0:T(8,128)S(1)}, f32[24,128]{1,0:T(8,128)S(1)}, u32[]{:S(2)}, u32[]{:S(2)}) collective-permute-start(f32[24,128]{1,0:T(8,128)S(1)} %get-tuple-element.49), channel_id=1, source_target_pairs={{8,0},{16,8},{24,16},{0,24},{9,1},{17,9},{25,17},{1,25},{10,2},{18... | collective-permute-start | bytes 36872 | tf_op jit(solution)/shard_map/ppermute | solution.py:610
  13.0 7.1 %shard_map.56 = (f32[6,2,192,128]{3,2,1,0:T(8,128)S(1)}, f32[3,2,256,128]{3,2,1,0:T(8,128)}) custom-call(f32[2,512,128]{2,1,0:T(8,128)S(1)} %get-tuple-element.43.phi, s32[6,256]{1,0:T(8,128)S(1)} %get-tuple-element.44.halo_code), custom_call_target="tpu_custom_call" | custom-call | flops 39321600 | bytes 2496512 | tf_op jit(solution)/shard_map/pallas_call | solution.py:591
  20.2 6.1 %shard_map.57 = (f32[2,512,128]{2,1,0:T(8,128)S(1)}, f32[8,24,128]{2,1,0:T(8,128)}, f32[8,128]{1,0:T(8,128)S(1)}, f32[8,128]{1,0:T(8,128)S(1)}) custom-call(f32[2,512,128]{2,1,0:T(8,128)S(1)} %get-tuple-element.43.phi, f32[6,2,192,128]{3,2,1,0:T(8,128)S(1)} %get-tuple-element.45.near, f32[3,2,256,128]{3,2,1,0:T(8,128)} %get-tuple-element.46.inner, ...), custom_call_target="tpu_custom_call" | custom-call | flops 39321600 | bytes 3942400 | tf_op jit(solution)/shard_map/pallas_call | solution.py:591
  26.3 5.1 %all-to-all-start.1 = ((f32[8,24,128]{2,1,0:T(8,128)}), f32[8,24,128]{2,1,0:T(8,128)S(1)}, u32[]{:S(2)}, u32[]{:S(2)}) async-start(f32[8,24,128]{2,1,0:T(8,128)} %get-tuple-element.54), calls=%async_computation.1 | async-start | bytes 196608 | tf_op jit(solution)/shard_map/all_to_all | solution.py:608
  32.0 2.3 %collective-permute-start.3 = (f32[8,128]{1,0:T(8,128)S(1)}, f32[8,128]{1,0:T(8,128)S(1)}, u32[]{:S(2)}, u32[]{:S(2)}) collective-permute-start(f32[8,128]{1,0:T(8,128)S(1)} %get-tuple-element.56), channel_id=1, source_target_pairs={{8,0},{16,8},{24,16},{0,24},{9,1},{17,9},{25,17},{1,25},{10,2},{18... | collective-permute-start | bytes 12296 | tf_op jit(solution)/shard_map/ppermute | solution.py:610
  34.3 2.2 %shard_map.58 = (f32[6,2,64,128]{3,2,1,0:T(8,128)S(1)}, f32[2,512,128]{2,1,0:T(8,128)S(1)}) custom-call(f32[2,512,128]{2,1,0:T(8,128)S(1)} %get-tuple-element.51.phi.origin, f32[2,512,128]{2,1,0:T(8,128)S(1)} %get-tuple-element.51.phi.origin, s32[6,256]{1,0:T(8,128)S(1)} %get-tuple-element.44.halo_code), custom_call_target="tpu_custom_call" | custom-call | flops 13107200 | bytes 1972224 | tf_op jit(solution)/shard_map/pallas_call | solution.py:591
  36.6 1.2 %all-to-all-done.1.arrived = f32[8,24,128]{2,1,0:T(8,128)S(1)} async-done(((f32[8,24,128]{2,1,0:T(8,128)}), f32[8,24,128]{2,1,0:T(8,128)S(1)}, u32[]{:S(2)}, u32[]{:S(2)}) %all-to-all-start.1) | async-done | bytes 98336 | tf_op jit(solution)/shard_map/all_to_all | solution.py:608
  37.8 2.9 %shard_map.59 = (f32[2,512,128]{2,1,0:T(8,128)S(1)}, f32[8,24,128]{2,1,0:T(8,128)}, f32[8,128]{1,0:T(8,128)S(1)}, f32[8,128]{1,0:T(8,128)S(1)}) custom-call(f32[2,512,128]{2,1,0:T(8,128)S(1)} %get-tuple-element.51.phi.origin, f32[2,512,128]{2,1,0:T(8,128)S(1)} %get-tuple-element.51.phi.origin, f32[6,2,64,128]{3,2,1,0:T(8,128)S(1)} %get-tuple-element.52.near, ...), custom_call_target="tpu_custom_call" | custom-call | flops 7864320 | bytes 2713600 | tf_op jit(solution)/shard_map/pallas_call | solution.py:591
  40.6 4.0 %all-to-all-start.2 = ((f32[8,24,128]{2,1,0:T(8,128)}), f32[8,24,128]{2,1,0:T(8,128)S(1)}, u32[]{:S(2)}, u32[]{:S(2)}) async-start(f32[8,24,128]{2,1,0:T(8,128)} %get-tuple-element.60), calls=%async_computation.2 | async-start | bytes 196608 | tf_op jit(solution)/shard_map/all_to_all | solution.py:608
  44.6 2.3 %collective-permute-start.4 = (f32[8,128]{1,0:T(8,128)S(1)}, f32[8,128]{1,0:T(8,128)S(1)}, u32[]{:S(2)}, u32[]{:S(2)}) collective-permute-start(f32[8,128]{1,0:T(8,128)S(1)} %get-tuple-element.61), channel_id=1, source_target_pairs={{0,8},{8,16},{16,24},{24,0},{1,9},{9,17},{17,25},{25,1},{2,10},{10... | collective-permute-start | bytes 12296 | tf_op jit(solution)/shard_map/ppermute | solution.py:609
  47.5 2.2 %shard_map.60 = (f32[6,2,64,128]{3,2,1,0:T(8,128)S(1)}, f32[2,512,128]{2,1,0:T(8,128)S(1)}) custom-call(f32[2,512,128]{2,1,0:T(8,128)S(1)} %get-tuple-element.57.phi, f32[2,512,128]{2,1,0:T(8,128)S(1)} %get-tuple-element.51.phi.origin, s32[6,256]{1,0:T(8,128)S(1)} %get-tuple-element.44.halo_code), custom_call_target="tpu_custom_call" | custom-call | flops 13107200 | bytes 1972224 | tf_op jit(solution)/shard_map/pallas_call | solution.py:591
  49.8 0.7 collective-permute-done.5.after
  50.9 4.2 %shard_map.61 = (f32[2,512,128]{2,1,0:T(8,128)S(1)}, f32[8,64,128]{2,1,0:T(8,128)}, f32[24,128]{1,0:T(8,128)S(1)}, f32[24,128]{1,0:T(8,128)S(1)}) custom-call(f32[2,512,128]{2,1,0:T(8,128)S(1)} %get-tuple-element.57.phi, f32[2,512,128]{2,1,0:T(8,128)S(1)} %get-tuple-element.51.phi.origin, f32[6,2,64,128]{3,2,1,0:T(8,128)S(1)} %get-tuple-element.58.near, ...), custom_call_target="tpu_custom_call" | custom-call | flops 7864320 | bytes 2893824 | tf_op jit(solution)/shard_map/pallas_call | solution.py:591
  55.1 4.7 %all-to-all-start.3 = ((f32[8,64,128]{2,1,0:T(8,128)}), f32[8,64,128]{2,1,0:T(8,128)S(1)}, u32[]{:S(2)}, u32[]{:S(2)}) async-start(f32[8,64,128]{2,1,0:T(8,128)} %get-tuple-element.66), calls=%async_computation.3 | async-start | bytes 524288 | tf_op jit(solution)/shard_map/all_to_all | solution.py:608
  59.8 1.6 %collective-permute-start.6 = (f32[24,128]{1,0:T(8,128)S(1)}, f32[24,128]{1,0:T(8,128)S(1)}, u32[]{:S(2)}, u32[]{:S(2)}) collective-permute-start(f32[24,128]{1,0:T(8,128)S(1)} %get-tuple-element.67), channel_id=1, source_target_pairs={{0,8},{8,16},{16,24},{24,0},{1,9},{9,17},{17,25},{25,1},{2,10},{10... | collective-permute-start | bytes 36872 | tf_op jit(solution)/shard_map/ppermute | solution.py:609
  61.4 1.3 %collective-permute-start.7 = (f32[24,128]{1,0:T(8,128)S(1)}, f32[24,128]{1,0:T(8,128)S(1)}, u32[]{:S(2)}, u32[]{:S(2)}) collective-permute-start(f32[24,128]{1,0:T(8,128)S(1)} %get-tuple-element.68), channel_id=1, source_target_pairs={{8,0},{16,8},{24,16},{0,24},{9,1},{17,9},{25,17},{1,25},{10,2},{18... | collective-permute-start | bytes 36872 | tf_op jit(solution)/shard_map/ppermute | solution.py:610
  62.7 7.1 %shard_map.62 = (f32[6,2,192,128]{3,2,1,0:T(8,128)S(1)}, f32[3,2,256,128]{3,2,1,0:T(8,128)}) custom-call(f32[2,512,128]{2,1,0:T(8,128)S(1)} %get-tuple-element.63.phi, s32[6,256]{1,0:T(8,128)S(1)} %get-tuple-element.44.halo_code), custom_call_target="tpu_custom_call" | custom-call | flops 39321600 | bytes 2496512 | tf_op jit(solution)/shard_map/pallas_call | solution.py:591
  69.9 6.1 %shard_map.63 = (f32[2,512,128]{2,1,0:T(8,128)S(1)}, f32[8,24,128]{2,1,0:T(8,128)}, f32[8,128]{1,0:T(8,128)S(1)}, f32[8,128]{1,0:T(8,128)S(1)}) custom-call(f32[2,512,128]{2,1,0:T(8,128)S(1)} %get-tuple-element.63.phi, f32[6,2,192,128]{3,2,1,0:T(8,128)S(1)} %get-tuple-element.64.near, f32[3,2,256,128]{3,2,1,0:T(8,128)} %get-tuple-element.65.inner, ...), custom_call_target="tpu_custom_call" | custom-call | flops 39321600 | bytes 3942400 | tf_op jit(solution)/shard_map/pallas_call | solution.py:591
  76.0 5.1 %all-to-all-start.4 = ((f32[8,24,128]{2,1,0:T(8,128)}), f32[8,24,128]{2,1,0:T(8,128)S(1)}, u32[]{:S(2)}, u32[]{:S(2)}) async-start(f32[8,24,128]{2,1,0:T(8,128)} %get-tuple-element.72), calls=%async_computation.4 | async-start | bytes 196608 | tf_op jit(solution)/shard_map/all_to_all | solution.py:608
  81.8 2.2 %collective-permute-start.9 = (f32[8,128]{1,0:T(8,128)S(1)}, f32[8,128]{1,0:T(8,128)S(1)}, u32[]{:S(2)}, u32[]{:S(2)}) collective-permute-start(f32[8,128]{1,0:T(8,128)S(1)} %get-tuple-element.74), channel_id=1, source_target_pairs={{8,0},{16,8},{24,16},{0,24},{9,1},{17,9},{25,17},{1,25},{10,2},{18... | collective-permute-start | bytes 12296 | tf_op jit(solution)/shard_map/ppermute | solution.py:610
  84.1 2.2 %shard_map.64 = (f32[6,2,64,128]{3,2,1,0:T(8,128)S(1)}, f32[2,512,128]{2,1,0:T(8,128)S(1)}) custom-call(f32[2,512,128]{2,1,0:T(8,128)S(1)} %get-tuple-element.69.phi.origin, f32[2,512,128]{2,1,0:T(8,128)S(1)} %get-tuple-element.69.phi.origin, s32[6,256]{1,0:T(8,128)S(1)} %get-tuple-element.44.halo_code), custom_call_target="tpu_custom_call" | custom-call | flops 13107200 | bytes 1972224 | tf_op jit(solution)/shard_map/pallas_call | solution.py:591
  86.3 1.2 %all-to-all-done.4.arrived = f32[8,24,128]{2,1,0:T(8,128)S(1)} async-done(((f32[8,24,128]{2,1,0:T(8,128)}), f32[8,24,128]{2,1,0:T(8,128)S(1)}, u32[]{:S(2)}, u32[]{:S(2)}) %all-to-all-start.4) | async-done | bytes 98336 | tf_op jit(solution)/shard_map/all_to_all | solution.py:608
  87.5 2.9 %shard_map.65 = (f32[2,512,128]{2,1,0:T(8,128)S(1)}, f32[8,24,128]{2,1,0:T(8,128)}, f32[8,128]{1,0:T(8,128)S(1)}, f32[8,128]{1,0:T(8,128)S(1)}) custom-call(f32[2,512,128]{2,1,0:T(8,128)S(1)} %get-tuple-element.69.phi.origin, f32[2,512,128]{2,1,0:T(8,128)S(1)} %get-tuple-element.69.phi.origin, f32[6,2,64,128]{3,2,1,0:T(8,128)S(1)} %get-tuple-element.70.near, ...), custom_call_target="tpu_custom_call" | custom-call | flops 7864320 | bytes 2713600 | tf_op jit(solution)/shard_map/pallas_call | solution.py:591
  90.4 4.0 %all-to-all-start.5 = ((f32[8,24,128]{2,1,0:T(8,128)}), f32[8,24,128]{2,1,0:T(8,128)S(1)}, u32[]{:S(2)}, u32[]{:S(2)}) async-start(f32[8,24,128]{2,1,0:T(8,128)} %get-tuple-element.78), calls=%async_computation.5 | async-start | bytes 196608 | tf_op jit(solution)/shard_map/all_to_all | solution.py:608
  94.3 1.6 %collective-permute-start.10 = (f32[8,128]{1,0:T(8,128)S(1)}, f32[8,128]{1,0:T(8,128)S(1)}, u32[]{:S(2)}, u32[]{:S(2)}) collective-permute-start(f32[8,128]{1,0:T(8,128)S(1)} %get-tuple-element.79), channel_id=1, source_target_pairs={{0,8},{8,16},{16,24},{24,0},{1,9},{9,17},{17,25},{25,1},{2,10},{10... | collective-permute-start | bytes 12296 | tf_op jit(solution)/shard_map/ppermute | solution.py:609
  95.9 1.3 %collective-permute-start.11 = (f32[8,128]{1,0:T(8,128)S(1)}, f32[8,128]{1,0:T(8,128)S(1)}, u32[]{:S(2)}, u32[]{:S(2)}) collective-permute-start(f32[8,128]{1,0:T(8,128)S(1)} %get-tuple-element.80), channel_id=1, source_target_pairs={{8,0},{16,8},{24,16},{0,24},{9,1},{17,9},{25,17},{1,25},{10,2},{18... | collective-permute-start | bytes 12296 | tf_op jit(solution)/shard_map/ppermute | solution.py:610
  97.3 2.2 %shard_map.66 = (f32[6,2,64,128]{3,2,1,0:T(8,128)S(1)}, f32[2,512,128]{2,1,0:T(8,128)S(1)}) custom-call(f32[2,512,128]{2,1,0:T(8,128)S(1)} %get-tuple-element.75.phi, f32[2,512,128]{2,1,0:T(8,128)S(1)} %get-tuple-element.69.phi.origin, s32[6,256]{1,0:T(8,128)S(1)} %get-tuple-element.44.halo_code), custom_call_target="tpu_custom_call" | custom-call | flops 13107200 | bytes 1972224 | tf_op jit(solution)/shard_map/pallas_call | solution.py:591
  99.5 1.1 %all-to-all-done.5.arrived = f32[8,24,128]{2,1,0:T(8,128)S(1)} async-done(((f32[8,24,128]{2,1,0:T(8,128)}), f32[8,24,128]{2,1,0:T(8,128)S(1)}, u32[]{:S(2)}, u32[]{:S(2)}) %all-to-all-start.5) | async-done | bytes 98336 | tf_op jit(solution)/shard_map/all_to_all | solution.py:608
  100.7 2.3 %shard_map.67 = f32[512,256]{1,0:T(8,128)} custom-call(f32[2,512,128]{2,1,0:T(8,128)S(1)} %get-tuple-element.75.phi, f32[2,512,128]{2,1,0:T(8,128)S(1)} %get-tuple-element.69.phi.origin, f32[6,2,64,128]{3,2,1,0:T(8,128)S(1)} %get-tuple-element.76.near, f32[2,512,128]{2,1,0:T(8,128)S(1)} %get-tuple-element.77.inner, ...), custom_call_target="tpu_custom_call" | custom-call | flops 7864320 | bytes 2607104 | tf_op jit(solution)/shard_map/pallas_call | solution.py:591
  (17 shorter events, 2.4 us)
Async XLA Ops:
  3.7 16.4 %all-to-all-start = ((f32[8,64,128]{2,1,0:T(8,128)}), f32[8,64,128]{2,1,0:T(8,128)S(1)}, u32[]{:S(2)}, u32[]{:S(2)}) async-start(f32[8,64,128]{2,1,0:T(8,128)} %get-tuple-element.47), calls=%async_computation | async-start | bytes 524288 | tf_op jit(solution)/shard_map/all_to_all | solution.py:608
  10.1 10.1 %collective-permute-start = (f32[24,128]{1,0:T(8,128)S(1)}, f32[24,128]{1,0:T(8,128)S(1)}, u32[]{:S(2)}, u32[]{:S(2)}) collective-permute-start(f32[24,128]{1,0:T(8,128)S(1)} %get-tuple-element.48), channel_id=1, source_target_pairs={{0,8},{8,16},{16,24},{24,0},{1,9},{9,17},{17,25},{25,1},{2,10},{10... | collective-permute-start | bytes 36872 | tf_op jit(solution)/shard_map/ppermute | solution.py:609
  11.6 8.6 %collective-permute-start.1 = (f32[24,128]{1,0:T(8,128)S(1)}, f32[24,128]{1,0:T(8,128)S(1)}, u32[]{:S(2)}, u32[]{:S(2)}) collective-permute-start(f32[24,128]{1,0:T(8,128)S(1)} %get-tuple-element.49), channel_id=1, source_target_pairs={{8,0},{16,8},{24,16},{0,24},{9,1},{17,9},{25,17},{1,25},{10,2},{18... | collective-permute-start | bytes 36872 | tf_op jit(solution)/shard_map/ppermute | solution.py:610
  26.3 11.5 %all-to-all-start.1 = ((f32[8,24,128]{2,1,0:T(8,128)}), f32[8,24,128]{2,1,0:T(8,128)S(1)}, u32[]{:S(2)}, u32[]{:S(2)}) async-start(f32[8,24,128]{2,1,0:T(8,128)} %get-tuple-element.54), calls=%async_computation.1 | async-start | bytes 196608 | tf_op jit(solution)/shard_map/all_to_all | solution.py:608
  31.4 5.2 %collective-permute-start.2 = (f32[8,128]{1,0:T(8,128)S(1)}, f32[8,128]{1,0:T(8,128)S(1)}, u32[]{:S(2)}, u32[]{:S(2)}) collective-permute-start(f32[8,128]{1,0:T(8,128)S(1)} %get-tuple-element.55), channel_id=1, source_target_pairs={{0,8},{8,16},{16,24},{24,0},{1,9},{9,17},{17,25},{25,1},{2,10},{10... | collective-permute-start | bytes 12296 | tf_op jit(solution)/shard_map/ppermute | solution.py:609
  32.0 4.6 %collective-permute-start.3 = (f32[8,128]{1,0:T(8,128)S(1)}, f32[8,128]{1,0:T(8,128)S(1)}, u32[]{:S(2)}, u32[]{:S(2)}) collective-permute-start(f32[8,128]{1,0:T(8,128)S(1)} %get-tuple-element.56), channel_id=1, source_target_pairs={{8,0},{16,8},{24,16},{0,24},{9,1},{17,9},{25,17},{1,25},{10,2},{18... | collective-permute-start | bytes 12296 | tf_op jit(solution)/shard_map/ppermute | solution.py:610
  40.6 10.3 %all-to-all-start.2 = ((f32[8,24,128]{2,1,0:T(8,128)}), f32[8,24,128]{2,1,0:T(8,128)S(1)}, u32[]{:S(2)}, u32[]{:S(2)}) async-start(f32[8,24,128]{2,1,0:T(8,128)} %get-tuple-element.60), calls=%async_computation.2 | async-start | bytes 196608 | tf_op jit(solution)/shard_map/all_to_all | solution.py:608
  44.6 5.2 %collective-permute-start.4 = (f32[8,128]{1,0:T(8,128)S(1)}, f32[8,128]{1,0:T(8,128)S(1)}, u32[]{:S(2)}, u32[]{:S(2)}) collective-permute-start(f32[8,128]{1,0:T(8,128)S(1)} %get-tuple-element.61), channel_id=1, source_target_pairs={{0,8},{8,16},{16,24},{24,0},{1,9},{9,17},{17,25},{25,1},{2,10},{10... | collective-permute-start | bytes 12296 | tf_op jit(solution)/shard_map/ppermute | solution.py:609
  46.9 3.6 %collective-permute-start.5 = (f32[8,128]{1,0:T(8,128)S(1)}, f32[8,128]{1,0:T(8,128)S(1)}, u32[]{:S(2)}, u32[]{:S(2)}) collective-permute-start(f32[8,128]{1,0:T(8,128)S(1)} %get-tuple-element.62), channel_id=1, source_target_pairs={{8,0},{16,8},{24,16},{0,24},{9,1},{17,9},{25,17},{1,25},{10,2},{18... | collective-permute-start | bytes 12296 | tf_op jit(solution)/shard_map/ppermute | solution.py:610
  55.1 14.8 %all-to-all-start.3 = ((f32[8,64,128]{2,1,0:T(8,128)}), f32[8,64,128]{2,1,0:T(8,128)S(1)}, u32[]{:S(2)}, u32[]{:S(2)}) async-start(f32[8,64,128]{2,1,0:T(8,128)} %get-tuple-element.66), calls=%async_computation.3 | async-start | bytes 524288 | tf_op jit(solution)/shard_map/all_to_all | solution.py:608
  59.8 10.1 %collective-permute-start.6 = (f32[24,128]{1,0:T(8,128)S(1)}, f32[24,128]{1,0:T(8,128)S(1)}, u32[]{:S(2)}, u32[]{:S(2)}) collective-permute-start(f32[24,128]{1,0:T(8,128)S(1)} %get-tuple-element.67), channel_id=1, source_target_pairs={{0,8},{8,16},{16,24},{24,0},{1,9},{9,17},{17,25},{25,1},{2,10},{10... | collective-permute-start | bytes 36872 | tf_op jit(solution)/shard_map/ppermute | solution.py:609
  61.4 8.5 %collective-permute-start.7 = (f32[24,128]{1,0:T(8,128)S(1)}, f32[24,128]{1,0:T(8,128)S(1)}, u32[]{:S(2)}, u32[]{:S(2)}) collective-permute-start(f32[24,128]{1,0:T(8,128)S(1)} %get-tuple-element.68), channel_id=1, source_target_pairs={{8,0},{16,8},{24,16},{0,24},{9,1},{17,9},{25,17},{1,25},{10,2},{18... | collective-permute-start | bytes 36872 | tf_op jit(solution)/shard_map/ppermute | solution.py:610
  76.0 11.5 %all-to-all-start.4 = ((f32[8,24,128]{2,1,0:T(8,128)}), f32[8,24,128]{2,1,0:T(8,128)S(1)}, u32[]{:S(2)}, u32[]{:S(2)}) async-start(f32[8,24,128]{2,1,0:T(8,128)} %get-tuple-element.72), calls=%async_computation.4 | async-start | bytes 196608 | tf_op jit(solution)/shard_map/all_to_all | solution.py:608
  81.2 5.2 %collective-permute-start.8 = (f32[8,128]{1,0:T(8,128)S(1)}, f32[8,128]{1,0:T(8,128)S(1)}, u32[]{:S(2)}, u32[]{:S(2)}) collective-permute-start(f32[8,128]{1,0:T(8,128)S(1)} %get-tuple-element.73), channel_id=1, source_target_pairs={{0,8},{8,16},{16,24},{24,0},{1,9},{9,17},{17,25},{25,1},{2,10},{10... | collective-permute-start | bytes 12296 | tf_op jit(solution)/shard_map/ppermute | solution.py:609
  81.8 4.5 %collective-permute-start.9 = (f32[8,128]{1,0:T(8,128)S(1)}, f32[8,128]{1,0:T(8,128)S(1)}, u32[]{:S(2)}, u32[]{:S(2)}) collective-permute-start(f32[8,128]{1,0:T(8,128)S(1)} %get-tuple-element.74), channel_id=1, source_target_pairs={{8,0},{16,8},{24,16},{0,24},{9,1},{17,9},{25,17},{1,25},{10,2},{18... | collective-permute-start | bytes 12296 | tf_op jit(solution)/shard_map/ppermute | solution.py:610
  90.4 10.3 %all-to-all-start.5 = ((f32[8,24,128]{2,1,0:T(8,128)}), f32[8,24,128]{2,1,0:T(8,128)S(1)}, u32[]{:S(2)}, u32[]{:S(2)}) async-start(f32[8,24,128]{2,1,0:T(8,128)} %get-tuple-element.78), calls=%async_computation.5 | async-start | bytes 196608 | tf_op jit(solution)/shard_map/all_to_all | solution.py:608
  94.3 5.2 %collective-permute-start.10 = (f32[8,128]{1,0:T(8,128)S(1)}, f32[8,128]{1,0:T(8,128)S(1)}, u32[]{:S(2)}, u32[]{:S(2)}) collective-permute-start(f32[8,128]{1,0:T(8,128)S(1)} %get-tuple-element.79), channel_id=1, source_target_pairs={{0,8},{8,16},{16,24},{24,0},{1,9},{9,17},{17,25},{25,1},{2,10},{10... | collective-permute-start | bytes 12296 | tf_op jit(solution)/shard_map/ppermute | solution.py:609
  95.9 3.6 %collective-permute-start.11 = (f32[8,128]{1,0:T(8,128)S(1)}, f32[8,128]{1,0:T(8,128)S(1)}, u32[]{:S(2)}, u32[]{:S(2)}) collective-permute-start(f32[8,128]{1,0:T(8,128)S(1)} %get-tuple-element.80), channel_id=1, source_target_pairs={{8,0},{16,8},{24,16},{0,24},{9,1},{17,9},{25,17},{1,25},{10,2},{18... | collective-permute-start | bytes 12296 | tf_op jit(solution)/shard_map/ppermute | solution.py:610

commit v7 on v6

--- a/solution.py
+++ b/solution.py
@@ -238,7 +238,7 @@
     first = [q[m + 1] - q[m] for m in range(7)]
     second = [first[m + 1] - first[m] for m in range(6)]
     third = [second[m + 1] - second[m] for m in range(5)]
-    fourth = [(third[m] - third[m + 1]) * (1.0 / 3.0) for m in range(4)]
+    fourth = [(third[m] - third[m + 1]) * (1.0 / 6.0) for m in range(4)]
     bend = [t * t * (4.0 / 3.0) + weno_floor for t in third]
     found = []
     for m in range(3):
@@ -248,14 +248,14 @@
         c = bend[m + 2] + s2 * (s2 - third[m + 2])
         a, b, c = (pl.reciprocal(value, approx=True) for value in (a, b, c))
         x, z = a * a, c * c
-        total = x + z + (6.0 * b) * b
+        total = 0.5 * (x + z) + (3.0 * b) * b
         xu = x * fourth[m]
         zu = z * fourth[m + 1]
         slope = 0.25 * (s1 + s2)
         middle = first[m + 2] + third[m + 1] * (1.0 / 12.0)
-        fix = (xu + 1.5 * zu) * pl.reciprocal(total + 2.0 * z, approx=True)
+        fix = (xu + 1.5 * zu) * pl.reciprocal(total + z, approx=True)
         backward = middle + slope + fix
-        fix = (zu + 1.5 * xu) * pl.reciprocal(total + 2.0 * x, approx=True)
+        fix = (zu + 1.5 * xu) * pl.reciprocal(total + x, approx=True)
         found.append((backward, fix + slope - middle))
     return found
 
@@ -369,8 +369,6 @@
 
 
 def relax_inner(plan, phi, origin, inner, i):
-    row = lax.broadcasted_iota(jnp.int32, (8, LANES), 0)
-    middle = jnp.logical_and(row > 0, row < 7)
     inside = jnp.where(jnp.logical_and(i > 0, i < 7), 1.0, 0.0)
     below, above = jnp.maximum(i - 1, 0), jnp.minimum(i + 1, 7)
     for h in range(plan.halves):
@@ -383,9 +381,12 @@
             total = inside * steepness(value, low, high, facing)
             if 0 < j < 7:
                 total += steepness(value, line[j - 1], line[j + 1], facing)
-            low, high = pltpu.roll(value, 1, 0), pltpu.roll(value, 7, 0)
-            total += jnp.where(middle, steepness(value, low, high, facing), 0.0)
             inner[h, here, :] = total
+        line = line_at(phi, h, 2, i)
+        for k in range(1, 7):
+            here = pl.ds(i * 64 + k, 8, stride=8)
+            facing = facing_of(origin[h, here, :])
+            inner[h, here, :] += steepness(line[k], line[k - 1], line[k + 1], facing)
 
 
 def relax(plan, phi, origin, near, inner, table, halo_code, part, moved, finish):

time: 104 us -> 104 us (level)
  no operation moved by 1% of the time
where the time goes in v7:
time: 104 us; the launch traced here: 103 us
  Pallas kernels  51.5 us (50%)
  starting transfers between devices  46.7 us (45%)
  waiting for transfers between devices  4.61 us (4%)
    pallas_call x13, Pallas kernels, call(): pl.pallas_call(kernel, out_shape=[pltpu.HBM(x.shape, x.dtype) if n in far...  51.5 us
    all_to_all x6, starting transfers between devices, exchange(): lax.all_to_all(outgoing, 'dev', split_axis=0, concat_axis=0, tiled=True)  29.1 us
    ppermute x6, starting transfers between devices, exchange(): after = lax.ppermute(low, 'group', down)  9.27 us
    ppermute x6, starting transfers between devices, exchange(): before = lax.ppermute(high, 'group', up)  8.28 us
    all_to_all x6, waiting for transfers between devices, exchange(): lax.all_to_all(outgoing, 'dev', split_axis=0, concat_axis=0, tiled=True)  3.87 us
  transfers between devices with their start and end apart: 18, of which 5 were waited for; matrix products, arithmetic and copies ran while one was open for 0% of the time, Pallas kernels for 23%

profile of v7, /device:TPU:0, one launch (start us, length us, event | category | flops | bytes accessed | tf_op | source)
XLA Modules:
  0.0 102.9 jit_solution(968650943342202933)
XLA Ops:
  0.0 3.7 %shard_map.55 = (f32[2,512,128]{2,1,0:T(8,128)S(1)}, f32[8,64,128]{2,1,0:T(8,128)}, f32[24,128]{1,0:T(8,128)S(1)}, f32[24,128]{1,0:T(8,128)S(1)}, s32[8,128]{1,0:T(8,128)S(1)}, /*index=5*/s32[6,256]{1,0:T(8,128)S(1)}) custom-call(f32[512,256]{1,0:T(8,128)} %level_set.1, s32[8,40]{1,0:T(8,128)} %peer_slabs.1, s32[2,16]{1,0:T(2,128)} %region_slabs.1, ...), custom_call_target="tpu_custom_call" | custom-call | flops 1000000 | bytes 1353088 | tf_op jit(solution)/shard_map/pallas_call | solution.py:592
  3.7 6.3 %all-to-all-start = ((f32[8,64,128]{2,1,0:T(8,128)}), f32[8,64,128]{2,1,0:T(8,128)S(1)}, u32[]{:S(2)}, u32[]{:S(2)}) async-start(f32[8,64,128]{2,1,0:T(8,128)} %get-tuple-element.47), calls=%async_computation | async-start | bytes 524288 | tf_op jit(solution)/shard_map/all_to_all | solution.py:609
  10.1 1.5 %collective-permute-start = (f32[24,128]{1,0:T(8,128)S(1)}, f32[24,128]{1,0:T(8,128)S(1)}, u32[]{:S(2)}, u32[]{:S(2)}) collective-permute-start(f32[24,128]{1,0:T(8,128)S(1)} %get-tuple-element.48), channel_id=1, source_target_pairs={{0,8},{8,16},{16,24},{24,0},{1,9},{9,17},{17,25},{25,1},{2,10},{10... | collective-permute-start | bytes 36872 | tf_op jit(solution)/shard_map/ppermute | solution.py:610
  11.6 1.4 %collective-permute-start.1 = (f32[24,128]{1,0:T(8,128)S(1)}, f32[24,128]{1,0:T(8,128)S(1)}, u32[]{:S(2)}, u32[]{:S(2)}) collective-permute-start(f32[24,128]{1,0:T(8,128)S(1)} %get-tuple-element.49), channel_id=1, source_target_pairs={{8,0},{16,8},{24,16},{0,24},{9,1},{17,9},{25,17},{1,25},{10,2},{18... | collective-permute-start | bytes 36872 | tf_op jit(solution)/shard_map/ppermute | solution.py:611
  13.0 7.1 %shard_map.56 = (f32[6,2,192,128]{3,2,1,0:T(8,128)S(1)}, f32[3,2,256,128]{3,2,1,0:T(8,128)}) custom-call(f32[2,512,128]{2,1,0:T(8,128)S(1)} %get-tuple-element.43.phi, s32[6,256]{1,0:T(8,128)S(1)} %get-tuple-element.44.halo_code), custom_call_target="tpu_custom_call" | custom-call | flops 39321600 | bytes 2496512 | tf_op jit(solution)/shard_map/pallas_call | solution.py:592
  20.2 6.1 %shard_map.57 = (f32[2,512,128]{2,1,0:T(8,128)S(1)}, f32[8,24,128]{2,1,0:T(8,128)}, f32[8,128]{1,0:T(8,128)S(1)}, f32[8,128]{1,0:T(8,128)S(1)}) custom-call(f32[2,512,128]{2,1,0:T(8,128)S(1)} %get-tuple-element.43.phi, f32[6,2,192,128]{3,2,1,0:T(8,128)S(1)} %get-tuple-element.45.near, f32[3,2,256,128]{3,2,1,0:T(8,128)} %get-tuple-element.46.inner, ...), custom_call_target="tpu_custom_call" | custom-call | flops 39321600 | bytes 3942400 | tf_op jit(solution)/shard_map/pallas_call | solution.py:592
  26.3 5.1 %all-to-all-start.1 = ((f32[8,24,128]{2,1,0:T(8,128)}), f32[8,24,128]{2,1,0:T(8,128)S(1)}, u32[]{:S(2)}, u32[]{:S(2)}) async-start(f32[8,24,128]{2,1,0:T(8,128)} %get-tuple-element.54), calls=%async_computation.1 | async-start | bytes 196608 | tf_op jit(solution)/shard_map/all_to_all | solution.py:609
  32.0 2.3 %collective-permute-start.3 = (f32[8,128]{1,0:T(8,128)S(1)}, f32[8,128]{1,0:T(8,128)S(1)}, u32[]{:S(2)}, u32[]{:S(2)}) collective-permute-start(f32[8,128]{1,0:T(8,128)S(1)} %get-tuple-element.56), channel_id=1, source_target_pairs={{8,0},{16,8},{24,16},{0,24},{9,1},{17,9},{25,17},{1,25},{10,2},{18... | collective-permute-start | bytes 12296 | tf_op jit(solution)/shard_map/ppermute | solution.py:611
  34.3 2.2 %shard_map.58 = (f32[6,2,64,128]{3,2,1,0:T(8,128)S(1)}, f32[2,512,128]{2,1,0:T(8,128)S(1)}) custom-call(f32[2,512,128]{2,1,0:T(8,128)S(1)} %get-tuple-element.51.phi.origin, f32[2,512,128]{2,1,0:T(8,128)S(1)} %get-tuple-element.51.phi.origin, s32[6,256]{1,0:T(8,128)S(1)} %get-tuple-element.44.halo_code), custom_call_target="tpu_custom_call" | custom-call | flops 13107200 | bytes 1972224 | tf_op jit(solution)/shard_map/pallas_call | solution.py:592
  36.6 1.1 %all-to-all-done.1.arrived = f32[8,24,128]{2,1,0:T(8,128)S(1)} async-done(((f32[8,24,128]{2,1,0:T(8,128)}), f32[8,24,128]{2,1,0:T(8,128)S(1)}, u32[]{:S(2)}, u32[]{:S(2)}) %all-to-all-start.1) | async-done | bytes 98336 | tf_op jit(solution)/shard_map/all_to_all | solution.py:609
  37.7 2.9 %shard_map.59 = (f32[2,512,128]{2,1,0:T(8,128)S(1)}, f32[8,24,128]{2,1,0:T(8,128)}, f32[8,128]{1,0:T(8,128)S(1)}, f32[8,128]{1,0:T(8,128)S(1)}) custom-call(f32[2,512,128]{2,1,0:T(8,128)S(1)} %get-tuple-element.51.phi.origin, f32[2,512,128]{2,1,0:T(8,128)S(1)} %get-tuple-element.51.phi.origin, f32[6,2,64,128]{3,2,1,0:T(8,128)S(1)} %get-tuple-element.52.near, ...), custom_call_target="tpu_custom_call" | custom-call | flops 7864320 | bytes 2713600 | tf_op jit(solution)/shard_map/pallas_call | solution.py:592
  40.6 4.0 %all-to-all-start.2 = ((f32[8,24,128]{2,1,0:T(8,128)}), f32[8,24,128]{2,1,0:T(8,128)S(1)}, u32[]{:S(2)}, u32[]{:S(2)}) async-start(f32[8,24,128]{2,1,0:T(8,128)} %get-tuple-element.60), calls=%async_computation.2 | async-start | bytes 196608 | tf_op jit(solution)/shard_map/all_to_all | solution.py:609
  44.6 2.3 %collective-permute-start.4 = (f32[8,128]{1,0:T(8,128)S(1)}, f32[8,128]{1,0:T(8,128)S(1)}, u32[]{:S(2)}, u32[]{:S(2)}) collective-permute-start(f32[8,128]{1,0:T(8,128)S(1)} %get-tuple-element.61), channel_id=1, source_target_pairs={{0,8},{8,16},{16,24},{24,0},{1,9},{9,17},{17,25},{25,1},{2,10},{10... | collective-permute-start | bytes 12296 | tf_op jit(solution)/shard_map/ppermute | solution.py:610
  47.5 2.3 %shard_map.60 = (f32[6,2,64,128]{3,2,1,0:T(8,128)S(1)}, f32[2,512,128]{2,1,0:T(8,128)S(1)}) custom-call(f32[2,512,128]{2,1,0:T(8,128)S(1)} %get-tuple-element.57.phi, f32[2,512,128]{2,1,0:T(8,128)S(1)} %get-tuple-element.51.phi.origin, s32[6,256]{1,0:T(8,128)S(1)} %get-tuple-element.44.halo_code), custom_call_target="tpu_custom_call" | custom-call | flops 13107200 | bytes 1972224 | tf_op jit(solution)/shard_map/pallas_call | solution.py:592
  50.9 4.2 %shard_map.61 = (f32[2,512,128]{2,1,0:T(8,128)S(1)}, f32[8,64,128]{2,1,0:T(8,128)}, f32[24,128]{1,0:T(8,128)S(1)}, f32[24,128]{1,0:T(8,128)S(1)}) custom-call(f32[2,512,128]{2,1,0:T(8,128)S(1)} %get-tuple-element.57.phi, f32[2,512,128]{2,1,0:T(8,128)S(1)} %get-tuple-element.51.phi.origin, f32[6,2,64,128]{3,2,1,0:T(8,128)S(1)} %get-tuple-element.58.near, ...), custom_call_target="tpu_custom_call" | custom-call | flops 7864320 | bytes 2893824 | tf_op jit(solution)/shard_map/pallas_call | solution.py:592
  55.1 4.6 %all-to-all-start.3 = ((f32[8,64,128]{2,1,0:T(8,128)}), f32[8,64,128]{2,1,0:T(8,128)S(1)}, u32[]{:S(2)}, u32[]{:S(2)}) async-start(f32[8,64,128]{2,1,0:T(8,128)} %get-tuple-element.66), calls=%async_computation.3 | async-start | bytes 524288 | tf_op jit(solution)/shard_map/all_to_all | solution.py:609
  59.8 1.6 %collective-permute-start.6 = (f32[24,128]{1,0:T(8,128)S(1)}, f32[24,128]{1,0:T(8,128)S(1)}, u32[]{:S(2)}, u32[]{:S(2)}) collective-permute-start(f32[24,128]{1,0:T(8,128)S(1)} %get-tuple-element.67), channel_id=1, source_target_pairs={{0,8},{8,16},{16,24},{24,0},{1,9},{9,17},{17,25},{25,1},{2,10},{10... | collective-permute-start | bytes 36872 | tf_op jit(solution)/shard_map/ppermute | solution.py:610
  61.4 1.3 %collective-permute-start.7 = (f32[24,128]{1,0:T(8,128)S(1)}, f32[24,128]{1,0:T(8,128)S(1)}, u32[]{:S(2)}, u32[]{:S(2)}) collective-permute-start(f32[24,128]{1,0:T(8,128)S(1)} %get-tuple-element.68), channel_id=1, source_target_pairs={{8,0},{16,8},{24,16},{0,24},{9,1},{17,9},{25,17},{1,25},{10,2},{18... | collective-permute-start | bytes 36872 | tf_op jit(solution)/shard_map/ppermute | solution.py:611
  62.7 7.1 %shard_map.62 = (f32[6,2,192,128]{3,2,1,0:T(8,128)S(1)}, f32[3,2,256,128]{3,2,1,0:T(8,128)}) custom-call(f32[2,512,128]{2,1,0:T(8,128)S(1)} %get-tuple-element.63.phi, s32[6,256]{1,0:T(8,128)S(1)} %get-tuple-element.44.halo_code), custom_call_target="tpu_custom_call" | custom-call | flops 39321600 | bytes 2496512 | tf_op jit(solution)/shard_map/pallas_call | solution.py:592
  69.9 6.1 %shard_map.63 = (f32[2,512,128]{2,1,0:T(8,128)S(1)}, f32[8,24,128]{2,1,0:T(8,128)}, f32[8,128]{1,0:T(8,128)S(1)}, f32[8,128]{1,0:T(8,128)S(1)}) custom-call(f32[2,512,128]{2,1,0:T(8,128)S(1)} %get-tuple-element.63.phi, f32[6,2,192,128]{3,2,1,0:T(8,128)S(1)} %get-tuple-element.64.near, f32[3,2,256,128]{3,2,1,0:T(8,128)} %get-tuple-element.65.inner, ...), custom_call_target="tpu_custom_call" | custom-call | flops 39321600 | bytes 3942400 | tf_op jit(solution)/shard_map/pallas_call | solution.py:592
  76.0 5.1 %all-to-all-start.4 = ((f32[8,24,128]{2,1,0:T(8,128)}), f32[8,24,128]{2,1,0:T(8,128)S(1)}, u32[]{:S(2)}, u32[]{:S(2)}) async-start(f32[8,24,128]{2,1,0:T(8,128)} %get-tuple-element.72), calls=%async_computation.4 | async-start | bytes 196608 | tf_op jit(solution)/shard_map/all_to_all | solution.py:609
  81.1 0.7 collective-permute-start.8
  81.8 2.2 %collective-permute-start.9 = (f32[8,128]{1,0:T(8,128)S(1)}, f32[8,128]{1,0:T(8,128)S(1)}, u32[]{:S(2)}, u32[]{:S(2)}) collective-permute-start(f32[8,128]{1,0:T(8,128)S(1)} %get-tuple-element.74), channel_id=1, source_target_pairs={{8,0},{16,8},{24,16},{0,24},{9,1},{17,9},{25,17},{1,25},{10,2},{18... | collective-permute-start | bytes 12296 | tf_op jit(solution)/shard_map/ppermute | solution.py:611
  84.0 2.2 %shard_map.64 = (f32[6,2,64,128]{3,2,1,0:T(8,128)S(1)}, f32[2,512,128]{2,1,0:T(8,128)S(1)}) custom-call(f32[2,512,128]{2,1,0:T(8,128)S(1)} %get-tuple-element.69.phi.origin, f32[2,512,128]{2,1,0:T(8,128)S(1)} %get-tuple-element.69.phi.origin, s32[6,256]{1,0:T(8,128)S(1)} %get-tuple-element.44.halo_code), custom_call_target="tpu_custom_call" | custom-call | flops 13107200 | bytes 1972224 | tf_op jit(solution)/shard_map/pallas_call | solution.py:592
  86.3 1.1 %all-to-all-done.4.arrived = f32[8,24,128]{2,1,0:T(8,128)S(1)} async-done(((f32[8,24,128]{2,1,0:T(8,128)}), f32[8,24,128]{2,1,0:T(8,128)S(1)}, u32[]{:S(2)}, u32[]{:S(2)}) %all-to-all-start.4) | async-done | bytes 98336 | tf_op jit(solution)/shard_map/all_to_all | solution.py:609
  87.5 2.9 %shard_map.65 = (f32[2,512,128]{2,1,0:T(8,128)S(1)}, f32[8,24,128]{2,1,0:T(8,128)}, f32[8,128]{1,0:T(8,128)S(1)}, f32[8,128]{1,0:T(8,128)S(1)}) custom-call(f32[2,512,128]{2,1,0:T(8,128)S(1)} %get-tuple-element.69.phi.origin, f32[2,512,128]{2,1,0:T(8,128)S(1)} %get-tuple-element.69.phi.origin, f32[6,2,64,128]{3,2,1,0:T(8,128)S(1)} %get-tuple-element.70.near, ...), custom_call_target="tpu_custom_call" | custom-call | flops 7864320 | bytes 2713600 | tf_op jit(solution)/shard_map/pallas_call | solution.py:592
  90.3 4.0 %all-to-all-start.5 = ((f32[8,24,128]{2,1,0:T(8,128)}), f32[8,24,128]{2,1,0:T(8,128)S(1)}, u32[]{:S(2)}, u32[]{:S(2)}) async-start(f32[8,24,128]{2,1,0:T(8,128)} %get-tuple-element.78), calls=%async_computation.5 | async-start | bytes 196608 | tf_op jit(solution)/shard_map/all_to_all | solution.py:609
  94.3 1.6 %collective-permute-start.10 = (f32[8,128]{1,0:T(8,128)S(1)}, f32[8,128]{1,0:T(8,128)S(1)}, u32[]{:S(2)}, u32[]{:S(2)}) collective-permute-start(f32[8,128]{1,0:T(8,128)S(1)} %get-tuple-element.79), channel_id=1, source_target_pairs={{0,8},{8,16},{16,24},{24,0},{1,9},{9,17},{17,25},{25,1},{2,10},{10... | collective-permute-start | bytes 12296 | tf_op jit(solution)/shard_map/ppermute | solution.py:610
  95.9 1.3 %collective-permute-start.11 = (f32[8,128]{1,0:T(8,128)S(1)}, f32[8,128]{1,0:T(8,128)S(1)}, u32[]{:S(2)}, u32[]{:S(2)}) collective-permute-start(f32[8,128]{1,0:T(8,128)S(1)} %get-tuple-element.80), channel_id=1, source_target_pairs={{8,0},{16,8},{24,16},{0,24},{9,1},{17,9},{25,17},{1,25},{10,2},{18... | collective-permute-start | bytes 12296 | tf_op jit(solution)/shard_map/ppermute | solution.py:611
  97.2 2.2 %shard_map.66 = (f32[6,2,64,128]{3,2,1,0:T(8,128)S(1)}, f32[2,512,128]{2,1,0:T(8,128)S(1)}) custom-call(f32[2,512,128]{2,1,0:T(8,128)S(1)} %get-tuple-element.75.phi, f32[2,512,128]{2,1,0:T(8,128)S(1)} %get-tuple-element.69.phi.origin, s32[6,256]{1,0:T(8,128)S(1)} %get-tuple-element.44.halo_code), custom_call_target="tpu_custom_call" | custom-call | flops 13107200 | bytes 1972224 | tf_op jit(solution)/shard_map/pallas_call | solution.py:592
  99.5 1.1 %all-to-all-done.5.arrived = f32[8,24,128]{2,1,0:T(8,128)S(1)} async-done(((f32[8,24,128]{2,1,0:T(8,128)}), f32[8,24,128]{2,1,0:T(8,128)S(1)}, u32[]{:S(2)}, u32[]{:S(2)}) %all-to-all-start.5) | async-done | bytes 98336 | tf_op jit(solution)/shard_map/all_to_all | solution.py:609
  100.7 2.3 %shard_map.67 = f32[512,256]{1,0:T(8,128)} custom-call(f32[2,512,128]{2,1,0:T(8,128)S(1)} %get-tuple-element.75.phi, f32[2,512,128]{2,1,0:T(8,128)S(1)} %get-tuple-element.69.phi.origin, f32[6,2,64,128]{3,2,1,0:T(8,128)S(1)} %get-tuple-element.76.near, f32[2,512,128]{2,1,0:T(8,128)S(1)} %get-tuple-element.77.inner, ...), custom_call_target="tpu_custom_call" | custom-call | flops 7864320 | bytes 2607104 | tf_op jit(solution)/shard_map/pallas_call | solution.py:592
  (17 shorter events, 2.4 us)
Async XLA Ops:
  3.7 16.4 %all-to-all-start = ((f32[8,64,128]{2,1,0:T(8,128)}), f32[8,64,128]{2,1,0:T(8,128)S(1)}, u32[]{:S(2)}, u32[]{:S(2)}) async-start(f32[8,64,128]{2,1,0:T(8,128)} %get-tuple-element.47), calls=%async_computation | async-start | bytes 524288 | tf_op jit(solution)/shard_map/all_to_all | solution.py:609
  10.1 10.1 %collective-permute-start = (f32[24,128]{1,0:T(8,128)S(1)}, f32[24,128]{1,0:T(8,128)S(1)}, u32[]{:S(2)}, u32[]{:S(2)}) collective-permute-start(f32[24,128]{1,0:T(8,128)S(1)} %get-tuple-element.48), channel_id=1, source_target_pairs={{0,8},{8,16},{16,24},{24,0},{1,9},{9,17},{17,25},{25,1},{2,10},{10... | collective-permute-start | bytes 36872 | tf_op jit(solution)/shard_map/ppermute | solution.py:610
  11.6 8.6 %collective-permute-start.1 = (f32[24,128]{1,0:T(8,128)S(1)}, f32[24,128]{1,0:T(8,128)S(1)}, u32[]{:S(2)}, u32[]{:S(2)}) collective-permute-start(f32[24,128]{1,0:T(8,128)S(1)} %get-tuple-element.49), channel_id=1, source_target_pairs={{8,0},{16,8},{24,16},{0,24},{9,1},{17,9},{25,17},{1,25},{10,2},{18... | collective-permute-start | bytes 36872 | tf_op jit(solution)/shard_map/ppermute | solution.py:611
  26.3 11.5 %all-to-all-start.1 = ((f32[8,24,128]{2,1,0:T(8,128)}), f32[8,24,128]{2,1,0:T(8,128)S(1)}, u32[]{:S(2)}, u32[]{:S(2)}) async-start(f32[8,24,128]{2,1,0:T(8,128)} %get-tuple-element.54), calls=%async_computation.1 | async-start | bytes 196608 | tf_op jit(solution)/shard_map/all_to_all | solution.py:609
  31.4 5.2 %collective-permute-start.2 = (f32[8,128]{1,0:T(8,128)S(1)}, f32[8,128]{1,0:T(8,128)S(1)}, u32[]{:S(2)}, u32[]{:S(2)}) collective-permute-start(f32[8,128]{1,0:T(8,128)S(1)} %get-tuple-element.55), channel_id=1, source_target_pairs={{0,8},{8,16},{16,24},{24,0},{1,9},{9,17},{17,25},{25,1},{2,10},{10... | collective-permute-start | bytes 12296 | tf_op jit(solution)/shard_map/ppermute | solution.py:610
  32.0 4.6 %collective-permute-start.3 = (f32[8,128]{1,0:T(8,128)S(1)}, f32[8,128]{1,0:T(8,128)S(1)}, u32[]{:S(2)}, u32[]{:S(2)}) collective-permute-start(f32[8,128]{1,0:T(8,128)S(1)} %get-tuple-element.56), channel_id=1, source_target_pairs={{8,0},{16,8},{24,16},{0,24},{9,1},{17,9},{25,17},{1,25},{10,2},{18... | collective-permute-start | bytes 12296 | tf_op jit(solution)/shard_map/ppermute | solution.py:611
  40.6 10.3 %all-to-all-start.2 = ((f32[8,24,128]{2,1,0:T(8,128)}), f32[8,24,128]{2,1,0:T(8,128)S(1)}, u32[]{:S(2)}, u32[]{:S(2)}) async-start(f32[8,24,128]{2,1,0:T(8,128)} %get-tuple-element.60), calls=%async_computation.2 | async-start | bytes 196608 | tf_op jit(solution)/shard_map/all_to_all | solution.py:609
  44.6 5.2 %collective-permute-start.4 = (f32[8,128]{1,0:T(8,128)S(1)}, f32[8,128]{1,0:T(8,128)S(1)}, u32[]{:S(2)}, u32[]{:S(2)}) collective-permute-start(f32[8,128]{1,0:T(8,128)S(1)} %get-tuple-element.61), channel_id=1, source_target_pairs={{0,8},{8,16},{16,24},{24,0},{1,9},{9,17},{17,25},{25,1},{2,10},{10... | collective-permute-start | bytes 12296 | tf_op jit(solution)/shard_map/ppermute | solution.py:610
  46.9 3.6 %collective-permute-start.5 = (f32[8,128]{1,0:T(8,128)S(1)}, f32[8,128]{1,0:T(8,128)S(1)}, u32[]{:S(2)}, u32[]{:S(2)}) collective-permute-start(f32[8,128]{1,0:T(8,128)S(1)} %get-tuple-element.62), channel_id=1, source_target_pairs={{8,0},{16,8},{24,16},{0,24},{9,1},{17,9},{25,17},{1,25},{10,2},{18... | collective-permute-start | bytes 12296 | tf_op jit(solution)/shard_map/ppermute | solution.py:611
  55.1 14.7 %all-to-all-start.3 = ((f32[8,64,128]{2,1,0:T(8,128)}), f32[8,64,128]{2,1,0:T(8,128)S(1)}, u32[]{:S(2)}, u32[]{:S(2)}) async-start(f32[8,64,128]{2,1,0:T(8,128)} %get-tuple-element.66), calls=%async_computation.3 | async-start | bytes 524288 | tf_op jit(solution)/shard_map/all_to_all | solution.py:609
  59.8 10.1 %collective-permute-start.6 = (f32[24,128]{1,0:T(8,128)S(1)}, f32[24,128]{1,0:T(8,128)S(1)}, u32[]{:S(2)}, u32[]{:S(2)}) collective-permute-start(f32[24,128]{1,0:T(8,128)S(1)} %get-tuple-element.67), channel_id=1, source_target_pairs={{0,8},{8,16},{16,24},{24,0},{1,9},{9,17},{17,25},{25,1},{2,10},{10... | collective-permute-start | bytes 36872 | tf_op jit(solution)/shard_map/ppermute | solution.py:610
  61.4 8.5 %collective-permute-start.7 = (f32[24,128]{1,0:T(8,128)S(1)}, f32[24,128]{1,0:T(8,128)S(1)}, u32[]{:S(2)}, u32[]{:S(2)}) collective-permute-start(f32[24,128]{1,0:T(8,128)S(1)} %get-tuple-element.68), channel_id=1, source_target_pairs={{8,0},{16,8},{24,16},{0,24},{9,1},{17,9},{25,17},{1,25},{10,2},{18... | collective-permute-start | bytes 36872 | tf_op jit(solution)/shard_map/ppermute | solution.py:611
  76.0 11.5 %all-to-all-start.4 = ((f32[8,24,128]{2,1,0:T(8,128)}), f32[8,24,128]{2,1,0:T(8,128)S(1)}, u32[]{:S(2)}, u32[]{:S(2)}) async-start(f32[8,24,128]{2,1,0:T(8,128)} %get-tuple-element.72), calls=%async_computation.4 | async-start | bytes 196608 | tf_op jit(solution)/shard_map/all_to_all | solution.py:609
  81.1 5.2 %collective-permute-start.8 = (f32[8,128]{1,0:T(8,128)S(1)}, f32[8,128]{1,0:T(8,128)S(1)}, u32[]{:S(2)}, u32[]{:S(2)}) collective-permute-start(f32[8,128]{1,0:T(8,128)S(1)} %get-tuple-element.73), channel_id=1, source_target_pairs={{0,8},{8,16},{16,24},{24,0},{1,9},{9,17},{17,25},{25,1},{2,10},{10... | collective-permute-start | bytes 12296 | tf_op jit(solution)/shard_map/ppermute | solution.py:610
  81.8 4.5 %collective-permute-start.9 = (f32[8,128]{1,0:T(8,128)S(1)}, f32[8,128]{1,0:T(8,128)S(1)}, u32[]{:S(2)}, u32[]{:S(2)}) collective-permute-start(f32[8,128]{1,0:T(8,128)S(1)} %get-tuple-element.74), channel_id=1, source_target_pairs={{8,0},{16,8},{24,16},{0,24},{9,1},{17,9},{25,17},{1,25},{10,2},{18... | collective-permute-start | bytes 12296 | tf_op jit(solution)/shard_map/ppermute | solution.py:611
  90.3 10.3 %all-to-all-start.5 = ((f32[8,24,128]{2,1,0:T(8,128)}), f32[8,24,128]{2,1,0:T(8,128)S(1)}, u32[]{:S(2)}, u32[]{:S(2)}) async-start(f32[8,24,128]{2,1,0:T(8,128)} %get-tuple-element.78), calls=%async_computation.5 | async-start | bytes 196608 | tf_op jit(solution)/shard_map/all_to_all | solution.py:609
  94.3 5.2 %collective-permute-start.10 = (f32[8,128]{1,0:T(8,128)S(1)}, f32[8,128]{1,0:T(8,128)S(1)}, u32[]{:S(2)}, u32[]{:S(2)}) collective-permute-start(f32[8,128]{1,0:T(8,128)S(1)} %get-tuple-element.79), channel_id=1, source_target_pairs={{0,8},{8,16},{16,24},{24,0},{1,9},{9,17},{17,25},{25,1},{2,10},{10... | collective-permute-start | bytes 12296 | tf_op jit(solution)/shard_map/ppermute | solution.py:610
  95.9 3.6 %collective-permute-start.11 = (f32[8,128]{1,0:T(8,128)S(1)}, f32[8,128]{1,0:T(8,128)S(1)}, u32[]{:S(2)}, u32[]{:S(2)}) collective-permute-start(f32[8,128]{1,0:T(8,128)S(1)} %get-tuple-element.80), channel_id=1, source_target_pairs={{8,0},{16,8},{24,16},{0,24},{9,1},{17,9},{25,17},{1,25},{10,2},{18... | collective-permute-start | bytes 12296 | tf_op jit(solution)/shard_map/ppermute | solution.py:611

commit v8 on v7

--- a/solution.py
+++ b/solution.py
@@ -142,10 +142,10 @@
     lanes = lane_ids()
     w = plan.layers
 
-    @pl.loop(0, plan.groups // 4)
+    @pl.loop(0, plan.groups // 8)
     def _(q):
-        for v in range(4):
-            g = q * 4 + v
+        for v in range(8):
+            g = q * 8 + v
             sources = local_sources(plan, phi, ends, g)
             for t in range(plan.far_tiles):
                 code = jnp.broadcast_to(send_code[pl.ds(t, 1), :], (8, LANES))
@@ -390,10 +390,10 @@
 
 
 def relax(plan, phi, origin, near, inner, table, halo_code, part, moved, finish):
-    @pl.loop(0, 4)
+    @pl.loop(0, 2)
     def _(q):
-        for v in range(2):
-            i = q * 2 + v
+        for v in range(4):
+            i = q * 4 + v
             halo = far_values(plan, table, halo_code, near, (2, 3, 4, 5), i)
             for h in range(plan.halves):
                 for j in range(8):
@@ -413,23 +413,20 @@
                     facing = facing_of(origin[h, here, :])
                     part[h, here, :] += steepness(value, halo[side, h], beside, facing)
 
+    for j in range(8):
+        halo = far_values(plan, table, halo_code, near, (0, 1), j)
+        for h in range(plan.halves):
+            for side, i, other in ((0, 0, 1), (1, 7, 6)):
+                here = rows8(i * 64 + j * 8)
+                value = phi[h, here, :]
+                beside = phi[h, rows8(other * 64 + j * 8), :]
+                facing = facing_of(origin[h, here, :])
+                part[h, here, :] += steepness(value, halo[side, h], beside, facing)
+
     @pl.loop(0, 2)
     def _(q):
         for v in range(4):
-            j = q * 4 + v
-            halo = far_values(plan, table, halo_code, near, (0, 1), j)
-            for h in range(plan.halves):
-                for side, i, other in ((0, 0, 1), (1, 7, 6)):
-                    here = rows8(i * 64 + j * 8)
-                    value = phi[h, here, :]
-                    beside = phi[h, rows8(other * 64 + j * 8), :]
-                    facing = facing_of(origin[h, here, :])
-                    part[h, here, :] += steepness(value, halo[side, h], beside, facing)
-
-    @pl.loop(0, 4)
-    def _(q):
-        for v in range(2):
-            i = q * 2 + v
+            i = q * 4 + v
             for h in range(plan.halves):
                 for j in range(8):
                     here = rows8(i * 64 + j * 8)
@@ -504,11 +501,11 @@
 
 
 def near_thin_kernel(plan, phi, origin, halo_code, near, inner):
-    @pl.loop(0, plan.groups // 2)
+    @pl.loop(0, plan.groups // 4)
     def _(q):
-        for v in range(2):
-            pull_local(plan, phi, None, halo_code, near, q * 2 + v)
-            relax_inner(plan, phi, origin, inner, q * 2 + v)
+        for v in range(4):
+            pull_local(plan, phi, None, halo_code, near, q * 4 + v)
+            relax_inner(plan, phi, origin, inner, q * 4 + v)
 
 
 def near_wide_kernel(plan, phi, halo_code, near, *rest):
@@ -517,13 +514,14 @@
     fill_ends(plan, phi, ends)
     for axis in range(3):
 
-        @pl.loop(0, 8)
-        def _(q):
-            lines = [line_at(phi, h, axis, q) for h in range(plan.halves)]
-            pull_local(plan, phi, ends, halo_code, near, axis * 8 + q)
-            for h in range(plan.halves):
-                for m, value in enumerate(inner_values(lines[h])):
-                    kept[axis, h, rows8(q * 32 + m * 8), :] = value
+        @pl.loop(0, 4)
+        def _(pair):
+            for v in range(2):
+                q = pair * 2 + v
+                pull_local(plan, phi, ends, halo_code, near, axis * 8 + q)
+                for h in range(plan.halves):
+                    for m, value in enumerate(inner_values(line_at(phi, h, axis, q))):
+                        kept[axis, h, rows8(q * 32 + m * 8), :] = value
 
         copies[axis].start()
     for copy in copies:

time: 104 us -> 100 us (0.962)
  Pallas kernels: 51.5 us -> 47.5 us
  waiting for transfers between devices: 4.61 us -> 5.69 us
    pallas_call x13, Pallas kernels: 51.5 us -> 47.5 us  [call(): pl.pallas_call(kernel, out_shape=[pltpu.HBM(x.shape, x.dtype) if n in far...]
  transfers between devices with their start and end apart: 18 -> 18, of which waited for: 5 -> 7; matrix products, arithmetic and copies ran while one was open for 0% -> 0% of each run, Pallas kernels for 23% -> 22%
where the time goes in v8:
time: 100 us; the launch traced here: 99.7 us
  Pallas kernels  47.5 us (48%)
  starting transfers between devices  46.2 us (46%)
  waiting for transfers between devices  5.69 us (6%)
    pallas_call x13, Pallas kernels, call(): pl.pallas_call(kernel, out_shape=[pltpu.HBM(x.shape, x.dtype) if n in far...  47.5 us
    all_to_all x6, starting transfers between devices, exchange(): lax.all_to_all(outgoing, 'dev', split_axis=0, concat_axis=0, tiled=True)  28.6 us
    ppermute x6, starting transfers between devices, exchange(): after = lax.ppermute(low, 'group', down)  9.52 us
    ppermute x6, starting transfers between devices, exchange(): before = lax.ppermute(high, 'group', up)  8.03 us
    all_to_all x6, waiting for transfers between devices, exchange(): lax.all_to_all(outgoing, 'dev', split_axis=0, concat_axis=0, tiled=True)  4.71 us
  transfers between devices with their start and end apart: 18, of which 7 were waited for; matrix products, arithmetic and copies ran while one was open for 0% of the time, Pallas kernels for 22%

profile of v8, /device:TPU:0, one launch (start us, length us, event | category | flops | bytes accessed | tf_op | source)
XLA Modules:
  0.0 99.7 jit_solution(9438980880872802096)
XLA Ops:
  0.0 3.5 %shard_map.55 = (f32[2,512,128]{2,1,0:T(8,128)S(1)}, f32[8,64,128]{2,1,0:T(8,128)}, f32[24,128]{1,0:T(8,128)S(1)}, f32[24,128]{1,0:T(8,128)S(1)}, s32[8,128]{1,0:T(8,128)S(1)}, /*index=5*/s32[6,256]{1,0:T(8,128)S(1)}) custom-call(f32[512,256]{1,0:T(8,128)} %level_set.1, s32[8,40]{1,0:T(8,128)} %peer_slabs.1, s32[2,16]{1,0:T(2,128)} %region_slabs.1, ...), custom_call_target="tpu_custom_call" | custom-call | flops 1000000 | bytes 1353088 | tf_op jit(solution)/shard_map/pallas_call | solution.py:590
  3.5 6.3 %all-to-all-start = ((f32[8,64,128]{2,1,0:T(8,128)}), f32[8,64,128]{2,1,0:T(8,128)S(1)}, u32[]{:S(2)}, u32[]{:S(2)}) async-start(f32[8,64,128]{2,1,0:T(8,128)} %get-tuple-element.47), calls=%async_computation | async-start | bytes 524288 | tf_op jit(solution)/shard_map/all_to_all | solution.py:607
  9.8 1.5 %collective-permute-start = (f32[24,128]{1,0:T(8,128)S(1)}, f32[24,128]{1,0:T(8,128)S(1)}, u32[]{:S(2)}, u32[]{:S(2)}) collective-permute-start(f32[24,128]{1,0:T(8,128)S(1)} %get-tuple-element.48), channel_id=1, source_target_pairs={{0,8},{8,16},{16,24},{24,0},{1,9},{9,17},{17,25},{25,1},{2,10},{10... | collective-permute-start | bytes 36872 | tf_op jit(solution)/shard_map/ppermute | solution.py:608
  11.3 1.4 %collective-permute-start.1 = (f32[24,128]{1,0:T(8,128)S(1)}, f32[24,128]{1,0:T(8,128)S(1)}, u32[]{:S(2)}, u32[]{:S(2)}) collective-permute-start(f32[24,128]{1,0:T(8,128)S(1)} %get-tuple-element.49), channel_id=1, source_target_pairs={{8,0},{16,8},{24,16},{0,24},{9,1},{17,9},{25,17},{1,25},{10,2},{18... | collective-permute-start | bytes 36872 | tf_op jit(solution)/shard_map/ppermute | solution.py:609
  12.8 6.5 %shard_map.56 = (f32[6,2,192,128]{3,2,1,0:T(8,128)S(1)}, f32[3,2,256,128]{3,2,1,0:T(8,128)}) custom-call(f32[2,512,128]{2,1,0:T(8,128)S(1)} %get-tuple-element.43.phi, s32[6,256]{1,0:T(8,128)S(1)} %get-tuple-element.44.halo_code), custom_call_target="tpu_custom_call" | custom-call | flops 39321600 | bytes 2496512 | tf_op jit(solution)/shard_map/pallas_call | solution.py:590
  19.6 6.0 %shard_map.57 = (f32[2,512,128]{2,1,0:T(8,128)S(1)}, f32[8,24,128]{2,1,0:T(8,128)}, f32[8,128]{1,0:T(8,128)S(1)}, f32[8,128]{1,0:T(8,128)S(1)}) custom-call(f32[2,512,128]{2,1,0:T(8,128)S(1)} %get-tuple-element.43.phi, f32[6,2,192,128]{3,2,1,0:T(8,128)S(1)} %get-tuple-element.45.near, f32[3,2,256,128]{3,2,1,0:T(8,128)} %get-tuple-element.46.inner, ...), custom_call_target="tpu_custom_call" | custom-call | flops 39321600 | bytes 3942400 | tf_op jit(solution)/shard_map/pallas_call | solution.py:590
  25.6 4.8 %all-to-all-start.1 = ((f32[8,24,128]{2,1,0:T(8,128)}), f32[8,24,128]{2,1,0:T(8,128)S(1)}, u32[]{:S(2)}, u32[]{:S(2)}) async-start(f32[8,24,128]{2,1,0:T(8,128)} %get-tuple-element.54), calls=%async_computation.1 | async-start | bytes 196608 | tf_op jit(solution)/shard_map/all_to_all | solution.py:607
  31.0 2.3 %collective-permute-start.3 = (f32[8,128]{1,0:T(8,128)S(1)}, f32[8,128]{1,0:T(8,128)S(1)}, u32[]{:S(2)}, u32[]{:S(2)}) collective-permute-start(f32[8,128]{1,0:T(8,128)S(1)} %get-tuple-element.56), channel_id=1, source_target_pairs={{8,0},{16,8},{24,16},{0,24},{9,1},{17,9},{25,17},{1,25},{10,2},{18... | collective-permute-start | bytes 12296 | tf_op jit(solution)/shard_map/ppermute | solution.py:609
  33.3 2.1 %shard_map.58 = (f32[6,2,64,128]{3,2,1,0:T(8,128)S(1)}, f32[2,512,128]{2,1,0:T(8,128)S(1)}) custom-call(f32[2,512,128]{2,1,0:T(8,128)S(1)} %get-tuple-element.51.phi.origin, f32[2,512,128]{2,1,0:T(8,128)S(1)} %get-tuple-element.51.phi.origin, s32[6,256]{1,0:T(8,128)S(1)} %get-tuple-element.44.halo_code), custom_call_target="tpu_custom_call" | custom-call | flops 13107200 | bytes 1972224 | tf_op jit(solution)/shard_map/pallas_call | solution.py:590
  35.5 1.3 %all-to-all-done.1.arrived = f32[8,24,128]{2,1,0:T(8,128)S(1)} async-done(((f32[8,24,128]{2,1,0:T(8,128)}), f32[8,24,128]{2,1,0:T(8,128)S(1)}, u32[]{:S(2)}, u32[]{:S(2)}) %all-to-all-start.1) | async-done | bytes 98336 | tf_op jit(solution)/shard_map/all_to_all | solution.py:607
  36.7 2.4 %shard_map.59 = (f32[2,512,128]{2,1,0:T(8,128)S(1)}, f32[8,24,128]{2,1,0:T(8,128)}, f32[8,128]{1,0:T(8,128)S(1)}, f32[8,128]{1,0:T(8,128)S(1)}) custom-call(f32[2,512,128]{2,1,0:T(8,128)S(1)} %get-tuple-element.51.phi.origin, f32[2,512,128]{2,1,0:T(8,128)S(1)} %get-tuple-element.51.phi.origin, f32[6,2,64,128]{3,2,1,0:T(8,128)S(1)} %get-tuple-element.52.near, ...), custom_call_target="tpu_custom_call" | custom-call | flops 7864320 | bytes 2713600 | tf_op jit(solution)/shard_map/pallas_call | solution.py:590
  39.2 3.8 %all-to-all-start.2 = ((f32[8,24,128]{2,1,0:T(8,128)}), f32[8,24,128]{2,1,0:T(8,128)S(1)}, u32[]{:S(2)}, u32[]{:S(2)}) async-start(f32[8,24,128]{2,1,0:T(8,128)} %get-tuple-element.60), calls=%async_computation.2 | async-start | bytes 196608 | tf_op jit(solution)/shard_map/all_to_all | solution.py:607
  43.0 2.4 %collective-permute-start.4 = (f32[8,128]{1,0:T(8,128)S(1)}, f32[8,128]{1,0:T(8,128)S(1)}, u32[]{:S(2)}, u32[]{:S(2)}) collective-permute-start(f32[8,128]{1,0:T(8,128)S(1)} %get-tuple-element.61), channel_id=1, source_target_pairs={{0,8},{8,16},{16,24},{24,0},{1,9},{9,17},{17,25},{25,1},{2,10},{10... | collective-permute-start | bytes 12296 | tf_op jit(solution)/shard_map/ppermute | solution.py:608
  45.9 2.1 %shard_map.60 = (f32[6,2,64,128]{3,2,1,0:T(8,128)S(1)}, f32[2,512,128]{2,1,0:T(8,128)S(1)}) custom-call(f32[2,512,128]{2,1,0:T(8,128)S(1)} %get-tuple-element.57.phi, f32[2,512,128]{2,1,0:T(8,128)S(1)} %get-tuple-element.51.phi.origin, s32[6,256]{1,0:T(8,128)S(1)} %get-tuple-element.44.halo_code), custom_call_target="tpu_custom_call" | custom-call | flops 13107200 | bytes 1972224 | tf_op jit(solution)/shard_map/pallas_call | solution.py:590
  48.1 0.9 collective-permute-done.5.after
  49.4 3.7 %shard_map.61 = (f32[2,512,128]{2,1,0:T(8,128)S(1)}, f32[8,64,128]{2,1,0:T(8,128)}, f32[24,128]{1,0:T(8,128)S(1)}, f32[24,128]{1,0:T(8,128)S(1)}) custom-call(f32[2,512,128]{2,1,0:T(8,128)S(1)} %get-tuple-element.57.phi, f32[2,512,128]{2,1,0:T(8,128)S(1)} %get-tuple-element.51.phi.origin, f32[6,2,64,128]{3,2,1,0:T(8,128)S(1)} %get-tuple-element.58.near, ...), custom_call_target="tpu_custom_call" | custom-call | flops 7864320 | bytes 2893824 | tf_op jit(solution)/shard_map/pallas_call | solution.py:590
  53.0 4.8 %all-to-all-start.3 = ((f32[8,64,128]{2,1,0:T(8,128)}), f32[8,64,128]{2,1,0:T(8,128)S(1)}, u32[]{:S(2)}, u32[]{:S(2)}) async-start(f32[8,64,128]{2,1,0:T(8,128)} %get-tuple-element.66), calls=%async_computation.3 | async-start | bytes 524288 | tf_op jit(solution)/shard_map/all_to_all | solution.py:607
  57.8 1.5 %collective-permute-start.6 = (f32[24,128]{1,0:T(8,128)S(1)}, f32[24,128]{1,0:T(8,128)S(1)}, u32[]{:S(2)}, u32[]{:S(2)}) collective-permute-start(f32[24,128]{1,0:T(8,128)S(1)} %get-tuple-element.67), channel_id=1, source_target_pairs={{0,8},{8,16},{16,24},{24,0},{1,9},{9,17},{17,25},{25,1},{2,10},{10... | collective-permute-start | bytes 36872 | tf_op jit(solution)/shard_map/ppermute | solution.py:608
  59.3 1.4 %collective-permute-start.7 = (f32[24,128]{1,0:T(8,128)S(1)}, f32[24,128]{1,0:T(8,128)S(1)}, u32[]{:S(2)}, u32[]{:S(2)}) collective-permute-start(f32[24,128]{1,0:T(8,128)S(1)} %get-tuple-element.68), channel_id=1, source_target_pairs={{8,0},{16,8},{24,16},{0,24},{9,1},{17,9},{25,17},{1,25},{10,2},{18... | collective-permute-start | bytes 36872 | tf_op jit(solution)/shard_map/ppermute | solution.py:609
  60.7 6.5 %shard_map.62 = (f32[6,2,192,128]{3,2,1,0:T(8,128)S(1)}, f32[3,2,256,128]{3,2,1,0:T(8,128)}) custom-call(f32[2,512,128]{2,1,0:T(8,128)S(1)} %get-tuple-element.63.phi, s32[6,256]{1,0:T(8,128)S(1)} %get-tuple-element.44.halo_code), custom_call_target="tpu_custom_call" | custom-call | flops 39321600 | bytes 2496512 | tf_op jit(solution)/shard_map/pallas_call | solution.py:590
  67.5 6.0 %shard_map.63 = (f32[2,512,128]{2,1,0:T(8,128)S(1)}, f32[8,24,128]{2,1,0:T(8,128)}, f32[8,128]{1,0:T(8,128)S(1)}, f32[8,128]{1,0:T(8,128)S(1)}) custom-call(f32[2,512,128]{2,1,0:T(8,128)S(1)} %get-tuple-element.63.phi, f32[6,2,192,128]{3,2,1,0:T(8,128)S(1)} %get-tuple-element.64.near, f32[3,2,256,128]{3,2,1,0:T(8,128)} %get-tuple-element.65.inner, ...), custom_call_target="tpu_custom_call" | custom-call | flops 39321600 | bytes 3942400 | tf_op jit(solution)/shard_map/pallas_call | solution.py:590
  73.5 5.0 %all-to-all-start.4 = ((f32[8,24,128]{2,1,0:T(8,128)}), f32[8,24,128]{2,1,0:T(8,128)S(1)}, u32[]{:S(2)}, u32[]{:S(2)}) async-start(f32[8,24,128]{2,1,0:T(8,128)} %get-tuple-element.72), calls=%async_computation.4 | async-start | bytes 196608 | tf_op jit(solution)/shard_map/all_to_all | solution.py:607
  79.1 2.3 %collective-permute-start.9 = (f32[8,128]{1,0:T(8,128)S(1)}, f32[8,128]{1,0:T(8,128)S(1)}, u32[]{:S(2)}, u32[]{:S(2)}) collective-permute-start(f32[8,128]{1,0:T(8,128)S(1)} %get-tuple-element.74), channel_id=1, source_target_pairs={{8,0},{16,8},{24,16},{0,24},{9,1},{17,9},{25,17},{1,25},{10,2},{18... | collective-permute-start | bytes 12296 | tf_op jit(solution)/shard_map/ppermute | solution.py:609
  81.5 2.1 %shard_map.64 = (f32[6,2,64,128]{3,2,1,0:T(8,128)S(1)}, f32[2,512,128]{2,1,0:T(8,128)S(1)}) custom-call(f32[2,512,128]{2,1,0:T(8,128)S(1)} %get-tuple-element.69.phi.origin, f32[2,512,128]{2,1,0:T(8,128)S(1)} %get-tuple-element.69.phi.origin, s32[6,256]{1,0:T(8,128)S(1)} %get-tuple-element.44.halo_code), custom_call_target="tpu_custom_call" | custom-call | flops 13107200 | bytes 1972224 | tf_op jit(solution)/shard_map/pallas_call | solution.py:590
  83.6 1.3 %all-to-all-done.4.arrived = f32[8,24,128]{2,1,0:T(8,128)S(1)} async-done(((f32[8,24,128]{2,1,0:T(8,128)}), f32[8,24,128]{2,1,0:T(8,128)S(1)}, u32[]{:S(2)}, u32[]{:S(2)}) %all-to-all-start.4) | async-done | bytes 98336 | tf_op jit(solution)/shard_map/all_to_all | solution.py:607
  84.9 2.4 %shard_map.65 = (f32[2,512,128]{2,1,0:T(8,128)S(1)}, f32[8,24,128]{2,1,0:T(8,128)}, f32[8,128]{1,0:T(8,128)S(1)}, f32[8,128]{1,0:T(8,128)S(1)}) custom-call(f32[2,512,128]{2,1,0:T(8,128)S(1)} %get-tuple-element.69.phi.origin, f32[2,512,128]{2,1,0:T(8,128)S(1)} %get-tuple-element.69.phi.origin, f32[6,2,64,128]{3,2,1,0:T(8,128)S(1)} %get-tuple-element.70.near, ...), custom_call_target="tpu_custom_call" | custom-call | flops 7864320 | bytes 2713600 | tf_op jit(solution)/shard_map/pallas_call | solution.py:590
  87.3 3.8 %all-to-all-start.5 = ((f32[8,24,128]{2,1,0:T(8,128)}), f32[8,24,128]{2,1,0:T(8,128)S(1)}, u32[]{:S(2)}, u32[]{:S(2)}) async-start(f32[8,24,128]{2,1,0:T(8,128)} %get-tuple-element.78), calls=%async_computation.5 | async-start | bytes 196608 | tf_op jit(solution)/shard_map/all_to_all | solution.py:607
  91.2 1.5 %collective-permute-start.10 = (f32[8,128]{1,0:T(8,128)S(1)}, f32[8,128]{1,0:T(8,128)S(1)}, u32[]{:S(2)}, u32[]{:S(2)}) collective-permute-start(f32[8,128]{1,0:T(8,128)S(1)} %get-tuple-element.79), channel_id=1, source_target_pairs={{0,8},{8,16},{16,24},{24,0},{1,9},{9,17},{17,25},{25,1},{2,10},{10... | collective-permute-start | bytes 12296 | tf_op jit(solution)/shard_map/ppermute | solution.py:608
  92.6 1.4 %collective-permute-start.11 = (f32[8,128]{1,0:T(8,128)S(1)}, f32[8,128]{1,0:T(8,128)S(1)}, u32[]{:S(2)}, u32[]{:S(2)}) collective-permute-start(f32[8,128]{1,0:T(8,128)S(1)} %get-tuple-element.80), channel_id=1, source_target_pairs={{8,0},{16,8},{24,16},{0,24},{9,1},{17,9},{25,17},{1,25},{10,2},{18... | collective-permute-start | bytes 12296 | tf_op jit(solution)/shard_map/ppermute | solution.py:609
  94.1 2.1 %shard_map.66 = (f32[6,2,64,128]{3,2,1,0:T(8,128)S(1)}, f32[2,512,128]{2,1,0:T(8,128)S(1)}) custom-call(f32[2,512,128]{2,1,0:T(8,128)S(1)} %get-tuple-element.75.phi, f32[2,512,128]{2,1,0:T(8,128)S(1)} %get-tuple-element.69.phi.origin, s32[6,256]{1,0:T(8,128)S(1)} %get-tuple-element.44.halo_code), custom_call_target="tpu_custom_call" | custom-call | flops 13107200 | bytes 1972224 | tf_op jit(solution)/shard_map/pallas_call | solution.py:590
  96.3 1.3 %all-to-all-done.5.arrived = f32[8,24,128]{2,1,0:T(8,128)S(1)} async-done(((f32[8,24,128]{2,1,0:T(8,128)}), f32[8,24,128]{2,1,0:T(8,128)S(1)}, u32[]{:S(2)}, u32[]{:S(2)}) %all-to-all-start.5) | async-done | bytes 98336 | tf_op jit(solution)/shard_map/all_to_all | solution.py:607
  97.5 2.0 %shard_map.67 = f32[512,256]{1,0:T(8,128)} custom-call(f32[2,512,128]{2,1,0:T(8,128)S(1)} %get-tuple-element.75.phi, f32[2,512,128]{2,1,0:T(8,128)S(1)} %get-tuple-element.69.phi.origin, f32[6,2,64,128]{3,2,1,0:T(8,128)S(1)} %get-tuple-element.76.near, f32[2,512,128]{2,1,0:T(8,128)S(1)} %get-tuple-element.77.inner, ...), custom_call_target="tpu_custom_call" | custom-call | flops 7864320 | bytes 2607104 | tf_op jit(solution)/shard_map/pallas_call | solution.py:590
  (17 shorter events, 2.7 us)
Async XLA Ops:
  3.5 16.1 %all-to-all-start = ((f32[8,64,128]{2,1,0:T(8,128)}), f32[8,64,128]{2,1,0:T(8,128)S(1)}, u32[]{:S(2)}, u32[]{:S(2)}) async-start(f32[8,64,128]{2,1,0:T(8,128)} %get-tuple-element.47), calls=%async_computation | async-start | bytes 524288 | tf_op jit(solution)/shard_map/all_to_all | solution.py:607
  9.8 9.4 %collective-permute-start = (f32[24,128]{1,0:T(8,128)S(1)}, f32[24,128]{1,0:T(8,128)S(1)}, u32[]{:S(2)}, u32[]{:S(2)}) collective-permute-start(f32[24,128]{1,0:T(8,128)S(1)} %get-tuple-element.48), channel_id=1, source_target_pairs={{0,8},{8,16},{16,24},{24,0},{1,9},{9,17},{17,25},{25,1},{2,10},{10... | collective-permute-start | bytes 36872 | tf_op jit(solution)/shard_map/ppermute | solution.py:608
  11.3 7.9 %collective-permute-start.1 = (f32[24,128]{1,0:T(8,128)S(1)}, f32[24,128]{1,0:T(8,128)S(1)}, u32[]{:S(2)}, u32[]{:S(2)}) collective-permute-start(f32[24,128]{1,0:T(8,128)S(1)} %get-tuple-element.49), channel_id=1, source_target_pairs={{8,0},{16,8},{24,16},{0,24},{9,1},{17,9},{25,17},{1,25},{10,2},{18... | collective-permute-start | bytes 36872 | tf_op jit(solution)/shard_map/ppermute | solution.py:609
  25.6 11.2 %all-to-all-start.1 = ((f32[8,24,128]{2,1,0:T(8,128)}), f32[8,24,128]{2,1,0:T(8,128)S(1)}, u32[]{:S(2)}, u32[]{:S(2)}) async-start(f32[8,24,128]{2,1,0:T(8,128)} %get-tuple-element.54), calls=%async_computation.1 | async-start | bytes 196608 | tf_op jit(solution)/shard_map/all_to_all | solution.py:607
  30.4 5.1 %collective-permute-start.2 = (f32[8,128]{1,0:T(8,128)S(1)}, f32[8,128]{1,0:T(8,128)S(1)}, u32[]{:S(2)}, u32[]{:S(2)}) collective-permute-start(f32[8,128]{1,0:T(8,128)S(1)} %get-tuple-element.55), channel_id=1, source_target_pairs={{0,8},{8,16},{16,24},{24,0},{1,9},{9,17},{17,25},{25,1},{2,10},{10... | collective-permute-start | bytes 12296 | tf_op jit(solution)/shard_map/ppermute | solution.py:608
  31.0 4.5 %collective-permute-start.3 = (f32[8,128]{1,0:T(8,128)S(1)}, f32[8,128]{1,0:T(8,128)S(1)}, u32[]{:S(2)}, u32[]{:S(2)}) collective-permute-start(f32[8,128]{1,0:T(8,128)S(1)} %get-tuple-element.56), channel_id=1, source_target_pairs={{8,0},{16,8},{24,16},{0,24},{9,1},{17,9},{25,17},{1,25},{10,2},{18... | collective-permute-start | bytes 12296 | tf_op jit(solution)/shard_map/ppermute | solution.py:609
  39.2 10.2 %all-to-all-start.2 = ((f32[8,24,128]{2,1,0:T(8,128)}), f32[8,24,128]{2,1,0:T(8,128)S(1)}, u32[]{:S(2)}, u32[]{:S(2)}) async-start(f32[8,24,128]{2,1,0:T(8,128)} %get-tuple-element.60), calls=%async_computation.2 | async-start | bytes 196608 | tf_op jit(solution)/shard_map/all_to_all | solution.py:607
  43.0 5.1 %collective-permute-start.4 = (f32[8,128]{1,0:T(8,128)S(1)}, f32[8,128]{1,0:T(8,128)S(1)}, u32[]{:S(2)}, u32[]{:S(2)}) collective-permute-start(f32[8,128]{1,0:T(8,128)S(1)} %get-tuple-element.61), channel_id=1, source_target_pairs={{0,8},{8,16},{16,24},{24,0},{1,9},{9,17},{17,25},{25,1},{2,10},{10... | collective-permute-start | bytes 12296 | tf_op jit(solution)/shard_map/ppermute | solution.py:608
  45.4 3.6 %collective-permute-start.5 = (f32[8,128]{1,0:T(8,128)S(1)}, f32[8,128]{1,0:T(8,128)S(1)}, u32[]{:S(2)}, u32[]{:S(2)}) collective-permute-start(f32[8,128]{1,0:T(8,128)S(1)} %get-tuple-element.62), channel_id=1, source_target_pairs={{8,0},{16,8},{24,16},{0,24},{9,1},{17,9},{25,17},{1,25},{10,2},{18... | collective-permute-start | bytes 12296 | tf_op jit(solution)/shard_map/ppermute | solution.py:609
  53.0 14.5 %all-to-all-start.3 = ((f32[8,64,128]{2,1,0:T(8,128)}), f32[8,64,128]{2,1,0:T(8,128)S(1)}, u32[]{:S(2)}, u32[]{:S(2)}) async-start(f32[8,64,128]{2,1,0:T(8,128)} %get-tuple-element.66), calls=%async_computation.3 | async-start | bytes 524288 | tf_op jit(solution)/shard_map/all_to_all | solution.py:607
  57.8 9.4 %collective-permute-start.6 = (f32[24,128]{1,0:T(8,128)S(1)}, f32[24,128]{1,0:T(8,128)S(1)}, u32[]{:S(2)}, u32[]{:S(2)}) collective-permute-start(f32[24,128]{1,0:T(8,128)S(1)} %get-tuple-element.67), channel_id=1, source_target_pairs={{0,8},{8,16},{16,24},{24,0},{1,9},{9,17},{17,25},{25,1},{2,10},{10... | collective-permute-start | bytes 36872 | tf_op jit(solution)/shard_map/ppermute | solution.py:608
  59.3 8.0 %collective-permute-start.7 = (f32[24,128]{1,0:T(8,128)S(1)}, f32[24,128]{1,0:T(8,128)S(1)}, u32[]{:S(2)}, u32[]{:S(2)}) collective-permute-start(f32[24,128]{1,0:T(8,128)S(1)} %get-tuple-element.68), channel_id=1, source_target_pairs={{8,0},{16,8},{24,16},{0,24},{9,1},{17,9},{25,17},{1,25},{10,2},{18... | collective-permute-start | bytes 36872 | tf_op jit(solution)/shard_map/ppermute | solution.py:609
  73.5 11.3 %all-to-all-start.4 = ((f32[8,24,128]{2,1,0:T(8,128)}), f32[8,24,128]{2,1,0:T(8,128)S(1)}, u32[]{:S(2)}, u32[]{:S(2)}) async-start(f32[8,24,128]{2,1,0:T(8,128)} %get-tuple-element.72), calls=%async_computation.4 | async-start | bytes 196608 | tf_op jit(solution)/shard_map/all_to_all | solution.py:607
  78.5 5.1 %collective-permute-start.8 = (f32[8,128]{1,0:T(8,128)S(1)}, f32[8,128]{1,0:T(8,128)S(1)}, u32[]{:S(2)}, u32[]{:S(2)}) collective-permute-start(f32[8,128]{1,0:T(8,128)S(1)} %get-tuple-element.73), channel_id=1, source_target_pairs={{0,8},{8,16},{16,24},{24,0},{1,9},{9,17},{17,25},{25,1},{2,10},{10... | collective-permute-start | bytes 12296 | tf_op jit(solution)/shard_map/ppermute | solution.py:608
  79.1 4.5 %collective-permute-start.9 = (f32[8,128]{1,0:T(8,128)S(1)}, f32[8,128]{1,0:T(8,128)S(1)}, u32[]{:S(2)}, u32[]{:S(2)}) collective-permute-start(f32[8,128]{1,0:T(8,128)S(1)} %get-tuple-element.74), channel_id=1, source_target_pairs={{8,0},{16,8},{24,16},{0,24},{9,1},{17,9},{25,17},{1,25},{10,2},{18... | collective-permute-start | bytes 12296 | tf_op jit(solution)/shard_map/ppermute | solution.py:609
  87.3 10.2 %all-to-all-start.5 = ((f32[8,24,128]{2,1,0:T(8,128)}), f32[8,24,128]{2,1,0:T(8,128)S(1)}, u32[]{:S(2)}, u32[]{:S(2)}) async-start(f32[8,24,128]{2,1,0:T(8,128)} %get-tuple-element.78), calls=%async_computation.5 | async-start | bytes 196608 | tf_op jit(solution)/shard_map/all_to_all | solution.py:607
  91.2 5.1 %collective-permute-start.10 = (f32[8,128]{1,0:T(8,128)S(1)}, f32[8,128]{1,0:T(8,128)S(1)}, u32[]{:S(2)}, u32[]{:S(2)}) collective-permute-start(f32[8,128]{1,0:T(8,128)S(1)} %get-tuple-element.79), channel_id=1, source_target_pairs={{0,8},{8,16},{16,24},{24,0},{1,9},{9,17},{17,25},{25,1},{2,10},{10... | collective-permute-start | bytes 12296 | tf_op jit(solution)/shard_map/ppermute | solution.py:608
  92.6 3.6 %collective-permute-start.11 = (f32[8,128]{1,0:T(8,128)S(1)}, f32[8,128]{1,0:T(8,128)S(1)}, u32[]{:S(2)}, u32[]{:S(2)}) collective-permute-start(f32[8,128]{1,0:T(8,128)S(1)} %get-tuple-element.80), channel_id=1, source_target_pairs={{8,0},{16,8},{24,16},{0,24},{9,1},{17,9},{25,17},{1,25},{10,2},{18... | collective-permute-start | bytes 12296 | tf_op jit(solution)/shard_map/ppermute | solution.py:609

commit v9 on v8

--- a/solution.py
+++ b/solution.py
@@ -142,10 +142,12 @@
     lanes = lane_ids()
     w = plan.layers
 
-    @pl.loop(0, plan.groups // 8)
+    together = 8 if plan.layers == 1 else 12
+
+    @pl.loop(0, plan.groups // together)
     def _(q):
-        for v in range(8):
-            g = q * 8 + v
+        for v in range(together):
+            g = q * together + v
             sources = local_sources(plan, phi, ends, g)
             for t in range(plan.far_tiles):
                 code = jnp.broadcast_to(send_code[pl.ds(t, 1), :], (8, LANES))
@@ -349,13 +351,14 @@
     stage_columns(0, even)
     ready(1)
 
-    @pl.loop(0, 4)
+    @pl.loop(0, 2)
     def _(q):
-        j = 2 * q
-        stage_columns(j + 1, odd)
-        column(j, even)
-        stage_columns(jnp.minimum(j + 2, 7), even)
-        column(j + 1, odd)
+        j = 4 * q
+        for v in (0, 2):
+            stage_columns(j + v + 1, odd)
+            column(j + v, even)
+            stage_columns(jnp.minimum(j + v + 2, 7), even)
+            column(j + v + 1, odd)
 
 
 def steepness(value, low, high, facing):
@@ -390,10 +393,10 @@
 
 
 def relax(plan, phi, origin, near, inner, table, halo_code, part, moved, finish):
-    @pl.loop(0, 2)
+    @pl.loop(0, 1)
     def _(q):
-        for v in range(4):
-            i = q * 4 + v
+        for v in range(8):
+            i = q * 8 + v
             halo = far_values(plan, table, halo_code, near, (2, 3, 4, 5), i)
             for h in range(plan.halves):
                 for j in range(8):
@@ -423,10 +426,10 @@
                 facing = facing_of(origin[h, here, :])
                 part[h, here, :] += steepness(value, halo[side, h], beside, facing)
 
-    @pl.loop(0, 2)
+    @pl.loop(0, 1)
     def _(q):
-        for v in range(4):
-            i = q * 4 + v
+        for v in range(8):
+            i = q * 8 + v
             for h in range(plan.halves):
                 for j in range(8):
                     here = rows8(i * 64 + j * 8)
@@ -501,11 +504,9 @@
 
 
 def near_thin_kernel(plan, phi, origin, halo_code, near, inner):
-    @pl.loop(0, plan.groups // 4)
-    def _(q):
-        for v in range(4):
-            pull_local(plan, phi, None, halo_code, near, q * 4 + v)
-            relax_inner(plan, phi, origin, inner, q * 4 + v)
+    for g in range(plan.groups):
+        pull_local(plan, phi, None, halo_code, near, g)
+        relax_inner(plan, phi, origin, inner, g)
 
 
 def near_wide_kernel(plan, phi, halo_code, near, *rest):
@@ -514,10 +515,10 @@
     fill_ends(plan, phi, ends)
     for axis in range(3):
 
-        @pl.loop(0, 4)
-        def _(pair):
-            for v in range(2):
-                q = pair * 2 + v
+        @pl.loop(0, 2)
+        def _(four):
+            for v in range(4):
+                q = four * 4 + v
                 pull_local(plan, phi, ends, halo_code, near, axis * 8 + q)
                 for h in range(plan.halves):
                     for m, value in enumerate(inner_values(line_at(phi, h, axis, q))):

time: 100 us -> 98 us (0.980)
  Pallas kernels: 47.5 us -> 44.6 us
    pallas_call x13, Pallas kernels: 47.5 us -> 44.6 us  [call(): pl.pallas_call(kernel, out_shape=[pltpu.HBM(x.shape, x.dtype) if n in far...]
  transfers between devices with their start and end apart: 18 -> 18, of which waited for: 7 -> 8; matrix products, arithmetic and copies ran while one was open for 0% -> 0% of each run, Pallas kernels for 22% -> 21%
where the time goes in v9:
time: 98 us; the launch traced here: 97.3 us
  starting transfers between devices  46 us (47%)
  Pallas kernels  44.6 us (46%)
  waiting for transfers between devices  6.34 us (6%)
    pallas_call x13, Pallas kernels, call(): pl.pallas_call(kernel, out_shape=[pltpu.HBM(x.shape, x.dtype) if n in far...  44.6 us
    all_to_all x6, starting transfers between devices, exchange(): lax.all_to_all(outgoing, 'dev', split_axis=0, concat_axis=0, tiled=True)  28.4 us
    ppermute x6, starting transfers between devices, exchange(): after = lax.ppermute(low, 'group', down)  9.62 us
    ppermute x6, starting transfers between devices, exchange(): before = lax.ppermute(high, 'group', up)  7.93 us
    all_to_all x6, waiting for transfers between devices, exchange(): lax.all_to_all(outgoing, 'dev', split_axis=0, concat_axis=0, tiled=True)  4.65 us
  transfers between devices with their start and end apart: 18, of which 8 were waited for; matrix products, arithmetic and copies ran while one was open for 0% of the time, Pallas kernels for 21%

profile of v9, /device:TPU:0, one launch (start us, length us, event | category | flops | bytes accessed | tf_op | source)
XLA Modules:
  0.0 97.3 jit_solution(8469451844294758414)
XLA Ops:
  0.0 3.4 %shard_map.55 = (f32[2,512,128]{2,1,0:T(8,128)S(1)}, f32[8,64,128]{2,1,0:T(8,128)}, f32[24,128]{1,0:T(8,128)S(1)}, f32[24,128]{1,0:T(8,128)S(1)}, s32[8,128]{1,0:T(8,128)S(1)}, /*index=5*/s32[6,256]{1,0:T(8,128)S(1)}) custom-call(f32[512,256]{1,0:T(8,128)} %level_set.1, s32[8,40]{1,0:T(8,128)} %peer_slabs.1, s32[2,16]{1,0:T(2,128)} %region_slabs.1, ...), custom_call_target="tpu_custom_call" | custom-call | flops 1000000 | bytes 1353088 | tf_op jit(solution)/shard_map/pallas_call | solution.py:591
  3.4 6.3 %all-to-all-start = ((f32[8,64,128]{2,1,0:T(8,128)}), f32[8,64,128]{2,1,0:T(8,128)S(1)}, u32[]{:S(2)}, u32[]{:S(2)}) async-start(f32[8,64,128]{2,1,0:T(8,128)} %get-tuple-element.47), calls=%async_computation | async-start | bytes 524288 | tf_op jit(solution)/shard_map/all_to_all | solution.py:608
  9.8 1.5 %collective-permute-start = (f32[24,128]{1,0:T(8,128)S(1)}, f32[24,128]{1,0:T(8,128)S(1)}, u32[]{:S(2)}, u32[]{:S(2)}) collective-permute-start(f32[24,128]{1,0:T(8,128)S(1)} %get-tuple-element.48), channel_id=1, source_target_pairs={{0,8},{8,16},{16,24},{24,0},{1,9},{9,17},{17,25},{25,1},{2,10},{10... | collective-permute-start | bytes 36872 | tf_op jit(solution)/shard_map/ppermute | solution.py:609
  11.2 1.4 %collective-permute-start.1 = (f32[24,128]{1,0:T(8,128)S(1)}, f32[24,128]{1,0:T(8,128)S(1)}, u32[]{:S(2)}, u32[]{:S(2)}) collective-permute-start(f32[24,128]{1,0:T(8,128)S(1)} %get-tuple-element.49), channel_id=1, source_target_pairs={{8,0},{16,8},{24,16},{0,24},{9,1},{17,9},{25,17},{1,25},{10,2},{18... | collective-permute-start | bytes 36872 | tf_op jit(solution)/shard_map/ppermute | solution.py:610
  12.7 6.6 %shard_map.56 = (f32[6,2,192,128]{3,2,1,0:T(8,128)S(1)}, f32[3,2,256,128]{3,2,1,0:T(8,128)}) custom-call(f32[2,512,128]{2,1,0:T(8,128)S(1)} %get-tuple-element.43.phi, s32[6,256]{1,0:T(8,128)S(1)} %get-tuple-element.44.halo_code), custom_call_target="tpu_custom_call" | custom-call | flops 39321600 | bytes 2496512 | tf_op jit(solution)/shard_map/pallas_call | solution.py:591
  19.5 5.8 %shard_map.57 = (f32[2,512,128]{2,1,0:T(8,128)S(1)}, f32[8,24,128]{2,1,0:T(8,128)}, f32[8,128]{1,0:T(8,128)S(1)}, f32[8,128]{1,0:T(8,128)S(1)}) custom-call(f32[2,512,128]{2,1,0:T(8,128)S(1)} %get-tuple-element.43.phi, f32[6,2,192,128]{3,2,1,0:T(8,128)S(1)} %get-tuple-element.45.near, f32[3,2,256,128]{3,2,1,0:T(8,128)} %get-tuple-element.46.inner, ...), custom_call_target="tpu_custom_call" | custom-call | flops 39321600 | bytes 3942400 | tf_op jit(solution)/shard_map/pallas_call | solution.py:591
  25.4 4.9 %all-to-all-start.1 = ((f32[8,24,128]{2,1,0:T(8,128)}), f32[8,24,128]{2,1,0:T(8,128)S(1)}, u32[]{:S(2)}, u32[]{:S(2)}) async-start(f32[8,24,128]{2,1,0:T(8,128)} %get-tuple-element.54), calls=%async_computation.1 | async-start | bytes 196608 | tf_op jit(solution)/shard_map/all_to_all | solution.py:608
  30.8 2.3 %collective-permute-start.3 = (f32[8,128]{1,0:T(8,128)S(1)}, f32[8,128]{1,0:T(8,128)S(1)}, u32[]{:S(2)}, u32[]{:S(2)}) collective-permute-start(f32[8,128]{1,0:T(8,128)S(1)} %get-tuple-element.56), channel_id=1, source_target_pairs={{8,0},{16,8},{24,16},{0,24},{9,1},{17,9},{25,17},{1,25},{10,2},{18... | collective-permute-start | bytes 12296 | tf_op jit(solution)/shard_map/ppermute | solution.py:610
  33.2 1.9 %shard_map.58 = (f32[6,2,64,128]{3,2,1,0:T(8,128)S(1)}, f32[2,512,128]{2,1,0:T(8,128)S(1)}) custom-call(f32[2,512,128]{2,1,0:T(8,128)S(1)} %get-tuple-element.51.phi.origin, f32[2,512,128]{2,1,0:T(8,128)S(1)} %get-tuple-element.51.phi.origin, s32[6,256]{1,0:T(8,128)S(1)} %get-tuple-element.44.halo_code), custom_call_target="tpu_custom_call" | custom-call | flops 13107200 | bytes 1972224 | tf_op jit(solution)/shard_map/pallas_call | solution.py:591
  35.1 1.5 %all-to-all-done.1.arrived = f32[8,24,128]{2,1,0:T(8,128)S(1)} async-done(((f32[8,24,128]{2,1,0:T(8,128)}), f32[8,24,128]{2,1,0:T(8,128)S(1)}, u32[]{:S(2)}, u32[]{:S(2)}) %all-to-all-start.1) | async-done | bytes 98336 | tf_op jit(solution)/shard_map/all_to_all | solution.py:608
  36.6 2.0 %shard_map.59 = (f32[2,512,128]{2,1,0:T(8,128)S(1)}, f32[8,24,128]{2,1,0:T(8,128)}, f32[8,128]{1,0:T(8,128)S(1)}, f32[8,128]{1,0:T(8,128)S(1)}) custom-call(f32[2,512,128]{2,1,0:T(8,128)S(1)} %get-tuple-element.51.phi.origin, f32[2,512,128]{2,1,0:T(8,128)S(1)} %get-tuple-element.51.phi.origin, f32[6,2,64,128]{3,2,1,0:T(8,128)S(1)} %get-tuple-element.52.near, ...), custom_call_target="tpu_custom_call" | custom-call | flops 7864320 | bytes 2713600 | tf_op jit(solution)/shard_map/pallas_call | solution.py:591
  38.6 3.6 %all-to-all-start.2 = ((f32[8,24,128]{2,1,0:T(8,128)}), f32[8,24,128]{2,1,0:T(8,128)S(1)}, u32[]{:S(2)}, u32[]{:S(2)}) async-start(f32[8,24,128]{2,1,0:T(8,128)} %get-tuple-element.60), calls=%async_computation.2 | async-start | bytes 196608 | tf_op jit(solution)/shard_map/all_to_all | solution.py:608
  42.2 2.6 %collective-permute-start.4 = (f32[8,128]{1,0:T(8,128)S(1)}, f32[8,128]{1,0:T(8,128)S(1)}, u32[]{:S(2)}, u32[]{:S(2)}) collective-permute-start(f32[8,128]{1,0:T(8,128)S(1)} %get-tuple-element.61), channel_id=1, source_target_pairs={{0,8},{8,16},{16,24},{24,0},{1,9},{9,17},{17,25},{25,1},{2,10},{10... | collective-permute-start | bytes 12296 | tf_op jit(solution)/shard_map/ppermute | solution.py:609
  45.1 1.9 %shard_map.60 = (f32[6,2,64,128]{3,2,1,0:T(8,128)S(1)}, f32[2,512,128]{2,1,0:T(8,128)S(1)}) custom-call(f32[2,512,128]{2,1,0:T(8,128)S(1)} %get-tuple-element.57.phi, f32[2,512,128]{2,1,0:T(8,128)S(1)} %get-tuple-element.51.phi.origin, s32[6,256]{1,0:T(8,128)S(1)} %get-tuple-element.44.halo_code), custom_call_target="tpu_custom_call" | custom-call | flops 13107200 | bytes 1972224 | tf_op jit(solution)/shard_map/pallas_call | solution.py:591
  47.1 1.3 %collective-permute-done.5.after = f32[8,128]{1,0:T(8,128)S(1)} collective-permute-done((f32[8,128]{1,0:T(8,128)S(1)}, f32[8,128]{1,0:T(8,128)S(1)}, u32[]{:S(2)}, u32[]{:S(2)}) %collective-permute-start.5) | collective-permute-done | bytes 4128 | tf_op jit(solution)/shard_map/ppermute | solution.py:610
  48.5 3.2 %shard_map.61 = (f32[2,512,128]{2,1,0:T(8,128)S(1)}, f32[8,64,128]{2,1,0:T(8,128)}, f32[24,128]{1,0:T(8,128)S(1)}, f32[24,128]{1,0:T(8,128)S(1)}) custom-call(f32[2,512,128]{2,1,0:T(8,128)S(1)} %get-tuple-element.57.phi, f32[2,512,128]{2,1,0:T(8,128)S(1)} %get-tuple-element.51.phi.origin, f32[6,2,64,128]{3,2,1,0:T(8,128)S(1)} %get-tuple-element.58.near, ...), custom_call_target="tpu_custom_call" | custom-call | flops 7864320 | bytes 2893824 | tf_op jit(solution)/shard_map/pallas_call | solution.py:591
  51.7 5.0 %all-to-all-start.3 = ((f32[8,64,128]{2,1,0:T(8,128)}), f32[8,64,128]{2,1,0:T(8,128)S(1)}, u32[]{:S(2)}, u32[]{:S(2)}) async-start(f32[8,64,128]{2,1,0:T(8,128)} %get-tuple-element.66), calls=%async_computation.3 | async-start | bytes 524288 | tf_op jit(solution)/shard_map/all_to_all | solution.py:608
  56.7 1.3 %collective-permute-start.6 = (f32[24,128]{1,0:T(8,128)S(1)}, f32[24,128]{1,0:T(8,128)S(1)}, u32[]{:S(2)}, u32[]{:S(2)}) collective-permute-start(f32[24,128]{1,0:T(8,128)S(1)} %get-tuple-element.67), channel_id=1, source_target_pairs={{0,8},{8,16},{16,24},{24,0},{1,9},{9,17},{17,25},{25,1},{2,10},{10... | collective-permute-start | bytes 36872 | tf_op jit(solution)/shard_map/ppermute | solution.py:609
  58.0 1.6 %collective-permute-start.7 = (f32[24,128]{1,0:T(8,128)S(1)}, f32[24,128]{1,0:T(8,128)S(1)}, u32[]{:S(2)}, u32[]{:S(2)}) collective-permute-start(f32[24,128]{1,0:T(8,128)S(1)} %get-tuple-element.68), channel_id=1, source_target_pairs={{8,0},{16,8},{24,16},{0,24},{9,1},{17,9},{25,17},{1,25},{10,2},{18... | collective-permute-start | bytes 36872 | tf_op jit(solution)/shard_map/ppermute | solution.py:610
  59.6 6.6 %shard_map.62 = (f32[6,2,192,128]{3,2,1,0:T(8,128)S(1)}, f32[3,2,256,128]{3,2,1,0:T(8,128)}) custom-call(f32[2,512,128]{2,1,0:T(8,128)S(1)} %get-tuple-element.63.phi, s32[6,256]{1,0:T(8,128)S(1)} %get-tuple-element.44.halo_code), custom_call_target="tpu_custom_call" | custom-call | flops 39321600 | bytes 2496512 | tf_op jit(solution)/shard_map/pallas_call | solution.py:591
  66.4 5.8 %shard_map.63 = (f32[2,512,128]{2,1,0:T(8,128)S(1)}, f32[8,24,128]{2,1,0:T(8,128)}, f32[8,128]{1,0:T(8,128)S(1)}, f32[8,128]{1,0:T(8,128)S(1)}) custom-call(f32[2,512,128]{2,1,0:T(8,128)S(1)} %get-tuple-element.63.phi, f32[6,2,192,128]{3,2,1,0:T(8,128)S(1)} %get-tuple-element.64.near, f32[3,2,256,128]{3,2,1,0:T(8,128)} %get-tuple-element.65.inner, ...), custom_call_target="tpu_custom_call" | custom-call | flops 39321600 | bytes 3942400 | tf_op jit(solution)/shard_map/pallas_call | solution.py:591
  72.3 4.9 %all-to-all-start.4 = ((f32[8,24,128]{2,1,0:T(8,128)}), f32[8,24,128]{2,1,0:T(8,128)S(1)}, u32[]{:S(2)}, u32[]{:S(2)}) async-start(f32[8,24,128]{2,1,0:T(8,128)} %get-tuple-element.72), calls=%async_computation.4 | async-start | bytes 196608 | tf_op jit(solution)/shard_map/all_to_all | solution.py:608
  77.6 2.5 %collective-permute-start.9 = (f32[8,128]{1,0:T(8,128)S(1)}, f32[8,128]{1,0:T(8,128)S(1)}, u32[]{:S(2)}, u32[]{:S(2)}) collective-permute-start(f32[8,128]{1,0:T(8,128)S(1)} %get-tuple-element.74), channel_id=1, source_target_pairs={{8,0},{16,8},{24,16},{0,24},{9,1},{17,9},{25,17},{1,25},{10,2},{18... | collective-permute-start | bytes 12296 | tf_op jit(solution)/shard_map/ppermute | solution.py:610
  80.1 1.9 %shard_map.64 = (f32[6,2,64,128]{3,2,1,0:T(8,128)S(1)}, f32[2,512,128]{2,1,0:T(8,128)S(1)}) custom-call(f32[2,512,128]{2,1,0:T(8,128)S(1)} %get-tuple-element.69.phi.origin, f32[2,512,128]{2,1,0:T(8,128)S(1)} %get-tuple-element.69.phi.origin, s32[6,256]{1,0:T(8,128)S(1)} %get-tuple-element.44.halo_code), custom_call_target="tpu_custom_call" | custom-call | flops 13107200 | bytes 1972224 | tf_op jit(solution)/shard_map/pallas_call | solution.py:591
  82.1 1.5 %all-to-all-done.4.arrived = f32[8,24,128]{2,1,0:T(8,128)S(1)} async-done(((f32[8,24,128]{2,1,0:T(8,128)}), f32[8,24,128]{2,1,0:T(8,128)S(1)}, u32[]{:S(2)}, u32[]{:S(2)}) %all-to-all-start.4) | async-done | bytes 98336 | tf_op jit(solution)/shard_map/all_to_all | solution.py:608
  83.5 2.0 %shard_map.65 = (f32[2,512,128]{2,1,0:T(8,128)S(1)}, f32[8,24,128]{2,1,0:T(8,128)}, f32[8,128]{1,0:T(8,128)S(1)}, f32[8,128]{1,0:T(8,128)S(1)}) custom-call(f32[2,512,128]{2,1,0:T(8,128)S(1)} %get-tuple-element.69.phi.origin, f32[2,512,128]{2,1,0:T(8,128)S(1)} %get-tuple-element.69.phi.origin, f32[6,2,64,128]{3,2,1,0:T(8,128)S(1)} %get-tuple-element.70.near, ...), custom_call_target="tpu_custom_call" | custom-call | flops 7864320 | bytes 2713600 | tf_op jit(solution)/shard_map/pallas_call | solution.py:591
  85.5 3.6 %all-to-all-start.5 = ((f32[8,24,128]{2,1,0:T(8,128)}), f32[8,24,128]{2,1,0:T(8,128)S(1)}, u32[]{:S(2)}, u32[]{:S(2)}) async-start(f32[8,24,128]{2,1,0:T(8,128)} %get-tuple-element.78), calls=%async_computation.5 | async-start | bytes 196608 | tf_op jit(solution)/shard_map/all_to_all | solution.py:608
  89.1 1.6 %collective-permute-start.10 = (f32[8,128]{1,0:T(8,128)S(1)}, f32[8,128]{1,0:T(8,128)S(1)}, u32[]{:S(2)}, u32[]{:S(2)}) collective-permute-start(f32[8,128]{1,0:T(8,128)S(1)} %get-tuple-element.79), channel_id=1, source_target_pairs={{0,8},{8,16},{16,24},{24,0},{1,9},{9,17},{17,25},{25,1},{2,10},{10... | collective-permute-start | bytes 12296 | tf_op jit(solution)/shard_map/ppermute | solution.py:609
  90.7 1.3 %collective-permute-start.11 = (f32[8,128]{1,0:T(8,128)S(1)}, f32[8,128]{1,0:T(8,128)S(1)}, u32[]{:S(2)}, u32[]{:S(2)}) collective-permute-start(f32[8,128]{1,0:T(8,128)S(1)} %get-tuple-element.80), channel_id=1, source_target_pairs={{8,0},{16,8},{24,16},{0,24},{9,1},{17,9},{25,17},{1,25},{10,2},{18... | collective-permute-start | bytes 12296 | tf_op jit(solution)/shard_map/ppermute | solution.py:610
  92.0 1.9 %shard_map.66 = (f32[6,2,64,128]{3,2,1,0:T(8,128)S(1)}, f32[2,512,128]{2,1,0:T(8,128)S(1)}) custom-call(f32[2,512,128]{2,1,0:T(8,128)S(1)} %get-tuple-element.75.phi, f32[2,512,128]{2,1,0:T(8,128)S(1)} %get-tuple-element.69.phi.origin, s32[6,256]{1,0:T(8,128)S(1)} %get-tuple-element.44.halo_code), custom_call_target="tpu_custom_call" | custom-call | flops 13107200 | bytes 1972224 | tf_op jit(solution)/shard_map/pallas_call | solution.py:591
  94.3 1.1 %all-to-all-done.5.arrived = f32[8,24,128]{2,1,0:T(8,128)S(1)} async-done(((f32[8,24,128]{2,1,0:T(8,128)}), f32[8,24,128]{2,1,0:T(8,128)S(1)}, u32[]{:S(2)}, u32[]{:S(2)}) %all-to-all-start.5) | async-done | bytes 98336 | tf_op jit(solution)/shard_map/all_to_all | solution.py:608
  95.5 1.6 %shard_map.67 = f32[512,256]{1,0:T(8,128)} custom-call(f32[2,512,128]{2,1,0:T(8,128)S(1)} %get-tuple-element.75.phi, f32[2,512,128]{2,1,0:T(8,128)S(1)} %get-tuple-element.69.phi.origin, f32[6,2,64,128]{3,2,1,0:T(8,128)S(1)} %get-tuple-element.76.near, f32[2,512,128]{2,1,0:T(8,128)S(1)} %get-tuple-element.77.inner, ...), custom_call_target="tpu_custom_call" | custom-call | flops 7864320 | bytes 2607104 | tf_op jit(solution)/shard_map/pallas_call | solution.py:591
  (17 shorter events, 2.2 us)
Async XLA Ops:
  3.4 16.1 %all-to-all-start = ((f32[8,64,128]{2,1,0:T(8,128)}), f32[8,64,128]{2,1,0:T(8,128)S(1)}, u32[]{:S(2)}, u32[]{:S(2)}) async-start(f32[8,64,128]{2,1,0:T(8,128)} %get-tuple-element.47), calls=%async_computation | async-start | bytes 524288 | tf_op jit(solution)/shard_map/all_to_all | solution.py:608
  9.8 9.5 %collective-permute-start = (f32[24,128]{1,0:T(8,128)S(1)}, f32[24,128]{1,0:T(8,128)S(1)}, u32[]{:S(2)}, u32[]{:S(2)}) collective-permute-start(f32[24,128]{1,0:T(8,128)S(1)} %get-tuple-element.48), channel_id=1, source_target_pairs={{0,8},{8,16},{16,24},{24,0},{1,9},{9,17},{17,25},{25,1},{2,10},{10... | collective-permute-start | bytes 36872 | tf_op jit(solution)/shard_map/ppermute | solution.py:609
  11.2 8.0 %collective-permute-start.1 = (f32[24,128]{1,0:T(8,128)S(1)}, f32[24,128]{1,0:T(8,128)S(1)}, u32[]{:S(2)}, u32[]{:S(2)}) collective-permute-start(f32[24,128]{1,0:T(8,128)S(1)} %get-tuple-element.49), channel_id=1, source_target_pairs={{8,0},{16,8},{24,16},{0,24},{9,1},{17,9},{25,17},{1,25},{10,2},{18... | collective-permute-start | bytes 36872 | tf_op jit(solution)/shard_map/ppermute | solution.py:610
  25.4 11.2 %all-to-all-start.1 = ((f32[8,24,128]{2,1,0:T(8,128)}), f32[8,24,128]{2,1,0:T(8,128)S(1)}, u32[]{:S(2)}, u32[]{:S(2)}) async-start(f32[8,24,128]{2,1,0:T(8,128)} %get-tuple-element.54), calls=%async_computation.1 | async-start | bytes 196608 | tf_op jit(solution)/shard_map/all_to_all | solution.py:608
  30.3 4.9 %collective-permute-start.2 = (f32[8,128]{1,0:T(8,128)S(1)}, f32[8,128]{1,0:T(8,128)S(1)}, u32[]{:S(2)}, u32[]{:S(2)}) collective-permute-start(f32[8,128]{1,0:T(8,128)S(1)} %get-tuple-element.55), channel_id=1, source_target_pairs={{0,8},{8,16},{16,24},{24,0},{1,9},{9,17},{17,25},{25,1},{2,10},{10... | collective-permute-start | bytes 12296 | tf_op jit(solution)/shard_map/ppermute | solution.py:609
  30.8 4.3 %collective-permute-start.3 = (f32[8,128]{1,0:T(8,128)S(1)}, f32[8,128]{1,0:T(8,128)S(1)}, u32[]{:S(2)}, u32[]{:S(2)}) collective-permute-start(f32[8,128]{1,0:T(8,128)S(1)} %get-tuple-element.56), channel_id=1, source_target_pairs={{8,0},{16,8},{24,16},{0,24},{9,1},{17,9},{25,17},{1,25},{10,2},{18... | collective-permute-start | bytes 12296 | tf_op jit(solution)/shard_map/ppermute | solution.py:610
  38.6 10.0 %all-to-all-start.2 = ((f32[8,24,128]{2,1,0:T(8,128)}), f32[8,24,128]{2,1,0:T(8,128)S(1)}, u32[]{:S(2)}, u32[]{:S(2)}) async-start(f32[8,24,128]{2,1,0:T(8,128)} %get-tuple-element.60), calls=%async_computation.2 | async-start | bytes 196608 | tf_op jit(solution)/shard_map/all_to_all | solution.py:608
  42.2 4.9 %collective-permute-start.4 = (f32[8,128]{1,0:T(8,128)S(1)}, f32[8,128]{1,0:T(8,128)S(1)}, u32[]{:S(2)}, u32[]{:S(2)}) collective-permute-start(f32[8,128]{1,0:T(8,128)S(1)} %get-tuple-element.61), channel_id=1, source_target_pairs={{0,8},{8,16},{16,24},{24,0},{1,9},{9,17},{17,25},{25,1},{2,10},{10... | collective-permute-start | bytes 12296 | tf_op jit(solution)/shard_map/ppermute | solution.py:609
  44.8 3.6 %collective-permute-start.5 = (f32[8,128]{1,0:T(8,128)S(1)}, f32[8,128]{1,0:T(8,128)S(1)}, u32[]{:S(2)}, u32[]{:S(2)}) collective-permute-start(f32[8,128]{1,0:T(8,128)S(1)} %get-tuple-element.62), channel_id=1, source_target_pairs={{8,0},{16,8},{24,16},{0,24},{9,1},{17,9},{25,17},{1,25},{10,2},{18... | collective-permute-start | bytes 12296 | tf_op jit(solution)/shard_map/ppermute | solution.py:610
  51.7 14.7 %all-to-all-start.3 = ((f32[8,64,128]{2,1,0:T(8,128)}), f32[8,64,128]{2,1,0:T(8,128)S(1)}, u32[]{:S(2)}, u32[]{:S(2)}) async-start(f32[8,64,128]{2,1,0:T(8,128)} %get-tuple-element.66), calls=%async_computation.3 | async-start | bytes 524288 | tf_op jit(solution)/shard_map/all_to_all | solution.py:608
  56.7 9.5 %collective-permute-start.6 = (f32[24,128]{1,0:T(8,128)S(1)}, f32[24,128]{1,0:T(8,128)S(1)}, u32[]{:S(2)}, u32[]{:S(2)}) collective-permute-start(f32[24,128]{1,0:T(8,128)S(1)} %get-tuple-element.67), channel_id=1, source_target_pairs={{0,8},{8,16},{16,24},{24,0},{1,9},{9,17},{17,25},{25,1},{2,10},{10... | collective-permute-start | bytes 36872 | tf_op jit(solution)/shard_map/ppermute | solution.py:609
  58.0 8.2 %collective-permute-start.7 = (f32[24,128]{1,0:T(8,128)S(1)}, f32[24,128]{1,0:T(8,128)S(1)}, u32[]{:S(2)}, u32[]{:S(2)}) collective-permute-start(f32[24,128]{1,0:T(8,128)S(1)} %get-tuple-element.68), channel_id=1, source_target_pairs={{8,0},{16,8},{24,16},{0,24},{9,1},{17,9},{25,17},{1,25},{10,2},{18... | collective-permute-start | bytes 36872 | tf_op jit(solution)/shard_map/ppermute | solution.py:610
  72.3 11.2 %all-to-all-start.4 = ((f32[8,24,128]{2,1,0:T(8,128)}), f32[8,24,128]{2,1,0:T(8,128)S(1)}, u32[]{:S(2)}, u32[]{:S(2)}) async-start(f32[8,24,128]{2,1,0:T(8,128)} %get-tuple-element.72), calls=%async_computation.4 | async-start | bytes 196608 | tf_op jit(solution)/shard_map/all_to_all | solution.py:608
  77.2 4.9 %collective-permute-start.8 = (f32[8,128]{1,0:T(8,128)S(1)}, f32[8,128]{1,0:T(8,128)S(1)}, u32[]{:S(2)}, u32[]{:S(2)}) collective-permute-start(f32[8,128]{1,0:T(8,128)S(1)} %get-tuple-element.73), channel_id=1, source_target_pairs={{0,8},{8,16},{16,24},{24,0},{1,9},{9,17},{17,25},{25,1},{2,10},{10... | collective-permute-start | bytes 12296 | tf_op jit(solution)/shard_map/ppermute | solution.py:609
  77.6 4.5 %collective-permute-start.9 = (f32[8,128]{1,0:T(8,128)S(1)}, f32[8,128]{1,0:T(8,128)S(1)}, u32[]{:S(2)}, u32[]{:S(2)}) collective-permute-start(f32[8,128]{1,0:T(8,128)S(1)} %get-tuple-element.74), channel_id=1, source_target_pairs={{8,0},{16,8},{24,16},{0,24},{9,1},{17,9},{25,17},{1,25},{10,2},{18... | collective-permute-start | bytes 12296 | tf_op jit(solution)/shard_map/ppermute | solution.py:610
  85.5 10.0 %all-to-all-start.5 = ((f32[8,24,128]{2,1,0:T(8,128)}), f32[8,24,128]{2,1,0:T(8,128)S(1)}, u32[]{:S(2)}, u32[]{:S(2)}) async-start(f32[8,24,128]{2,1,0:T(8,128)} %get-tuple-element.78), calls=%async_computation.5 | async-start | bytes 196608 | tf_op jit(solution)/shard_map/all_to_all | solution.py:608
  89.1 4.9 %collective-permute-start.10 = (f32[8,128]{1,0:T(8,128)S(1)}, f32[8,128]{1,0:T(8,128)S(1)}, u32[]{:S(2)}, u32[]{:S(2)}) collective-permute-start(f32[8,128]{1,0:T(8,128)S(1)} %get-tuple-element.79), channel_id=1, source_target_pairs={{0,8},{8,16},{16,24},{24,0},{1,9},{9,17},{17,25},{25,1},{2,10},{10... | collective-permute-start | bytes 12296 | tf_op jit(solution)/shard_map/ppermute | solution.py:609
  90.7 3.6 %collective-permute-start.11 = (f32[8,128]{1,0:T(8,128)S(1)}, f32[8,128]{1,0:T(8,128)S(1)}, u32[]{:S(2)}, u32[]{:S(2)}) collective-permute-start(f32[8,128]{1,0:T(8,128)S(1)} %get-tuple-element.80), channel_id=1, source_target_pairs={{8,0},{16,8},{24,16},{0,24},{9,1},{17,9},{25,17},{1,25},{10,2},{18... | collective-permute-start | bytes 12296 | tf_op jit(solution)/shard_map/ppermute | solution.py:610

commit v10 on v9

--- a/solution.py
+++ b/solution.py
@@ -231,9 +231,21 @@
     return found
 
 
-def pull_far(plan, table, halo_code, near, halos, sides, g, row):
-    for (s, h), value in far_values(plan, table, halo_code, near, sides, g).items():
-        halos[s - sides[0], h, rows8(row * 8), :] = value
+def pull_far(plan, table, halo_code, near, halos, sides, groups):
+    start = plan.local_tiles * LANES
+    sources = [
+        [table[t, rows8(g * 8), :] for t in range(plan.far_tiles)] for g in groups
+    ]
+    for s in sides:
+        for h in range(plan.halves):
+            code = jnp.broadcast_to(halo_code[pl.ds(s, 1), half(h)], (8, LANES))
+            local = code < start
+            lane = (code - start) & (LANES - 1)
+            masks = bits_of((code - start) >> 7, plan.far_tiles)
+            for row, g in enumerate(groups):
+                far = pick_tile(Taken(sources[row], lane), masks)
+                here = near[s, h, rows8(g * 8), :]
+                halos[s - sides[0], h, pl.ds(row * 8, 8), :] = jnp.where(local, here, far)
 
 
 def weno_windows(q):
@@ -300,12 +312,12 @@
     w = plan.layers
 
     def stage_planes(i, target):
-        for l in range(w):
-            pull_far(plan, table, halo_code, near, target, (2, 3, 4, 5), i * w + l, l)
+        groups = [i * w + l for l in range(w)]
+        pull_far(plan, table, halo_code, near, target, (2, 3, 4, 5), groups)
 
     def stage_columns(j, target):
-        for l in range(w):
-            pull_far(plan, table, halo_code, near, target, (0, 1), l * 8 + j, l)
+        groups = [l * 8 + j for l in range(w)]
+        pull_far(plan, table, halo_code, near, target, (0, 1), groups)
 
     def stacked(source, side, h):
         return [source[side, h, pl.ds(l * 8, 8), :] for l in range(w)]
@@ -515,10 +527,10 @@
     fill_ends(plan, phi, ends)
     for axis in range(3):
 
-        @pl.loop(0, 2)
-        def _(four):
-            for v in range(4):
-                q = four * 4 + v
+        @pl.loop(0, 4)
+        def _(pair):
+            for v in range(2):
+                q = pair * 2 + v
                 pull_local(plan, phi, ends, halo_code, near, axis * 8 + q)
                 for h in range(plan.halves):
                     for m, value in enumerate(inner_values(line_at(phi, h, axis, q))):

time: 98 us -> 97.3 us (level)
  no operation moved by 1% of the time
where the time goes in v10:
time: 97.3 us; the launch traced here: 96.5 us
  starting transfers between devices  45.8 us (47%)
  Pallas kernels  43.9 us (45%)
  waiting for transfers between devices  6.49 us (7%)
    pallas_call x13, Pallas kernels, call(): pl.pallas_call(kernel, out_shape=[pltpu.HBM(x.shape, x.dtype) if n in far...  43.9 us
    all_to_all x6, starting transfers between devices, exchange(): lax.all_to_all(outgoing, 'dev', split_axis=0, concat_axis=0, tiled=True)  28.3 us
    ppermute x6, starting transfers between devices, exchange(): after = lax.ppermute(low, 'group', down)  9.62 us
    ppermute x6, starting transfers between devices, exchange(): before = lax.ppermute(high, 'group', up)  7.93 us
    all_to_all x6, waiting for transfers between devices, exchange(): lax.all_to_all(outgoing, 'dev', split_axis=0, concat_axis=0, tiled=True)  4.8 us
  transfers between devices with their start and end apart: 18, of which 8 were waited for; matrix products, arithmetic and copies ran while one was open for 0% of the time, Pallas kernels for 21%

profile of v10, /device:TPU:0, one launch (start us, length us, event | category | flops | bytes accessed | tf_op | source)
XLA Modules:
  0.0 96.5 jit_solution(9354297870422657466)
XLA Ops:
  0.0 3.4 %shard_map.55 = (f32[2,512,128]{2,1,0:T(8,128)S(1)}, f32[8,64,128]{2,1,0:T(8,128)}, f32[24,128]{1,0:T(8,128)S(1)}, f32[24,128]{1,0:T(8,128)S(1)}, s32[8,128]{1,0:T(8,128)S(1)}, /*index=5*/s32[6,256]{1,0:T(8,128)S(1)}) custom-call(f32[512,256]{1,0:T(8,128)} %level_set.1, s32[8,40]{1,0:T(8,128)} %peer_slabs.1, s32[2,16]{1,0:T(2,128)} %region_slabs.1, ...), custom_call_target="tpu_custom_call" | custom-call | flops 1000000 | bytes 1353088 | tf_op jit(solution)/shard_map/pallas_call | solution.py:603
  3.4 6.3 %all-to-all-start = ((f32[8,64,128]{2,1,0:T(8,128)}), f32[8,64,128]{2,1,0:T(8,128)S(1)}, u32[]{:S(2)}, u32[]{:S(2)}) async-start(f32[8,64,128]{2,1,0:T(8,128)} %get-tuple-element.47), calls=%async_computation | async-start | bytes 524288 | tf_op jit(solution)/shard_map/all_to_all | solution.py:620
  9.8 1.5 %collective-permute-start = (f32[24,128]{1,0:T(8,128)S(1)}, f32[24,128]{1,0:T(8,128)S(1)}, u32[]{:S(2)}, u32[]{:S(2)}) collective-permute-start(f32[24,128]{1,0:T(8,128)S(1)} %get-tuple-element.48), channel_id=1, source_target_pairs={{0,8},{8,16},{16,24},{24,0},{1,9},{9,17},{17,25},{25,1},{2,10},{10... | collective-permute-start | bytes 36872 | tf_op jit(solution)/shard_map/ppermute | solution.py:621
  11.2 1.4 %collective-permute-start.1 = (f32[24,128]{1,0:T(8,128)S(1)}, f32[24,128]{1,0:T(8,128)S(1)}, u32[]{:S(2)}, u32[]{:S(2)}) collective-permute-start(f32[24,128]{1,0:T(8,128)S(1)} %get-tuple-element.49), channel_id=1, source_target_pairs={{8,0},{16,8},{24,16},{0,24},{9,1},{17,9},{25,17},{1,25},{10,2},{18... | collective-permute-start | bytes 36872 | tf_op jit(solution)/shard_map/ppermute | solution.py:622
  12.7 6.5 %shard_map.56 = (f32[6,2,192,128]{3,2,1,0:T(8,128)S(1)}, f32[3,2,256,128]{3,2,1,0:T(8,128)}) custom-call(f32[2,512,128]{2,1,0:T(8,128)S(1)} %get-tuple-element.43.phi, s32[6,256]{1,0:T(8,128)S(1)} %get-tuple-element.44.halo_code), custom_call_target="tpu_custom_call" | custom-call | flops 39321600 | bytes 2496512 | tf_op jit(solution)/shard_map/pallas_call | solution.py:603
  19.5 5.6 %shard_map.57 = (f32[2,512,128]{2,1,0:T(8,128)S(1)}, f32[8,24,128]{2,1,0:T(8,128)}, f32[8,128]{1,0:T(8,128)S(1)}, f32[8,128]{1,0:T(8,128)S(1)}) custom-call(f32[2,512,128]{2,1,0:T(8,128)S(1)} %get-tuple-element.43.phi, f32[6,2,192,128]{3,2,1,0:T(8,128)S(1)} %get-tuple-element.45.near, f32[3,2,256,128]{3,2,1,0:T(8,128)} %get-tuple-element.46.inner, ...), custom_call_target="tpu_custom_call" | custom-call | flops 39321600 | bytes 3942400 | tf_op jit(solution)/shard_map/pallas_call | solution.py:603
  25.1 4.8 %all-to-all-start.1 = ((f32[8,24,128]{2,1,0:T(8,128)}), f32[8,24,128]{2,1,0:T(8,128)S(1)}, u32[]{:S(2)}, u32[]{:S(2)}) async-start(f32[8,24,128]{2,1,0:T(8,128)} %get-tuple-element.54), calls=%async_computation.1 | async-start | bytes 196608 | tf_op jit(solution)/shard_map/all_to_all | solution.py:620
  30.5 2.3 %collective-permute-start.3 = (f32[8,128]{1,0:T(8,128)S(1)}, f32[8,128]{1,0:T(8,128)S(1)}, u32[]{:S(2)}, u32[]{:S(2)}) collective-permute-start(f32[8,128]{1,0:T(8,128)S(1)} %get-tuple-element.56), channel_id=1, source_target_pairs={{8,0},{16,8},{24,16},{0,24},{9,1},{17,9},{25,17},{1,25},{10,2},{18... | collective-permute-start | bytes 12296 | tf_op jit(solution)/shard_map/ppermute | solution.py:622
  32.8 1.9 %shard_map.58 = (f32[6,2,64,128]{3,2,1,0:T(8,128)S(1)}, f32[2,512,128]{2,1,0:T(8,128)S(1)}) custom-call(f32[2,512,128]{2,1,0:T(8,128)S(1)} %get-tuple-element.51.phi.origin, f32[2,512,128]{2,1,0:T(8,128)S(1)} %get-tuple-element.51.phi.origin, s32[6,256]{1,0:T(8,128)S(1)} %get-tuple-element.44.halo_code), custom_call_target="tpu_custom_call" | custom-call | flops 13107200 | bytes 1972224 | tf_op jit(solution)/shard_map/pallas_call | solution.py:603
  34.8 1.5 %all-to-all-done.1.arrived = f32[8,24,128]{2,1,0:T(8,128)S(1)} async-done(((f32[8,24,128]{2,1,0:T(8,128)}), f32[8,24,128]{2,1,0:T(8,128)S(1)}, u32[]{:S(2)}, u32[]{:S(2)}) %all-to-all-start.1) | async-done | bytes 98336 | tf_op jit(solution)/shard_map/all_to_all | solution.py:620
  36.3 2.0 %shard_map.59 = (f32[2,512,128]{2,1,0:T(8,128)S(1)}, f32[8,24,128]{2,1,0:T(8,128)}, f32[8,128]{1,0:T(8,128)S(1)}, f32[8,128]{1,0:T(8,128)S(1)}) custom-call(f32[2,512,128]{2,1,0:T(8,128)S(1)} %get-tuple-element.51.phi.origin, f32[2,512,128]{2,1,0:T(8,128)S(1)} %get-tuple-element.51.phi.origin, f32[6,2,64,128]{3,2,1,0:T(8,128)S(1)} %get-tuple-element.52.near, ...), custom_call_target="tpu_custom_call" | custom-call | flops 7864320 | bytes 2713600 | tf_op jit(solution)/shard_map/pallas_call | solution.py:603
  38.2 3.6 %all-to-all-start.2 = ((f32[8,24,128]{2,1,0:T(8,128)}), f32[8,24,128]{2,1,0:T(8,128)S(1)}, u32[]{:S(2)}, u32[]{:S(2)}) async-start(f32[8,24,128]{2,1,0:T(8,128)} %get-tuple-element.60), calls=%async_computation.2 | async-start | bytes 196608 | tf_op jit(solution)/shard_map/all_to_all | solution.py:620
  41.9 2.6 %collective-permute-start.4 = (f32[8,128]{1,0:T(8,128)S(1)}, f32[8,128]{1,0:T(8,128)S(1)}, u32[]{:S(2)}, u32[]{:S(2)}) collective-permute-start(f32[8,128]{1,0:T(8,128)S(1)} %get-tuple-element.61), channel_id=1, source_target_pairs={{0,8},{8,16},{16,24},{24,0},{1,9},{9,17},{17,25},{25,1},{2,10},{10... | collective-permute-start | bytes 12296 | tf_op jit(solution)/shard_map/ppermute | solution.py:621
  44.8 1.9 %shard_map.60 = (f32[6,2,64,128]{3,2,1,0:T(8,128)S(1)}, f32[2,512,128]{2,1,0:T(8,128)S(1)}) custom-call(f32[2,512,128]{2,1,0:T(8,128)S(1)} %get-tuple-element.57.phi, f32[2,512,128]{2,1,0:T(8,128)S(1)} %get-tuple-element.51.phi.origin, s32[6,256]{1,0:T(8,128)S(1)} %get-tuple-element.44.halo_code), custom_call_target="tpu_custom_call" | custom-call | flops 13107200 | bytes 1972224 | tf_op jit(solution)/shard_map/pallas_call | solution.py:603
  46.7 1.3 %collective-permute-done.5.after = f32[8,128]{1,0:T(8,128)S(1)} collective-permute-done((f32[8,128]{1,0:T(8,128)S(1)}, f32[8,128]{1,0:T(8,128)S(1)}, u32[]{:S(2)}, u32[]{:S(2)}) %collective-permute-start.5) | collective-permute-done | bytes 4128 | tf_op jit(solution)/shard_map/ppermute | solution.py:622
  48.2 3.2 %shard_map.61 = (f32[2,512,128]{2,1,0:T(8,128)S(1)}, f32[8,64,128]{2,1,0:T(8,128)}, f32[24,128]{1,0:T(8,128)S(1)}, f32[24,128]{1,0:T(8,128)S(1)}) custom-call(f32[2,512,128]{2,1,0:T(8,128)S(1)} %get-tuple-element.57.phi, f32[2,512,128]{2,1,0:T(8,128)S(1)} %get-tuple-element.51.phi.origin, f32[6,2,64,128]{3,2,1,0:T(8,128)S(1)} %get-tuple-element.58.near, ...), custom_call_target="tpu_custom_call" | custom-call | flops 7864320 | bytes 2893824 | tf_op jit(solution)/shard_map/pallas_call | solution.py:603
  51.4 5.0 %all-to-all-start.3 = ((f32[8,64,128]{2,1,0:T(8,128)}), f32[8,64,128]{2,1,0:T(8,128)S(1)}, u32[]{:S(2)}, u32[]{:S(2)}) async-start(f32[8,64,128]{2,1,0:T(8,128)} %get-tuple-element.66), calls=%async_computation.3 | async-start | bytes 524288 | tf_op jit(solution)/shard_map/all_to_all | solution.py:620
  56.3 1.3 %collective-permute-start.6 = (f32[24,128]{1,0:T(8,128)S(1)}, f32[24,128]{1,0:T(8,128)S(1)}, u32[]{:S(2)}, u32[]{:S(2)}) collective-permute-start(f32[24,128]{1,0:T(8,128)S(1)} %get-tuple-element.67), channel_id=1, source_target_pairs={{0,8},{8,16},{16,24},{24,0},{1,9},{9,17},{17,25},{25,1},{2,10},{10... | collective-permute-start | bytes 36872 | tf_op jit(solution)/shard_map/ppermute | solution.py:621
  57.6 1.6 %collective-permute-start.7 = (f32[24,128]{1,0:T(8,128)S(1)}, f32[24,128]{1,0:T(8,128)S(1)}, u32[]{:S(2)}, u32[]{:S(2)}) collective-permute-start(f32[24,128]{1,0:T(8,128)S(1)} %get-tuple-element.68), channel_id=1, source_target_pairs={{8,0},{16,8},{24,16},{0,24},{9,1},{17,9},{25,17},{1,25},{10,2},{18... | collective-permute-start | bytes 36872 | tf_op jit(solution)/shard_map/ppermute | solution.py:622
  59.3 6.5 %shard_map.62 = (f32[6,2,192,128]{3,2,1,0:T(8,128)S(1)}, f32[3,2,256,128]{3,2,1,0:T(8,128)}) custom-call(f32[2,512,128]{2,1,0:T(8,128)S(1)} %get-tuple-element.63.phi, s32[6,256]{1,0:T(8,128)S(1)} %get-tuple-element.44.halo_code), custom_call_target="tpu_custom_call" | custom-call | flops 39321600 | bytes 2496512 | tf_op jit(solution)/shard_map/pallas_call | solution.py:603
  66.1 5.6 %shard_map.63 = (f32[2,512,128]{2,1,0:T(8,128)S(1)}, f32[8,24,128]{2,1,0:T(8,128)}, f32[8,128]{1,0:T(8,128)S(1)}, f32[8,128]{1,0:T(8,128)S(1)}) custom-call(f32[2,512,128]{2,1,0:T(8,128)S(1)} %get-tuple-element.63.phi, f32[6,2,192,128]{3,2,1,0:T(8,128)S(1)} %get-tuple-element.64.near, f32[3,2,256,128]{3,2,1,0:T(8,128)} %get-tuple-element.65.inner, ...), custom_call_target="tpu_custom_call" | custom-call | flops 39321600 | bytes 3942400 | tf_op jit(solution)/shard_map/pallas_call | solution.py:603
  71.7 4.8 %all-to-all-start.4 = ((f32[8,24,128]{2,1,0:T(8,128)}), f32[8,24,128]{2,1,0:T(8,128)S(1)}, u32[]{:S(2)}, u32[]{:S(2)}) async-start(f32[8,24,128]{2,1,0:T(8,128)} %get-tuple-element.72), calls=%async_computation.4 | async-start | bytes 196608 | tf_op jit(solution)/shard_map/all_to_all | solution.py:620
  76.9 2.5 %collective-permute-start.9 = (f32[8,128]{1,0:T(8,128)S(1)}, f32[8,128]{1,0:T(8,128)S(1)}, u32[]{:S(2)}, u32[]{:S(2)}) collective-permute-start(f32[8,128]{1,0:T(8,128)S(1)} %get-tuple-element.74), channel_id=1, source_target_pairs={{8,0},{16,8},{24,16},{0,24},{9,1},{17,9},{25,17},{1,25},{10,2},{18... | collective-permute-start | bytes 12296 | tf_op jit(solution)/shard_map/ppermute | solution.py:622
  79.4 1.9 %shard_map.64 = (f32[6,2,64,128]{3,2,1,0:T(8,128)S(1)}, f32[2,512,128]{2,1,0:T(8,128)S(1)}) custom-call(f32[2,512,128]{2,1,0:T(8,128)S(1)} %get-tuple-element.69.phi.origin, f32[2,512,128]{2,1,0:T(8,128)S(1)} %get-tuple-element.69.phi.origin, s32[6,256]{1,0:T(8,128)S(1)} %get-tuple-element.44.halo_code), custom_call_target="tpu_custom_call" | custom-call | flops 13107200 | bytes 1972224 | tf_op jit(solution)/shard_map/pallas_call | solution.py:603
  81.4 1.5 %all-to-all-done.4.arrived = f32[8,24,128]{2,1,0:T(8,128)S(1)} async-done(((f32[8,24,128]{2,1,0:T(8,128)}), f32[8,24,128]{2,1,0:T(8,128)S(1)}, u32[]{:S(2)}, u32[]{:S(2)}) %all-to-all-start.4) | async-done | bytes 98336 | tf_op jit(solution)/shard_map/all_to_all | solution.py:620
  82.8 2.0 %shard_map.65 = (f32[2,512,128]{2,1,0:T(8,128)S(1)}, f32[8,24,128]{2,1,0:T(8,128)}, f32[8,128]{1,0:T(8,128)S(1)}, f32[8,128]{1,0:T(8,128)S(1)}) custom-call(f32[2,512,128]{2,1,0:T(8,128)S(1)} %get-tuple-element.69.phi.origin, f32[2,512,128]{2,1,0:T(8,128)S(1)} %get-tuple-element.69.phi.origin, f32[6,2,64,128]{3,2,1,0:T(8,128)S(1)} %get-tuple-element.70.near, ...), custom_call_target="tpu_custom_call" | custom-call | flops 7864320 | bytes 2713600 | tf_op jit(solution)/shard_map/pallas_call | solution.py:603
  84.8 3.6 %all-to-all-start.5 = ((f32[8,24,128]{2,1,0:T(8,128)}), f32[8,24,128]{2,1,0:T(8,128)S(1)}, u32[]{:S(2)}, u32[]{:S(2)}) async-start(f32[8,24,128]{2,1,0:T(8,128)} %get-tuple-element.78), calls=%async_computation.5 | async-start | bytes 196608 | tf_op jit(solution)/shard_map/all_to_all | solution.py:620
  88.4 1.6 %collective-permute-start.10 = (f32[8,128]{1,0:T(8,128)S(1)}, f32[8,128]{1,0:T(8,128)S(1)}, u32[]{:S(2)}, u32[]{:S(2)}) collective-permute-start(f32[8,128]{1,0:T(8,128)S(1)} %get-tuple-element.79), channel_id=1, source_target_pairs={{0,8},{8,16},{16,24},{24,0},{1,9},{9,17},{17,25},{25,1},{2,10},{10... | collective-permute-start | bytes 12296 | tf_op jit(solution)/shard_map/ppermute | solution.py:621
  90.0 1.3 %collective-permute-start.11 = (f32[8,128]{1,0:T(8,128)S(1)}, f32[8,128]{1,0:T(8,128)S(1)}, u32[]{:S(2)}, u32[]{:S(2)}) collective-permute-start(f32[8,128]{1,0:T(8,128)S(1)} %get-tuple-element.80), channel_id=1, source_target_pairs={{8,0},{16,8},{24,16},{0,24},{9,1},{17,9},{25,17},{1,25},{10,2},{18... | collective-permute-start | bytes 12296 | tf_op jit(solution)/shard_map/ppermute | solution.py:622
  91.3 1.9 %shard_map.66 = (f32[6,2,64,128]{3,2,1,0:T(8,128)S(1)}, f32[2,512,128]{2,1,0:T(8,128)S(1)}) custom-call(f32[2,512,128]{2,1,0:T(8,128)S(1)} %get-tuple-element.75.phi, f32[2,512,128]{2,1,0:T(8,128)S(1)} %get-tuple-element.69.phi.origin, s32[6,256]{1,0:T(8,128)S(1)} %get-tuple-element.44.halo_code), custom_call_target="tpu_custom_call" | custom-call | flops 13107200 | bytes 1972224 | tf_op jit(solution)/shard_map/pallas_call | solution.py:603
  93.6 1.1 %all-to-all-done.5.arrived = f32[8,24,128]{2,1,0:T(8,128)S(1)} async-done(((f32[8,24,128]{2,1,0:T(8,128)}), f32[8,24,128]{2,1,0:T(8,128)S(1)}, u32[]{:S(2)}, u32[]{:S(2)}) %all-to-all-start.5) | async-done | bytes 98336 | tf_op jit(solution)/shard_map/all_to_all | solution.py:620
  94.8 1.6 %shard_map.67 = f32[512,256]{1,0:T(8,128)} custom-call(f32[2,512,128]{2,1,0:T(8,128)S(1)} %get-tuple-element.75.phi, f32[2,512,128]{2,1,0:T(8,128)S(1)} %get-tuple-element.69.phi.origin, f32[6,2,64,128]{3,2,1,0:T(8,128)S(1)} %get-tuple-element.76.near, f32[2,512,128]{2,1,0:T(8,128)S(1)} %get-tuple-element.77.inner, ...), custom_call_target="tpu_custom_call" | custom-call | flops 7864320 | bytes 2607104 | tf_op jit(solution)/shard_map/pallas_call | solution.py:603
  (17 shorter events, 2.4 us)
Async XLA Ops:
  3.4 16.1 %all-to-all-start = ((f32[8,64,128]{2,1,0:T(8,128)}), f32[8,64,128]{2,1,0:T(8,128)S(1)}, u32[]{:S(2)}, u32[]{:S(2)}) async-start(f32[8,64,128]{2,1,0:T(8,128)} %get-tuple-element.47), calls=%async_computation | async-start | bytes 524288 | tf_op jit(solution)/shard_map/all_to_all | solution.py:620
  9.8 9.4 %collective-permute-start = (f32[24,128]{1,0:T(8,128)S(1)}, f32[24,128]{1,0:T(8,128)S(1)}, u32[]{:S(2)}, u32[]{:S(2)}) collective-permute-start(f32[24,128]{1,0:T(8,128)S(1)} %get-tuple-element.48), channel_id=1, source_target_pairs={{0,8},{8,16},{16,24},{24,0},{1,9},{9,17},{17,25},{25,1},{2,10},{10... | collective-permute-start | bytes 36872 | tf_op jit(solution)/shard_map/ppermute | solution.py:621
  11.2 7.9 %collective-permute-start.1 = (f32[24,128]{1,0:T(8,128)S(1)}, f32[24,128]{1,0:T(8,128)S(1)}, u32[]{:S(2)}, u32[]{:S(2)}) collective-permute-start(f32[24,128]{1,0:T(8,128)S(1)} %get-tuple-element.49), channel_id=1, source_target_pairs={{8,0},{16,8},{24,16},{0,24},{9,1},{17,9},{25,17},{1,25},{10,2},{18... | collective-permute-start | bytes 36872 | tf_op jit(solution)/shard_map/ppermute | solution.py:622
  25.1 11.2 %all-to-all-start.1 = ((f32[8,24,128]{2,1,0:T(8,128)}), f32[8,24,128]{2,1,0:T(8,128)S(1)}, u32[]{:S(2)}, u32[]{:S(2)}) async-start(f32[8,24,128]{2,1,0:T(8,128)} %get-tuple-element.54), calls=%async_computation.1 | async-start | bytes 196608 | tf_op jit(solution)/shard_map/all_to_all | solution.py:620
  29.9 4.9 %collective-permute-start.2 = (f32[8,128]{1,0:T(8,128)S(1)}, f32[8,128]{1,0:T(8,128)S(1)}, u32[]{:S(2)}, u32[]{:S(2)}) collective-permute-start(f32[8,128]{1,0:T(8,128)S(1)} %get-tuple-element.55), channel_id=1, source_target_pairs={{0,8},{8,16},{16,24},{24,0},{1,9},{9,17},{17,25},{25,1},{2,10},{10... | collective-permute-start | bytes 12296 | tf_op jit(solution)/shard_map/ppermute | solution.py:621
  30.5 4.3 %collective-permute-start.3 = (f32[8,128]{1,0:T(8,128)S(1)}, f32[8,128]{1,0:T(8,128)S(1)}, u32[]{:S(2)}, u32[]{:S(2)}) collective-permute-start(f32[8,128]{1,0:T(8,128)S(1)} %get-tuple-element.56), channel_id=1, source_target_pairs={{8,0},{16,8},{24,16},{0,24},{9,1},{17,9},{25,17},{1,25},{10,2},{18... | collective-permute-start | bytes 12296 | tf_op jit(solution)/shard_map/ppermute | solution.py:622
  38.2 10.0 %all-to-all-start.2 = ((f32[8,24,128]{2,1,0:T(8,128)}), f32[8,24,128]{2,1,0:T(8,128)S(1)}, u32[]{:S(2)}, u32[]{:S(2)}) async-start(f32[8,24,128]{2,1,0:T(8,128)} %get-tuple-element.60), calls=%async_computation.2 | async-start | bytes 196608 | tf_op jit(solution)/shard_map/all_to_all | solution.py:620
  41.9 4.9 %collective-permute-start.4 = (f32[8,128]{1,0:T(8,128)S(1)}, f32[8,128]{1,0:T(8,128)S(1)}, u32[]{:S(2)}, u32[]{:S(2)}) collective-permute-start(f32[8,128]{1,0:T(8,128)S(1)} %get-tuple-element.61), channel_id=1, source_target_pairs={{0,8},{8,16},{16,24},{24,0},{1,9},{9,17},{17,25},{25,1},{2,10},{10... | collective-permute-start | bytes 12296 | tf_op jit(solution)/shard_map/ppermute | solution.py:621
  44.5 3.6 %collective-permute-start.5 = (f32[8,128]{1,0:T(8,128)S(1)}, f32[8,128]{1,0:T(8,128)S(1)}, u32[]{:S(2)}, u32[]{:S(2)}) collective-permute-start(f32[8,128]{1,0:T(8,128)S(1)} %get-tuple-element.62), channel_id=1, source_target_pairs={{8,0},{16,8},{24,16},{0,24},{9,1},{17,9},{25,17},{1,25},{10,2},{18... | collective-permute-start | bytes 12296 | tf_op jit(solution)/shard_map/ppermute | solution.py:622
  51.4 14.7 %all-to-all-start.3 = ((f32[8,64,128]{2,1,0:T(8,128)}), f32[8,64,128]{2,1,0:T(8,128)S(1)}, u32[]{:S(2)}, u32[]{:S(2)}) async-start(f32[8,64,128]{2,1,0:T(8,128)} %get-tuple-element.66), calls=%async_computation.3 | async-start | bytes 524288 | tf_op jit(solution)/shard_map/all_to_all | solution.py:620
  56.3 9.4 %collective-permute-start.6 = (f32[24,128]{1,0:T(8,128)S(1)}, f32[24,128]{1,0:T(8,128)S(1)}, u32[]{:S(2)}, u32[]{:S(2)}) collective-permute-start(f32[24,128]{1,0:T(8,128)S(1)} %get-tuple-element.67), channel_id=1, source_target_pairs={{0,8},{8,16},{16,24},{24,0},{1,9},{9,17},{17,25},{25,1},{2,10},{10... | collective-permute-start | bytes 36872 | tf_op jit(solution)/shard_map/ppermute | solution.py:621
  57.6 8.2 %collective-permute-start.7 = (f32[24,128]{1,0:T(8,128)S(1)}, f32[24,128]{1,0:T(8,128)S(1)}, u32[]{:S(2)}, u32[]{:S(2)}) collective-permute-start(f32[24,128]{1,0:T(8,128)S(1)} %get-tuple-element.68), channel_id=1, source_target_pairs={{8,0},{16,8},{24,16},{0,24},{9,1},{17,9},{25,17},{1,25},{10,2},{18... | collective-permute-start | bytes 36872 | tf_op jit(solution)/shard_map/ppermute | solution.py:622
  71.7 11.2 %all-to-all-start.4 = ((f32[8,24,128]{2,1,0:T(8,128)}), f32[8,24,128]{2,1,0:T(8,128)S(1)}, u32[]{:S(2)}, u32[]{:S(2)}) async-start(f32[8,24,128]{2,1,0:T(8,128)} %get-tuple-element.72), calls=%async_computation.4 | async-start | bytes 196608 | tf_op jit(solution)/shard_map/all_to_all | solution.py:620
  76.5 4.9 %collective-permute-start.8 = (f32[8,128]{1,0:T(8,128)S(1)}, f32[8,128]{1,0:T(8,128)S(1)}, u32[]{:S(2)}, u32[]{:S(2)}) collective-permute-start(f32[8,128]{1,0:T(8,128)S(1)} %get-tuple-element.73), channel_id=1, source_target_pairs={{0,8},{8,16},{16,24},{24,0},{1,9},{9,17},{17,25},{25,1},{2,10},{10... | collective-permute-start | bytes 12296 | tf_op jit(solution)/shard_map/ppermute | solution.py:621
  76.9 4.5 %collective-permute-start.9 = (f32[8,128]{1,0:T(8,128)S(1)}, f32[8,128]{1,0:T(8,128)S(1)}, u32[]{:S(2)}, u32[]{:S(2)}) collective-permute-start(f32[8,128]{1,0:T(8,128)S(1)} %get-tuple-element.74), channel_id=1, source_target_pairs={{8,0},{16,8},{24,16},{0,24},{9,1},{17,9},{25,17},{1,25},{10,2},{18... | collective-permute-start | bytes 12296 | tf_op jit(solution)/shard_map/ppermute | solution.py:622
  84.8 10.0 %all-to-all-start.5 = ((f32[8,24,128]{2,1,0:T(8,128)}), f32[8,24,128]{2,1,0:T(8,128)S(1)}, u32[]{:S(2)}, u32[]{:S(2)}) async-start(f32[8,24,128]{2,1,0:T(8,128)} %get-tuple-element.78), calls=%async_computation.5 | async-start | bytes 196608 | tf_op jit(solution)/shard_map/all_to_all | solution.py:620
  88.4 4.9 %collective-permute-start.10 = (f32[8,128]{1,0:T(8,128)S(1)}, f32[8,128]{1,0:T(8,128)S(1)}, u32[]{:S(2)}, u32[]{:S(2)}) collective-permute-start(f32[8,128]{1,0:T(8,128)S(1)} %get-tuple-element.79), channel_id=1, source_target_pairs={{0,8},{8,16},{16,24},{24,0},{1,9},{9,17},{17,25},{25,1},{2,10},{10... | collective-permute-start | bytes 12296 | tf_op jit(solution)/shard_map/ppermute | solution.py:621
  90.0 3.6 %collective-permute-start.11 = (f32[8,128]{1,0:T(8,128)S(1)}, f32[8,128]{1,0:T(8,128)S(1)}, u32[]{:S(2)}, u32[]{:S(2)}) collective-permute-start(f32[8,128]{1,0:T(8,128)S(1)} %get-tuple-element.80), channel_id=1, source_target_pairs={{8,0},{16,8},{24,16},{0,24},{9,1},{17,9},{25,17},{1,25},{10,2},{18... | collective-permute-start | bytes 12296 | tf_op jit(solution)/shard_map/ppermute | solution.py:622
